TPU v7x, 256 devices: a whole 4x4x8 slice. The times are simulated.
256 devices in a mesh: grp: 8 (over z_hi, core), dev: 32 (over y, z_lo, x).
Axes of the slice: x: 4, y: 4, z: 8 (z_hi: 4, z_lo: 2; z = z_hi * 2 + z_lo), core: 2. Of those that a mesh axis runs over, the one named last changes fastest.
Arguments:
- forcing: float32 [4, 32, 512, 256], P(None, 'grp', 'dev'), may hold values from -6 to 6
- viscosity: float32 [32, 512, 256], P('grp', 'dev'), may hold values from 0.0316 to 31.6
Outputs:
- solution: float32 [4, 32, 512, 256], P(None, 'grp', 'dev')
- final_residual: float32 [4, 32, 512, 256], P(None, 'grp', 'dev')
All inputs are finite; a program needn't handle non-finite values.
Results may differ from a plain program's by a relative error of at most 0.00002.
Values sent between devices are 32-bit elements; how exact they have to be, the bound alone decides.
No kernel may reach another device: no remote copies, remote signals or barrier semaphores. Data moves between devices by JAX's collectives and lax.ppermute only.
A program may use at most 64 MiB of HBM per device.

v0:
```python
import jax
import jax.numpy as jnp
from jax import lax
from jax.sharding import PartitionSpec as P

NU = 2
COARSE = 6


OMEGA = 0.6
BETA = 0.25


def extended_2(value, sides, width):
    for axis, dim in sides:
        peers, length = (lax.axis_size(axis), value.shape[dim])
        up = [(i, (i + 1) % peers) for i in range(peers - 1)]
        down = [(j, i) for i, j in up]
        last = lax.slice_in_dim(value, length - width, length, axis=dim)
        leading = lax.slice_in_dim(value, 0, width, axis=dim)
        before = lax.ppermute(last, axis, up)
        after = lax.ppermute(leading, axis, down)
        value = jnp.concatenate([before, value, after], axis=dim)
    return value


def pad_split(array):
    extended = extended_2(array, (("grp", 1), ("dev", 2)), 1)
    return jnp.pad(extended, ((0, 0), (0, 0), (0, 0), (1, 1)))


def pad_group(array):
    extended = extended_2(array, (("dev", 2),), 1)
    return jnp.pad(extended, ((0, 0), (1, 1), (0, 0), (1, 1)))


def neighbours_of(padded):
    return [
        padded[:, 2:, 1:-1, 1:-1],
        padded[:, :-2, 1:-1, 1:-1],
        padded[:, 1:-1, 2:, 1:-1],
        padded[:, 1:-1, :-2, 1:-1],
        padded[:, 1:-1, 1:-1, 2:],
        padded[:, 1:-1, 1:-1, :-2],
    ]


def prepare(viscous, spacing, pad_rule):
    neighbours = neighbours_of(pad_rule(viscous))
    faces = [(viscous + other) * 0.5 for other in neighbours]
    total = faces[0]
    for face in faces[1:]:
        total = total + face
    diagonal = total / (spacing * spacing)
    weight = jnp.concatenate(
        [jnp.broadcast_to(OMEGA / diagonal, (3,) + diagonal.shape[1:]), BETA * viscous], axis=0
    )
    return (faces, weight)


def operate(field, faces, spacing, padded):
    neighbours = neighbours_of(padded)
    total = faces[0] * (field[:3] - neighbours[0][:3])
    for index in range(1, 6):
        total = total + faces[index] * (field[:3] - neighbours[index][:3])
    gradient = jnp.concatenate(
        [
            neighbours[0][3:4] - neighbours[1][3:4],
            neighbours[2][3:4] - neighbours[3][3:4],
            neighbours[4][3:4] - neighbours[5][3:4],
        ],
        axis=0,
    )
    velocity = total / (spacing * spacing) + gradient / (2.0 * spacing)
    divergence = (
        neighbours[0][0:1]
        - neighbours[1][0:1]
        + (neighbours[2][1:2] - neighbours[3][1:2])
        + (neighbours[4][2:3] - neighbours[5][2:3])
    )
    return jnp.concatenate([velocity, divergence / (2.0 * spacing)], axis=0)


def residual_of(source, field, faces, spacing, pad_rule):
    return source - operate(field, faces, spacing, pad_rule(field))


def smooth(source, field, faces, weight, spacing, pad_rule, count):
    for sweep in range(count):
        field = field + weight * residual_of(source, field, faces, spacing, pad_rule)
    return field


def restrict(array):
    comps, xsize, ysize, zsize = array.shape
    return array.reshape(comps, xsize // 2, 2, ysize // 2, 2, zsize // 2, 2).mean(axis=(2, 4, 6))


def prolong(array):
    return jnp.repeat(jnp.repeat(jnp.repeat(array, 2, axis=1), 2, axis=2), 2, axis=3)


def bottom_level(source_low, viscous_low):
    faces_low, weight_low = prepare(viscous_low, 4.0, pad_group)
    update_low = weight_low * source_low
    return smooth(source_low, update_low, faces_low, weight_low, 4.0, pad_group, COARSE - 1)


def gathered_bottom(source_low, viscous_low):
    row_count = source_low.shape[1]
    whole_source, whole_viscous = (
        lax.all_gather(source_low, "grp", axis=1, tiled=True),
        lax.all_gather(viscous_low, "grp", axis=1, tiled=True),
    )
    update_low = bottom_level(whole_source, whole_viscous)
    return lax.dynamic_slice_in_dim(update_low, lax.axis_index("grp") * row_count, row_count, 1)


def middle_level(source_mid, viscous_mid, pad_rule, descend):
    faces_mid, weight_mid = prepare(viscous_mid, 2.0, pad_rule)
    update_mid = weight_mid * source_mid
    update_mid = smooth(source_mid, update_mid, faces_mid, weight_mid, 2.0, pad_rule, NU - 1)
    source_low = restrict(residual_of(source_mid, update_mid, faces_mid, 2.0, pad_rule))
    update_low = descend(source_low, restrict(viscous_mid))
    update_mid = update_mid + prolong(update_low)
    return smooth(source_mid, update_mid, faces_mid, weight_mid, 2.0, pad_rule, NU)


def local(forcing, viscosity):
    viscous = viscosity[None]
    faces_fine, weight_fine = prepare(viscous, 1.0, pad_split)
    field = weight_fine * forcing
    field = smooth(forcing, field, faces_fine, weight_fine, 1.0, pad_split, NU - 1)
    source_mid = restrict(residual_of(forcing, field, faces_fine, 1.0, pad_split))
    viscous_mid = restrict(viscous)
    update_mid = middle_level(source_mid, viscous_mid, pad_split, gathered_bottom)
    field = field + prolong(update_mid)
    field = smooth(forcing, field, faces_fine, weight_fine, 1.0, pad_split, NU)
    return (field, residual_of(forcing, field, faces_fine, 1.0, pad_split))


def solution(mesh):
    in_specs = (P(None, "grp", "dev", None), P("grp", "dev", None))
    out_specs = (P(None, "grp", "dev", None), P(None, "grp", "dev", None))
    return jax.shard_map(local, mesh=mesh, in_specs=in_specs, out_specs=out_specs, check_vma=False)
```

profile of v0, /device:TPU:152, one launch (start us, length us, event | category | flops | bytes accessed | tf_op | source)
XLA Modules:
  0.0 342.6 jit_solution(16453993961961562359)
XLA Ops:
  3.3 2.5 collective-permute-start.1
  5.9 6.3 %reshape_broadcast_in_dim.3 = f32[2,2,8,2,128,2]{5,4,3,2,1,0:T(8,128)} reshape(f32[4,16,256]{2,1,0:T(8,128)} %param.3) | data formatting | bytes 131072 | tf_op jit(solution)/shard_map/reshape;broadcast_in_dim | solution.py:96
  12.1 2.5 reduce_sum.39
  14.7 5.3 %collective-permute-start.8 = (f32[1,1,8,128]{3,2,1,0:T(8,128)S(1)}, f32[1,1,8,128]{3,2,1,0:T(8,128)S(1)}, u32[]{:S(2)}, u32[]{:S(2)}) collective-permute-start(f32[1,1,8,128]{3,2,1,0:T(8,128)S(1)} %get-tuple-element.162), channel_id=1, source_target_pairs={{32,0},{64,32},{96,64},{128,96},{160,128},{192,160},{224,192},{33,... | collective-permute-start | bytes 12296 | tf_op jit(solution)/shard_map/ppermute | solution.py:22
  22.3 5.3 %collective-permute-start.2 = (f32[1,6,1,256]{3,2,1,0:T(1,128)S(1)}, f32[1,6,1,256]{3,2,1,0:T(1,128)S(1)}, u32[]{:S(2)}, u32[]{:S(2)}) collective-permute-start(f32[1,6,1,256]{3,2,1,0:T(1,128)S(1)} %get-tuple-element.100), channel_id=1, source_target_pairs={{1,0},{2,1},{3,2},{4,3},{5,4},{6,5},{7,6},{8,7},{9,8},{10,9},{11,1... | collective-permute-start | bytes 18440 | tf_op jit(solution)/shard_map/ppermute | solution.py:22
  29.5 13.4 %all-gather.2 = f32[8,4,64]{2,1,0:T(4,128)S(1)} all-gather(f32[1,4,64]{2,1,0:T(4,128)S(1)} %multiply_bitcast_fusion.3), channel_id=2, replica_groups=mesh['grp'=8,'dev'=32] {'grp'}, dimensions={0}, use_global_device_ids=true | all-gather | bytes 9216 | tf_op jit(solution)/shard_map/all_gather | solution.py:113
  43.3 3.0 collective-permute-start.4
  48.2 6.9 %collective-permute-start.10 = (f32[1,4,1,128]{3,2,1,0:T(1,128)S(1)}, f32[1,4,1,128]{3,2,1,0:T(1,128)S(1)}, u32[]{:S(2)}, u32[]{:S(2)}) collective-permute-start(f32[1,4,1,128]{3,2,1,0:T(1,128)S(1)} %get-tuple-element.155), channel_id=1, source_target_pairs={{1,0},{2,1},{3,2},{4,3},{5,4},{6,5},{7,6},{8,7},{9,8},{10,9},{11,1... | collective-permute-start | bytes 6152 | tf_op jit(solution)/shard_map/ppermute | solution.py:22
  57.2 6.9 %collective-permute-start.6 = (f32[4,6,1,256]{3,0,2,1:T(4,128)S(1)}, f32[4,6,1,256]{3,0,2,1:T(4,128)S(1)}, u32[]{:S(2)}, u32[]{:S(2)}) collective-permute-start(f32[4,6,1,256]{3,0,2,1:T(4,128)S(1)} %copy.1240), channel_id=1, source_target_pairs={{1,0},{2,1},{3,2},{4,3},{5,4},{6,5},{7,6},{8,7},{9,8},{10,9},{11,1... | collective-permute-start | bytes 73736 | tf_op jit(solution)/shard_map/ppermute | solution.py:22
  66.2 6.9 %collective-permute-done.7 = f32[4,6,1,256]{3,0,2,1:T(4,128)S(1)} collective-permute-done((f32[4,6,1,256]{3,0,2,1:T(4,128)S(1)}, f32[4,6,1,256]{3,0,2,1:T(4,128)S(1)}, u32[]{:S(2)}, u32[]{:S(2)}) %collective-permute-start.7) | collective-permute-done | bytes 24608 | tf_op jit(solution)/shard_map/ppermute | solution.py:21
  74.1 3.6 %collective-permute-start.12 = (f32[4,1,16,256]{3,2,1,0:T(8,128)S(1)}, f32[4,1,16,256]{3,2,1,0:T(8,128)S(1)}, u32[]{:S(2)}, u32[]{:S(2)}) collective-permute-start(f32[4,1,16,256]{3,2,1,0:T(8,128)S(1)} %get-tuple-element.73), channel_id=1, source_target_pairs={{32,0},{64,32},{96,64},{128,96},{160,128},{192,160},{224,192},{33,... | collective-permute-start | bytes 196616 | tf_op jit(solution)/shard_map/ppermute | solution.py:22
  79.8 5.6 %collective-permute-done.13 = f32[4,1,16,256]{3,2,1,0:T(8,128)S(1)} collective-permute-done((f32[4,1,16,256]{3,2,1,0:T(8,128)S(1)}, f32[4,1,16,256]{3,2,1,0:T(8,128)S(1)}, u32[]{:S(2)}, u32[]{:S(2)}) %collective-permute-start.13) | collective-permute-done | bytes 65568 | tf_op jit(solution)/shard_map/ppermute | solution.py:21
  87.4 4.1 %collective-permute-start.15 = (f32[4,6,1,256]{3,0,2,1:T(4,128)S(1)}, f32[4,6,1,256]{3,0,2,1:T(4,128)S(1)}, u32[]{:S(2)}, u32[]{:S(2)}) collective-permute-start(f32[4,6,1,256]{3,0,2,1:T(4,128)S(1)} %copy.1248), channel_id=1, source_target_pairs={{0,1},{1,2},{2,3},{3,4},{4,5},{5,6},{6,7},{7,8},{8,9},{9,10},{10,1... | collective-permute-start | bytes 73736 | tf_op jit(solution)/shard_map/ppermute | solution.py:21
  91.7 4.5 %collective-permute-done.15 = f32[4,6,1,256]{3,0,2,1:T(4,128)S(1)} collective-permute-done((f32[4,6,1,256]{3,0,2,1:T(4,128)S(1)}, f32[4,6,1,256]{3,0,2,1:T(4,128)S(1)}, u32[]{:S(2)}, u32[]{:S(2)}) %collective-permute-start.15) | collective-permute-done | bytes 24608 | tf_op jit(solution)/shard_map/ppermute | solution.py:21
  97.2 4.7 %copy.1252 = f32[4,4,16,256]{0,3,2,1:T(8,128)} copy(f32[4,4,16,256]{3,2,1,0:T(8,128)S(1)} %maximum_subtract_fusion.1) | data formatting | bytes 524288 | tf_op jit(solution)/shard_map/sub | solution.py:85
  101.9 8.7 %reduce_sum.43 = f32[4,2,8,128]{0,3,2,1:T(8,128)S(1)} reduce(f32[4,2,2,8,2,128,2]{0,6,5,4,3,2,1:T(2,128)} %bitcast.73, f32[]{:T(128)} %constant.77.clone.1), dimensions={2,4,6}, to_apply=%region_1.2 | reduce | flops 57344 | bytes 294916 | tf_op jit(solution)/shard_map/reduce_sum | solution.py:96
  112.8 2.4 collective-permute-start.17
  117.2 6.9 %collective-permute-start.21 = (f32[1,8,1,64]{3,2,1,0:T(1,128)S(1)}, f32[1,8,1,64]{3,2,1,0:T(1,128)S(1)}, u32[]{:S(2)}, u32[]{:S(2)}) collective-permute-start(f32[1,8,1,64]{3,2,1,0:T(1,128)S(1)} %get-tuple-element.151), channel_id=1, source_target_pairs={{1,0},{2,1},{3,2},{4,3},{5,4},{6,5},{7,6},{8,7},{9,8},{10,9},{11,1... | collective-permute-start | bytes 6152 | tf_op jit(solution)/shard_map/ppermute | solution.py:22
  126.1 3.9 %collective-permute-start.19 = (f32[4,4,1,128]{3,2,1,0:T(1,128)S(1)}, f32[4,4,1,128]{3,2,1,0:T(1,128)S(1)}, u32[]{:S(2)}, u32[]{:S(2)}) collective-permute-start(f32[4,4,1,128]{3,2,1,0:T(1,128)S(1)} %get-tuple-element.130), channel_id=1, source_target_pairs={{0,1},{1,2},{2,3},{3,4},{4,5},{5,6},{6,7},{7,8},{8,9},{9,10},{10,1... | collective-permute-start | bytes 24584 | tf_op jit(solution)/shard_map/ppermute | solution.py:21
  130.1 4.6 %collective-permute-done.19 = f32[4,4,1,128]{3,2,1,0:T(1,128)S(1)} collective-permute-done((f32[4,4,1,128]{3,2,1,0:T(1,128)S(1)}, f32[4,4,1,128]{3,2,1,0:T(1,128)S(1)}, u32[]{:S(2)}, u32[]{:S(2)}) %collective-permute-start.19) | collective-permute-done | bytes 8224 | tf_op jit(solution)/shard_map/ppermute | solution.py:21
  135.1 3.6 %collective-permute-start.22 = (f32[4,1,8,128]{3,2,1,0:T(8,128)S(1)}, f32[4,1,8,128]{3,2,1,0:T(8,128)S(1)}, u32[]{:S(2)}, u32[]{:S(2)}) collective-permute-start(f32[4,1,8,128]{3,2,1,0:T(8,128)S(1)} %get-tuple-element.144), channel_id=1, source_target_pairs={{32,0},{64,32},{96,64},{128,96},{160,128},{192,160},{224,192},{33,... | collective-permute-start | bytes 49160 | tf_op jit(solution)/shard_map/ppermute | solution.py:22
  140.7 5.1 %collective-permute-done.23 = f32[4,1,8,128]{3,2,1,0:T(8,128)S(1)} collective-permute-done((f32[4,1,8,128]{3,2,1,0:T(8,128)S(1)}, f32[4,1,8,128]{3,2,1,0:T(8,128)S(1)}, u32[]{:S(2)}, u32[]{:S(2)}) %collective-permute-start.23) | collective-permute-done | bytes 16416 | tf_op jit(solution)/shard_map/ppermute | solution.py:21
  147.8 3.9 %collective-permute-start.25 = (f32[4,4,1,128]{3,2,1,0:T(1,128)S(1)}, f32[4,4,1,128]{3,2,1,0:T(1,128)S(1)}, u32[]{:S(2)}, u32[]{:S(2)}) collective-permute-start(f32[4,4,1,128]{3,2,1,0:T(1,128)S(1)} %get-tuple-element.125), channel_id=1, source_target_pairs={{0,1},{1,2},{2,3},{3,4},{4,5},{5,6},{6,7},{7,8},{8,9},{9,10},{10,1... | collective-permute-start | bytes 24584 | tf_op jit(solution)/shard_map/ppermute | solution.py:21
  151.8 4.5 %collective-permute-done.25 = f32[4,4,1,128]{3,2,1,0:T(1,128)S(1)} collective-permute-done((f32[4,4,1,128]{3,2,1,0:T(1,128)S(1)}, f32[4,4,1,128]{3,2,1,0:T(1,128)S(1)}, u32[]{:S(2)}, u32[]{:S(2)}) %collective-permute-start.25) | collective-permute-done | bytes 8224 | tf_op jit(solution)/shard_map/ppermute | solution.py:21
  157.5 14.5 %all-gather.1 = f32[4,32,64]{2,0,1:T(4,128)S(1)} all-gather(f32[4,4,64]{2,0,1:T(4,128)S(1)} %copy.1256), channel_id=3, replica_groups=mesh['grp'=8,'dev'=32] {'grp'}, dimensions={1}, use_global_device_ids=true | all-gather | bytes 36864 | tf_op jit(solution)/shard_map/all_gather | solution.py:112
  174.1 6.9 %collective-permute-start.27 = (f32[4,8,1,64]{3,2,1,0:T(1,128)S(1)}, f32[4,8,1,64]{3,2,1,0:T(1,128)S(1)}, u32[]{:S(2)}, u32[]{:S(2)}) collective-permute-start(f32[4,8,1,64]{3,2,1,0:T(1,128)S(1)} %get-tuple-element.122), channel_id=1, source_target_pairs={{1,0},{2,1},{3,2},{4,3},{5,4},{6,5},{7,6},{8,7},{9,8},{10,9},{11,1... | collective-permute-start | bytes 24584 | tf_op jit(solution)/shard_map/ppermute | solution.py:22
  184.9 7.2 %collective-permute-start.29 = (f32[4,8,1,64]{3,2,1,0:T(1,128)S(1)}, f32[4,8,1,64]{3,2,1,0:T(1,128)S(1)}, u32[]{:S(2)}, u32[]{:S(2)}) collective-permute-start(f32[4,8,1,64]{3,2,1,0:T(1,128)S(1)} %get-tuple-element.120), channel_id=1, source_target_pairs={{1,0},{2,1},{3,2},{4,3},{5,4},{6,5},{7,6},{8,7},{9,8},{10,9},{11,1... | collective-permute-start | bytes 24584 | tf_op jit(solution)/shard_map/ppermute | solution.py:22
  196.1 7.2 %collective-permute-start.31 = (f32[4,8,1,64]{3,2,1,0:T(1,128)S(1)}, f32[4,8,1,64]{3,2,1,0:T(1,128)S(1)}, u32[]{:S(2)}, u32[]{:S(2)}) collective-permute-start(f32[4,8,1,64]{3,2,1,0:T(1,128)S(1)} %get-tuple-element.118), channel_id=1, source_target_pairs={{1,0},{2,1},{3,2},{4,3},{5,4},{6,5},{7,6},{8,7},{9,8},{10,9},{11,1... | collective-permute-start | bytes 24584 | tf_op jit(solution)/shard_map/ppermute | solution.py:22
  207.2 7.4 %collective-permute-start.33 = (f32[4,8,1,64]{3,2,1,0:T(1,128)S(1)}, f32[4,8,1,64]{3,2,1,0:T(1,128)S(1)}, u32[]{:S(2)}, u32[]{:S(2)}) collective-permute-start(f32[4,8,1,64]{3,2,1,0:T(1,128)S(1)} %get-tuple-element.116), channel_id=1, source_target_pairs={{1,0},{2,1},{3,2},{4,3},{5,4},{6,5},{7,6},{8,7},{9,8},{10,9},{11,1... | collective-permute-start | bytes 24584 | tf_op jit(solution)/shard_map/ppermute | solution.py:22
  218.3 7.2 %collective-permute-start.35 = (f32[4,8,1,64]{3,2,1,0:T(1,128)S(1)}, f32[4,8,1,64]{3,2,1,0:T(1,128)S(1)}, u32[]{:S(2)}, u32[]{:S(2)}) collective-permute-start(f32[4,8,1,64]{3,2,1,0:T(1,128)S(1)} %get-tuple-element.114), channel_id=1, source_target_pairs={{1,0},{2,1},{3,2},{4,3},{5,4},{6,5},{7,6},{8,7},{9,8},{10,9},{11,1... | collective-permute-start | bytes 24584 | tf_op jit(solution)/shard_map/ppermute | solution.py:22
  229.7 2.4 collective-permute-start.37
  232.1 4.7 %collective-permute-done.37 = f32[4,1,8,128]{3,2,1,0:T(8,128)S(1)} collective-permute-done((f32[4,1,8,128]{3,2,1,0:T(8,128)S(1)}, f32[4,1,8,128]{3,2,1,0:T(8,128)S(1)}, u32[]{:S(2)}, u32[]{:S(2)}) %collective-permute-start.37) | collective-permute-done | bytes 16416 | tf_op jit(solution)/shard_map/ppermute | solution.py:21
  236.9 7.2 %collective-permute-start.38 = (f32[4,4,1,128]{3,2,1,0:T(1,128)S(1)}, f32[4,4,1,128]{3,2,1,0:T(1,128)S(1)}, u32[]{:S(2)}, u32[]{:S(2)}) collective-permute-start(f32[4,4,1,128]{3,2,1,0:T(1,128)S(1)} %get-tuple-element.112), channel_id=1, source_target_pairs={{1,0},{2,1},{3,2},{4,3},{5,4},{6,5},{7,6},{8,7},{9,8},{10,9},{11,1... | collective-permute-start | bytes 24584 | tf_op jit(solution)/shard_map/ppermute | solution.py:22
  246.0 6.6 %collective-permute-done.39 = f32[4,4,1,128]{3,2,1,0:T(1,128)S(1)} collective-permute-done((f32[4,4,1,128]{3,2,1,0:T(1,128)S(1)}, f32[4,4,1,128]{3,2,1,0:T(1,128)S(1)}, u32[]{:S(2)}, u32[]{:S(2)}) %collective-permute-start.39) | collective-permute-done | bytes 8224 | tf_op jit(solution)/shard_map/ppermute | solution.py:21
  255.0 2.4 collective-permute-start.41
  257.4 4.7 %collective-permute-done.41 = f32[4,1,8,128]{3,2,1,0:T(8,128)S(1)} collective-permute-done((f32[4,1,8,128]{3,2,1,0:T(8,128)S(1)}, f32[4,1,8,128]{3,2,1,0:T(8,128)S(1)}, u32[]{:S(2)}, u32[]{:S(2)}) %collective-permute-start.41) | collective-permute-done | bytes 16416 | tf_op jit(solution)/shard_map/ppermute | solution.py:21
  264.1 3.9 %collective-permute-start.43 = (f32[4,4,1,128]{3,2,1,0:T(1,128)S(1)}, f32[4,4,1,128]{3,2,1,0:T(1,128)S(1)}, u32[]{:S(2)}, u32[]{:S(2)}) collective-permute-start(f32[4,4,1,128]{3,2,1,0:T(1,128)S(1)} %get-tuple-element.107), channel_id=1, source_target_pairs={{0,1},{1,2},{2,3},{3,4},{4,5},{5,6},{6,7},{7,8},{8,9},{9,10},{10,1... | collective-permute-start | bytes 24584 | tf_op jit(solution)/shard_map/ppermute | solution.py:21
  268.1 4.6 %collective-permute-done.43 = f32[4,4,1,128]{3,2,1,0:T(1,128)S(1)} collective-permute-done((f32[4,4,1,128]{3,2,1,0:T(1,128)S(1)}, f32[4,4,1,128]{3,2,1,0:T(1,128)S(1)}, u32[]{:S(2)}, u32[]{:S(2)}) %collective-permute-start.43) | collective-permute-done | bytes 8224 | tf_op jit(solution)/shard_map/ppermute | solution.py:21
  279.0 2.4 collective-permute-start.45
  281.4 5.3 %collective-permute-done.45 = f32[4,1,16,256]{3,2,1,0:T(8,128)S(1)} collective-permute-done((f32[4,1,16,256]{3,2,1,0:T(8,128)S(1)}, f32[4,1,16,256]{3,2,1,0:T(8,128)S(1)}, u32[]{:S(2)}, u32[]{:S(2)}) %collective-permute-start.45) | collective-permute-done | bytes 65568 | tf_op jit(solution)/shard_map/ppermute | solution.py:21
  288.7 3.9 %collective-permute-start.47 = (f32[4,6,1,256]{3,0,2,1:T(4,128)S(1)}, f32[4,6,1,256]{3,0,2,1:T(4,128)S(1)}, u32[]{:S(2)}, u32[]{:S(2)}) collective-permute-start(f32[4,6,1,256]{3,0,2,1:T(4,128)S(1)} %copy.1264), channel_id=1, source_target_pairs={{0,1},{1,2},{2,3},{3,4},{4,5},{5,6},{6,7},{7,8},{8,9},{9,10},{10,1... | collective-permute-start | bytes 73736 | tf_op jit(solution)/shard_map/ppermute | solution.py:21
  292.7 5.4 %collective-permute-done.47 = f32[4,6,1,256]{3,0,2,1:T(4,128)S(1)} collective-permute-done((f32[4,6,1,256]{3,0,2,1:T(4,128)S(1)}, f32[4,6,1,256]{3,0,2,1:T(4,128)S(1)}, u32[]{:S(2)}, u32[]{:S(2)}) %collective-permute-start.47) | collective-permute-done | bytes 24608 | tf_op jit(solution)/shard_map/ppermute | solution.py:21
  303.5 5.3 %collective-permute-done.49 = f32[4,1,16,256]{3,2,1,0:T(8,128)S(1)} collective-permute-done((f32[4,1,16,256]{3,2,1,0:T(8,128)S(1)}, f32[4,1,16,256]{3,2,1,0:T(8,128)S(1)}, u32[]{:S(2)}, u32[]{:S(2)}) %collective-permute-start.49) | collective-permute-done | bytes 65568 | tf_op jit(solution)/shard_map/ppermute | solution.py:21
  310.7 3.9 %collective-permute-start.51 = (f32[4,6,1,256]{3,0,2,1:T(4,128)S(1)}, f32[4,6,1,256]{3,0,2,1:T(4,128)S(1)}, u32[]{:S(2)}, u32[]{:S(2)}) collective-permute-start(f32[4,6,1,256]{3,0,2,1:T(4,128)S(1)} %copy.1270), channel_id=1, source_target_pairs={{0,1},{1,2},{2,3},{3,4},{4,5},{5,6},{6,7},{7,8},{8,9},{9,10},{10,1... | collective-permute-start | bytes 73736 | tf_op jit(solution)/shard_map/ppermute | solution.py:21
  314.7 4.8 %collective-permute-done.51 = f32[4,6,1,256]{3,0,2,1:T(4,128)S(1)} collective-permute-done((f32[4,6,1,256]{3,0,2,1:T(4,128)S(1)}, f32[4,6,1,256]{3,0,2,1:T(4,128)S(1)}, u32[]{:S(2)}, u32[]{:S(2)}) %collective-permute-start.51) | collective-permute-done | bytes 24608 | tf_op jit(solution)/shard_map/ppermute | solution.py:21
  324.9 5.3 %collective-permute-done.53 = f32[4,1,16,256]{3,2,1,0:T(8,128)S(1)} collective-permute-done((f32[4,1,16,256]{3,2,1,0:T(8,128)S(1)}, f32[4,1,16,256]{3,2,1,0:T(8,128)S(1)}, u32[]{:S(2)}, u32[]{:S(2)}) %collective-permute-start.53) | collective-permute-done | bytes 65568 | tf_op jit(solution)/shard_map/ppermute | solution.py:21
  332.2 3.9 %collective-permute-start.55 = (f32[4,6,1,256]{3,0,2,1:T(4,128)S(1)}, f32[4,6,1,256]{3,0,2,1:T(4,128)S(1)}, u32[]{:S(2)}, u32[]{:S(2)}) collective-permute-start(f32[4,6,1,256]{3,0,2,1:T(4,128)S(1)} %copy.1276), channel_id=1, source_target_pairs={{0,1},{1,2},{2,3},{3,4},{4,5},{5,6},{6,7},{7,8},{8,9},{9,10},{10,1... | collective-permute-start | bytes 73736 | tf_op jit(solution)/shard_map/ppermute | solution.py:21
  336.2 4.8 %collective-permute-done.55 = f32[4,6,1,256]{3,0,2,1:T(4,128)S(1)} collective-permute-done((f32[4,6,1,256]{3,0,2,1:T(4,128)S(1)}, f32[4,6,1,256]{3,0,2,1:T(4,128)S(1)}, u32[]{:S(2)}, u32[]{:S(2)}) %collective-permute-start.55) | collective-permute-done | bytes 24608 | tf_op jit(solution)/shard_map/ppermute | solution.py:21
  (230 shorter events, 83.2 us)
Async XLA Ops:
  1.4 20.9 %collective-permute-start = (f32[1,1,16,256]{3,2,1,0:T(8,128)S(1)}, f32[1,1,16,256]{3,2,1,0:T(8,128)S(1)}, u32[]{:S(2)}, u32[]{:S(2)}) collective-permute-start(f32[1,1,16,256]{3,2,1,0:T(8,128)S(1)} %get-tuple-element.133), channel_id=1, source_target_pairs={{32,0},{64,32},{96,64},{128,96},{160,128},{192,160},{224,192},{33,... | collective-permute-start | bytes 49160 | tf_op jit(solution)/shard_map/ppermute | solution.py:22
  3.3 18.9 %collective-permute-start.1 = (f32[1,1,16,256]{3,2,1,0:T(8,128)S(1)}, f32[1,1,16,256]{3,2,1,0:T(8,128)S(1)}, u32[]{:S(2)}, u32[]{:S(2)}) collective-permute-start(f32[1,1,16,256]{3,2,1,0:T(8,128)S(1)} %get-tuple-element.132), channel_id=1, source_target_pairs={{0,32},{32,64},{64,96},{96,128},{128,160},{160,192},{192,224},{1,3... | collective-permute-start | bytes 49160 | tf_op jit(solution)/shard_map/ppermute | solution.py:21
  14.7 33.5 %collective-permute-start.8 = (f32[1,1,8,128]{3,2,1,0:T(8,128)S(1)}, f32[1,1,8,128]{3,2,1,0:T(8,128)S(1)}, u32[]{:S(2)}, u32[]{:S(2)}) collective-permute-start(f32[1,1,8,128]{3,2,1,0:T(8,128)S(1)} %get-tuple-element.162), channel_id=1, source_target_pairs={{32,0},{64,32},{96,64},{128,96},{160,128},{192,160},{224,192},{33,... | collective-permute-start | bytes 12296 | tf_op jit(solution)/shard_map/ppermute | solution.py:22
  20.0 28.2 %collective-permute-start.9 = (f32[1,1,8,128]{3,2,1,0:T(8,128)S(1)}, f32[1,1,8,128]{3,2,1,0:T(8,128)S(1)}, u32[]{:S(2)}, u32[]{:S(2)}) collective-permute-start(f32[1,1,8,128]{3,2,1,0:T(8,128)S(1)} %get-tuple-element.161), channel_id=1, source_target_pairs={{0,32},{32,64},{64,96},{96,128},{128,160},{160,192},{192,224},{1,3... | collective-permute-start | bytes 12296 | tf_op jit(solution)/shard_map/ppermute | solution.py:21
  22.3 20.6 %collective-permute-start.2 = (f32[1,6,1,256]{3,2,1,0:T(1,128)S(1)}, f32[1,6,1,256]{3,2,1,0:T(1,128)S(1)}, u32[]{:S(2)}, u32[]{:S(2)}) collective-permute-start(f32[1,6,1,256]{3,2,1,0:T(1,128)S(1)} %get-tuple-element.100), channel_id=1, source_target_pairs={{1,0},{2,1},{3,2},{4,3},{5,4},{6,5},{7,6},{8,7},{9,8},{10,9},{11,1... | collective-permute-start | bytes 18440 | tf_op jit(solution)/shard_map/ppermute | solution.py:22
  27.6 15.3 %collective-permute-start.3 = (f32[1,6,1,256]{3,2,1,0:T(1,128)S(1)}, f32[1,6,1,256]{3,2,1,0:T(1,128)S(1)}, u32[]{:S(2)}, u32[]{:S(2)}) collective-permute-start(f32[1,6,1,256]{3,2,1,0:T(1,128)S(1)} %get-tuple-element.99), channel_id=1, source_target_pairs={{0,1},{1,2},{2,3},{3,4},{4,5},{5,6},{6,7},{7,8},{8,9},{9,10},{10,1... | collective-permute-start | bytes 18440 | tf_op jit(solution)/shard_map/ppermute | solution.py:21
  43.3 13.8 %collective-permute-start.4 = (f32[4,1,16,256]{3,2,1,0:T(8,128)S(1)}, f32[4,1,16,256]{3,2,1,0:T(8,128)S(1)}, u32[]{:S(2)}, u32[]{:S(2)}) collective-permute-start(f32[4,1,16,256]{3,2,1,0:T(8,128)S(1)} %get-tuple-element.75), channel_id=1, source_target_pairs={{32,0},{64,32},{96,64},{128,96},{160,128},{192,160},{224,192},{33,... | collective-permute-start | bytes 196616 | tf_op jit(solution)/shard_map/ppermute | solution.py:22
  46.3 10.8 %collective-permute-start.5 = (f32[4,1,16,256]{3,2,1,0:T(8,128)S(1)}, f32[4,1,16,256]{3,2,1,0:T(8,128)S(1)}, u32[]{:S(2)}, u32[]{:S(2)}) collective-permute-start(f32[4,1,16,256]{3,2,1,0:T(8,128)S(1)} %get-tuple-element.74), channel_id=1, source_target_pairs={{0,32},{32,64},{64,96},{96,128},{128,160},{160,192},{192,224},{1,3... | collective-permute-start | bytes 196616 | tf_op jit(solution)/shard_map/ppermute | solution.py:21
  48.2 31.4 %collective-permute-start.10 = (f32[1,4,1,128]{3,2,1,0:T(1,128)S(1)}, f32[1,4,1,128]{3,2,1,0:T(1,128)S(1)}, u32[]{:S(2)}, u32[]{:S(2)}) collective-permute-start(f32[1,4,1,128]{3,2,1,0:T(1,128)S(1)} %get-tuple-element.155), channel_id=1, source_target_pairs={{1,0},{2,1},{3,2},{4,3},{5,4},{6,5},{7,6},{8,7},{9,8},{10,9},{11,1... | collective-permute-start | bytes 6152 | tf_op jit(solution)/shard_map/ppermute | solution.py:22
  55.2 24.5 %collective-permute-start.11 = (f32[1,4,1,128]{3,2,1,0:T(1,128)S(1)}, f32[1,4,1,128]{3,2,1,0:T(1,128)S(1)}, u32[]{:S(2)}, u32[]{:S(2)}) collective-permute-start(f32[1,4,1,128]{3,2,1,0:T(1,128)S(1)} %get-tuple-element.154), channel_id=1, source_target_pairs={{0,1},{1,2},{2,3},{3,4},{4,5},{5,6},{6,7},{7,8},{8,9},{9,10},{10,1... | collective-permute-start | bytes 6152 | tf_op jit(solution)/shard_map/ppermute | solution.py:21
  57.2 8.9 %collective-permute-start.6 = (f32[4,6,1,256]{3,0,2,1:T(4,128)S(1)}, f32[4,6,1,256]{3,0,2,1:T(4,128)S(1)}, u32[]{:S(2)}, u32[]{:S(2)}) collective-permute-start(f32[4,6,1,256]{3,0,2,1:T(4,128)S(1)} %copy.1240), channel_id=1, source_target_pairs={{1,0},{2,1},{3,2},{4,3},{5,4},{6,5},{7,6},{8,7},{9,8},{10,9},{11,1... | collective-permute-start | bytes 73736 | tf_op jit(solution)/shard_map/ppermute | solution.py:22
  64.1 8.9 %collective-permute-start.7 = (f32[4,6,1,256]{3,0,2,1:T(4,128)S(1)}, f32[4,6,1,256]{3,0,2,1:T(4,128)S(1)}, u32[]{:S(2)}, u32[]{:S(2)}) collective-permute-start(f32[4,6,1,256]{3,0,2,1:T(4,128)S(1)} %copy.1242), channel_id=1, source_target_pairs={{0,1},{1,2},{2,3},{3,4},{4,5},{5,6},{6,7},{7,8},{8,9},{9,10},{10,1... | collective-permute-start | bytes 73736 | tf_op jit(solution)/shard_map/ppermute | solution.py:21
  77.7 7.7 %collective-permute-start.13 = (f32[4,1,16,256]{3,2,1,0:T(8,128)S(1)}, f32[4,1,16,256]{3,2,1,0:T(8,128)S(1)}, u32[]{:S(2)}, u32[]{:S(2)}) collective-permute-start(f32[4,1,16,256]{3,2,1,0:T(8,128)S(1)} %get-tuple-element.72), channel_id=1, source_target_pairs={{0,32},{32,64},{64,96},{96,128},{128,160},{160,192},{192,224},{1,3... | collective-permute-start | bytes 196616 | tf_op jit(solution)/shard_map/ppermute | solution.py:21
  85.5 6.1 %collective-permute-start.14 = (f32[4,6,1,256]{3,0,2,1:T(4,128)S(1)}, f32[4,6,1,256]{3,0,2,1:T(4,128)S(1)}, u32[]{:S(2)}, u32[]{:S(2)}) collective-permute-start(f32[4,6,1,256]{3,0,2,1:T(4,128)S(1)} %copy.1246), channel_id=1, source_target_pairs={{1,0},{2,1},{3,2},{4,3},{5,4},{6,5},{7,6},{8,7},{9,8},{10,9},{11,1... | collective-permute-start | bytes 73736 | tf_op jit(solution)/shard_map/ppermute | solution.py:22
  87.4 8.7 %collective-permute-start.15 = (f32[4,6,1,256]{3,0,2,1:T(4,128)S(1)}, f32[4,6,1,256]{3,0,2,1:T(4,128)S(1)}, u32[]{:S(2)}, u32[]{:S(2)}) collective-permute-start(f32[4,6,1,256]{3,0,2,1:T(4,128)S(1)} %copy.1248), channel_id=1, source_target_pairs={{0,1},{1,2},{2,3},{3,4},{4,5},{5,6},{6,7},{7,8},{8,9},{9,10},{10,1... | collective-permute-start | bytes 73736 | tf_op jit(solution)/shard_map/ppermute | solution.py:21
  110.9 13.2 %collective-permute-start.16 = (f32[4,1,8,128]{3,2,1,0:T(8,128)S(1)}, f32[4,1,8,128]{3,2,1,0:T(8,128)S(1)}, u32[]{:S(2)}, u32[]{:S(2)}) collective-permute-start(f32[4,1,8,128]{3,2,1,0:T(8,128)S(1)} %get-tuple-element.146), channel_id=1, source_target_pairs={{32,0},{64,32},{96,64},{128,96},{160,128},{192,160},{224,192},{33,... | collective-permute-start | bytes 49160 | tf_op jit(solution)/shard_map/ppermute | solution.py:22
  112.8 11.3 %collective-permute-start.17 = (f32[4,1,8,128]{3,2,1,0:T(8,128)S(1)}, f32[4,1,8,128]{3,2,1,0:T(8,128)S(1)}, u32[]{:S(2)}, u32[]{:S(2)}) collective-permute-start(f32[4,1,8,128]{3,2,1,0:T(8,128)S(1)} %get-tuple-element.145), channel_id=1, source_target_pairs={{0,32},{32,64},{64,96},{96,128},{128,160},{160,192},{192,224},{1,3... | collective-permute-start | bytes 49160 | tf_op jit(solution)/shard_map/ppermute | solution.py:21
  115.3 25.3 %collective-permute-start.20 = (f32[1,8,1,64]{3,2,1,0:T(1,128)S(1)}, f32[1,8,1,64]{3,2,1,0:T(1,128)S(1)}, u32[]{:S(2)}, u32[]{:S(2)}) collective-permute-start(f32[1,8,1,64]{3,2,1,0:T(1,128)S(1)} %get-tuple-element.150), channel_id=1, source_target_pairs={{0,1},{1,2},{2,3},{3,4},{4,5},{5,6},{6,7},{7,8},{8,9},{9,10},{10,1... | collective-permute-start | bytes 6152 | tf_op jit(solution)/shard_map/ppermute | solution.py:21
  117.2 23.4 %collective-permute-start.21 = (f32[1,8,1,64]{3,2,1,0:T(1,128)S(1)}, f32[1,8,1,64]{3,2,1,0:T(1,128)S(1)}, u32[]{:S(2)}, u32[]{:S(2)}) collective-permute-start(f32[1,8,1,64]{3,2,1,0:T(1,128)S(1)} %get-tuple-element.151), channel_id=1, source_target_pairs={{1,0},{2,1},{3,2},{4,3},{5,4},{6,5},{7,6},{8,7},{9,8},{10,9},{11,1... | collective-permute-start | bytes 6152 | tf_op jit(solution)/shard_map/ppermute | solution.py:22
  124.2 5.9 %collective-permute-start.18 = (f32[4,4,1,128]{3,2,1,0:T(1,128)S(1)}, f32[4,4,1,128]{3,2,1,0:T(1,128)S(1)}, u32[]{:S(2)}, u32[]{:S(2)}) collective-permute-start(f32[4,4,1,128]{3,2,1,0:T(1,128)S(1)} %get-tuple-element.131), channel_id=1, source_target_pairs={{1,0},{2,1},{3,2},{4,3},{5,4},{6,5},{7,6},{8,7},{9,8},{10,9},{11,1... | collective-permute-start | bytes 24584 | tf_op jit(solution)/shard_map/ppermute | solution.py:22
  126.1 8.6 %collective-permute-start.19 = (f32[4,4,1,128]{3,2,1,0:T(1,128)S(1)}, f32[4,4,1,128]{3,2,1,0:T(1,128)S(1)}, u32[]{:S(2)}, u32[]{:S(2)}) collective-permute-start(f32[4,4,1,128]{3,2,1,0:T(1,128)S(1)} %get-tuple-element.130), channel_id=1, source_target_pairs={{0,1},{1,2},{2,3},{3,4},{4,5},{5,6},{6,7},{7,8},{8,9},{9,10},{10,1... | collective-permute-start | bytes 24584 | tf_op jit(solution)/shard_map/ppermute | solution.py:21
  138.7 7.2 %collective-permute-start.23 = (f32[4,1,8,128]{3,2,1,0:T(8,128)S(1)}, f32[4,1,8,128]{3,2,1,0:T(8,128)S(1)}, u32[]{:S(2)}, u32[]{:S(2)}) collective-permute-start(f32[4,1,8,128]{3,2,1,0:T(8,128)S(1)} %get-tuple-element.143), channel_id=1, source_target_pairs={{0,32},{32,64},{64,96},{96,128},{128,160},{160,192},{192,224},{1,3... | collective-permute-start | bytes 49160 | tf_op jit(solution)/shard_map/ppermute | solution.py:21
  145.8 6.0 %collective-permute-start.24 = (f32[4,4,1,128]{3,2,1,0:T(1,128)S(1)}, f32[4,4,1,128]{3,2,1,0:T(1,128)S(1)}, u32[]{:S(2)}, u32[]{:S(2)}) collective-permute-start(f32[4,4,1,128]{3,2,1,0:T(1,128)S(1)} %get-tuple-element.126), channel_id=1, source_target_pairs={{1,0},{2,1},{3,2},{4,3},{5,4},{6,5},{7,6},{8,7},{9,8},{10,9},{11,1... | collective-permute-start | bytes 24584 | tf_op jit(solution)/shard_map/ppermute | solution.py:22
  147.8 8.6 %collective-permute-start.25 = (f32[4,4,1,128]{3,2,1,0:T(1,128)S(1)}, f32[4,4,1,128]{3,2,1,0:T(1,128)S(1)}, u32[]{:S(2)}, u32[]{:S(2)}) collective-permute-start(f32[4,4,1,128]{3,2,1,0:T(1,128)S(1)} %get-tuple-element.125), channel_id=1, source_target_pairs={{0,1},{1,2},{2,3},{3,4},{4,5},{5,6},{6,7},{7,8},{8,9},{9,10},{10,1... | collective-permute-start | bytes 24584 | tf_op jit(solution)/shard_map/ppermute | solution.py:21
  172.2 8.9 %collective-permute-start.26 = (f32[4,8,1,64]{3,2,1,0:T(1,128)S(1)}, f32[4,8,1,64]{3,2,1,0:T(1,128)S(1)}, u32[]{:S(2)}, u32[]{:S(2)}) collective-permute-start(f32[4,8,1,64]{3,2,1,0:T(1,128)S(1)} %get-tuple-element.121), channel_id=1, source_target_pairs={{0,1},{1,2},{2,3},{3,4},{4,5},{5,6},{6,7},{7,8},{8,9},{9,10},{10,1... | collective-permute-start | bytes 24584 | tf_op jit(solution)/shard_map/ppermute | solution.py:21
  174.1 8.4 %collective-permute-start.27 = (f32[4,8,1,64]{3,2,1,0:T(1,128)S(1)}, f32[4,8,1,64]{3,2,1,0:T(1,128)S(1)}, u32[]{:S(2)}, u32[]{:S(2)}) collective-permute-start(f32[4,8,1,64]{3,2,1,0:T(1,128)S(1)} %get-tuple-element.122), channel_id=1, source_target_pairs={{1,0},{2,1},{3,2},{4,3},{5,4},{6,5},{7,6},{8,7},{9,8},{10,9},{11,1... | collective-permute-start | bytes 24584 | tf_op jit(solution)/shard_map/ppermute | solution.py:22
  183.0 9.2 %collective-permute-start.28 = (f32[4,8,1,64]{3,2,1,0:T(1,128)S(1)}, f32[4,8,1,64]{3,2,1,0:T(1,128)S(1)}, u32[]{:S(2)}, u32[]{:S(2)}) collective-permute-start(f32[4,8,1,64]{3,2,1,0:T(1,128)S(1)} %get-tuple-element.119), channel_id=1, source_target_pairs={{0,1},{1,2},{2,3},{3,4},{4,5},{5,6},{6,7},{7,8},{8,9},{9,10},{10,1... | collective-permute-start | bytes 24584 | tf_op jit(solution)/shard_map/ppermute | solution.py:21
  184.9 8.6 %collective-permute-start.29 = (f32[4,8,1,64]{3,2,1,0:T(1,128)S(1)}, f32[4,8,1,64]{3,2,1,0:T(1,128)S(1)}, u32[]{:S(2)}, u32[]{:S(2)}) collective-permute-start(f32[4,8,1,64]{3,2,1,0:T(1,128)S(1)} %get-tuple-element.120), channel_id=1, source_target_pairs={{1,0},{2,1},{3,2},{4,3},{5,4},{6,5},{7,6},{8,7},{9,8},{10,9},{11,1... | collective-permute-start | bytes 24584 | tf_op jit(solution)/shard_map/ppermute | solution.py:22
  194.1 9.2 %collective-permute-start.30 = (f32[4,8,1,64]{3,2,1,0:T(1,128)S(1)}, f32[4,8,1,64]{3,2,1,0:T(1,128)S(1)}, u32[]{:S(2)}, u32[]{:S(2)}) collective-permute-start(f32[4,8,1,64]{3,2,1,0:T(1,128)S(1)} %get-tuple-element.117), channel_id=1, source_target_pairs={{0,1},{1,2},{2,3},{3,4},{4,5},{5,6},{6,7},{7,8},{8,9},{9,10},{10,1... | collective-permute-start | bytes 24584 | tf_op jit(solution)/shard_map/ppermute | solution.py:21
  196.1 8.6 %collective-permute-start.31 = (f32[4,8,1,64]{3,2,1,0:T(1,128)S(1)}, f32[4,8,1,64]{3,2,1,0:T(1,128)S(1)}, u32[]{:S(2)}, u32[]{:S(2)}) collective-permute-start(f32[4,8,1,64]{3,2,1,0:T(1,128)S(1)} %get-tuple-element.118), channel_id=1, source_target_pairs={{1,0},{2,1},{3,2},{4,3},{5,4},{6,5},{7,6},{8,7},{9,8},{10,9},{11,1... | collective-permute-start | bytes 24584 | tf_op jit(solution)/shard_map/ppermute | solution.py:22
  205.3 9.4 %collective-permute-start.32 = (f32[4,8,1,64]{3,2,1,0:T(1,128)S(1)}, f32[4,8,1,64]{3,2,1,0:T(1,128)S(1)}, u32[]{:S(2)}, u32[]{:S(2)}) collective-permute-start(f32[4,8,1,64]{3,2,1,0:T(1,128)S(1)} %get-tuple-element.115), channel_id=1, source_target_pairs={{0,1},{1,2},{2,3},{3,4},{4,5},{5,6},{6,7},{7,8},{8,9},{9,10},{10,1... | collective-permute-start | bytes 24584 | tf_op jit(solution)/shard_map/ppermute | solution.py:21
  207.2 8.6 %collective-permute-start.33 = (f32[4,8,1,64]{3,2,1,0:T(1,128)S(1)}, f32[4,8,1,64]{3,2,1,0:T(1,128)S(1)}, u32[]{:S(2)}, u32[]{:S(2)}) collective-permute-start(f32[4,8,1,64]{3,2,1,0:T(1,128)S(1)} %get-tuple-element.116), channel_id=1, source_target_pairs={{1,0},{2,1},{3,2},{4,3},{5,4},{6,5},{7,6},{8,7},{9,8},{10,9},{11,1... | collective-permute-start | bytes 24584 | tf_op jit(solution)/shard_map/ppermute | solution.py:22
  216.4 9.2 %collective-permute-start.34 = (f32[4,8,1,64]{3,2,1,0:T(1,128)S(1)}, f32[4,8,1,64]{3,2,1,0:T(1,128)S(1)}, u32[]{:S(2)}, u32[]{:S(2)}) collective-permute-start(f32[4,8,1,64]{3,2,1,0:T(1,128)S(1)} %get-tuple-element.113), channel_id=1, source_target_pairs={{0,1},{1,2},{2,3},{3,4},{4,5},{5,6},{6,7},{7,8},{8,9},{9,10},{10,1... | collective-permute-start | bytes 24584 | tf_op jit(solution)/shard_map/ppermute | solution.py:21
  218.3 8.6 %collective-permute-start.35 = (f32[4,8,1,64]{3,2,1,0:T(1,128)S(1)}, f32[4,8,1,64]{3,2,1,0:T(1,128)S(1)}, u32[]{:S(2)}, u32[]{:S(2)}) collective-permute-start(f32[4,8,1,64]{3,2,1,0:T(1,128)S(1)} %get-tuple-element.114), channel_id=1, source_target_pairs={{1,0},{2,1},{3,2},{4,3},{5,4},{6,5},{7,6},{8,7},{9,8},{10,9},{11,1... | collective-permute-start | bytes 24584 | tf_op jit(solution)/shard_map/ppermute | solution.py:22
  229.7 7.2 %collective-permute-start.37 = (f32[4,1,8,128]{3,2,1,0:T(8,128)S(1)}, f32[4,1,8,128]{3,2,1,0:T(8,128)S(1)}, u32[]{:S(2)}, u32[]{:S(2)}) collective-permute-start(f32[4,1,8,128]{3,2,1,0:T(8,128)S(1)} %get-tuple-element.141), channel_id=1, source_target_pairs={{0,32},{32,64},{64,96},{96,128},{128,160},{160,192},{192,224},{1,3... | collective-permute-start | bytes 49160 | tf_op jit(solution)/shard_map/ppermute | solution.py:21
  236.9 9.2 %collective-permute-start.38 = (f32[4,4,1,128]{3,2,1,0:T(1,128)S(1)}, f32[4,4,1,128]{3,2,1,0:T(1,128)S(1)}, u32[]{:S(2)}, u32[]{:S(2)}) collective-permute-start(f32[4,4,1,128]{3,2,1,0:T(1,128)S(1)} %get-tuple-element.112), channel_id=1, source_target_pairs={{1,0},{2,1},{3,2},{4,3},{5,4},{6,5},{7,6},{8,7},{9,8},{10,9},{11,1... | collective-permute-start | bytes 24584 | tf_op jit(solution)/shard_map/ppermute | solution.py:22
  244.1 8.6 %collective-permute-start.39 = (f32[4,4,1,128]{3,2,1,0:T(1,128)S(1)}, f32[4,4,1,128]{3,2,1,0:T(1,128)S(1)}, u32[]{:S(2)}, u32[]{:S(2)}) collective-permute-start(f32[4,4,1,128]{3,2,1,0:T(1,128)S(1)} %get-tuple-element.111), channel_id=1, source_target_pairs={{0,1},{1,2},{2,3},{3,4},{4,5},{5,6},{6,7},{7,8},{8,9},{9,10},{10,1... | collective-permute-start | bytes 24584 | tf_op jit(solution)/shard_map/ppermute | solution.py:21
  255.0 7.2 %collective-permute-start.41 = (f32[4,1,8,128]{3,2,1,0:T(8,128)S(1)}, f32[4,1,8,128]{3,2,1,0:T(8,128)S(1)}, u32[]{:S(2)}, u32[]{:S(2)}) collective-permute-start(f32[4,1,8,128]{3,2,1,0:T(8,128)S(1)} %get-tuple-element.139), channel_id=1, source_target_pairs={{0,32},{32,64},{64,96},{96,128},{128,160},{160,192},{192,224},{1,3... | collective-permute-start | bytes 49160 | tf_op jit(solution)/shard_map/ppermute | solution.py:21
  264.1 8.6 %collective-permute-start.43 = (f32[4,4,1,128]{3,2,1,0:T(1,128)S(1)}, f32[4,4,1,128]{3,2,1,0:T(1,128)S(1)}, u32[]{:S(2)}, u32[]{:S(2)}) collective-permute-start(f32[4,4,1,128]{3,2,1,0:T(1,128)S(1)} %get-tuple-element.107), channel_id=1, source_target_pairs={{0,1},{1,2},{2,3},{3,4},{4,5},{5,6},{6,7},{7,8},{8,9},{9,10},{10,1... | collective-permute-start | bytes 24584 | tf_op jit(solution)/shard_map/ppermute | solution.py:21
  279.0 7.7 %collective-permute-start.45 = (f32[4,1,16,256]{3,2,1,0:T(8,128)S(1)}, f32[4,1,16,256]{3,2,1,0:T(8,128)S(1)}, u32[]{:S(2)}, u32[]{:S(2)}) collective-permute-start(f32[4,1,16,256]{3,2,1,0:T(8,128)S(1)} %get-tuple-element.62), channel_id=1, source_target_pairs={{0,32},{32,64},{64,96},{96,128},{128,160},{160,192},{192,224},{1,3... | collective-permute-start | bytes 196616 | tf_op jit(solution)/shard_map/ppermute | solution.py:21
  286.8 5.9 %collective-permute-start.46 = (f32[4,6,1,256]{3,0,2,1:T(4,128)S(1)}, f32[4,6,1,256]{3,0,2,1:T(4,128)S(1)}, u32[]{:S(2)}, u32[]{:S(2)}) collective-permute-start(f32[4,6,1,256]{3,0,2,1:T(4,128)S(1)} %copy.1262), channel_id=1, source_target_pairs={{1,0},{2,1},{3,2},{4,3},{5,4},{6,5},{7,6},{8,7},{9,8},{10,9},{11,1... | collective-permute-start | bytes 73736 | tf_op jit(solution)/shard_map/ppermute | solution.py:22
  288.7 9.3 %collective-permute-start.47 = (f32[4,6,1,256]{3,0,2,1:T(4,128)S(1)}, f32[4,6,1,256]{3,0,2,1:T(4,128)S(1)}, u32[]{:S(2)}, u32[]{:S(2)}) collective-permute-start(f32[4,6,1,256]{3,0,2,1:T(4,128)S(1)} %copy.1264), channel_id=1, source_target_pairs={{0,1},{1,2},{2,3},{3,4},{4,5},{5,6},{6,7},{7,8},{8,9},{9,10},{10,1... | collective-permute-start | bytes 73736 | tf_op jit(solution)/shard_map/ppermute | solution.py:21
  301.0 7.7 %collective-permute-start.49 = (f32[4,1,16,256]{3,2,1,0:T(8,128)S(1)}, f32[4,1,16,256]{3,2,1,0:T(8,128)S(1)}, u32[]{:S(2)}, u32[]{:S(2)}) collective-permute-start(f32[4,1,16,256]{3,2,1,0:T(8,128)S(1)} %get-tuple-element.60), channel_id=1, source_target_pairs={{0,32},{32,64},{64,96},{96,128},{128,160},{160,192},{192,224},{1,3... | collective-permute-start | bytes 196616 | tf_op jit(solution)/shard_map/ppermute | solution.py:21
  308.8 5.9 %collective-permute-start.50 = (f32[4,6,1,256]{3,0,2,1:T(4,128)S(1)}, f32[4,6,1,256]{3,0,2,1:T(4,128)S(1)}, u32[]{:S(2)}, u32[]{:S(2)}) collective-permute-start(f32[4,6,1,256]{3,0,2,1:T(4,128)S(1)} %copy.1268), channel_id=1, source_target_pairs={{1,0},{2,1},{3,2},{4,3},{5,4},{6,5},{7,6},{8,7},{9,8},{10,9},{11,1... | collective-permute-start | bytes 73736 | tf_op jit(solution)/shard_map/ppermute | solution.py:22
  310.7 8.7 %collective-permute-start.51 = (f32[4,6,1,256]{3,0,2,1:T(4,128)S(1)}, f32[4,6,1,256]{3,0,2,1:T(4,128)S(1)}, u32[]{:S(2)}, u32[]{:S(2)}) collective-permute-start(f32[4,6,1,256]{3,0,2,1:T(4,128)S(1)} %copy.1270), channel_id=1, source_target_pairs={{0,1},{1,2},{2,3},{3,4},{4,5},{5,6},{6,7},{7,8},{8,9},{9,10},{10,1... | collective-permute-start | bytes 73736 | tf_op jit(solution)/shard_map/ppermute | solution.py:21
  322.5 7.7 %collective-permute-start.53 = (f32[4,1,16,256]{3,2,1,0:T(8,128)S(1)}, f32[4,1,16,256]{3,2,1,0:T(8,128)S(1)}, u32[]{:S(2)}, u32[]{:S(2)}) collective-permute-start(f32[4,1,16,256]{3,2,1,0:T(8,128)S(1)} %get-tuple-element.58), channel_id=1, source_target_pairs={{0,32},{32,64},{64,96},{96,128},{128,160},{160,192},{192,224},{1,3... | collective-permute-start | bytes 196616 | tf_op jit(solution)/shard_map/ppermute | solution.py:21
  330.3 5.9 %collective-permute-start.54 = (f32[4,6,1,256]{3,0,2,1:T(4,128)S(1)}, f32[4,6,1,256]{3,0,2,1:T(4,128)S(1)}, u32[]{:S(2)}, u32[]{:S(2)}) collective-permute-start(f32[4,6,1,256]{3,0,2,1:T(4,128)S(1)} %copy.1274), channel_id=1, source_target_pairs={{1,0},{2,1},{3,2},{4,3},{5,4},{6,5},{7,6},{8,7},{9,8},{10,9},{11,1... | collective-permute-start | bytes 73736 | tf_op jit(solution)/shard_map/ppermute | solution.py:22
  332.2 8.7 %collective-permute-start.55 = (f32[4,6,1,256]{3,0,2,1:T(4,128)S(1)}, f32[4,6,1,256]{3,0,2,1:T(4,128)S(1)}, u32[]{:S(2)}, u32[]{:S(2)}) collective-permute-start(f32[4,6,1,256]{3,0,2,1:T(4,128)S(1)} %copy.1276), channel_id=1, source_target_pairs={{0,1},{1,2},{2,3},{3,4},{4,5},{5,6},{6,7},{7,8},{8,9},{9,10},{10,1... | collective-permute-start | bytes 73736 | tf_op jit(solution)/shard_map/ppermute | solution.py:21
  (11 other events, 119.5 us)
where the time goes:
time: 345 us; the launch traced here: 343 us
  starting transfers between devices  183 us (53%)
  waiting for transfers between devices  89.6 us (26%)
  blocking collectives  27.9 us (8%)
  other arithmetic  22.5 us (7%)
  local copies, waits for them, and re-layouts  17.4 us (5%)
    ppermute x28, starting transfers between devices, extended_2(): after = lax.ppermute(leading, axis, down)  112 us
    ppermute x28, waiting for transfers between devices, extended_2(): before = lax.ppermute(last, axis, up)  82.7 us
    ppermute x28, starting transfers between devices, extended_2(): before = lax.ppermute(last, axis, up)  71.5 us
    all_gather x1, blocking collectives, gathered_bottom(): lax.all_gather(source_low, 'grp', axis=1, tiled=True)  14.5 us
    all_gather x1, blocking collectives, gathered_bottom(): lax.all_gather(viscous_low, 'grp', axis=1, tiled=True)  13.4 us
    reduce_sum x6, other arithmetic, restrict(): array.reshape(comps, xsize // 2, 2, ysize // 2, 2, zsize // 2, 2)  11.8 us
  transfers between devices with their start and end apart: 56, of which 21 were waited for; matrix products, arithmetic and copies ran while one was open for 3% of the time, Pallas kernels for 0%

commit v1 on v0

v1 whole, which is shorter than its diff:
```python
import jax
import jax.numpy as jnp
from jax import lax
from jax.experimental import pallas as pl
from jax.experimental.pallas import tpu as pltpu
from jax.sharding import PartitionSpec as P

COARSE = 6
OMEGA = 0.6
BETA = 0.25
F32 = jnp.float32
VMEM_LIMIT = 48 * 1024 * 1024


def shifts(value, step):
    rows, lanes = value.shape
    lane = lax.broadcasted_iota(jnp.int32, (rows, 128), 1)
    if lanes == 256:
        low, high = value[:, :128], value[:, 128:]
        low_up, high_up = pltpu.roll(low, 127, 1), pltpu.roll(high, 127, 1)
        low_dn, high_dn = pltpu.roll(low, 1, 1), pltpu.roll(high, 1, 1)
        last, first = lane == 127, lane == 0
        plus = jnp.concatenate([jnp.where(last, high_up, low_up), jnp.where(last, 0.0, high_up)], 1)
        minus = jnp.concatenate([jnp.where(first, 0.0, low_dn), jnp.where(first, low_dn, high_dn)], 1)
        return plus, minus
    plus = jnp.where(lane >= 128 - step, 0.0, pltpu.roll(value, 128 - step, 1))
    minus = jnp.where(lane < step, 0.0, pltpu.roll(value, step, 1))
    return plus, minus


def around(load, layer, row, step):
    here = load(layer, row)
    return here, [load(layer + 1, row), load(layer - 1, row), load(layer, row + 1), load(layer, row - 1), *shifts(here, step)]


def sums_of(visc, layer, row, step):
    here, near = around(lambda i, r: visc[i, pl.ds(r, 8), :], layer, row, step)
    sums = [here + other for other in near]
    return here, sums, sum(sums[1:], sums[0])


def stencil(field, layer, row, step, sums):
    here, flux, grad, div = [], [], None, None
    for comp in range(4):
        centre, near = around(lambda i, r: field[comp, i, pl.ds(r, 8), :], layer, row, step)
        here.append(centre)
        if comp < 3:
            terms = [s * n for s, n in zip(sums, near)]
            flux.append(sum(terms[1:], terms[0]))
            diff = near[2 * comp] - near[2 * comp + 1]
            div = diff if div is None else div + diff
        else:
            grad = [near[2 * c] - near[2 * c + 1] for c in range(3)]
    return here, flux, grad, div


def sweep_chunk(out, field, out_layer, layer, row, step, spacing, visc, visc_layer, weight, weight_layer, source, source_layer):
    e_here, sums, _ = sums_of(visc, visc_layer, row, step)
    here, flux, grad, div = stencil(field, layer, row, step, sums)
    w = weight[weight_layer, pl.ds(row, 8), :]
    for c in range(3):
        b = source[c, source_layer, pl.ds(row, 8), :]
        out[c, out_layer, pl.ds(row, 8), :] = (1.0 - OMEGA) * here[c] + w * (
            b + (0.5 / (spacing * spacing)) * flux[c] - (0.5 / spacing) * grad[c]
        )
    b = source[3, source_layer, pl.ds(row, 8), :]
    out[3, out_layer, pl.ds(row, 8), :] = here[3] + (BETA * e_here) * (b - (0.5 / spacing) * div)


def residual_chunk(field, layer, row, step, spacing, visc, visc_layer, source, source_layer):
    _, sums, total = sums_of(visc, visc_layer, row, step)
    here, flux, grad, div = stencil(field, layer, row, step, sums)
    out = []
    for c in range(3):
        b = source[c, source_layer, pl.ds(row, 8), :]
        out.append(b - ((0.5 / (spacing * spacing)) * (total * here[c] - flux[c]) + (0.5 / spacing) * grad[c]))
    out.append(source[3, source_layer, pl.ds(row, 8), :] - (0.5 / spacing) * div)
    return out


def start_chunk(out, out_layer, row, step, spacing, visc, visc_layer, weight, weight_layer, source, source_layer, inside):
    e_here, _, total = sums_of(visc, visc_layer, row, step)
    w = jnp.where(inside, (2.0 * OMEGA * spacing * spacing) / total, 0.0)
    weight[weight_layer, pl.ds(row, 8), :] = w
    for c in range(3):
        out[c, out_layer, pl.ds(row, 8), :] = w * source[c, source_layer, pl.ds(row, 8), :]
    out[3, out_layer, pl.ds(row, 8), :] = (BETA * e_here) * source[3, source_layer, pl.ds(row, 8), :]


def rows_inside(row, first, count, lanes):
    at = lax.broadcasted_iota(jnp.int32, (8, lanes), 0) + (row + first)
    return (at >= 0) & (at < count)


def loop(count, body):
    lax.fori_loop(0, count, lambda i, carry: (body(i), carry)[1], 0)


def fold_matrix(fine, transpose=False):
    shape = (fine // 2, fine) if transpose else (fine, fine // 2)
    a = lax.broadcasted_iota(jnp.int32, shape, 1 if transpose else 0)
    b = lax.broadcasted_iota(jnp.int32, shape, 0 if transpose else 1)
    return jnp.where(a // 2 == b, 1.0, 0.0).astype(F32)


def exact_dot(a, b):
    return jnp.dot(a, b, precision=lax.Precision.HIGHEST, preferred_element_type=F32)


def fine_down(groups, devs, idx, f, e, xm, xp, ym, yp, pay_o, x1_o, ew_o, w_o, fw_o, fw, ew, wt, x0, x1, pair, half):
    g, d = idx[0], idx[1]
    zero8 = jnp.zeros((8, 256), F32)
    low_x, high_x = jnp.where(g > 0, 1.0, 0.0), jnp.where(g < groups - 1, 1.0, 0.0)
    low_y, high_y = jnp.where(d > 0, 1.0, 0.0), jnp.where(d < devs - 1, 1.0, 0.0)

    def scale_of(layer):
        return low_x if layer < 3 else high_x if layer > 6 else 1.0

    for layer in range(10):
        for row in (0, 40):
            ew[layer, row : row + 8, :] = zero8
        own = xm[8 + layer] if layer < 3 else xp[8 + layer - 7] if layer > 6 else e[layer - 3]
        s = scale_of(layer)
        ew[layer, 16:32, :] = own * s
        ew[layer, 8:16, :] = ym[192 + 8 * layer : 200 + 8 * layer, :] * (s * low_y)
        ew[layer, 32:40, :] = yp[192 + 8 * layer : 200 + 8 * layer, :] * (s * high_y)
    for layer in range(8):
        for c in range(4):
            own = xm[2 * c + layer] if layer < 2 else xp[2 * c + layer - 6] if layer > 5 else f[c, layer - 2]
            fw[c, layer, 16:32, :] = own
            fw[c, layer, 8:16, :] = zero8
            fw[c, layer, 32:40, :] = zero8
            at = 24 * layer + 6 * c
            fw[c, layer, 10:16, :] = ym[at : at + 6, :]
            fw[c, layer, 32:38, :] = yp[at : at + 6, :]
    for layer in range(8):
        for c in range(4):
            for row in (0, 40):
                x0[c, layer, row : row + 8, :] = zero8
                x1[c, layer, row : row + 8, :] = zero8

    def start(i):
        layer_in = (4 * g - 2 + i >= 0) & (4 * g - 2 + i < 4 * groups)
        for row in (8, 16, 24, 32):
            inside = rows_inside(row, 16 * d - 16, 16 * devs, 256) & layer_in
            start_chunk(x0, i, row, 1, 1.0, ew, i + 1, wt, i, fw, i, inside)

    loop(8, start)

    def sweep(i):
        for row in (8, 16, 24, 32):
            sweep_chunk(x1, x0, i + 1, i + 1, row, 1, 1.0, ew, i + 2, wt, i + 1, fw, i + 1)

    loop(6, sweep)

    def restrict(m):
        for row in (8, 16, 24, 32):
            a = residual_chunk(x1, 2 * m + 2, row, 1, 1.0, ew, 2 * m + 3, fw, 2 * m + 2)
            b = residual_chunk(x1, 2 * m + 3, row, 1, 1.0, ew, 2 * m + 4, fw, 2 * m + 3)
            for c in range(4):
                pair[2 * c + m, row - 8 : row, :] = a[c] + b[c]
            pair[8 + m, row - 8 : row, :] = ew[2 * m + 3, pl.ds(row, 8), :] + ew[2 * m + 4, pl.ds(row, 8), :]

    loop(2, restrict)
    half[...] = exact_dot(pair[...].reshape(320, 256), fold_matrix(256)) * 0.125
    coarse = half[pl.ds(0, 160, stride=2), :] + half[pl.ds(1, 160, stride=2), :]
    coarse = coarse.reshape(10, 16, 128)
    for m in range(2):
        lanes = slice(128 * m, 128 * m + 128)
        for c in range(4):
            pay_o[12 * c : 12 * c + 12, lanes] = coarse[2 * c + m, 2:14, :]
        pay_o[48:64, lanes] = coarse[8 + m]
    for c in range(4):
        for j in range(2):
            at = 64 + 18 * (2 * c + j)
            pay_o[at : at + 18, :] = x1[c, 3 + j, 15:33, :]
    x1_o[...] = x1[:, 1:7, 8:40, :]
    ew_o[...] = ew[:, 8:40, :]
    w_o[...] = wt[:, 8:40, :]
    fw_o[...] = fw[:, :, 8:40, :]


def mid_down(groups, devs, idx, own, partner, xr, c2, s3, up_o, dn_o, low_o, y_o, b_o, e_o, w_o, bw, ew, wt, y0, y1, pair, low):
    g, d = idx[0], idx[1]
    chips = groups // 2
    chip, core = g // 2, g % 2
    other = 1 - core
    beside = (chip + chips - 1 + 2 * core) % chips
    across = (chip + 1 + (chips - 2) * core) % chips
    far = (chip + 2) % chips
    zero8 = jnp.zeros((8, 128), F32)

    def clear(i):
        for row in (0, 8, 16, 24):
            ew[i, row : row + 8, :] = zero8
            wt[i, row : row + 8, :] = zero8
            for c in range(4):
                bw[c, i, row : row + 8, :] = zero8
                y0[c, i, row : row + 8, :] = zero8
                y1[c, i, row : row + 8, :] = zero8

    loop(2 * groups + 8, clear)

    def place(block, at, which, core_at):
        base = 4 + 4 * which + 2 * core_at
        for m in range(2):
            lanes = slice(128 * m, 128 * m + 128)
            for c in range(4):
                bw[c, base + m, 10:22, :] = block[at + 12 * c : at + 12 * c + 12, lanes]
            ew[base + m, 8:24, :] = block[at + 48 : at + 64, lanes]

    place(own, 0, chip, core)
    place(partner, 0, chip, other)
    place(xr, 0, beside, other)
    place(xr, 208, beside, core)
    place(s3, 0, across, core)
    place(s3, 64, across, other)
    place(c2, 0, far, core)
    place(s3, 128, far, other)

    def start(i):
        for row in (8, 16):
            inside = rows_inside(row, 8 * d - 12, 8 * devs, 128)
            start_chunk(y0, i + 4, row, 1, 2.0, ew, i + 4, wt, i + 4, bw, i + 4, inside)

    loop(2 * groups, start)

    def sweep(i):
        for row in (8, 16):
            sweep_chunk(y1, y0, i + 4, i + 4, row, 1, 2.0, ew, i + 4, wt, i + 4, bw, i + 4)

    loop(2 * groups, sweep)
    lane = lax.broadcasted_iota(jnp.int32, (4, 128), 1)

    def restrict(m):
        at = 2 * m + 4
        for row in (8, 16):
            a = residual_chunk(y1, at, row, 1, 2.0, ew, at, bw, at)
            b = residual_chunk(y1, at + 1, row, 1, 2.0, ew, at + 1, bw, at + 1)
            for c in range(4):
                pair[c, row - 8 : row, :] = a[c] + b[c]
            pair[4, row - 8 : row, :] = ew[at, pl.ds(row, 8), :] + ew[at + 1, pl.ds(row, 8), :]
        for c in range(5):
            rows = pair[c, pl.ds(4, 4, stride=2), :] + pair[c, pl.ds(5, 4, stride=2), :]
            mate = jnp.where(lane % 2 == 0, pltpu.roll(rows, 127, 1), pltpu.roll(rows, 1, 1))
            low[c, m, 0:4, :] = (rows + mate) * 0.125

    loop(groups, restrict)
    for c in range(5):
        for q in range(groups // 2):
            packed = jnp.where(lane % 2 == 0, low[c, 2 * q, 0:4, :], low[c, 2 * q + 1, 0:4, :])
            at = 4 * (c * (groups // 2) + q)
            for out in (up_o, dn_o, low_o):
                out[at : at + 4, :] = packed
    base = 20 * (groups // 2)
    for c in range(4):
        for j in range(6):
            at = base + 4 * (6 * c + j)
            up_o[at : at + 4, :] = y1[c, 2 * g + 2 + j, 16:20, :]
            dn_o[at : at + 4, :] = y1[c, 2 * g + 2 + j, 12:16, :]
        for j in range(2):
            at = base + 96 + 4 * (2 * c + j)
            up_o[at : at + 4, :] = bw[c, 2 * g + 4 + j, 16:20, :]
            dn_o[at : at + 4, :] = bw[c, 2 * g + 4 + j, 12:16, :]

    def keep(j):
        e_o[j] = ew[2 * g + j, 8:24, :]
        w_o[j] = wt[2 * g + j, 8:24, :]
        for c in range(4):
            y_o[c, j] = y1[c, 2 * g + j, 8:24, :]
            b_o[c, j] = bw[c, 2 * g + j, 8:24, :]

    loop(10, keep)


def up_all(groups, devs, idx, low, m1, p1, m2, p2, y_i, b_i, e_i, w_i, x1, fe, fwt, ff, own_edge, far_edge, sol_o, res_o,
           e2, w2, b2, z0, z1, e1, w1, b1, ya, yb, rep, half, va, vb, ew, wt, fw):
    g, d = idx[0], idx[1]
    core = g % 2
    zero8 = jnp.zeros((8, 128), F32)
    zero8w = jnp.zeros((8, 256), F32)
    lane = lax.broadcasted_iota(jnp.int32, (4, 128), 1)
    even = lane % 2 == 0

    def clear(i):
        for row in (0, 8, 16, 24, 32):
            e2[i, row : row + 8, :] = zero8
            for c in range(4):
                b2[c, i, row : row + 8, :] = zero8
                z0[c, i, row : row + 8, :] = zero8
                z1[c, i, row : row + 8, :] = zero8

    loop(groups + 4, clear)
    for source, away in ((m2, -2), (m1, -1), (low, 0), (p1, 1), (p2, 2)):
        row = 16 + 4 * away
        there = 1.0 if away == 0 else jnp.where((d + away >= 0) & (d + away < devs), 1.0, 0.0)
        for c in range(5):
            for q in range(groups // 2):
                at = 4 * (c * (groups // 2) + q)
                packed = source[at : at + 4, :]
                first = jnp.where(even, packed, pltpu.roll(packed, 1, 1))
                second = jnp.where(even, pltpu.roll(packed, 127, 1), packed)
                if c == 4:
                    e2[2 * q + 2, row : row + 4, :] = first * there
                    e2[2 * q + 3, row : row + 4, :] = second * there
                else:
                    b2[c, 2 * q + 2, row : row + 4, :] = first
                    b2[c, 2 * q + 3, row : row + 4, :] = second

    def start_low(i):
        for row in (8, 16, 24):
            inside = rows_inside(row, 4 * d - 16, 4 * devs, 128)
            start_chunk(z0, i + 2, row, 2, 4.0, e2, i + 2, w2, i + 2, b2, i + 2, inside)

    loop(groups, start_low)
    here, there_ = z0, z1
    for _ in range(COARSE - 1):

        def sweep_low(i, here=here, there_=there_):
            for row in (8, 16, 24):
                sweep_chunk(there_, here, i + 2, i + 2, row, 2, 4.0, e2, i + 2, w2, i + 2, b2, i + 2)

        loop(groups, sweep_low)
        here, there_ = there_, here
    z = here

    low_y, high_y = jnp.where(d > 0, 1.0, 0.0), jnp.where(d < devs - 1, 1.0, 0.0)
    base = 20 * (groups // 2)
    for j in range(10):
        e1[j, 0:8, :] = zero8
        e1[j, 24:32, :] = zero8
        e1[j, 8:24, :] = e_i[j]
        w1[j, 8:24, :] = w_i[j]
        for c in range(4):
            b1[c, j, 8:24, :] = b_i[c, j]
            for row in (0, 24):
                ya[c, j, row : row + 8, :] = zero8
                yb[c, j, row : row + 8, :] = zero8
            ya[c, j, 8:24, :] = y_i[c, j]
    for c in range(4):
        for j in range(2):
            at = base + 96 + 4 * (2 * c + j)
            b1[c, 4 + j, 8:12, :] = m1[at : at + 4, :]
            b1[c, 4 + j, 20:24, :] = p1[at : at + 4, :]
        for j in range(6):
            at = base + 4 * (6 * c + j)
            ya[c, 2 + j, 8:12, :] = m1[at : at + 4, :] * low_y
            ya[c, 2 + j, 20:24, :] = p1[at : at + 4, :] * high_y
    for k in range(5):
        for c in range(4):
            rows = z[c, g + k, 14:22, :]
            rep[pl.ds(0, 8, stride=2), :] = rows
            rep[pl.ds(1, 8, stride=2), :] = rows
            twice = rep[...]
            ya[c, 2 * k, 8:24, :] = ya[c, 2 * k, 8:24, :] + twice
            ya[c, 2 * k + 1, 8:24, :] = ya[c, 2 * k + 1, 8:24, :] + twice

    def sweep_mid(out, field, first):
        def body(i):
            for row in (8, 16):
                at = i + first
                sweep_chunk(out, field, at, at, row, 1, 2.0, e1, at, w1, at, b1, at)

        return body

    loop(8, sweep_mid(yb, ya, 1))
    loop(6, sweep_mid(ya, yb, 2))

    spread = fold_matrix(256, True)
    wide = exact_dot(ya[:, 2:8, 8:24, :].reshape(384, 128), spread)
    for n in range(2):
        for parity in range(2):
            half[n, pl.ds(parity, 384, stride=2), :] = wide[:, 128 * n : 128 * n + 128]
    for layer in range(10):
        ew[layer, 0:8, :] = zero8w
        ew[layer, 40:48, :] = zero8w
        ew[layer, 8:40, :] = fe[layer]
    wt[:, 8:40, :] = fwt[...]
    fw[:, :, 8:40, :] = ff[...]
    low_x, high_x = jnp.where(g > 0, 1.0, 0.0), jnp.where(g < groups - 1, 1.0, 0.0)
    on_chip = jnp.where(core == 0, 1.0, 0.0)
    for c in range(4):
        for layer in range(12):
            for row in (0, 40):
                va[c, layer, row : row + 8, :] = zero8w
                vb[c, layer, row : row + 8, :] = zero8w
            at = (6 * c + layer // 2) * 32
            rows = jnp.concatenate([half[0, at : at + 32, :], half[1, at : at + 32, :]], 1)
            va[c, layer, 8:40, :] = rows + x1[c, layer - 3] if 3 <= layer <= 8 else rows
        for j in range(2):
            at = 18 * (2 * c + j)
            own, far = own_edge[at : at + 18, :], far_edge[at : at + 18, :]
            before = jnp.where(core == 0, far, own) * low_x
            after = jnp.where(core == 0, own, far) * high_x
            va[c, 1 + j, 15:33, :] = va[c, 1 + j, 15:33, :] + before
            va[c, 9 + j, 15:33, :] = va[c, 9 + j, 15:33, :] + after

    def sweep_fine(out, field, first, rows):
        def body(i):
            for row in rows:
                at = i + first
                sweep_chunk(out, field, at, at, row, 1, 1.0, ew, at - 1, wt, at - 2, fw, at - 2)

        return body

    loop(8, sweep_fine(vb, va, 2, (8, 16, 24, 32)))
    loop(6, sweep_fine(va, vb, 3, (8, 16, 24, 32)))

    def last(i):
        for row in (16, 24):
            out = residual_chunk(va, i + 4, row, 1, 1.0, ew, i + 3, fw, i + 2)
            for c in range(4):
                sol_o[c, i, row - 16 : row - 8, :] = va[c, i + 4, row : row + 8, :]
                res_o[c, i, row - 16 : row - 8, :] = out[c]

    loop(4, last)


def call(kernel, outs, scratch, *args):
    specs = [pl.BlockSpec(memory_space=pltpu.SMEM)] + [pl.BlockSpec(memory_space=pltpu.VMEM)] * (len(args) - 1)
    return pl.pallas_call(
        kernel,
        out_shape=[jax.ShapeDtypeStruct(shape, F32) for shape in outs],
        in_specs=specs,
        out_specs=[pl.BlockSpec(memory_space=pltpu.VMEM)] * len(outs),
        scratch_shapes=[pltpu.VMEM(shape, F32) for shape in scratch],
        compiler_params=pltpu.CompilerParams(vmem_limit_bytes=VMEM_LIMIT),
    )(*args)


def shift(value, axis, by):
    peers = lax.axis_size(axis)
    return lax.ppermute(value, axis, [(i, (i + by) % peers) for i in range(peers)])


def local(forcing, viscosity):
    groups, devs = lax.axis_size("grp"), lax.axis_size("dev")
    idx = jnp.stack([lax.axis_index("grp"), lax.axis_index("dev")]).astype(jnp.int32)

    def x_pack(f, e):
        return jnp.concatenate([f.reshape(8, 16, 256), e], axis=0)

    xm = shift(x_pack(forcing[:, 2:4], viscosity[1:4]), "grp", 1)
    xp = shift(x_pack(forcing[:, 0:2], viscosity[0:3]), "grp", -1)
    f8 = jnp.concatenate([xm[:8].reshape(4, 2, 16, 256), forcing, xp[:8].reshape(4, 2, 16, 256)], axis=1)
    e10 = jnp.concatenate([xm[8:], viscosity, xp[8:]], axis=0)

    def y_pack(f, e):
        return jnp.concatenate([jnp.swapaxes(f, 0, 1).reshape(192, 256), e.reshape(80, 256)], axis=0)

    ym = shift(y_pack(f8[:, :, 10:16], e10[:, 8:16]), "dev", 1)
    yp = shift(y_pack(f8[:, :, 0:6], e10[:, 0:8]), "dev", -1)

    pay, x1, ew, wt, fw = call(
        lambda *refs: fine_down(groups, devs, *refs),
        [(208, 256), (4, 6, 32, 256), (10, 32, 256), (8, 32, 256), (4, 8, 32, 256)],
        [(4, 8, 48, 256), (10, 48, 256), (8, 48, 256), (4, 8, 48, 256), (4, 8, 48, 256), (10, 32, 256), (320, 128)],
        idx, forcing, viscosity, xm, xp, ym, yp,
    )

    swap = [(i, i ^ 1) for i in range(groups)]
    beside = [(i, (i + 1) % groups if i % 2 else (i - 1) % groups) for i in range(groups)]
    got = lax.ppermute(pay, "grp", swap)
    xr = lax.ppermute(jnp.concatenate([pay, got[:64]], axis=0), "grp", beside)
    c2 = shift(pay[:64], "grp", 4)
    s3 = lax.ppermute(jnp.concatenate([xr[:64], xr[208:], c2], axis=0), "grp", swap)

    layers = 2 * groups + 8
    tall = 20 * (groups // 2)
    up, dn, low, y_w, b_w, e_w, w_w = call(
        lambda *refs: mid_down(groups, devs, *refs),
        [(tall + 128, 128), (tall + 128, 128), (tall, 128), (4, 10, 16, 128), (4, 10, 16, 128), (10, 16, 128), (10, 16, 128)],
        [(4, layers, 32, 128), (layers, 32, 128), (layers, 32, 128), (4, layers, 32, 128), (4, layers, 32, 128), (5, 16, 128), (5, groups, 8, 128)],
        idx, pay[:64], got[:64], xr, c2, s3,
    )

    m1, p1 = shift(up, "dev", 1), shift(dn, "dev", -1)
    m2, p2 = shift(low, "dev", 2), shift(low, "dev", -2)
    deep = groups + 4
    return tuple(call(
        lambda *refs: up_all(groups, devs, *refs),
        [(4, 4, 16, 256), (4, 4, 16, 256)],
        [(deep, 40, 128), (deep, 40, 128), (4, deep, 40, 128), (4, deep, 40, 128), (4, deep, 40, 128),
         (10, 32, 128), (10, 32, 128), (4, 10, 32, 128), (4, 10, 32, 128), (4, 10, 32, 128), (16, 128), (2, 768, 128),
         (4, 12, 48, 256), (4, 12, 48, 256), (10, 48, 256), (8, 48, 256), (4, 8, 48, 256)],
        idx, low, m1, p1, m2, p2, y_w, b_w, e_w, w_w, x1, ew, wt, fw, got[64:], xr[64:208],
    ))


def solution(mesh):
    in_specs = (P(None, "grp", "dev", None), P("grp", "dev", None))
    out_specs = (P(None, "grp", "dev", None), P(None, "grp", "dev", None))
    return jax.shard_map(local, mesh=mesh, in_specs=in_specs, out_specs=out_specs, check_vma=False)
```

time: 345 us -> 83.2 us (0.24)
  the two profiles are of different devices: /device:TPU:152 before, /device:TPU:1 now
where the time goes in v1:
time: 83.2 us; the launch traced here: 83 us
  waiting for transfers between devices  29.6 us (36%)
  starting transfers between devices  29.3 us (35%)
  Pallas kernels  20.9 us (25%)
  local copies, waits for them, and re-layouts  2.05 us (2%)
  between operations  0.88 us (1%)
    ppermute x9, starting transfers between devices, shift(): lax.ppermute(value, axis, [(i, (i + by) % peers) for i in range(peers)])  24.5 us
    ppermute x9, waiting for transfers between devices, shift(): lax.ppermute(value, axis, [(i, (i + by) % peers) for i in range(peers)])  22.9 us
    pallas_call x3, Pallas kernels, call(): pl.pallas_call(kernel, out_shape=[jax.ShapeDtypeStruct(shape, F32) for sh...  20.9 us
    ppermute x1, waiting for transfers between devices, local(): xr = lax.ppermute(jnp.concatenate([pay, got[:64]], axis=0), 'grp', beside)  4.17 us
    ppermute x1, starting transfers between devices, local(): got = lax.ppermute(pay, 'grp', swap)  2.58 us
    ppermute x1, starting transfers between devices, local(): xr = lax.ppermute(jnp.concatenate([pay, got[:64]], axis=0), 'grp', beside)  2.18 us
  transfers between devices with their start and end apart: 12, of which 9 were waited for; matrix products, arithmetic and copies ran while one was open for 0% of the time, Pallas kernels for 0%

profile of v1, /device:TPU:1, one launch (start us, length us, event | category | flops | bytes accessed | tf_op | source)
XLA Modules:
  0.0 83.0 jit_solution(14576307263571408317)
XLA Ops:
  0.6 0.0 copy-start.1
  0.6 1.0 %fusion.1 = (f32[4,2,16,256]{3,2,1,0:T(8,128)S(1)}, f32[4,2,16,256]{3,2,1,0:T(8,128)S(1)}) fusion(f32[4,4,16,256]{3,2,1,0:T(8,128)} %refs_1_.1), kind=kLoop, calls=%fused_computation.14 | loop fusion | bytes 524288 | tf_op jit(solution)/shard_map/slice | solution.py:444
  1.7 0.0 copy-done.1
  1.7 4.5 %collective-permute-start = (f32[11,16,256]{2,1,0:T(8,128)S(1)}, f32[11,16,256]{2,1,0:T(8,128)S(1)}, u32[]{:S(2)}, u32[]{:S(2)}) collective-permute-start(f32[11,16,256]{2,1,0:T(8,128)S(1)} %pad_maximum_fusion.5), channel_id=1, source_target_pairs={{0,32},{32,64},{64,96},{96,128},{128,160},{160,192},{192,224},{224... | collective-permute-start | bytes 540680 | tf_op jit(solution)/shard_map/ppermute | solution.py:433
  6.2 0.0 copy-start
  6.2 0.1 collective-permute-start.1
  6.3 2.3 %collective-permute-done.refs_3_ = f32[11,16,256]{2,1,0:T(8,128)S(1)} collective-permute-done((f32[11,16,256]{2,1,0:T(8,128)S(1)}, f32[11,16,256]{2,1,0:T(8,128)S(1)}, u32[]{:S(2)}, u32[]{:S(2)}) %collective-permute-start) | collective-permute-done | bytes 180256 | tf_op jit(solution)/shard_map/ppermute | solution.py:433
  8.6 0.0 copy-start.2
  8.6 5.4 %collective-permute-done.1.refs_4_ = f32[11,16,256]{2,1,0:T(8,128)S(1)} collective-permute-done((f32[11,16,256]{2,1,0:T(8,128)S(1)}, f32[11,16,256]{2,1,0:T(8,128)S(1)}, u32[]{:S(2)}, u32[]{:S(2)}) %collective-permute-start.1) | collective-permute-done | bytes 180256 | tf_op jit(solution)/shard_map/ppermute | solution.py:433
  14.1 0.0 copy-done
  14.3 0.0 copy-done.2
  14.3 0.0 slice-start
  14.3 0.8 slice-done
  15.1 4.7 %collective-permute-start.3 = (f32[272,256]{1,0:T(8,128)S(1)}, f32[272,256]{1,0:T(8,128)S(1)}, u32[]{:S(2)}, u32[]{:S(2)}) collective-permute-start(f32[272,256]{1,0:T(8,128)S(1)} %pad_maximum_fusion.2), channel_id=1, source_target_pairs={{0,31},{1,0},{2,1},{3,2},{4,3},{5,4},{6,5},{7,6},{8,7},{9,8},{10,9... | collective-permute-start | bytes 835592 | tf_op jit(solution)/shard_map/ppermute | solution.py:433
  19.9 0.0 copy-start.3
  20.0 0.1 collective-permute-start.2
  20.0 0.1 pad_add_fusion.refs_0_
  20.1 4.4 %collective-permute-done.3.refs_6_ = f32[272,256]{1,0:T(8,128)S(1)} collective-permute-done((f32[272,256]{1,0:T(8,128)S(1)}, f32[272,256]{1,0:T(8,128)S(1)}, u32[]{:S(2)}, u32[]{:S(2)}) %collective-permute-start.3) | collective-permute-done | bytes 278560 | tf_op jit(solution)/shard_map/ppermute | solution.py:433
  24.5 6.3 %collective-permute-done.2.refs_5_ = f32[272,256]{1,0:T(8,128)S(1)} collective-permute-done((f32[272,256]{1,0:T(8,128)S(1)}, f32[272,256]{1,0:T(8,128)S(1)}, u32[]{:S(2)}, u32[]{:S(2)}) %collective-permute-start.2) | collective-permute-done | bytes 278560 | tf_op jit(solution)/shard_map/ppermute | solution.py:433
  30.8 0.0 copy-done.3
  30.8 3.6 %shard_map.41 = (f32[208,256]{1,0:T(8,128)S(1)}, f32[4,6,32,256]{3,2,1,0:T(8,128)S(1)}, f32[10,32,256]{2,1,0:T(8,128)S(1)}, f32[8,32,256]{2,1,0:T(8,128)S(1)}, f32[4,8,32,256]{3,2,1,0:T(8,128)S(1)}) custom-call(s32[2]{0:T(128)S(1)} %pad_add_fusion.refs_0_, f32[4,4,16,256]{3,2,1,0:T(8,128)S(1)} %copy-done, f32[4,16,256]{2,1,0:T(8,128)S(1)} %copy-done.1, ...), custom_call_target="tpu_custom_call" | custom-call | tf_op jit(solution)/shard_map/pallas_call | solution.py:421
  34.4 2.6 %collective-permute-start.4 = (f32[208,256]{1,0:T(8,128)S(1)}, f32[208,256]{1,0:T(8,128)S(1)}, u32[]{:S(2)}, u32[]{:S(2)}) collective-permute-start(f32[208,256]{1,0:T(8,128)S(1)} %get-tuple-element.14), channel_id=1, source_target_pairs={{0,32},{32,0},{64,96},{96,64},{128,160},{160,128},{192,224},{224,1... | collective-permute-start | bytes 638984 | tf_op jit(solution)/shard_map/ppermute | solution.py:463
  37.0 1.1 %collective-permute-done.4 = f32[208,256]{1,0:T(8,128)S(1)} collective-permute-done((f32[208,256]{1,0:T(8,128)S(1)}, f32[208,256]{1,0:T(8,128)S(1)}, u32[]{:S(2)}, u32[]{:S(2)}) %collective-permute-start.4) | collective-permute-done | bytes 213024 | tf_op jit(solution)/shard_map/ppermute | solution.py:463
  38.1 2.2 %collective-permute-start.5 = (f32[272,256]{1,0:T(8,128)S(1)}, f32[272,256]{1,0:T(8,128)S(1)}, u32[]{:S(2)}, u32[]{:S(2)}) collective-permute-start(f32[272,256]{1,0:T(8,128)S(1)} %pad_maximum_fusion.3), channel_id=1, source_target_pairs={{0,224},{32,64},{64,32},{96,128},{128,96},{160,192},{192,160},{224... | collective-permute-start | bytes 835592 | tf_op jit(solution)/shard_map/ppermute | solution.py:464
  40.3 3.4 %collective-permute-start.6 = (f32[64,256]{1,0:T(8,128)S(1)}, f32[64,256]{1,0:T(8,128)S(1)}, u32[]{:S(2)}, u32[]{:S(2)}) collective-permute-start(f32[64,256]{1,0:T(8,128)S(1)} %slice.68.refs_1_), channel_id=1, source_target_pairs={{0,128},{32,160},{64,192},{96,224},{128,0},{160,32},{192,64},{224,... | collective-permute-start | bytes 196616 | tf_op jit(solution)/shard_map/ppermute | solution.py:433
  43.7 4.2 %collective-permute-done.5.refs_3_ = f32[272,256]{1,0:T(8,128)S(1)} collective-permute-done((f32[272,256]{1,0:T(8,128)S(1)}, f32[272,256]{1,0:T(8,128)S(1)}, u32[]{:S(2)}, u32[]{:S(2)}) %collective-permute-start.5) | collective-permute-done | bytes 278560 | tf_op jit(solution)/shard_map/ppermute | solution.py:464
  47.9 3.1 %collective-permute-done.6.refs_4_ = f32[64,256]{1,0:T(8,128)S(1)} collective-permute-done((f32[64,256]{1,0:T(8,128)S(1)}, f32[64,256]{1,0:T(8,128)S(1)}, u32[]{:S(2)}, u32[]{:S(2)}) %collective-permute-start.6) | collective-permute-done | bytes 65568 | tf_op jit(solution)/shard_map/ppermute | solution.py:433
  51.0 0.1 collective-permute-start.7
  51.1 1.4 %collective-permute-done.7.refs_5_ = f32[192,256]{1,0:T(8,128)S(1)} collective-permute-done((f32[192,256]{1,0:T(8,128)S(1)}, f32[192,256]{1,0:T(8,128)S(1)}, u32[]{:S(2)}, u32[]{:S(2)}) %collective-permute-start.7) | collective-permute-done | bytes 196640 | tf_op jit(solution)/shard_map/ppermute | solution.py:466
  52.5 5.6 %shard_map.42 = (f32[208,128]{1,0:T(8,128)S(1)}, f32[208,128]{1,0:T(8,128)S(1)}, f32[80,128]{1,0:T(8,128)S(1)}, f32[4,10,16,128]{3,2,1,0:T(8,128)S(1)}, f32[4,10...) custom-call(s32[2]{0:T(128)S(1)} %pad_add_fusion.refs_0_, ...), custom_call_target="tpu_custom_call" | custom-call | tf_op jit(solution)/shard_map/pallas_call | solution.py:421
  58.1 0.1 collective-permute-start.8
  58.2 5.7 %collective-permute-start.9 = (f32[208,128]{1,0:T(8,128)S(1)}, f32[208,128]{1,0:T(8,128)S(1)}, u32[]{:S(2)}, u32[]{:S(2)}) collective-permute-start(f32[208,128]{1,0:T(8,128)S(1)} %get-tuple-element.17), channel_id=1, source_target_pairs={{0,31},{1,0},{2,1},{3,2},{4,3},{5,4},{6,5},{7,6},{8,7},{9,8},{10,9... | collective-permute-start | bytes 319496 | tf_op jit(solution)/shard_map/ppermute | solution.py:433
  63.9 0.0 collective-permute-start.10
  63.9 6.0 %collective-permute-start.11 = (f32[80,128]{1,0:T(8,128)S(1)}, f32[80,128]{1,0:T(8,128)S(1)}, u32[]{:S(2)}, u32[]{:S(2)}) collective-permute-start(f32[80,128]{1,0:T(8,128)S(1)} %get-tuple-element.15.refs_1_), channel_id=1, source_target_pairs={{0,30},{1,31},{2,0},{3,1},{4,2},{5,3},{6,4},{7,5},{8,6},{9,7},{10,... | collective-permute-start | bytes 122888 | tf_op jit(solution)/shard_map/ppermute | solution.py:433
  69.9 1.4 %collective-permute-done.10.refs_4_ = f32[80,128]{1,0:T(8,128)S(1)} collective-permute-done((f32[80,128]{1,0:T(8,128)S(1)}, f32[80,128]{1,0:T(8,128)S(1)}, u32[]{:S(2)}, u32[]{:S(2)}) %collective-permute-start.10) | collective-permute-done | bytes 40992 | tf_op jit(solution)/shard_map/ppermute | solution.py:433
  71.3 0.0 collective-permute-done.11.refs_5_
  71.3 0.0 collective-permute-done.8.refs_2_
  71.3 0.0 collective-permute-done.9.refs_3_
  71.3 11.7 %shard_map.43 = (f32[4,4,16,256]{3,2,1,0:T(8,128)}, f32[4,4,16,256]{3,2,1,0:T(8,128)}) custom-call(s32[2]{0:T(128)S(1)} %pad_add_fusion.refs_0_, f32[80,128]{1,0:T(8,128)S(1)} %get-tuple-element.15.refs_1_, f32[208,128]{1,0:T(8,128)S(1)} %collective-permute-done.8.refs_2_, f32[208,128]{1,0:T(8,128)S(1)} %collective-permute-done.9.refs_3_, ...), custom_call_target="tpu_custom_call" | custom-call | tf_op jit(solution)/shard_map/pallas_call | solution.py:421
  (23 shorter events, 0.4 us)
Async XLA Ops:
  0.6 1.0 %copy-start.1 = (f32[4,16,256]{2,1,0:T(8,128)S(1)}, f32[4,16,256]{2,1,0:T(8,128)}, u32[]{:S(2)}) copy-start(f32[4,16,256]{2,1,0:T(8,128)} %refs_2_.1) | copy-start | bytes 196612
  1.7 6.9 %collective-permute-start = (f32[11,16,256]{2,1,0:T(8,128)S(1)}, f32[11,16,256]{2,1,0:T(8,128)S(1)}, u32[]{:S(2)}, u32[]{:S(2)}) collective-permute-start(f32[11,16,256]{2,1,0:T(8,128)S(1)} %pad_maximum_fusion.5), channel_id=1, source_target_pairs={{0,32},{32,64},{64,96},{96,128},{128,160},{160,192},{192,224},{224... | collective-permute-start | bytes 540680 | tf_op jit(solution)/shard_map/ppermute | solution.py:433
  6.2 7.9 %copy-start = (f32[4,4,16,256]{3,2,1,0:T(8,128)S(1)}, f32[4,4,16,256]{3,2,1,0:T(8,128)}, u32[]{:S(2)}) copy-start(f32[4,4,16,256]{3,2,1,0:T(8,128)} %refs_1_.1) | copy-start | bytes 786436
  6.2 7.9 %collective-permute-start.1 = (f32[11,16,256]{2,1,0:T(8,128)S(1)}, f32[11,16,256]{2,1,0:T(8,128)S(1)}, u32[]{:S(2)}, u32[]{:S(2)}) collective-permute-start(f32[11,16,256]{2,1,0:T(8,128)S(1)} %pad_maximum_fusion.6), channel_id=1, source_target_pairs={{0,224},{32,0},{64,32},{96,64},{128,96},{160,128},{192,160},{224,1... | collective-permute-start | bytes 540680 | tf_op jit(solution)/shard_map/ppermute | solution.py:433
  8.6 5.6 %copy-start.2 = (f32[11,16,256]{2,1,0:T(8,128)}, f32[11,16,256]{2,1,0:T(8,128)S(1)}, u32[]{:S(2)}) copy-start(f32[11,16,256]{2,1,0:T(8,128)S(1)} %collective-permute-done.refs_3_) | copy-start | bytes 540676
  14.3 0.8 slice-start
  15.1 9.4 %collective-permute-start.3 = (f32[272,256]{1,0:T(8,128)S(1)}, f32[272,256]{1,0:T(8,128)S(1)}, u32[]{:S(2)}, u32[]{:S(2)}) collective-permute-start(f32[272,256]{1,0:T(8,128)S(1)} %pad_maximum_fusion.2), channel_id=1, source_target_pairs={{0,31},{1,0},{2,1},{3,2},{4,3},{5,4},{6,5},{7,6},{8,7},{9,8},{10,9... | collective-permute-start | bytes 835592 | tf_op jit(solution)/shard_map/ppermute | solution.py:433
  19.9 10.9 %copy-start.3 = (f32[11,16,256]{2,1,0:T(8,128)S(1)}, f32[11,16,256]{2,1,0:T(8,128)}, u32[]{:S(2)}) copy-start(f32[11,16,256]{2,1,0:T(8,128)} %copy-done.2) | copy-start | bytes 540676
  20.0 10.9 %collective-permute-start.2 = (f32[272,256]{1,0:T(8,128)S(1)}, f32[272,256]{1,0:T(8,128)S(1)}, u32[]{:S(2)}, u32[]{:S(2)}) collective-permute-start(f32[272,256]{1,0:T(8,128)S(1)} %pad_maximum_fusion.1), channel_id=1, source_target_pairs={{0,1},{1,2},{2,3},{3,4},{4,5},{5,6},{6,7},{7,8},{8,9},{9,10},{10,1... | collective-permute-start | bytes 835592 | tf_op jit(solution)/shard_map/ppermute | solution.py:433
  34.4 3.7 %collective-permute-start.4 = (f32[208,256]{1,0:T(8,128)S(1)}, f32[208,256]{1,0:T(8,128)S(1)}, u32[]{:S(2)}, u32[]{:S(2)}) collective-permute-start(f32[208,256]{1,0:T(8,128)S(1)} %get-tuple-element.14), channel_id=1, source_target_pairs={{0,32},{32,0},{64,96},{96,64},{128,160},{160,128},{192,224},{224,1... | collective-permute-start | bytes 638984 | tf_op jit(solution)/shard_map/ppermute | solution.py:463
  38.1 9.8 %collective-permute-start.5 = (f32[272,256]{1,0:T(8,128)S(1)}, f32[272,256]{1,0:T(8,128)S(1)}, u32[]{:S(2)}, u32[]{:S(2)}) collective-permute-start(f32[272,256]{1,0:T(8,128)S(1)} %pad_maximum_fusion.3), channel_id=1, source_target_pairs={{0,224},{32,64},{64,32},{96,128},{128,96},{160,192},{192,160},{224... | collective-permute-start | bytes 835592 | tf_op jit(solution)/shard_map/ppermute | solution.py:464
  40.3 10.7 %collective-permute-start.6 = (f32[64,256]{1,0:T(8,128)S(1)}, f32[64,256]{1,0:T(8,128)S(1)}, u32[]{:S(2)}, u32[]{:S(2)}) collective-permute-start(f32[64,256]{1,0:T(8,128)S(1)} %slice.68.refs_1_), channel_id=1, source_target_pairs={{0,128},{32,160},{64,192},{96,224},{128,0},{160,32},{192,64},{224,... | collective-permute-start | bytes 196616 | tf_op jit(solution)/shard_map/ppermute | solution.py:433
  51.0 1.5 %collective-permute-start.7 = (f32[192,256]{1,0:T(8,128)S(1)}, f32[192,256]{1,0:T(8,128)S(1)}, u32[]{:S(2)}, u32[]{:S(2)}) collective-permute-start(f32[192,256]{1,0:T(8,128)S(1)} %pad_maximum_fusion.4), channel_id=1, source_target_pairs={{0,32},{32,0},{64,96},{96,64},{128,160},{160,128},{192,224},{224,1... | collective-permute-start | bytes 589832 | tf_op jit(solution)/shard_map/ppermute | solution.py:466
  58.1 13.1 %collective-permute-start.8 = (f32[208,128]{1,0:T(8,128)S(1)}, f32[208,128]{1,0:T(8,128)S(1)}, u32[]{:S(2)}, u32[]{:S(2)}) collective-permute-start(f32[208,128]{1,0:T(8,128)S(1)} %get-tuple-element.16), channel_id=1, source_target_pairs={{0,1},{1,2},{2,3},{3,4},{4,5},{5,6},{6,7},{7,8},{8,9},{9,10},{10,1... | collective-permute-start | bytes 319496 | tf_op jit(solution)/shard_map/ppermute | solution.py:433
  58.2 13.0 %collective-permute-start.9 = (f32[208,128]{1,0:T(8,128)S(1)}, f32[208,128]{1,0:T(8,128)S(1)}, u32[]{:S(2)}, u32[]{:S(2)}) collective-permute-start(f32[208,128]{1,0:T(8,128)S(1)} %get-tuple-element.17), channel_id=1, source_target_pairs={{0,31},{1,0},{2,1},{3,2},{4,3},{5,4},{6,5},{7,6},{8,7},{9,8},{10,9... | collective-permute-start | bytes 319496 | tf_op jit(solution)/shard_map/ppermute | solution.py:433
  63.9 7.4 %collective-permute-start.10 = (f32[80,128]{1,0:T(8,128)S(1)}, f32[80,128]{1,0:T(8,128)S(1)}, u32[]{:S(2)}, u32[]{:S(2)}) collective-permute-start(f32[80,128]{1,0:T(8,128)S(1)} %get-tuple-element.15.refs_1_), channel_id=1, source_target_pairs={{0,2},{1,3},{2,4},{3,5},{4,6},{5,7},{6,8},{7,9},{8,10},{9,11},{10,... | collective-permute-start | bytes 122888 | tf_op jit(solution)/shard_map/ppermute | solution.py:433
  63.9 7.4 %collective-permute-start.11 = (f32[80,128]{1,0:T(8,128)S(1)}, f32[80,128]{1,0:T(8,128)S(1)}, u32[]{:S(2)}, u32[]{:S(2)}) collective-permute-start(f32[80,128]{1,0:T(8,128)S(1)} %get-tuple-element.15.refs_1_), channel_id=1, source_target_pairs={{0,30},{1,31},{2,0},{3,1},{4,2},{5,3},{6,4},{7,5},{8,6},{9,7},{10,... | collective-permute-start | bytes 122888 | tf_op jit(solution)/shard_map/ppermute | solution.py:433

commit v2 on v1

v2 whole, which is shorter than its diff:
```python
import jax
import jax.numpy as jnp
from jax import lax
from jax.experimental import pallas as pl
from jax.experimental.pallas import tpu as pltpu
from jax.sharding import PartitionSpec as P

COARSE = 6
OMEGA = 0.6
BETA = 0.25
F32 = jnp.float32
VMEM_LIMIT = 48 * 1024 * 1024


def shifts(value, step):
    rows, lanes = value.shape
    lane = lax.broadcasted_iota(jnp.int32, (rows, 128), 1)
    if lanes == 256:
        low, high = value[:, :128], value[:, 128:]
        low_up, high_up = pltpu.roll(low, 127, 1), pltpu.roll(high, 127, 1)
        low_dn, high_dn = pltpu.roll(low, 1, 1), pltpu.roll(high, 1, 1)
        last, first = lane == 127, lane == 0
        plus = jnp.concatenate([jnp.where(last, high_up, low_up), jnp.where(last, 0.0, high_up)], 1)
        minus = jnp.concatenate([jnp.where(first, 0.0, low_dn), jnp.where(first, low_dn, high_dn)], 1)
        return plus, minus
    plus = jnp.where(lane >= 128 - step, 0.0, pltpu.roll(value, 128 - step, 1))
    minus = jnp.where(lane < step, 0.0, pltpu.roll(value, step, 1))
    return plus, minus


def get(ref, lead, row, count=8):
    if len(ref.shape) == len(lead) + 3:
        return jnp.concatenate([ref[(*lead, n, pl.ds(row, count))] for n in range(2)], 1)
    return ref[(*lead, pl.ds(row, count))]


def put(ref, lead, row, value):
    rows = pl.ds(row, value.shape[0])
    if len(ref.shape) == len(lead) + 3:
        for n in range(2):
            ref[(*lead, n, rows)] = value[:, 128 * n : 128 * n + 128]
    else:
        ref[(*lead, rows)] = value


def around(ref, lead, layer, row, step):
    rows = ref.shape[-2]
    here = get(ref, (*lead, layer), row)
    near = [get(ref, (*lead, layer + 1), row), get(ref, (*lead, layer - 1), row)]
    near.append(get(ref, (*lead, layer), row + 1) if row + 9 <= rows else pltpu.roll(here, 7, 0))
    near.append(get(ref, (*lead, layer), row - 1) if row >= 1 else pltpu.roll(here, 1, 0))
    return here, [*near, *shifts(here, step)]


def sums_of(visc, layer, row, step):
    here, near = around(visc, (), layer, row, step)
    sums = [here + other for other in near]
    return here, sums, sum(sums[1:], sums[0])


def stencil(field, layer, row, step, sums):
    here, flux, grad, div = [], [], None, None
    for comp in range(4):
        centre, near = around(field, (comp,), layer, row, step)
        here.append(centre)
        if comp < 3:
            terms = [s * n for s, n in zip(sums, near)]
            flux.append(sum(terms[1:], terms[0]))
            diff = near[2 * comp] - near[2 * comp + 1]
            div = diff if div is None else div + diff
        else:
            grad = [near[2 * c] - near[2 * c + 1] for c in range(3)]
    return here, flux, grad, div


def sweep_chunk(out, field, layer, row, step, spacing, visc, visc_layer, weight, weight_layer, source, source_layer):
    e_here, sums, _ = sums_of(visc, visc_layer, row, step)
    here, flux, grad, div = stencil(field, layer, row, step, sums)
    w = get(weight, (weight_layer,), row)
    for c in range(3):
        b = get(source, (c, source_layer), row)
        value = (1.0 - OMEGA) * here[c] + w * (b + (0.5 / (spacing * spacing)) * flux[c] - (0.5 / spacing) * grad[c])
        put(out, (c, layer), row, value)
    b = get(source, (3, source_layer), row)
    put(out, (3, layer), row, here[3] + (BETA * e_here) * (b - (0.5 / spacing) * div))


def residual_chunk(field, layer, row, step, spacing, visc, visc_layer, source, source_layer):
    _, sums, total = sums_of(visc, visc_layer, row, step)
    here, flux, grad, div = stencil(field, layer, row, step, sums)
    out = []
    for c in range(3):
        b = get(source, (c, source_layer), row)
        out.append(b - ((0.5 / (spacing * spacing)) * (total * here[c] - flux[c]) + (0.5 / spacing) * grad[c]))
    out.append(get(source, (3, source_layer), row) - (0.5 / spacing) * div)
    return out


def start_chunk(out, layer, row, step, spacing, visc, visc_layer, weight, weight_layer, source, source_layer, inside):
    e_here, _, total = sums_of(visc, visc_layer, row, step)
    w = jnp.where(inside, (2.0 * OMEGA * spacing * spacing) / total, 0.0)
    put(weight, (weight_layer,), row, w)
    for c in range(4):
        scale = w if c < 3 else BETA * e_here
        put(out, (c, layer), row, scale * get(source, (c, source_layer), row))


def rows_inside(row, first, count, lanes):
    at = lax.broadcasted_iota(jnp.int32, (8, lanes), 0) + (row + first)
    return (at >= 0) & (at < count)


def fold_matrix(fine, transpose=False):
    shape = (fine // 2, fine) if transpose else (fine, fine // 2)
    a = lax.broadcasted_iota(jnp.int32, shape, 1 if transpose else 0)
    b = lax.broadcasted_iota(jnp.int32, shape, 0 if transpose else 1)
    return jnp.where(a // 2 == b, 1.0, 0.0).astype(F32)


def exact_dot(a, b):
    return jnp.dot(a, b, precision=lax.Precision.HIGHEST, preferred_element_type=F32)


def fine_down(groups, devs, idx, f, e, xm, xp, ym, yp, pay_o, x1, ew, wt, fw, x0, pair, half):
    g, d = idx[0], idx[1]
    low_x, high_x = jnp.where(g > 0, 1.0, 0.0), jnp.where(g < groups - 1, 1.0, 0.0)
    low_y, high_y = jnp.where(d > 0, 1.0, 0.0), jnp.where(d < devs - 1, 1.0, 0.0)
    zero = jnp.zeros((2, 256), F32)
    for layer in range(10):
        own = xm[8 + layer] if layer < 3 else xp[8 + layer - 7] if layer > 6 else e[layer - 3]
        s = low_x if layer < 3 else high_x if layer > 6 else 1.0
        at = slice(192 + 8 * layer, 200 + 8 * layer)
        put(ew, (layer,), 0, ym[at, :] * (s * low_y))
        put(ew, (layer,), 8, own * s)
        put(ew, (layer,), 24, yp[at, :] * (s * high_y))
    for layer in range(8):
        for c in range(4):
            own = xm[2 * c + layer] if layer < 2 else xp[2 * c + layer - 6] if layer > 5 else f[c, layer - 2]
            at = slice(24 * layer + 6 * c, 24 * layer + 6 * c + 6)
            put(fw, (c, layer), 0, jnp.concatenate([zero, ym[at, :]], 0))
            put(fw, (c, layer), 8, own)
            put(fw, (c, layer), 24, jnp.concatenate([yp[at, :], zero], 0))
    for layer in range(8):
        layer_in = (4 * g - 2 + layer >= 0) & (4 * g - 2 + layer < 4 * groups)
        for row in (0, 8, 16, 24):
            inside = rows_inside(row, 16 * d - 8, 16 * devs, 256) & layer_in
            start_chunk(x0, layer, row, 1, 1.0, ew, layer + 1, wt, layer, fw, layer, inside)
    for layer in range(1, 7):
        for row in (0, 8, 16, 24):
            sweep_chunk(x1, x0, layer, row, 1, 1.0, ew, layer + 1, wt, layer, fw, layer)
    for m in range(2):
        for row in (4, 12, 20):
            a = residual_chunk(x1, 2 * m + 2, row, 1, 1.0, ew, 2 * m + 3, fw, 2 * m + 2)
            b = residual_chunk(x1, 2 * m + 3, row, 1, 1.0, ew, 2 * m + 4, fw, 2 * m + 3)
            for c in range(4):
                pair[2 * c + m, row : row + 8, :] = a[c] + b[c]
        for c in range(4):
            pair[2 * c + m, 0:4, :] = jnp.zeros((4, 256), F32)
            pair[2 * c + m, 28:32, :] = jnp.zeros((4, 256), F32)
        pair[8 + m] = get(ew, (2 * m + 3,), 0, 32) + get(ew, (2 * m + 4,), 0, 32)
    half[...] = exact_dot(pair[...].reshape(320, 256), fold_matrix(256)) * 0.125
    coarse = half[pl.ds(0, 160, stride=2), :] + half[pl.ds(1, 160, stride=2), :]
    coarse = coarse.reshape(10, 16, 128)
    for m in range(2):
        lanes = slice(128 * m, 128 * m + 128)
        for c in range(4):
            pay_o[12 * c : 12 * c + 12, lanes] = coarse[2 * c + m, 2:14, :]
        pay_o[48:64, lanes] = coarse[8 + m]
    for c in range(4):
        for j in range(2):
            at = 64 + 18 * (2 * c + j)
            pay_o[at : at + 18, :] = get(x1, (c, 3 + j), 7, 18)


def mid_down(groups, devs, idx, own, partner, xr, c2, s3, up_o, dn_o, low_o, y_o, b_o, e_o, w_o, bw, ew, wt, y0, y1, pair, low):
    g, d = idx[0], idx[1]
    chips = groups // 2
    chip, core = g // 2, g % 2
    other = 1 - core
    beside = (chip + chips - 1 + 2 * core) % chips
    across = (chip + 1 + (chips - 2) * core) % chips
    far = (chip + 2) % chips
    layers = 2 * groups
    zero = jnp.zeros((16, 128), F32)
    for i in (0, 1, 2, 3, layers + 4, layers + 5, layers + 6, layers + 7):
        ew[i] = zero
        wt[i] = zero
        for c in range(4):
            bw[c, i] = zero
            y0[c, i] = zero
            y1[c, i] = zero
    for i in range(layers):
        for c in range(4):
            bw[c, i + 4, 0:2, :] = zero[0:2]
            bw[c, i + 4, 14:16, :] = zero[0:2]

    def place(block, at, which, core_at):
        base = 4 + 4 * which + 2 * core_at
        for m in range(2):
            lanes = slice(128 * m, 128 * m + 128)
            for c in range(4):
                bw[c, base + m, 2:14, :] = block[at + 12 * c : at + 12 * c + 12, lanes]
            ew[base + m] = block[at + 48 : at + 64, lanes]

    place(own, 0, chip, core)
    place(partner, 0, chip, other)
    place(xr, 0, beside, other)
    place(xr, 208, beside, core)
    place(s3, 0, across, core)
    place(s3, 64, across, other)
    place(c2, 0, far, core)
    place(s3, 128, far, other)
    for i in range(4, layers + 4):
        for row in (0, 8):
            inside = rows_inside(row, 8 * d - 4, 8 * devs, 128)
            start_chunk(y0, i, row, 1, 2.0, ew, i, wt, i, bw, i, inside)
    for i in range(4, layers + 4):
        for row in (0, 8):
            sweep_chunk(y1, y0, i, row, 1, 2.0, ew, i, wt, i, bw, i)
    lane = lax.broadcasted_iota(jnp.int32, (4, 128), 1)
    for m in range(groups):
        at = 2 * m + 4
        a = residual_chunk(y1, at, 4, 1, 2.0, ew, at, bw, at)
        b = residual_chunk(y1, at + 1, 4, 1, 2.0, ew, at + 1, bw, at + 1)
        for c in range(5):
            pair[m, c] = a[c] + b[c] if c < 4 else get(ew, (at,), 4) + get(ew, (at + 1,), 4)
    for m in range(groups):
        for c in range(5):
            rows = pair[m, c, pl.ds(0, 4, stride=2), :] + pair[m, c, pl.ds(1, 4, stride=2), :]
            mate = jnp.where(lane % 2 == 0, pltpu.roll(rows, 127, 1), pltpu.roll(rows, 1, 1))
            low[c, m, 0:4, :] = (rows + mate) * 0.125
    for c in range(5):
        for q in range(groups // 2):
            packed = jnp.where(lane % 2 == 0, low[c, 2 * q, 0:4, :], low[c, 2 * q + 1, 0:4, :])
            at = 4 * (c * (groups // 2) + q)
            for out in (up_o, dn_o, low_o):
                out[at : at + 4, :] = packed
    base = 20 * (groups // 2)
    for c in range(4):
        for j in range(6):
            at = base + 4 * (6 * c + j)
            up_o[at : at + 4, :] = y1[c, 2 * g + 2 + j, 8:12, :]
            dn_o[at : at + 4, :] = y1[c, 2 * g + 2 + j, 4:8, :]
        for j in range(2):
            at = base + 96 + 4 * (2 * c + j)
            up_o[at : at + 4, :] = bw[c, 2 * g + 4 + j, 8:12, :]
            dn_o[at : at + 4, :] = bw[c, 2 * g + 4 + j, 4:8, :]
    for j in range(10):
        e_o[j] = ew[2 * g + j]
        w_o[j] = wt[2 * g + j]
        for c in range(4):
            y_o[c, j] = y1[c, 2 * g + j]
            b_o[c, j] = bw[c, 2 * g + j]


def up_all(groups, devs, idx, low, m1, p1, m2, p2, y_i, b_i, e1, w1, x1, ew, wt, fw, own_edge, far_edge, sol_o, res_o,
           e2, w2, b2, z0, z1, b1, ya, yb, rep, half, va, vb):
    g, d = idx[0], idx[1]
    core = g % 2
    zero = jnp.zeros((32, 128), F32)
    lane = lax.broadcasted_iota(jnp.int32, (4, 128), 1)
    even = lane % 2 == 0

    for i in (0, 1, groups + 2, groups + 3):
        e2[i] = zero
        for c in range(4):
            z0[c, i] = zero
            z1[c, i] = zero
    for i in range(2, groups + 2):
        e2[i, 0:8, :] = zero[0:8]
        e2[i, 16:32, :] = zero[0:16]
        for c in range(4):
            b2[c, i, 0:8, :] = zero[0:8]
            b2[c, i, 16:32, :] = zero[0:16]
    for source, away in ((m2, -2), (m1, -1), (low, 0), (p1, 1), (p2, 2)):
        row = 10 + 4 * away
        there = 1.0 if away == 0 else jnp.where((d + away >= 0) & (d + away < devs), 1.0, 0.0)
        for c in range(5):
            for q in range(groups // 2):
                at = 4 * (c * (groups // 2) + q)
                packed = source[at : at + 4, :]
                first = jnp.where(even, packed, pltpu.roll(packed, 1, 1))
                second = jnp.where(even, pltpu.roll(packed, 127, 1), packed)
                if c == 4:
                    e2[2 * q + 2, row : row + 4, :] = first * there
                    e2[2 * q + 3, row : row + 4, :] = second * there
                else:
                    b2[c, 2 * q + 2, row : row + 4, :] = first
                    b2[c, 2 * q + 3, row : row + 4, :] = second
    for i in range(2, groups + 2):
        for row in (0, 8, 16):
            inside = rows_inside(row, 4 * d - 10, 4 * devs, 128)
            start_chunk(z0, i, row, 2, 4.0, e2, i, w2, i, b2, i, inside)
    here, other = z0, z1
    for _ in range(COARSE - 1):
        for i in range(2, groups + 2):
            for row in (4, 12):
                sweep_chunk(other, here, i, row, 2, 4.0, e2, i, w2, i, b2, i)
        here, other = other, here
    z = here

    low_y, high_y = jnp.where(d > 0, 1.0, 0.0), jnp.where(d < devs - 1, 1.0, 0.0)
    base = 20 * (groups // 2)
    for c in range(4):
        for k in range(5):
            rows = z[c, g + k, 8:16, :]
            rep[c, k, pl.ds(0, 8, stride=2), :] = rows
            rep[c, k, pl.ds(1, 8, stride=2), :] = rows
    for c in range(4):
        for j in range(10):
            b1[c, j] = b_i[c, j]
            ya[c, j] = y_i[c, j]
        for j in range(2):
            at = base + 96 + 4 * (2 * c + j)
            b1[c, 4 + j, 0:4, :] = m1[at : at + 4, :]
            b1[c, 4 + j, 12:16, :] = p1[at : at + 4, :]
        for j in range(6):
            at = base + 4 * (6 * c + j)
            ya[c, 2 + j, 0:4, :] = m1[at : at + 4, :] * low_y
            ya[c, 2 + j, 12:16, :] = p1[at : at + 4, :] * high_y
        for j in range(10):
            ya[c, j] = ya[c, j] + rep[c, j // 2]
    for at in range(1, 9):
        for row in (0, 8):
            sweep_chunk(yb, ya, at, row, 1, 2.0, e1, at, w1, at, b1, at)
    for at in range(2, 8):
        for row in (0, 8):
            sweep_chunk(ya, yb, at, row, 1, 2.0, e1, at, w1, at, b1, at)

    spread = fold_matrix(256, True)
    wide = exact_dot(ya[:, 2:8].reshape(384, 128), spread)
    for n in range(2):
        for parity in range(2):
            half[n, pl.ds(parity, 384, stride=2), :] = wide[:, 128 * n : 128 * n + 128]
    low_x, high_x = jnp.where(g > 0, 1.0, 0.0), jnp.where(g < groups - 1, 1.0, 0.0)
    for c in range(4):
        for layer in range(1, 11):
            for n in range(2):
                at = (6 * c + layer // 2) * 32
                rows = half[n, at : at + 32, :]
                va[c, layer, n] = rows + x1[c, layer - 2, n] if 3 <= layer <= 8 else rows
        for j in range(2):
            at = 18 * (2 * c + j)
            own, far = own_edge[at : at + 18, :], far_edge[at : at + 18, :]
            before = jnp.where(core == 0, far, own) * low_x
            after = jnp.where(core == 0, own, far) * high_x
            put(va, (c, 1 + j), 7, get(va, (c, 1 + j), 7, 18) + before)
            put(va, (c, 9 + j), 7, get(va, (c, 9 + j), 7, 18) + after)
    for at in range(2, 10):
        for row in (4, 12, 20):
            sweep_chunk(vb, va, at, row, 1, 1.0, ew, at - 1, wt, at - 2, fw, at - 2)
    for at in range(3, 9):
        for row in (4, 12, 20):
            sweep_chunk(va, vb, at, row, 1, 1.0, ew, at - 1, wt, at - 2, fw, at - 2)
    for i in range(4):
        for row in (8, 16):
            out = residual_chunk(va, i + 4, row, 1, 1.0, ew, i + 3, fw, i + 2)
            for c in range(4):
                sol_o[c, i, row - 8 : row, :] = get(va, (c, i + 4), row)
                res_o[c, i, row - 8 : row, :] = out[c]


def call(kernel, outs, scratch, *args):
    specs = [pl.BlockSpec(memory_space=pltpu.SMEM)] + [pl.BlockSpec(memory_space=pltpu.VMEM)] * (len(args) - 1)
    return pl.pallas_call(
        kernel,
        out_shape=[jax.ShapeDtypeStruct(shape, F32) for shape in outs],
        in_specs=specs,
        out_specs=[pl.BlockSpec(memory_space=pltpu.VMEM)] * len(outs),
        scratch_shapes=[pltpu.VMEM(shape, F32) for shape in scratch],
        compiler_params=pltpu.CompilerParams(vmem_limit_bytes=VMEM_LIMIT),
    )(*args)


def shift(value, axis, by):
    peers = lax.axis_size(axis)
    return lax.ppermute(value, axis, [(i, (i + by) % peers) for i in range(peers)])


def local(forcing, viscosity):
    groups, devs = lax.axis_size("grp"), lax.axis_size("dev")
    idx = jnp.stack([lax.axis_index("grp"), lax.axis_index("dev")]).astype(jnp.int32)

    def x_pack(f, e):
        return jnp.concatenate([f.reshape(8, 16, 256), e], axis=0)

    xm = shift(x_pack(forcing[:, 2:4], viscosity[1:4]), "grp", 1)
    xp = shift(x_pack(forcing[:, 0:2], viscosity[0:3]), "grp", -1)
    f8 = jnp.concatenate([xm[:8].reshape(4, 2, 16, 256), forcing, xp[:8].reshape(4, 2, 16, 256)], axis=1)
    e10 = jnp.concatenate([xm[8:], viscosity, xp[8:]], axis=0)

    def y_pack(f, e):
        return jnp.concatenate([jnp.swapaxes(f, 0, 1).reshape(192, 256), e.reshape(80, 256)], axis=0)

    ym = shift(y_pack(f8[:, :, 10:16], e10[:, 8:16]), "dev", 1)
    yp = shift(y_pack(f8[:, :, 0:6], e10[:, 0:8]), "dev", -1)

    pay, x1, ew, wt, fw = call(
        lambda *refs: fine_down(groups, devs, *refs),
        [(208, 256), (4, 8, 2, 32, 128), (10, 2, 32, 128), (8, 2, 32, 128), (4, 8, 2, 32, 128)],
        [(4, 8, 2, 32, 128), (10, 32, 256), (320, 128)],
        idx, forcing, viscosity, xm, xp, ym, yp,
    )

    swap = [(i, i ^ 1) for i in range(groups)]
    beside = [(i, (i + 1) % groups if i % 2 else (i - 1) % groups) for i in range(groups)]
    got = lax.ppermute(pay, "grp", swap)
    xr = lax.ppermute(jnp.concatenate([pay, got[:64]], axis=0), "grp", beside)
    c2 = shift(pay[:64], "grp", 4)
    s3 = lax.ppermute(jnp.concatenate([xr[:64], xr[208:], c2], axis=0), "grp", swap)

    layers = 2 * groups + 8
    tall = 20 * (groups // 2)
    up, dn, low, y_w, b_w, e_w, w_w = call(
        lambda *refs: mid_down(groups, devs, *refs),
        [(tall + 128, 128), (tall + 128, 128), (tall, 128), (4, 10, 16, 128), (4, 10, 16, 128), (10, 16, 128), (10, 16, 128)],
        [(4, layers, 16, 128), (layers, 16, 128), (layers, 16, 128), (4, layers, 16, 128), (4, layers, 16, 128),
         (groups, 5, 8, 128), (5, groups, 8, 128)],
        idx, pay[:64], got[:64], xr, c2, s3,
    )

    m1, p1 = shift(up, "dev", 1), shift(dn, "dev", -1)
    m2, p2 = shift(low, "dev", 2), shift(low, "dev", -2)
    deep = groups + 4
    return tuple(call(
        lambda *refs: up_all(groups, devs, *refs),
        [(4, 4, 16, 256), (4, 4, 16, 256)],
        [(deep, 32, 128), (deep, 32, 128), (4, deep, 32, 128), (4, deep, 32, 128), (4, deep, 32, 128),
         (4, 10, 16, 128), (4, 10, 16, 128), (4, 10, 16, 128), (4, 5, 16, 128), (2, 768, 128),
         (4, 12, 2, 32, 128), (4, 12, 2, 32, 128)],
        idx, low, m1, p1, m2, p2, y_w, b_w, e_w, w_w, x1, ew, wt, fw, got[64:], xr[64:208],
    ))


def solution(mesh):
    in_specs = (P(None, "grp", "dev", None), P("grp", "dev", None))
    out_specs = (P(None, "grp", "dev", None), P(None, "grp", "dev", None))
    return jax.shard_map(local, mesh=mesh, in_specs=in_specs, out_specs=out_specs, check_vma=False)
```

time: 83.2 us -> 71.9 us (0.86)
  Pallas kernels: 20.9 us -> 9.57 us
    pallas_call x3, Pallas kernels: 20.9 us -> 9.57 us  [call(): pl.pallas_call(kernel, out_shape=[jax.ShapeDtypeStruct(shape, F32) for sh...]
where the time goes in v2:
time: 71.9 us; the launch traced here: 71.7 us
  waiting for transfers between devices  29.6 us (41%)
  starting transfers between devices  29.3 us (41%)
  Pallas kernels  9.57 us (13%)
  local copies, waits for them, and re-layouts  2.05 us (3%)
  between operations  0.88 us (1%)
    ppermute x9, starting transfers between devices, shift(): lax.ppermute(value, axis, [(i, (i + by) % peers) for i in range(peers)])  24.5 us
    ppermute x9, waiting for transfers between devices, shift(): lax.ppermute(value, axis, [(i, (i + by) % peers) for i in range(peers)])  22.9 us
    pallas_call x3, Pallas kernels, call(): pl.pallas_call(kernel, out_shape=[jax.ShapeDtypeStruct(shape, F32) for sh...  9.57 us
    ppermute x1, waiting for transfers between devices, local(): xr = lax.ppermute(jnp.concatenate([pay, got[:64]], axis=0), 'grp', beside)  4.17 us
    ppermute x1, starting transfers between devices, local(): got = lax.ppermute(pay, 'grp', swap)  2.58 us
    ppermute x1, starting transfers between devices, local(): xr = lax.ppermute(jnp.concatenate([pay, got[:64]], axis=0), 'grp', beside)  2.18 us
  transfers between devices with their start and end apart: 12, of which 9 were waited for; matrix products, arithmetic and copies ran while one was open for 0% of the time, Pallas kernels for 0%

profile of v2, /device:TPU:1, one launch (start us, length us, event | category | flops | bytes accessed | tf_op | source)
XLA Modules:
  0.0 71.7 jit_solution(14155746200660723054)
XLA Ops:
  0.6 0.0 copy-start.1
  0.6 1.0 %fusion.1 = (f32[4,2,16,256]{3,2,1,0:T(8,128)S(1)}, f32[4,2,16,256]{3,2,1,0:T(8,128)S(1)}) fusion(f32[4,4,16,256]{3,2,1,0:T(8,128)} %refs_1_.1), kind=kLoop, calls=%fused_computation.14 | loop fusion | bytes 524288 | tf_op jit(solution)/shard_map/slice | solution.py:388
  1.7 0.0 copy-done.1
  1.7 4.5 %collective-permute-start = (f32[11,16,256]{2,1,0:T(8,128)S(1)}, f32[11,16,256]{2,1,0:T(8,128)S(1)}, u32[]{:S(2)}, u32[]{:S(2)}) collective-permute-start(f32[11,16,256]{2,1,0:T(8,128)S(1)} %pad_maximum_fusion.5), channel_id=1, source_target_pairs={{0,32},{32,64},{64,96},{96,128},{128,160},{160,192},{192,224},{224... | collective-permute-start | bytes 540680 | tf_op jit(solution)/shard_map/ppermute | solution.py:377
  6.2 0.0 copy-start
  6.2 0.1 collective-permute-start.1
  6.3 2.3 %collective-permute-done.refs_3_ = f32[11,16,256]{2,1,0:T(8,128)S(1)} collective-permute-done((f32[11,16,256]{2,1,0:T(8,128)S(1)}, f32[11,16,256]{2,1,0:T(8,128)S(1)}, u32[]{:S(2)}, u32[]{:S(2)}) %collective-permute-start) | collective-permute-done | bytes 180256 | tf_op jit(solution)/shard_map/ppermute | solution.py:377
  8.6 0.0 copy-start.2
  8.6 5.4 %collective-permute-done.1.refs_4_ = f32[11,16,256]{2,1,0:T(8,128)S(1)} collective-permute-done((f32[11,16,256]{2,1,0:T(8,128)S(1)}, f32[11,16,256]{2,1,0:T(8,128)S(1)}, u32[]{:S(2)}, u32[]{:S(2)}) %collective-permute-start.1) | collective-permute-done | bytes 180256 | tf_op jit(solution)/shard_map/ppermute | solution.py:377
  14.1 0.0 copy-done
  14.3 0.0 copy-done.2
  14.3 0.0 slice-start
  14.3 0.8 %slice-done = f32[3,16,256]{2,1,0:T(8,128)S(1)} async-done(((f32[11,16,256]{2,1,0:T(8,128)}), f32[3,16,256]{2,1,0:T(8,128)S(1)}, s32[]{:S(2)}) %slice-start) | async-done | bytes 49176 | tf_op jit(solution)/shard_map/slice | solution.py:390
  15.1 4.7 %collective-permute-start.3 = (f32[272,256]{1,0:T(8,128)S(1)}, f32[272,256]{1,0:T(8,128)S(1)}, u32[]{:S(2)}, u32[]{:S(2)}) collective-permute-start(f32[272,256]{1,0:T(8,128)S(1)} %pad_maximum_fusion.2), channel_id=1, source_target_pairs={{0,31},{1,0},{2,1},{3,2},{4,3},{5,4},{6,5},{7,6},{8,7},{9,8},{10,9... | collective-permute-start | bytes 835592 | tf_op jit(solution)/shard_map/ppermute | solution.py:377
  19.9 0.0 copy-start.3
  20.0 0.1 collective-permute-start.2
  20.0 0.1 pad_add_fusion.refs_0_
  20.1 4.4 %collective-permute-done.3.refs_6_ = f32[272,256]{1,0:T(8,128)S(1)} collective-permute-done((f32[272,256]{1,0:T(8,128)S(1)}, f32[272,256]{1,0:T(8,128)S(1)}, u32[]{:S(2)}, u32[]{:S(2)}) %collective-permute-start.3) | collective-permute-done | bytes 278560 | tf_op jit(solution)/shard_map/ppermute | solution.py:377
  24.5 6.3 %collective-permute-done.2.refs_5_ = f32[272,256]{1,0:T(8,128)S(1)} collective-permute-done((f32[272,256]{1,0:T(8,128)S(1)}, f32[272,256]{1,0:T(8,128)S(1)}, u32[]{:S(2)}, u32[]{:S(2)}) %collective-permute-start.2) | collective-permute-done | bytes 278560 | tf_op jit(solution)/shard_map/ppermute | solution.py:377
  30.8 0.0 copy-done.3
  30.8 2.6 %shard_map.41 = (f32[208,256]{1,0:T(8,128)S(1)}, f32[4,8,2,32,128]{4,3,2,1,0:T(8,128)S(1)}, f32[10,2,32,128]{3,2,1,0:T(8,128)S(1)}, f32[8,2,32,128]{3,2,1,0:T(8,128)S(1)}, f32[4,8,2,32,128]{4,3,2,1,0:T(8,128)S(1)}) custom-call(s32[2]{0:T(128)S(1)} %pad_add_fusion.refs_0_, f32[4,4,16,256]{3,2,1,0:T(8,128)S(1)} %copy-done, f32[4,16,256]{2,1,0:T(8,128)S(1)} %copy-done.1, ...), custom_call_target="tpu_custom_call" | custom-call | tf_op jit(solution)/shard_map/pallas_call | solution.py:365
  33.5 2.6 %collective-permute-start.4 = (f32[208,256]{1,0:T(8,128)S(1)}, f32[208,256]{1,0:T(8,128)S(1)}, u32[]{:S(2)}, u32[]{:S(2)}) collective-permute-start(f32[208,256]{1,0:T(8,128)S(1)} %get-tuple-element.14), channel_id=1, source_target_pairs={{0,32},{32,0},{64,96},{96,64},{128,160},{160,128},{192,224},{224,1... | collective-permute-start | bytes 638984 | tf_op jit(solution)/shard_map/ppermute | solution.py:407
  36.0 1.1 %collective-permute-done.4 = f32[208,256]{1,0:T(8,128)S(1)} collective-permute-done((f32[208,256]{1,0:T(8,128)S(1)}, f32[208,256]{1,0:T(8,128)S(1)}, u32[]{:S(2)}, u32[]{:S(2)}) %collective-permute-start.4) | collective-permute-done | bytes 213024 | tf_op jit(solution)/shard_map/ppermute | solution.py:407
  37.2 2.2 %collective-permute-start.5 = (f32[272,256]{1,0:T(8,128)S(1)}, f32[272,256]{1,0:T(8,128)S(1)}, u32[]{:S(2)}, u32[]{:S(2)}) collective-permute-start(f32[272,256]{1,0:T(8,128)S(1)} %pad_maximum_fusion.3), channel_id=1, source_target_pairs={{0,224},{32,64},{64,32},{96,128},{128,96},{160,192},{192,160},{224... | collective-permute-start | bytes 835592 | tf_op jit(solution)/shard_map/ppermute | solution.py:408
  39.3 3.4 %collective-permute-start.6 = (f32[64,256]{1,0:T(8,128)S(1)}, f32[64,256]{1,0:T(8,128)S(1)}, u32[]{:S(2)}, u32[]{:S(2)}) collective-permute-start(f32[64,256]{1,0:T(8,128)S(1)} %slice.68.refs_1_), channel_id=1, source_target_pairs={{0,128},{32,160},{64,192},{96,224},{128,0},{160,32},{192,64},{224,... | collective-permute-start | bytes 196616 | tf_op jit(solution)/shard_map/ppermute | solution.py:377
  42.7 4.2 %collective-permute-done.5.refs_3_ = f32[272,256]{1,0:T(8,128)S(1)} collective-permute-done((f32[272,256]{1,0:T(8,128)S(1)}, f32[272,256]{1,0:T(8,128)S(1)}, u32[]{:S(2)}, u32[]{:S(2)}) %collective-permute-start.5) | collective-permute-done | bytes 278560 | tf_op jit(solution)/shard_map/ppermute | solution.py:408
  46.9 3.1 %collective-permute-done.6.refs_4_ = f32[64,256]{1,0:T(8,128)S(1)} collective-permute-done((f32[64,256]{1,0:T(8,128)S(1)}, f32[64,256]{1,0:T(8,128)S(1)}, u32[]{:S(2)}, u32[]{:S(2)}) %collective-permute-start.6) | collective-permute-done | bytes 65568 | tf_op jit(solution)/shard_map/ppermute | solution.py:377
  50.0 0.1 collective-permute-start.7
  50.1 1.4 %collective-permute-done.7.refs_5_ = f32[192,256]{1,0:T(8,128)S(1)} collective-permute-done((f32[192,256]{1,0:T(8,128)S(1)}, f32[192,256]{1,0:T(8,128)S(1)}, u32[]{:S(2)}, u32[]{:S(2)}) %collective-permute-start.7) | collective-permute-done | bytes 196640 | tf_op jit(solution)/shard_map/ppermute | solution.py:410
  51.6 1.6 %shard_map.42 = (f32[208,128]{1,0:T(8,128)S(1)}, f32[208,128]{1,0:T(8,128)S(1)}, f32[80,128]{1,0:T(8,128)S(1)}, f32[4,10,16,128]{3,2,1,0:T(8,128)S(1)}, f32[4,10...) custom-call(s32[2]{0:T(128)S(1)} %pad_add_fusion.refs_0_, ...), custom_call_target="tpu_custom_call" | custom-call | tf_op jit(solution)/shard_map/pallas_call | solution.py:365
  53.1 0.1 collective-permute-start.8
  53.2 5.7 %collective-permute-start.9 = (f32[208,128]{1,0:T(8,128)S(1)}, f32[208,128]{1,0:T(8,128)S(1)}, u32[]{:S(2)}, u32[]{:S(2)}) collective-permute-start(f32[208,128]{1,0:T(8,128)S(1)} %get-tuple-element.17), channel_id=1, source_target_pairs={{0,31},{1,0},{2,1},{3,2},{4,3},{5,4},{6,5},{7,6},{8,7},{9,8},{10,9... | collective-permute-start | bytes 319496 | tf_op jit(solution)/shard_map/ppermute | solution.py:377
  58.9 0.0 collective-permute-start.10
  58.9 6.0 %collective-permute-start.11 = (f32[80,128]{1,0:T(8,128)S(1)}, f32[80,128]{1,0:T(8,128)S(1)}, u32[]{:S(2)}, u32[]{:S(2)}) collective-permute-start(f32[80,128]{1,0:T(8,128)S(1)} %get-tuple-element.15.refs_1_), channel_id=1, source_target_pairs={{0,30},{1,31},{2,0},{3,1},{4,2},{5,3},{6,4},{7,5},{8,6},{9,7},{10,... | collective-permute-start | bytes 122888 | tf_op jit(solution)/shard_map/ppermute | solution.py:377
  64.9 1.4 %collective-permute-done.10.refs_4_ = f32[80,128]{1,0:T(8,128)S(1)} collective-permute-done((f32[80,128]{1,0:T(8,128)S(1)}, f32[80,128]{1,0:T(8,128)S(1)}, u32[]{:S(2)}, u32[]{:S(2)}) %collective-permute-start.10) | collective-permute-done | bytes 40992 | tf_op jit(solution)/shard_map/ppermute | solution.py:377
  66.3 0.0 collective-permute-done.11.refs_5_
  66.3 0.0 collective-permute-done.8.refs_2_
  66.3 0.0 collective-permute-done.9.refs_3_
  66.3 5.4 %shard_map.43 = (f32[4,4,16,256]{3,2,1,0:T(8,128)}, f32[4,4,16,256]{3,2,1,0:T(8,128)}) custom-call(s32[2]{0:T(128)S(1)} %pad_add_fusion.refs_0_, f32[80,128]{1,0:T(8,128)S(1)} %get-tuple-element.15.refs_1_, f32[208,128]{1,0:T(8,128)S(1)} %collective-permute-done.8.refs_2_, f32[208,128]{1,0:T(8,128)S(1)} %collective-permute-done.9.refs_3_, ...), custom_call_target="tpu_custom_call" | custom-call | tf_op jit(solution)/shard_map/pallas_call | solution.py:365
  (23 shorter events, 0.4 us)
Async XLA Ops:
  0.6 1.0 %copy-start.1 = (f32[4,16,256]{2,1,0:T(8,128)S(1)}, f32[4,16,256]{2,1,0:T(8,128)}, u32[]{:S(2)}) copy-start(f32[4,16,256]{2,1,0:T(8,128)} %refs_2_.1) | copy-start | bytes 196612
  1.7 6.9 %collective-permute-start = (f32[11,16,256]{2,1,0:T(8,128)S(1)}, f32[11,16,256]{2,1,0:T(8,128)S(1)}, u32[]{:S(2)}, u32[]{:S(2)}) collective-permute-start(f32[11,16,256]{2,1,0:T(8,128)S(1)} %pad_maximum_fusion.5), channel_id=1, source_target_pairs={{0,32},{32,64},{64,96},{96,128},{128,160},{160,192},{192,224},{224... | collective-permute-start | bytes 540680 | tf_op jit(solution)/shard_map/ppermute | solution.py:377
  6.2 7.9 %copy-start = (f32[4,4,16,256]{3,2,1,0:T(8,128)S(1)}, f32[4,4,16,256]{3,2,1,0:T(8,128)}, u32[]{:S(2)}) copy-start(f32[4,4,16,256]{3,2,1,0:T(8,128)} %refs_1_.1) | copy-start | bytes 786436
  6.2 7.9 %collective-permute-start.1 = (f32[11,16,256]{2,1,0:T(8,128)S(1)}, f32[11,16,256]{2,1,0:T(8,128)S(1)}, u32[]{:S(2)}, u32[]{:S(2)}) collective-permute-start(f32[11,16,256]{2,1,0:T(8,128)S(1)} %pad_maximum_fusion.6), channel_id=1, source_target_pairs={{0,224},{32,0},{64,32},{96,64},{128,96},{160,128},{192,160},{224,1... | collective-permute-start | bytes 540680 | tf_op jit(solution)/shard_map/ppermute | solution.py:377
  8.6 5.6 %copy-start.2 = (f32[11,16,256]{2,1,0:T(8,128)}, f32[11,16,256]{2,1,0:T(8,128)S(1)}, u32[]{:S(2)}) copy-start(f32[11,16,256]{2,1,0:T(8,128)S(1)} %collective-permute-done.refs_3_) | copy-start | bytes 540676
  14.3 0.8 %slice-start = ((f32[11,16,256]{2,1,0:T(8,128)}), f32[3,16,256]{2,1,0:T(8,128)S(1)}, s32[]{:S(2)}) async-start(f32[11,16,256]{2,1,0:T(8,128)} %copy-done.2), calls=%async_computation | async-start | bytes 98304 | tf_op jit(solution)/shard_map/slice | solution.py:390
  15.1 9.4 %collective-permute-start.3 = (f32[272,256]{1,0:T(8,128)S(1)}, f32[272,256]{1,0:T(8,128)S(1)}, u32[]{:S(2)}, u32[]{:S(2)}) collective-permute-start(f32[272,256]{1,0:T(8,128)S(1)} %pad_maximum_fusion.2), channel_id=1, source_target_pairs={{0,31},{1,0},{2,1},{3,2},{4,3},{5,4},{6,5},{7,6},{8,7},{9,8},{10,9... | collective-permute-start | bytes 835592 | tf_op jit(solution)/shard_map/ppermute | solution.py:377
  19.9 10.9 %copy-start.3 = (f32[11,16,256]{2,1,0:T(8,128)S(1)}, f32[11,16,256]{2,1,0:T(8,128)}, u32[]{:S(2)}) copy-start(f32[11,16,256]{2,1,0:T(8,128)} %copy-done.2) | copy-start | bytes 540676
  20.0 10.9 %collective-permute-start.2 = (f32[272,256]{1,0:T(8,128)S(1)}, f32[272,256]{1,0:T(8,128)S(1)}, u32[]{:S(2)}, u32[]{:S(2)}) collective-permute-start(f32[272,256]{1,0:T(8,128)S(1)} %pad_maximum_fusion.1), channel_id=1, source_target_pairs={{0,1},{1,2},{2,3},{3,4},{4,5},{5,6},{6,7},{7,8},{8,9},{9,10},{10,1... | collective-permute-start | bytes 835592 | tf_op jit(solution)/shard_map/ppermute | solution.py:377
  33.5 3.7 %collective-permute-start.4 = (f32[208,256]{1,0:T(8,128)S(1)}, f32[208,256]{1,0:T(8,128)S(1)}, u32[]{:S(2)}, u32[]{:S(2)}) collective-permute-start(f32[208,256]{1,0:T(8,128)S(1)} %get-tuple-element.14), channel_id=1, source_target_pairs={{0,32},{32,0},{64,96},{96,64},{128,160},{160,128},{192,224},{224,1... | collective-permute-start | bytes 638984 | tf_op jit(solution)/shard_map/ppermute | solution.py:407
  37.2 9.8 %collective-permute-start.5 = (f32[272,256]{1,0:T(8,128)S(1)}, f32[272,256]{1,0:T(8,128)S(1)}, u32[]{:S(2)}, u32[]{:S(2)}) collective-permute-start(f32[272,256]{1,0:T(8,128)S(1)} %pad_maximum_fusion.3), channel_id=1, source_target_pairs={{0,224},{32,64},{64,32},{96,128},{128,96},{160,192},{192,160},{224... | collective-permute-start | bytes 835592 | tf_op jit(solution)/shard_map/ppermute | solution.py:408
  39.3 10.7 %collective-permute-start.6 = (f32[64,256]{1,0:T(8,128)S(1)}, f32[64,256]{1,0:T(8,128)S(1)}, u32[]{:S(2)}, u32[]{:S(2)}) collective-permute-start(f32[64,256]{1,0:T(8,128)S(1)} %slice.68.refs_1_), channel_id=1, source_target_pairs={{0,128},{32,160},{64,192},{96,224},{128,0},{160,32},{192,64},{224,... | collective-permute-start | bytes 196616 | tf_op jit(solution)/shard_map/ppermute | solution.py:377
  50.0 1.5 %collective-permute-start.7 = (f32[192,256]{1,0:T(8,128)S(1)}, f32[192,256]{1,0:T(8,128)S(1)}, u32[]{:S(2)}, u32[]{:S(2)}) collective-permute-start(f32[192,256]{1,0:T(8,128)S(1)} %pad_maximum_fusion.4), channel_id=1, source_target_pairs={{0,32},{32,0},{64,96},{96,64},{128,160},{160,128},{192,224},{224,1... | collective-permute-start | bytes 589832 | tf_op jit(solution)/shard_map/ppermute | solution.py:410
  53.1 13.1 %collective-permute-start.8 = (f32[208,128]{1,0:T(8,128)S(1)}, f32[208,128]{1,0:T(8,128)S(1)}, u32[]{:S(2)}, u32[]{:S(2)}) collective-permute-start(f32[208,128]{1,0:T(8,128)S(1)} %get-tuple-element.16), channel_id=1, source_target_pairs={{0,1},{1,2},{2,3},{3,4},{4,5},{5,6},{6,7},{7,8},{8,9},{9,10},{10,1... | collective-permute-start | bytes 319496 | tf_op jit(solution)/shard_map/ppermute | solution.py:377
  53.2 13.0 %collective-permute-start.9 = (f32[208,128]{1,0:T(8,128)S(1)}, f32[208,128]{1,0:T(8,128)S(1)}, u32[]{:S(2)}, u32[]{:S(2)}) collective-permute-start(f32[208,128]{1,0:T(8,128)S(1)} %get-tuple-element.17), channel_id=1, source_target_pairs={{0,31},{1,0},{2,1},{3,2},{4,3},{5,4},{6,5},{7,6},{8,7},{9,8},{10,9... | collective-permute-start | bytes 319496 | tf_op jit(solution)/shard_map/ppermute | solution.py:377
  58.9 7.4 %collective-permute-start.10 = (f32[80,128]{1,0:T(8,128)S(1)}, f32[80,128]{1,0:T(8,128)S(1)}, u32[]{:S(2)}, u32[]{:S(2)}) collective-permute-start(f32[80,128]{1,0:T(8,128)S(1)} %get-tuple-element.15.refs_1_), channel_id=1, source_target_pairs={{0,2},{1,3},{2,4},{3,5},{4,6},{5,7},{6,8},{7,9},{8,10},{9,11},{10,... | collective-permute-start | bytes 122888 | tf_op jit(solution)/shard_map/ppermute | solution.py:377
  58.9 7.4 %collective-permute-start.11 = (f32[80,128]{1,0:T(8,128)S(1)}, f32[80,128]{1,0:T(8,128)S(1)}, u32[]{:S(2)}, u32[]{:S(2)}) collective-permute-start(f32[80,128]{1,0:T(8,128)S(1)} %get-tuple-element.15.refs_1_), channel_id=1, source_target_pairs={{0,30},{1,31},{2,0},{3,1},{4,2},{5,3},{6,4},{7,5},{8,6},{9,7},{10,... | collective-permute-start | bytes 122888 | tf_op jit(solution)/shard_map/ppermute | solution.py:377

commit v3 on v2

--- a/solution.py
+++ b/solution.py
@@ -121,25 +121,80 @@
     return jnp.dot(a, b, precision=lax.Precision.HIGHEST, preferred_element_type=F32)
 
 
-def fine_down(groups, devs, idx, f, e, xm, xp, ym, yp, pay_o, x1, ew, wt, fw, x0, pair, half):
+def pick(condition, a, b):
+    return jnp.where(condition, a, b)
+
+
+def pack_first(idx, f, e, cross_o, inner_o):
+    even = idx[0] % 2 == 0
+    for n in range(11):
+        first = f[n // 2, n % 2] if n < 8 else e[n - 8]
+        last = f[n // 2, 2 + n % 2] if n < 8 else e[n - 7]
+        cross_o[16 * n : 16 * n + 16, :] = pick(even, first, last)
+        inner_o[16 * n : 16 * n + 16, :] = pick(even, last, first)
+
+
+def halo_first(idx, cross, inner, n):
+    even = idx[0] % 2 == 0
+    a, b = cross[16 * n : 16 * n + 16, :], inner[16 * n : 16 * n + 16, :]
+    return pick(even, a, b), pick(even, b, a)
+
+
+def pack_second(idx, f, e, cross, inner, even_o, odd_o):
+    even = idx[1] % 2 == 0
+
+    def write(at, rows, value):
+        size = value.shape[0]
+        low, high = value[0:rows, :], value[size - rows : size, :]
+        even_o[at : at + rows, :] = pick(even, high, low)
+        odd_o[at : at + rows, :] = pick(even, low, high)
+
+    for j in range(3):
+        before, after = halo_first(idx, cross, inner, 8 + j)
+        write(192 + 8 * j, 8, before)
+        write(192 + 8 * (7 + j), 8, after)
+    for j in range(4):
+        write(192 + 8 * (3 + j), 8, e[j])
+    for c in range(4):
+        for j in range(2):
+            before, after = halo_first(idx, cross, inner, 2 * c + j)
+            write(24 * j + 6 * c, 6, before)
+            write(24 * (6 + j) + 6 * c, 6, after)
+        for j in range(4):
+            write(24 * (2 + j) + 6 * c, 6, f[c, j])
+
+
+def fine_down(groups, devs, idx, f, e, cross, inner, odd, even, mid_o, edge_o, x1, ew, wt, fw, x0, pair, half):
     g, d = idx[0], idx[1]
     low_x, high_x = jnp.where(g > 0, 1.0, 0.0), jnp.where(g < groups - 1, 1.0, 0.0)
     low_y, high_y = jnp.where(d > 0, 1.0, 0.0), jnp.where(d < devs - 1, 1.0, 0.0)
     zero = jnp.zeros((2, 256), F32)
+    even_dev = d % 2 == 0
+
+    def halo_second(at):
+        a, b = odd[at, :], even[at, :]
+        return pick(even_dev, a, b), pick(even_dev, b, a)
+
     for layer in range(10):
-        own = xm[8 + layer] if layer < 3 else xp[8 + layer - 7] if layer > 6 else e[layer - 3]
+        if layer < 3:
+            own = halo_first(idx, cross, inner, 8 + layer)[0]
+        else:
+            own = halo_first(idx, cross, inner, 1 + layer)[1] if layer > 6 else e[layer - 3]
         s = low_x if layer < 3 else high_x if layer > 6 else 1.0
-        at = slice(192 + 8 * layer, 200 + 8 * layer)
-        put(ew, (layer,), 0, ym[at, :] * (s * low_y))
+        before, after = halo_second(slice(192 + 8 * layer, 200 + 8 * layer))
+        put(ew, (layer,), 0, before * (s * low_y))
         put(ew, (layer,), 8, own * s)
-        put(ew, (layer,), 24, yp[at, :] * (s * high_y))
+        put(ew, (layer,), 24, after * (s * high_y))
     for layer in range(8):
         for c in range(4):
-            own = xm[2 * c + layer] if layer < 2 else xp[2 * c + layer - 6] if layer > 5 else f[c, layer - 2]
-            at = slice(24 * layer + 6 * c, 24 * layer + 6 * c + 6)
-            put(fw, (c, layer), 0, jnp.concatenate([zero, ym[at, :]], 0))
+            if layer < 2:
+                own = halo_first(idx, cross, inner, 2 * c + layer)[0]
+            else:
+                own = halo_first(idx, cross, inner, 2 * c + layer - 6)[1] if layer > 5 else f[c, layer - 2]
+            before, after = halo_second(slice(24 * layer + 6 * c, 24 * layer + 6 * c + 6))
+            put(fw, (c, layer), 0, jnp.concatenate([zero, before], 0))
             put(fw, (c, layer), 8, own)
-            put(fw, (c, layer), 24, jnp.concatenate([yp[at, :], zero], 0))
+            put(fw, (c, layer), 24, jnp.concatenate([after, zero], 0))
     for layer in range(8):
         layer_in = (4 * g - 2 + layer >= 0) & (4 * g - 2 + layer < 4 * groups)
         for row in (0, 8, 16, 24):
@@ -164,15 +219,15 @@
     for m in range(2):
         lanes = slice(128 * m, 128 * m + 128)
         for c in range(4):
-            pay_o[12 * c : 12 * c + 12, lanes] = coarse[2 * c + m, 2:14, :]
-        pay_o[48:64, lanes] = coarse[8 + m]
+            mid_o[12 * c : 12 * c + 12, lanes] = coarse[2 * c + m, 2:14, :]
+        mid_o[48:64, lanes] = coarse[8 + m]
     for c in range(4):
         for j in range(2):
-            at = 64 + 18 * (2 * c + j)
-            pay_o[at : at + 18, :] = get(x1, (c, 3 + j), 7, 18)
-
-
-def mid_down(groups, devs, idx, own, partner, xr, c2, s3, up_o, dn_o, low_o, y_o, b_o, e_o, w_o, bw, ew, wt, y0, y1, pair, low):
+            at = 18 * (2 * c + j)
+            edge_o[at : at + 18, :] = get(x1, (c, 3 + j), 7, 18)
+
+
+def mid_down(groups, devs, idx, own, partner, xco, cpm, c2, s3, next_o, low_o, y_o, b_o, e_o, w_o, bw, ew, wt, y0, y1, pair, low):
     g, d = idx[0], idx[1]
     chips = groups // 2
     chip, core = g // 2, g % 2
@@ -204,8 +259,8 @@
 
     place(own, 0, chip, core)
     place(partner, 0, chip, other)
-    place(xr, 0, beside, other)
-    place(xr, 208, beside, core)
+    place(xco, 0, beside, other)
+    place(cpm, 0, beside, core)
     place(s3, 0, across, core)
     place(s3, 64, across, other)
     place(c2, 0, far, core)
@@ -233,18 +288,17 @@
         for q in range(groups // 2):
             packed = jnp.where(lane % 2 == 0, low[c, 2 * q, 0:4, :], low[c, 2 * q + 1, 0:4, :])
             at = 4 * (c * (groups // 2) + q)
-            for out in (up_o, dn_o, low_o):
+            for out in (next_o, low_o):
                 out[at : at + 4, :] = packed
     base = 20 * (groups // 2)
-    for c in range(4):
-        for j in range(6):
-            at = base + 4 * (6 * c + j)
-            up_o[at : at + 4, :] = y1[c, 2 * g + 2 + j, 8:12, :]
-            dn_o[at : at + 4, :] = y1[c, 2 * g + 2 + j, 4:8, :]
-        for j in range(2):
-            at = base + 96 + 4 * (2 * c + j)
-            up_o[at : at + 4, :] = bw[c, 2 * g + 4 + j, 8:12, :]
-            dn_o[at : at + 4, :] = bw[c, 2 * g + 4 + j, 4:8, :]
+    up = core == 0
+    for c in range(4):
+        for j in range(8):
+            at, i = base + 4 * (8 * c + j), 4 * chip + 2 + j
+            next_o[at : at + 4, :] = pick(up, y1[c, i, 8:12, :], y1[c, i, 4:8, :])
+        for j in range(4):
+            at, i = base + 128 + 4 * (4 * c + j), 4 * chip + 4 + j
+            next_o[at : at + 4, :] = pick(up, bw[c, i, 8:12, :], bw[c, i, 4:8, :])
     for j in range(10):
         e_o[j] = ew[2 * g + j]
         w_o[j] = wt[2 * g + j]
@@ -253,7 +307,7 @@
             b_o[c, j] = bw[c, 2 * g + j]
 
 
-def up_all(groups, devs, idx, low, m1, p1, m2, p2, y_i, b_i, e1, w1, x1, ew, wt, fw, own_edge, far_edge, sol_o, res_o,
+def up_all(groups, devs, idx, low, by1, by2, swapped, y_i, b_i, e1, w1, x1, ew, wt, fw, own_edge, far_edge, sol_o, res_o,
            e2, w2, b2, z0, z1, b1, ya, yb, rep, half, va, vb):
     g, d = idx[0], idx[1]
     core = g % 2
@@ -272,13 +326,25 @@
         for c in range(4):
             b2[c, i, 0:8, :] = zero[0:8]
             b2[c, i, 16:32, :] = zero[0:16]
-    for source, away in ((m2, -2), (m1, -1), (low, 0), (p1, 1), (p2, 2)):
+    tall = 20 * (groups // 2)
+    by1_rows = tall + 192
+    first_core = core == 0
+
+    def from_second(by, offset, at):
+        a, b = by[at : at + 4, :], swapped[offset + at : offset + at + 4, :]
+        return pick(first_core, a, b), pick(first_core, b, a)
+
+    for away in (-2, -1, 0, 1, 2):
         row = 10 + 4 * away
         there = 1.0 if away == 0 else jnp.where((d + away >= 0) & (d + away < devs), 1.0, 0.0)
         for c in range(5):
             for q in range(groups // 2):
                 at = 4 * (c * (groups // 2) + q)
-                packed = source[at : at + 4, :]
+                if away == 0:
+                    packed = low[at : at + 4, :]
+                else:
+                    by, offset = (by1, 0) if away in (-1, 1) else (by2, by1_rows)
+                    packed = from_second(by, offset, at)[0 if away < 0 else 1]
                 first = jnp.where(even, packed, pltpu.roll(packed, 1, 1))
                 second = jnp.where(even, pltpu.roll(packed, 127, 1), packed)
                 if c == 4:
@@ -300,7 +366,11 @@
     z = here
 
     low_y, high_y = jnp.where(d > 0, 1.0, 0.0), jnp.where(d < devs - 1, 1.0, 0.0)
-    base = 20 * (groups // 2)
+
+    def mid_halo(at, step):
+        a, b = from_second(by1, 0, at), from_second(by1, 0, at + step)
+        return pick(first_core, a[0], b[0]), pick(first_core, a[1], b[1])
+
     for c in range(4):
         for k in range(5):
             rows = z[c, g + k, 8:16, :]
@@ -311,13 +381,13 @@
             b1[c, j] = b_i[c, j]
             ya[c, j] = y_i[c, j]
         for j in range(2):
-            at = base + 96 + 4 * (2 * c + j)
-            b1[c, 4 + j, 0:4, :] = m1[at : at + 4, :]
-            b1[c, 4 + j, 12:16, :] = p1[at : at + 4, :]
+            before, after = mid_halo(tall + 128 + 4 * (4 * c + j), 8)
+            b1[c, 4 + j, 0:4, :] = before
+            b1[c, 4 + j, 12:16, :] = after
         for j in range(6):
-            at = base + 4 * (6 * c + j)
-            ya[c, 2 + j, 0:4, :] = m1[at : at + 4, :] * low_y
-            ya[c, 2 + j, 12:16, :] = p1[at : at + 4, :] * high_y
+            before, after = mid_halo(tall + 4 * (8 * c + j), 8)
+            ya[c, 2 + j, 0:4, :] = before * low_y
+            ya[c, 2 + j, 12:16, :] = after * high_y
         for j in range(10):
             ya[c, j] = ya[c, j] + rep[c, j // 2]
     for at in range(1, 9):
@@ -372,55 +442,52 @@
     )(*args)
 
 
-def shift(value, axis, by):
-    peers = lax.axis_size(axis)
-    return lax.ppermute(value, axis, [(i, (i + by) % peers) for i in range(peers)])
-
-
 def local(forcing, viscosity):
     groups, devs = lax.axis_size("grp"), lax.axis_size("dev")
     idx = jnp.stack([lax.axis_index("grp"), lax.axis_index("dev")]).astype(jnp.int32)
-
-    def x_pack(f, e):
-        return jnp.concatenate([f.reshape(8, 16, 256), e], axis=0)
-
-    xm = shift(x_pack(forcing[:, 2:4], viscosity[1:4]), "grp", 1)
-    xp = shift(x_pack(forcing[:, 0:2], viscosity[0:3]), "grp", -1)
-    f8 = jnp.concatenate([xm[:8].reshape(4, 2, 16, 256), forcing, xp[:8].reshape(4, 2, 16, 256)], axis=1)
-    e10 = jnp.concatenate([xm[8:], viscosity, xp[8:]], axis=0)
-
-    def y_pack(f, e):
-        return jnp.concatenate([jnp.swapaxes(f, 0, 1).reshape(192, 256), e.reshape(80, 256)], axis=0)
-
-    ym = shift(y_pack(f8[:, :, 10:16], e10[:, 8:16]), "dev", 1)
-    yp = shift(y_pack(f8[:, :, 0:6], e10[:, 0:8]), "dev", -1)
-
-    pay, x1, ew, wt, fw = call(
-        lambda *refs: fine_down(groups, devs, *refs),
-        [(208, 256), (4, 8, 2, 32, 128), (10, 2, 32, 128), (8, 2, 32, 128), (4, 8, 2, 32, 128)],
-        [(4, 8, 2, 32, 128), (10, 32, 256), (320, 128)],
-        idx, forcing, viscosity, xm, xp, ym, yp,
-    )
-
     swap = [(i, i ^ 1) for i in range(groups)]
     beside = [(i, (i + 1) % groups if i % 2 else (i - 1) % groups) for i in range(groups)]
-    got = lax.ppermute(pay, "grp", swap)
-    xr = lax.ppermute(jnp.concatenate([pay, got[:64]], axis=0), "grp", beside)
-    c2 = shift(pay[:64], "grp", 4)
-    s3 = lax.ppermute(jnp.concatenate([xr[:64], xr[208:], c2], axis=0), "grp", swap)
+    next_chip = [(i, (i - 2) % groups if i % 2 else (i + 2) % groups) for i in range(groups)]
+    far_chip = [(i, (i + 4) % groups) for i in range(groups)]
+    even = [(i, i ^ 1) for i in range(devs)]
+    odd = [(i, (i + 1) % devs if i % 2 else (i - 1) % devs) for i in range(devs)]
+
+    def along(step):
+        to = [(g, (d - step if g % 2 else d + step) % devs) for g in range(groups) for d in range(devs)]
+        return [(i, g * devs + d) for i, (g, d) in enumerate(to)]
+
+    cross, inner = call(pack_first, [(176, 256)] * 2, [], idx, forcing, viscosity)
+    cross, inner = lax.ppermute(cross, "grp", beside), lax.ppermute(inner, "grp", swap)
+    to_even, to_odd = call(pack_second, [(272, 256)] * 2, [], idx, forcing, viscosity, cross, inner)
+    from_odd, from_even = lax.ppermute(to_odd, "dev", odd), lax.ppermute(to_even, "dev", even)
+    mid, edge, x1, ew, wt, fw = call(
+        lambda *refs: fine_down(groups, devs, *refs),
+        [(64, 256), (144, 256), (4, 8, 2, 32, 128), (10, 2, 32, 128), (8, 2, 32, 128), (4, 8, 2, 32, 128)],
+        [(4, 8, 2, 32, 128), (10, 32, 256), (320, 128)],
+        idx, forcing, viscosity, cross, inner, from_odd, from_even,
+    )
+
+    c2 = lax.ppermute(mid, "grp", far_chip)
+    xco = lax.ppermute(mid, "grp", beside)
+    cpm = lax.ppermute(mid, "grp", next_chip)
+    partner = lax.ppermute(mid, "grp", swap)
+    own_edge = lax.ppermute(edge, "grp", swap)
+    far_edge = lax.ppermute(edge, "grp", beside)
+    s3 = lax.ppermute(jnp.concatenate([xco, cpm, c2], axis=0), "grp", swap)
 
     layers = 2 * groups + 8
     tall = 20 * (groups // 2)
-    up, dn, low, y_w, b_w, e_w, w_w = call(
+    to_next, low, y_w, b_w, e_w, w_w = call(
         lambda *refs: mid_down(groups, devs, *refs),
-        [(tall + 128, 128), (tall + 128, 128), (tall, 128), (4, 10, 16, 128), (4, 10, 16, 128), (10, 16, 128), (10, 16, 128)],
+        [(tall + 192, 128), (tall, 128), (4, 10, 16, 128), (4, 10, 16, 128), (10, 16, 128), (10, 16, 128)],
         [(4, layers, 16, 128), (layers, 16, 128), (layers, 16, 128), (4, layers, 16, 128), (4, layers, 16, 128),
          (groups, 5, 8, 128), (5, groups, 8, 128)],
-        idx, pay[:64], got[:64], xr, c2, s3,
+        idx, mid, partner, xco, cpm, c2, s3,
     )
 
-    m1, p1 = shift(up, "dev", 1), shift(dn, "dev", -1)
-    m2, p2 = shift(low, "dev", 2), shift(low, "dev", -2)
+    by1 = lax.ppermute(to_next, ("grp", "dev"), along(1))
+    by2 = lax.ppermute(low, ("grp", "dev"), along(2))
+    swapped = lax.ppermute(jnp.concatenate([by1, by2], axis=0), "grp", swap)
     deep = groups + 4
     return tuple(call(
         lambda *refs: up_all(groups, devs, *refs),
@@ -428,7 +495,7 @@
         [(deep, 32, 128), (deep, 32, 128), (4, deep, 32, 128), (4, deep, 32, 128), (4, deep, 32, 128),
          (4, 10, 16, 128), (4, 10, 16, 128), (4, 10, 16, 128), (4, 5, 16, 128), (2, 768, 128),
          (4, 12, 2, 32, 128), (4, 12, 2, 32, 128)],
-        idx, low, m1, p1, m2, p2, y_w, b_w, e_w, w_w, x1, ew, wt, fw, got[64:], xr[64:208],
+        idx, low, by1, by2, swapped, y_w, b_w, e_w, w_w, x1, ew, wt, fw, own_edge, far_edge,
     ))
 
 

time: 71.9 us -> 68.8 us (0.957)
  waiting for transfers between devices: 29.6 us -> 21.2 us
  starting transfers between devices: 29.3 us -> 34.1 us
  Pallas kernels: 9.57 us -> 10.8 us
    ppermute x12 -> x14, waiting for transfers between devices: 29.6 us -> 21.2 us  [the longest x1 5.14 us: local(): lax.ppermute(to_odd, 'dev', odd)]
    ppermute x12 -> x14, starting transfers between devices: 29.3 us -> 34.1 us  [the longest x1 7.2 us: local(): c2 = lax.ppermute(mid, 'grp', far_chip)]
    slice x12 -> x0, local copies, waits for them, and re-layouts: 1.88 us -> none  [the longest x2 1.03 us: local(): xp = shift(x_pack(forcing[:, 0:2], viscosity[0:3]), 'grp', -1)]
    unnamed x8 -> x4, local copies, waits for them, and re-layouts: 0.02 us -> 1.79 us
    pallas_call x3 -> x5, Pallas kernels: 9.57 us -> 10.8 us  [call(): pl.pallas_call(kernel, out_shape=[jax.ShapeDtypeStruct(shape, F32) for sh...]
  transfers between devices with their start and end apart: 12 -> 14, of which waited for: 9 -> 8; matrix products, arithmetic and copies ran while one was open for 0% -> 0% of each run, Pallas kernels for 0% -> 0%
where the time goes in v3:
time: 68.8 us; the launch traced here: 68.7 us
  starting transfers between devices  34.1 us (50%)
  waiting for transfers between devices  21.2 us (31%)
  Pallas kernels  10.8 us (16%)
  local copies, waits for them, and re-layouts  1.79 us (3%)
    pallas_call x5, Pallas kernels, call(): pl.pallas_call(kernel, out_shape=[jax.ShapeDtypeStruct(shape, F32) for sh...  10.8 us
    ppermute x1, starting transfers between devices, local(): c2 = lax.ppermute(mid, 'grp', far_chip)  7.2 us
    ppermute x1, waiting for transfers between devices, local(): lax.ppermute(to_odd, 'dev', odd)  5.14 us
    ppermute x1, starting transfers between devices, local(): lax.ppermute(to_odd, 'dev', odd)  4.88 us
    ppermute x1, waiting for transfers between devices, local(): by2 = lax.ppermute(low, ('grp', 'dev'), along(2))  4.65 us
    ppermute x1, starting transfers between devices, local(): by1 = lax.ppermute(to_next, ('grp', 'dev'), along(1))  4.56 us
    ppermute x1, starting transfers between devices, local(): lax.ppermute(cross, 'grp', beside)  4.47 us
    ppermute x1, waiting for transfers between devices, local(): cpm = lax.ppermute(mid, 'grp', next_chip)  3.72 us
  transfers between devices with their start and end apart: 14, of which 8 were waited for; matrix products, arithmetic and copies ran while one was open for 0% of the time, Pallas kernels for 0%

profile of v3, /device:TPU:1, one launch (start us, length us, event | category | flops | bytes accessed | tf_op | source)
XLA Modules:
  0.0 68.7 jit_solution(14217312652430562457)
XLA Ops:
  0.6 0.1 pad_add_fusion.idx.refs_0_
  0.7 0.0 copy-start
  0.7 0.9 %copy-done = f32[4,4,16,256]{3,2,1,0:T(8,128)S(1)} copy-done((f32[4,4,16,256]{3,2,1,0:T(8,128)S(1)}, f32[4,4,16,256]{3,2,1,0:T(8,128)}, u32[]{:S(2)}) %copy-start) | copy-done | bytes 262168
  1.7 0.0 copy-start.1
  1.7 0.8 %copy-done.1 = f32[4,16,256]{2,1,0:T(8,128)S(1)} copy-done((f32[4,16,256]{2,1,0:T(8,128)S(1)}, f32[4,16,256]{2,1,0:T(8,128)}, u32[]{:S(2)}) %copy-start.1) | copy-done | bytes 65560
  2.5 0.6 shard_map.41
  3.1 4.5 %collective-permute-start = (f32[176,256]{1,0:T(8,128)S(1)}, f32[176,256]{1,0:T(8,128)S(1)}, u32[]{:S(2)}, u32[]{:S(2)}) collective-permute-start(f32[176,256]{1,0:T(8,128)S(1)} %get-tuple-element.18), channel_id=1, source_target_pairs={{0,224},{32,64},{64,32},{96,128},{128,96},{160,192},{192,160},{224... | collective-permute-start | bytes 540680 | tf_op jit(solution)/shard_map/ppermute | solution.py:460
  7.5 2.9 %collective-permute-start.1 = (f32[176,256]{1,0:T(8,128)S(1)}, f32[176,256]{1,0:T(8,128)S(1)}, u32[]{:S(2)}, u32[]{:S(2)}) collective-permute-start(f32[176,256]{1,0:T(8,128)S(1)} %get-tuple-element.19), channel_id=1, source_target_pairs={{0,32},{32,0},{64,96},{96,64},{128,160},{160,128},{192,224},{224,1... | collective-permute-start | bytes 540680 | tf_op jit(solution)/shard_map/ppermute | solution.py:460
  10.4 2.5 %collective-permute-done.cross.refs_3_ = f32[176,256]{1,0:T(8,128)S(1)} collective-permute-done((f32[176,256]{1,0:T(8,128)S(1)}, f32[176,256]{1,0:T(8,128)S(1)}, u32[]{:S(2)}, u32[]{:S(2)}) %collective-permute-start) | collective-permute-done | bytes 180256 | tf_op jit(solution)/shard_map/ppermute | solution.py:460
  13.0 0.0 collective-permute-done.1.inner.refs_4_
  13.0 0.6 shard_map.42
  13.6 4.9 %collective-permute-start.2 = (f32[272,256]{1,0:T(8,128)S(1)}, f32[272,256]{1,0:T(8,128)S(1)}, u32[]{:S(2)}, u32[]{:S(2)}) collective-permute-start(f32[272,256]{1,0:T(8,128)S(1)} %get-tuple-element.20), channel_id=1, source_target_pairs={{0,31},{1,2},{2,1},{3,4},{4,3},{5,6},{6,5},{7,8},{8,7},{9,10},{10,... | collective-permute-start | bytes 835592 | tf_op jit(solution)/shard_map/ppermute | solution.py:462
  18.5 0.0 collective-permute-start.3
  18.5 5.1 %collective-permute-done.2.refs_5_ = f32[272,256]{1,0:T(8,128)S(1)} collective-permute-done((f32[272,256]{1,0:T(8,128)S(1)}, f32[272,256]{1,0:T(8,128)S(1)}, u32[]{:S(2)}, u32[]{:S(2)}) %collective-permute-start.2) | collective-permute-done | bytes 278560 | tf_op jit(solution)/shard_map/ppermute | solution.py:462
  23.6 0.6 collective-permute-done.3.refs_6_
  24.2 2.7 %shard_map.43 = (f32[64,256]{1,0:T(8,128)S(1)}, f32[144,256]{1,0:T(8,128)S(1)}, f32[4,8,2,32,128]{4,3,2,1,0:T(8,128)S(1)}, f32[10,2,32,128]{3,2,1,0:T(8,128)S(1)...) custom-call(s32[2]{0:T(128)S(1)} %pad_add_fusion.idx.refs_0_, f32[4,4,16,256]{3,2,1,0:T(8,128)S(1)} %copy-done, ...), custom_call_target="tpu_custom_call" | custom-call | tf_op jit(solution)/shard_map/pallas_call | solution.py:435
  26.9 7.2 %collective-permute-start.7 = (f32[64,256]{1,0:T(8,128)S(1)}, f32[64,256]{1,0:T(8,128)S(1)}, u32[]{:S(2)}, u32[]{:S(2)}) collective-permute-start(f32[64,256]{1,0:T(8,128)S(1)} %get-tuple-element.22.refs_1_), channel_id=1, source_target_pairs={{0,128},{32,160},{64,192},{96,224},{128,0},{160,32},{192,64},{224,... | collective-permute-start | bytes 196616 | tf_op jit(solution)/shard_map/ppermute | solution.py:470
  34.0 1.4 %collective-permute-start.6 = (f32[64,256]{1,0:T(8,128)S(1)}, f32[64,256]{1,0:T(8,128)S(1)}, u32[]{:S(2)}, u32[]{:S(2)}) collective-permute-start(f32[64,256]{1,0:T(8,128)S(1)} %get-tuple-element.22.refs_1_), channel_id=1, source_target_pairs={{0,64},{32,224},{64,128},{96,32},{128,192},{160,96},{192,0},{224,1... | collective-permute-start | bytes 196616 | tf_op jit(solution)/shard_map/ppermute | solution.py:472
  35.4 2.6 %collective-permute-start.5 = (f32[64,256]{1,0:T(8,128)S(1)}, f32[64,256]{1,0:T(8,128)S(1)}, u32[]{:S(2)}, u32[]{:S(2)}) collective-permute-start(f32[64,256]{1,0:T(8,128)S(1)} %get-tuple-element.22.refs_1_), channel_id=1, source_target_pairs={{0,224},{32,64},{64,32},{96,128},{128,96},{160,192},{192,160},{224... | collective-permute-start | bytes 196616 | tf_op jit(solution)/shard_map/ppermute | solution.py:471
  38.0 0.0 collective-permute-done.7.refs_5_
  38.0 3.7 %collective-permute-done.6.refs_4_ = f32[64,256]{1,0:T(8,128)S(1)} collective-permute-done((f32[64,256]{1,0:T(8,128)S(1)}, f32[64,256]{1,0:T(8,128)S(1)}, u32[]{:S(2)}, u32[]{:S(2)}) %collective-permute-start.6) | collective-permute-done | bytes 65568 | tf_op jit(solution)/shard_map/ppermute | solution.py:472
  41.7 0.1 collective-permute-done.5.refs_3_
  41.8 2.4 %collective-permute-start.8 = (f32[192,256]{1,0:T(8,128)S(1)}, f32[192,256]{1,0:T(8,128)S(1)}, u32[]{:S(2)}, u32[]{:S(2)}) collective-permute-start(f32[192,256]{1,0:T(8,128)S(1)} %pad_maximum_fusion), channel_id=1, source_target_pairs={{0,32},{32,0},{64,96},{96,64},{128,160},{160,128},{192,224},{224,1... | collective-permute-start | bytes 589832 | tf_op jit(solution)/shard_map/ppermute | solution.py:476
  44.3 0.1 collective-permute-start.4
  44.4 1.2 %collective-permute-done.4.refs_2_ = f32[64,256]{1,0:T(8,128)S(1)} collective-permute-done((f32[64,256]{1,0:T(8,128)S(1)}, f32[64,256]{1,0:T(8,128)S(1)}, u32[]{:S(2)}, u32[]{:S(2)}) %collective-permute-start.4) | collective-permute-done | bytes 65568 | tf_op jit(solution)/shard_map/ppermute | solution.py:473
  45.5 0.0 collective-permute-done.8.refs_6_
  45.5 1.6 %shard_map.44 = (f32[272,128]{1,0:T(8,128)S(1)}, f32[80,128]{1,0:T(8,128)S(1)}, f32[4,10,16,128]{3,2,1,0:T(8,128)S(1)}, f32[4,10,16,128]{3,2,1,0:T(8,128)S(1)}, ...) custom-call(s32[2]{0:T(128)S(1)} %pad_add_fusion.idx.refs_0_, f32[64,256]{1,0:T(8,128)S(1)} %get-tuple-element.22.refs_1_, ...), custom_call_target="tpu_custom_call" | custom-call | tf_op jit(solution)/shard_map/pallas_call | solution.py:435
  47.1 4.6 %collective-permute-start.9 = (f32[272,128]{1,0:T(8,128)S(1)}, f32[272,128]{1,0:T(8,128)S(1)}, u32[]{:S(2)}, u32[]{:S(2)}) collective-permute-start(f32[272,128]{1,0:T(8,128)S(1)} %get-tuple-element.24), channel_id=1, source_target_pairs={{0,1},{1,2},{2,3},{3,4},{4,5},{5,6},{6,7},{7,8},{8,9},{9,10},{10,1... | collective-permute-start | bytes 417800 | tf_op jit(solution)/shard_map/ppermute | solution.py:488
  51.6 0.0 collective-permute-start.10
  51.6 4.6 %collective-permute-done.10.refs_3_ = f32[80,128]{1,0:T(8,128)S(1)} collective-permute-done((f32[80,128]{1,0:T(8,128)S(1)}, f32[80,128]{1,0:T(8,128)S(1)}, u32[]{:S(2)}, u32[]{:S(2)}) %collective-permute-start.10) | collective-permute-done | bytes 40992 | tf_op jit(solution)/shard_map/ppermute | solution.py:489
  56.3 0.0 collective-permute-done.9.refs_2_
  56.3 1.2 %collective-permute-start.11 = (f32[352,128]{1,0:T(8,128)S(1)}, f32[352,128]{1,0:T(8,128)S(1)}, u32[]{:S(2)}, u32[]{:S(2)}) collective-permute-start(f32[352,128]{1,0:T(8,128)S(1)} %pad_maximum_fusion.1), channel_id=1, source_target_pairs={{0,32},{32,0},{64,96},{96,64},{128,160},{160,128},{192,224},{224,1... | collective-permute-start | bytes 540680 | tf_op jit(solution)/shard_map/ppermute | solution.py:490
  57.5 1.0 %collective-permute-start.13 = (f32[144,256]{1,0:T(8,128)S(1)}, f32[144,256]{1,0:T(8,128)S(1)}, u32[]{:S(2)}, u32[]{:S(2)}) collective-permute-start(f32[144,256]{1,0:T(8,128)S(1)} %get-tuple-element.33), channel_id=1, source_target_pairs={{0,224},{32,64},{64,32},{96,128},{128,96},{160,192},{192,160},{224... | collective-permute-start | bytes 442376 | tf_op jit(solution)/shard_map/ppermute | solution.py:475
  58.6 1.4 %collective-permute-start.12 = (f32[144,256]{1,0:T(8,128)S(1)}, f32[144,256]{1,0:T(8,128)S(1)}, u32[]{:S(2)}, u32[]{:S(2)}) collective-permute-start(f32[144,256]{1,0:T(8,128)S(1)} %get-tuple-element.33), channel_id=1, source_target_pairs={{0,32},{32,0},{64,96},{96,64},{128,160},{160,128},{192,224},{224,1... | collective-permute-start | bytes 442376 | tf_op jit(solution)/shard_map/ppermute | solution.py:474
  60.0 3.3 %collective-permute-done.13.refs_14_ = f32[144,256]{1,0:T(8,128)S(1)} collective-permute-done((f32[144,256]{1,0:T(8,128)S(1)}, f32[144,256]{1,0:T(8,128)S(1)}, u32[]{:S(2)}, u32[]{:S(2)}) %collective-permute-start.13) | collective-permute-done | bytes 147488 | tf_op jit(solution)/shard_map/ppermute | solution.py:475
  63.3 0.0 collective-permute-done.12.refs_13_
  63.3 0.0 collective-permute-done.11.refs_4_
  63.3 5.4 %shard_map.45 = (f32[4,4,16,256]{3,2,1,0:T(8,128)}, f32[4,4,16,256]{3,2,1,0:T(8,128)}) custom-call(s32[2]{0:T(128)S(1)} %pad_add_fusion.idx.refs_0_, f32[80,128]{1,0:T(8,128)S(1)} %get-tuple-element.23.refs_1_, f32[272,128]{1,0:T(8,128)S(1)} %collective-permute-done.9.refs_2_, f32[80,128]{1,0:T(8,128)S(1)} %collective-permute-done.10.refs_3_, ...), custom_call_target="tpu_custom_call" | custom-call | tf_op jit(solution)/shard_map/pallas_call | solution.py:435
  (2 shorter events, 0.0 us)
Async XLA Ops:
  0.7 1.0 %copy-start = (f32[4,4,16,256]{3,2,1,0:T(8,128)S(1)}, f32[4,4,16,256]{3,2,1,0:T(8,128)}, u32[]{:S(2)}) copy-start(f32[4,4,16,256]{3,2,1,0:T(8,128)} %refs_1_.1) | copy-start | bytes 786436
  1.7 0.8 %copy-start.1 = (f32[4,16,256]{2,1,0:T(8,128)S(1)}, f32[4,16,256]{2,1,0:T(8,128)}, u32[]{:S(2)}) copy-start(f32[4,16,256]{2,1,0:T(8,128)} %refs_2_.1) | copy-start | bytes 196612
  3.1 9.9 %collective-permute-start = (f32[176,256]{1,0:T(8,128)S(1)}, f32[176,256]{1,0:T(8,128)S(1)}, u32[]{:S(2)}, u32[]{:S(2)}) collective-permute-start(f32[176,256]{1,0:T(8,128)S(1)} %get-tuple-element.18), channel_id=1, source_target_pairs={{0,224},{32,64},{64,32},{96,128},{128,96},{160,192},{192,160},{224... | collective-permute-start | bytes 540680 | tf_op jit(solution)/shard_map/ppermute | solution.py:460
  7.5 5.4 %collective-permute-start.1 = (f32[176,256]{1,0:T(8,128)S(1)}, f32[176,256]{1,0:T(8,128)S(1)}, u32[]{:S(2)}, u32[]{:S(2)}) collective-permute-start(f32[176,256]{1,0:T(8,128)S(1)} %get-tuple-element.19), channel_id=1, source_target_pairs={{0,32},{32,0},{64,96},{96,64},{128,160},{160,128},{192,224},{224,1... | collective-permute-start | bytes 540680 | tf_op jit(solution)/shard_map/ppermute | solution.py:460
  13.6 10.0 %collective-permute-start.2 = (f32[272,256]{1,0:T(8,128)S(1)}, f32[272,256]{1,0:T(8,128)S(1)}, u32[]{:S(2)}, u32[]{:S(2)}) collective-permute-start(f32[272,256]{1,0:T(8,128)S(1)} %get-tuple-element.20), channel_id=1, source_target_pairs={{0,31},{1,2},{2,1},{3,4},{4,3},{5,6},{6,5},{7,8},{8,7},{9,10},{10,... | collective-permute-start | bytes 835592 | tf_op jit(solution)/shard_map/ppermute | solution.py:462
  18.5 5.7 %collective-permute-start.3 = (f32[272,256]{1,0:T(8,128)S(1)}, f32[272,256]{1,0:T(8,128)S(1)}, u32[]{:S(2)}, u32[]{:S(2)}) collective-permute-start(f32[272,256]{1,0:T(8,128)S(1)} %get-tuple-element.21), channel_id=1, source_target_pairs={{0,1},{1,0},{2,3},{3,2},{4,5},{5,4},{6,7},{7,6},{8,9},{9,8},{10,11... | collective-permute-start | bytes 835592 | tf_op jit(solution)/shard_map/ppermute | solution.py:462
  26.9 11.1 %collective-permute-start.7 = (f32[64,256]{1,0:T(8,128)S(1)}, f32[64,256]{1,0:T(8,128)S(1)}, u32[]{:S(2)}, u32[]{:S(2)}) collective-permute-start(f32[64,256]{1,0:T(8,128)S(1)} %get-tuple-element.22.refs_1_), channel_id=1, source_target_pairs={{0,128},{32,160},{64,192},{96,224},{128,0},{160,32},{192,64},{224,... | collective-permute-start | bytes 196616 | tf_op jit(solution)/shard_map/ppermute | solution.py:470
  34.0 7.7 %collective-permute-start.6 = (f32[64,256]{1,0:T(8,128)S(1)}, f32[64,256]{1,0:T(8,128)S(1)}, u32[]{:S(2)}, u32[]{:S(2)}) collective-permute-start(f32[64,256]{1,0:T(8,128)S(1)} %get-tuple-element.22.refs_1_), channel_id=1, source_target_pairs={{0,64},{32,224},{64,128},{96,32},{128,192},{160,96},{192,0},{224,1... | collective-permute-start | bytes 196616 | tf_op jit(solution)/shard_map/ppermute | solution.py:472
  35.4 6.4 %collective-permute-start.5 = (f32[64,256]{1,0:T(8,128)S(1)}, f32[64,256]{1,0:T(8,128)S(1)}, u32[]{:S(2)}, u32[]{:S(2)}) collective-permute-start(f32[64,256]{1,0:T(8,128)S(1)} %get-tuple-element.22.refs_1_), channel_id=1, source_target_pairs={{0,224},{32,64},{64,32},{96,128},{128,96},{160,192},{192,160},{224... | collective-permute-start | bytes 196616 | tf_op jit(solution)/shard_map/ppermute | solution.py:471
  41.8 3.7 %collective-permute-start.8 = (f32[192,256]{1,0:T(8,128)S(1)}, f32[192,256]{1,0:T(8,128)S(1)}, u32[]{:S(2)}, u32[]{:S(2)}) collective-permute-start(f32[192,256]{1,0:T(8,128)S(1)} %pad_maximum_fusion), channel_id=1, source_target_pairs={{0,32},{32,0},{64,96},{96,64},{128,160},{160,128},{192,224},{224,1... | collective-permute-start | bytes 589832 | tf_op jit(solution)/shard_map/ppermute | solution.py:476
  44.3 1.3 %collective-permute-start.4 = (f32[64,256]{1,0:T(8,128)S(1)}, f32[64,256]{1,0:T(8,128)S(1)}, u32[]{:S(2)}, u32[]{:S(2)}) collective-permute-start(f32[64,256]{1,0:T(8,128)S(1)} %get-tuple-element.22.refs_1_), channel_id=1, source_target_pairs={{0,32},{32,0},{64,96},{96,64},{128,160},{160,128},{192,224},{224,1... | collective-permute-start | bytes 196616 | tf_op jit(solution)/shard_map/ppermute | solution.py:473
  47.1 9.2 %collective-permute-start.9 = (f32[272,128]{1,0:T(8,128)S(1)}, f32[272,128]{1,0:T(8,128)S(1)}, u32[]{:S(2)}, u32[]{:S(2)}) collective-permute-start(f32[272,128]{1,0:T(8,128)S(1)} %get-tuple-element.24), channel_id=1, source_target_pairs={{0,1},{1,2},{2,3},{3,4},{4,5},{5,6},{6,7},{7,8},{8,9},{9,10},{10,1... | collective-permute-start | bytes 417800 | tf_op jit(solution)/shard_map/ppermute | solution.py:488
  51.6 4.7 %collective-permute-start.10 = (f32[80,128]{1,0:T(8,128)S(1)}, f32[80,128]{1,0:T(8,128)S(1)}, u32[]{:S(2)}, u32[]{:S(2)}) collective-permute-start(f32[80,128]{1,0:T(8,128)S(1)} %get-tuple-element.23.refs_1_), channel_id=1, source_target_pairs={{0,2},{1,3},{2,4},{3,5},{4,6},{5,7},{6,8},{7,9},{8,10},{9,11},{10,... | collective-permute-start | bytes 122888 | tf_op jit(solution)/shard_map/ppermute | solution.py:489
  56.3 7.0 %collective-permute-start.11 = (f32[352,128]{1,0:T(8,128)S(1)}, f32[352,128]{1,0:T(8,128)S(1)}, u32[]{:S(2)}, u32[]{:S(2)}) collective-permute-start(f32[352,128]{1,0:T(8,128)S(1)} %pad_maximum_fusion.1), channel_id=1, source_target_pairs={{0,32},{32,0},{64,96},{96,64},{128,160},{160,128},{192,224},{224,1... | collective-permute-start | bytes 540680 | tf_op jit(solution)/shard_map/ppermute | solution.py:490
  57.5 5.8 %collective-permute-start.13 = (f32[144,256]{1,0:T(8,128)S(1)}, f32[144,256]{1,0:T(8,128)S(1)}, u32[]{:S(2)}, u32[]{:S(2)}) collective-permute-start(f32[144,256]{1,0:T(8,128)S(1)} %get-tuple-element.33), channel_id=1, source_target_pairs={{0,224},{32,64},{64,32},{96,128},{128,96},{160,192},{192,160},{224... | collective-permute-start | bytes 442376 | tf_op jit(solution)/shard_map/ppermute | solution.py:475
  58.6 4.7 %collective-permute-start.12 = (f32[144,256]{1,0:T(8,128)S(1)}, f32[144,256]{1,0:T(8,128)S(1)}, u32[]{:S(2)}, u32[]{:S(2)}) collective-permute-start(f32[144,256]{1,0:T(8,128)S(1)} %get-tuple-element.33), channel_id=1, source_target_pairs={{0,32},{32,0},{64,96},{96,64},{128,160},{160,128},{192,224},{224,1... | collective-permute-start | bytes 442376 | tf_op jit(solution)/shard_map/ppermute | solution.py:474

commit v4 on v3

--- a/solution.py
+++ b/solution.py
@@ -125,19 +125,30 @@
     return jnp.where(condition, a, b)
 
 
-def pack_first(idx, f, e, cross_o, inner_o):
-    even = idx[0] % 2 == 0
-    for n in range(11):
-        first = f[n // 2, n % 2] if n < 8 else e[n - 8]
-        last = f[n // 2, 2 + n % 2] if n < 8 else e[n - 7]
-        cross_o[16 * n : 16 * n + 16, :] = pick(even, first, last)
-        inner_o[16 * n : 16 * n + 16, :] = pick(even, last, first)
+def pack_first(idx, f, e, cross_o, inner_o, sems):
+    core = idx[0] % 2
+    copies = []
+    for n, (out, side) in enumerate(((cross_o, core), (inner_o, 1 - core))):
+        for c in range(4):
+            copies.append(pltpu.make_async_copy(f.at[c, pl.ds(2 * side, 2)], out.at[pl.ds(2 * c, 2)], sems.at[n, c]))
+        copies.append(pltpu.make_async_copy(e.at[pl.ds(side, 3)], out.at[pl.ds(8, 3)], sems.at[n, 4]))
+    for copy in copies:
+        copy.start()
+    for copy in copies:
+        copy.wait()
 
 
 def halo_first(idx, cross, inner, n):
     even = idx[0] % 2 == 0
-    a, b = cross[16 * n : 16 * n + 16, :], inner[16 * n : 16 * n + 16, :]
+    a, b = cross[n], inner[n]
     return pick(even, a, b), pick(even, b, a)
+
+
+F_ROWS = (4, 5, 6, 6, 6, 6, 5, 4)
+E_ROWS = (4, 5, 6, 8, 8, 8, 8, 6, 5, 4)
+F_AT = tuple(4 * sum(F_ROWS[:n]) for n in range(9))
+E_AT = tuple(F_AT[8] + sum(E_ROWS[:n]) for n in range(11))
+SECOND_ROWS = 232
 
 
 def pack_second(idx, f, e, cross, inner, even_o, odd_o):
@@ -149,26 +160,29 @@
         even_o[at : at + rows, :] = pick(even, high, low)
         odd_o[at : at + rows, :] = pick(even, low, high)
 
-    for j in range(3):
-        before, after = halo_first(idx, cross, inner, 8 + j)
-        write(192 + 8 * j, 8, before)
-        write(192 + 8 * (7 + j), 8, after)
-    for j in range(4):
-        write(192 + 8 * (3 + j), 8, e[j])
-    for c in range(4):
-        for j in range(2):
-            before, after = halo_first(idx, cross, inner, 2 * c + j)
-            write(24 * j + 6 * c, 6, before)
-            write(24 * (6 + j) + 6 * c, 6, after)
-        for j in range(4):
-            write(24 * (2 + j) + 6 * c, 6, f[c, j])
-
-
-def fine_down(groups, devs, idx, f, e, cross, inner, odd, even, mid_o, edge_o, x1, ew, wt, fw, x0, pair, half):
+    for layer in range(10):
+        if 3 <= layer <= 6:
+            value = e[layer - 3]
+        else:
+            value = halo_first(idx, cross, inner, 8 + layer)[0] if layer < 3 else halo_first(idx, cross, inner, 1 + layer)[1]
+        write(E_AT[layer], E_ROWS[layer], value)
+    for layer in range(8):
+        for c in range(4):
+            if 2 <= layer <= 5:
+                value = f[c, layer - 2]
+            elif layer < 2:
+                value = halo_first(idx, cross, inner, 2 * c + layer)[0]
+            else:
+                value = halo_first(idx, cross, inner, 2 * c + layer - 6)[1]
+            write(F_AT[layer] + F_ROWS[layer] * c, F_ROWS[layer], value)
+    even_o[E_AT[10] : SECOND_ROWS, :] = jnp.zeros((SECOND_ROWS - E_AT[10], 256), F32)
+    odd_o[E_AT[10] : SECOND_ROWS, :] = jnp.zeros((SECOND_ROWS - E_AT[10], 256), F32)
+
+
+def fine_down(groups, devs, idx, f, e, cross, inner, odd, even, mid_o, pay_o, x1, ew, wt, fw, x0, pair, half):
     g, d = idx[0], idx[1]
     low_x, high_x = jnp.where(g > 0, 1.0, 0.0), jnp.where(g < groups - 1, 1.0, 0.0)
     low_y, high_y = jnp.where(d > 0, 1.0, 0.0), jnp.where(d < devs - 1, 1.0, 0.0)
-    zero = jnp.zeros((2, 256), F32)
     even_dev = d % 2 == 0
 
     def halo_second(at):
@@ -181,17 +195,24 @@
         else:
             own = halo_first(idx, cross, inner, 1 + layer)[1] if layer > 6 else e[layer - 3]
         s = low_x if layer < 3 else high_x if layer > 6 else 1.0
-        before, after = halo_second(slice(192 + 8 * layer, 200 + 8 * layer))
-        put(ew, (layer,), 0, before * (s * low_y))
+        rows = E_ROWS[layer]
+        before, after = halo_second(slice(E_AT[layer], E_AT[layer] + rows))
+        before, after = before * (s * low_y), after * (s * high_y)
+        if rows < 8:
+            ones = jnp.ones((8 - rows, 256), F32)
+            before, after = jnp.concatenate([ones, before], 0), jnp.concatenate([after, ones], 0)
+        put(ew, (layer,), 0, before)
         put(ew, (layer,), 8, own * s)
-        put(ew, (layer,), 24, after * (s * high_y))
+        put(ew, (layer,), 24, after)
     for layer in range(8):
         for c in range(4):
             if layer < 2:
                 own = halo_first(idx, cross, inner, 2 * c + layer)[0]
             else:
                 own = halo_first(idx, cross, inner, 2 * c + layer - 6)[1] if layer > 5 else f[c, layer - 2]
-            before, after = halo_second(slice(24 * layer + 6 * c, 24 * layer + 6 * c + 6))
+            at = F_AT[layer] + F_ROWS[layer] * c
+            before, after = halo_second(slice(at, at + F_ROWS[layer]))
+            zero = jnp.zeros((8 - F_ROWS[layer], 256), F32)
             put(fw, (c, layer), 0, jnp.concatenate([zero, before], 0))
             put(fw, (c, layer), 8, own)
             put(fw, (c, layer), 24, jnp.concatenate([after, zero], 0))
@@ -219,12 +240,12 @@
     for m in range(2):
         lanes = slice(128 * m, 128 * m + 128)
         for c in range(4):
-            mid_o[12 * c : 12 * c + 12, lanes] = coarse[2 * c + m, 2:14, :]
-        mid_o[48:64, lanes] = coarse[8 + m]
+            mid_o[12 * c : 12 * c + 12, lanes] = pay_o[12 * c : 12 * c + 12, lanes] = coarse[2 * c + m, 2:14, :]
+        mid_o[48:64, lanes] = pay_o[48:64, lanes] = coarse[8 + m]
     for c in range(4):
         for j in range(2):
-            at = 18 * (2 * c + j)
-            edge_o[at : at + 18, :] = get(x1, (c, 3 + j), 7, 18)
+            at = 64 + 18 * (2 * c + j)
+            pay_o[at : at + 18, :] = get(x1, (c, 3 + j), 7, 18)
 
 
 def mid_down(groups, devs, idx, own, partner, xco, cpm, c2, s3, next_o, low_o, y_o, b_o, e_o, w_o, bw, ew, wt, y0, y1, pair, low):
@@ -294,11 +315,11 @@
     up = core == 0
     for c in range(4):
         for j in range(8):
-            at, i = base + 4 * (8 * c + j), 4 * chip + 2 + j
-            next_o[at : at + 4, :] = pick(up, y1[c, i, 8:12, :], y1[c, i, 4:8, :])
+            at, i = base + 3 * (8 * c + j), 4 * chip + 2 + j
+            next_o[at : at + 3, :] = pick(up, y1[c, i, 8:11, :], y1[c, i, 5:8, :])
         for j in range(4):
-            at, i = base + 128 + 4 * (4 * c + j), 4 * chip + 4 + j
-            next_o[at : at + 4, :] = pick(up, bw[c, i, 8:12, :], bw[c, i, 4:8, :])
+            at, i = base + 96 + 4 * c + j, 4 * chip + 4 + j
+            next_o[at : at + 1, :] = pick(up, bw[c, i, 9:10, :], bw[c, i, 6:7, :])
     for j in range(10):
         e_o[j] = ew[2 * g + j]
         w_o[j] = wt[2 * g + j]
@@ -327,11 +348,11 @@
             b2[c, i, 0:8, :] = zero[0:8]
             b2[c, i, 16:32, :] = zero[0:16]
     tall = 20 * (groups // 2)
-    by1_rows = tall + 192
+    by1_rows = tall + 112
     first_core = core == 0
 
-    def from_second(by, offset, at):
-        a, b = by[at : at + 4, :], swapped[offset + at : offset + at + 4, :]
+    def from_second(by, offset, at, rows=4):
+        a, b = by[at : at + rows, :], swapped[offset + at : offset + at + rows, :]
         return pick(first_core, a, b), pick(first_core, b, a)
 
     for away in (-2, -1, 0, 1, 2):
@@ -367,8 +388,8 @@
 
     low_y, high_y = jnp.where(d > 0, 1.0, 0.0), jnp.where(d < devs - 1, 1.0, 0.0)
 
-    def mid_halo(at, step):
-        a, b = from_second(by1, 0, at), from_second(by1, 0, at + step)
+    def mid_halo(at, rows):
+        a, b = from_second(by1, 0, at, rows), from_second(by1, 0, at + 2 * rows, rows)
         return pick(first_core, a[0], b[0]), pick(first_core, a[1], b[1])
 
     for c in range(4):
@@ -381,13 +402,13 @@
             b1[c, j] = b_i[c, j]
             ya[c, j] = y_i[c, j]
         for j in range(2):
-            before, after = mid_halo(tall + 128 + 4 * (4 * c + j), 8)
-            b1[c, 4 + j, 0:4, :] = before
-            b1[c, 4 + j, 12:16, :] = after
+            before, after = mid_halo(tall + 96 + 4 * c + j, 1)
+            b1[c, 4 + j, 1:2, :] = before
+            b1[c, 4 + j, 14:15, :] = after
         for j in range(6):
-            before, after = mid_halo(tall + 4 * (8 * c + j), 8)
-            ya[c, 2 + j, 0:4, :] = before * low_y
-            ya[c, 2 + j, 12:16, :] = after * high_y
+            before, after = mid_halo(tall + 3 * (8 * c + j), 3)
+            ya[c, 2 + j, 0:3, :] = before * low_y
+            ya[c, 2 + j, 13:16, :] = after * high_y
         for j in range(10):
             ya[c, j] = ya[c, j] + rep[c, j // 2]
     for at in range(1, 9):
@@ -410,7 +431,7 @@
                 rows = half[n, at : at + 32, :]
                 va[c, layer, n] = rows + x1[c, layer - 2, n] if 3 <= layer <= 8 else rows
         for j in range(2):
-            at = 18 * (2 * c + j)
+            at = 64 + 18 * (2 * c + j)
             own, far = own_edge[at : at + 18, :], far_edge[at : at + 18, :]
             before = jnp.where(core == 0, far, own) * low_x
             after = jnp.where(core == 0, own, far) * high_x
@@ -456,30 +477,35 @@
         to = [(g, (d - step if g % 2 else d + step) % devs) for g in range(groups) for d in range(devs)]
         return [(i, g * devs + d) for i, (g, d) in enumerate(to)]
 
-    cross, inner = call(pack_first, [(176, 256)] * 2, [], idx, forcing, viscosity)
+    cross, inner = pl.pallas_call(
+        pack_first,
+        out_shape=[jax.ShapeDtypeStruct((11, 16, 256), F32)] * 2,
+        in_specs=[pl.BlockSpec(memory_space=pltpu.SMEM), pl.BlockSpec(memory_space=pl.ANY), pl.BlockSpec(memory_space=pl.ANY)],
+        out_specs=[pl.BlockSpec(memory_space=pl.ANY)] * 2,
+        scratch_shapes=[pltpu.SemaphoreType.DMA((2, 5))],
+        compiler_params=pltpu.CompilerParams(vmem_limit_bytes=56 * 1024 * 1024),
+    )(idx, forcing, viscosity)
     cross, inner = lax.ppermute(cross, "grp", beside), lax.ppermute(inner, "grp", swap)
-    to_even, to_odd = call(pack_second, [(272, 256)] * 2, [], idx, forcing, viscosity, cross, inner)
+    to_even, to_odd = call(pack_second, [(SECOND_ROWS, 256)] * 2, [], idx, forcing, viscosity, cross, inner)
     from_odd, from_even = lax.ppermute(to_odd, "dev", odd), lax.ppermute(to_even, "dev", even)
-    mid, edge, x1, ew, wt, fw = call(
+    mid, pay, x1, ew, wt, fw = call(
         lambda *refs: fine_down(groups, devs, *refs),
-        [(64, 256), (144, 256), (4, 8, 2, 32, 128), (10, 2, 32, 128), (8, 2, 32, 128), (4, 8, 2, 32, 128)],
+        [(64, 256), (208, 256), (4, 8, 2, 32, 128), (10, 2, 32, 128), (8, 2, 32, 128), (4, 8, 2, 32, 128)],
         [(4, 8, 2, 32, 128), (10, 32, 256), (320, 128)],
         idx, forcing, viscosity, cross, inner, from_odd, from_even,
     )
 
+    xco = lax.ppermute(pay, "grp", beside)
     c2 = lax.ppermute(mid, "grp", far_chip)
-    xco = lax.ppermute(mid, "grp", beside)
     cpm = lax.ppermute(mid, "grp", next_chip)
-    partner = lax.ppermute(mid, "grp", swap)
-    own_edge = lax.ppermute(edge, "grp", swap)
-    far_edge = lax.ppermute(edge, "grp", beside)
-    s3 = lax.ppermute(jnp.concatenate([xco, cpm, c2], axis=0), "grp", swap)
+    partner = lax.ppermute(pay, "grp", swap)
+    s3 = lax.ppermute(jnp.concatenate([xco[:64], cpm, c2], axis=0), "grp", swap)
 
     layers = 2 * groups + 8
     tall = 20 * (groups // 2)
     to_next, low, y_w, b_w, e_w, w_w = call(
         lambda *refs: mid_down(groups, devs, *refs),
-        [(tall + 192, 128), (tall, 128), (4, 10, 16, 128), (4, 10, 16, 128), (10, 16, 128), (10, 16, 128)],
+        [(tall + 112, 128), (tall, 128), (4, 10, 16, 128), (4, 10, 16, 128), (10, 16, 128), (10, 16, 128)],
         [(4, layers, 16, 128), (layers, 16, 128), (layers, 16, 128), (4, layers, 16, 128), (4, layers, 16, 128),
          (groups, 5, 8, 128), (5, groups, 8, 128)],
         idx, mid, partner, xco, cpm, c2, s3,
@@ -495,7 +521,7 @@
         [(deep, 32, 128), (deep, 32, 128), (4, deep, 32, 128), (4, deep, 32, 128), (4, deep, 32, 128),
          (4, 10, 16, 128), (4, 10, 16, 128), (4, 10, 16, 128), (4, 5, 16, 128), (2, 768, 128),
          (4, 12, 2, 32, 128), (4, 12, 2, 32, 128)],
-        idx, low, by1, by2, swapped, y_w, b_w, e_w, w_w, x1, ew, wt, fw, own_edge, far_edge,
+        idx, low, by1, by2, swapped, y_w, b_w, e_w, w_w, x1, ew, wt, fw, partner, xco,
     ))
 
 

time: 68.8 us -> 76.7 us (1.11)
  Pallas kernels: 10.8 us -> 23.2 us
  starting transfers between devices: 34.1 us -> 30.2 us
  local copies, waits for them, and re-layouts: 1.79 us -> 0.02 us
    pallas_call x0 -> x1, Pallas kernels: none -> 12.9 us  [local(): pl.pallas_call(pack_first, out_shape=[jax.ShapeDtypeStruct((11, 16, 256),...]
    ppermute x1, waiting for transfers between devices: 0.01 us -> 7.07 us  [local(): c2 = lax.ppermute(mid, 'grp', far_chip)]
    ppermute x1, waiting for transfers between devices: 3.72 us -> 0.01 us  [local(): cpm = lax.ppermute(mid, 'grp', next_chip)]
    ppermute x5 -> x3, waiting for transfers between devices: 4.56 us -> 1.07 us  [the longest x1 1.07 us: local(): s3 = lax.ppermute(jnp.concatenate([xco[:64], cpm, c2], axis=0), 'grp', swap)]
    ppermute x1, starting transfers between devices: 7.2 us -> 4.32 us  [local(): c2 = lax.ppermute(mid, 'grp', far_chip)]
    unnamed x4 -> x6, local copies, waits for them, and re-layouts: 1.79 us -> 0.01 us
    ppermute x1, starting transfers between devices: 4.56 us -> 2.97 us  [local(): by1 = lax.ppermute(to_next, ('grp', 'dev'), along(1))]
    ppermute x1, starting transfers between devices: 1.2 us -> 2.37 us  [local(): swapped = lax.ppermute(jnp.concatenate([by1, by2], axis=0), 'grp', swap)]
  transfers between devices with their start and end apart: 14 -> 12, of which waited for: 8 -> 7; matrix products, arithmetic and copies ran while one was open for 0% -> 0% of each run, Pallas kernels for 0% -> 0%
where the time goes in v4:
time: 76.7 us; the launch traced here: 76.6 us
  starting transfers between devices  30.2 us (39%)
  Pallas kernels  23.2 us (30%)
  waiting for transfers between devices  21.8 us (28%)
    pallas_call x1, Pallas kernels, local(): pl.pallas_call(pack_first, out_shape=[jax.ShapeDtypeStruct((11, 16, 256),...  12.9 us
    pallas_call x4, Pallas kernels, call(): pl.pallas_call(kernel, out_shape=[jax.ShapeDtypeStruct(shape, F32) for sh...  10.3 us
    ppermute x1, waiting for transfers between devices, local(): c2 = lax.ppermute(mid, 'grp', far_chip)  7.07 us
    ppermute x1, starting transfers between devices, local(): xco = lax.ppermute(pay, 'grp', beside)  5.98 us
    ppermute x1, starting transfers between devices, local(): lax.ppermute(to_odd, 'dev', odd)  4.98 us
    ppermute x1, waiting for transfers between devices, local(): by2 = lax.ppermute(low, ('grp', 'dev'), along(2))  4.61 us
    ppermute x1, starting transfers between devices, local(): lax.ppermute(cross, 'grp', beside)  4.47 us
    ppermute x1, starting transfers between devices, local(): c2 = lax.ppermute(mid, 'grp', far_chip)  4.32 us
  transfers between devices with their start and end apart: 12, of which 7 were waited for; matrix products, arithmetic and copies ran while one was open for 0% of the time, Pallas kernels for 0%

profile of v4, /device:TPU:1, one launch (start us, length us, event | category | flops | bytes accessed | tf_op | source)
XLA Modules:
  0.0 76.6 jit_solution(982213178383413203)
XLA Ops:
  0.6 0.0 copy-start
  0.6 0.7 pad_add_fusion.idx.refs_0_
  1.3 0.0 copy-start.1
  1.3 12.9 %shard_map.41 = (f32[11,16,256]{2,1,0:T(8,128)}, f32[11,16,256]{2,1,0:T(8,128)}) custom-call(s32[2]{0:T(128)} %pad_add_fusion.idx.refs_0_, f32[4,4,16,256]{3,2,1,0:T(8,128)} %refs_1_.1, f32[4,16,256]{2,1,0:T(8,128)} %refs_2_.1), custom_call_target="tpu_custom_call" | custom-call | tf_op jit(solution)/shard_map/pallas_call | solution.py:480
  14.2 0.0 copy-start.2
  14.2 4.5 %collective-permute-start = (f32[11,16,256]{2,1,0:T(8,128)}, f32[11,16,256]{2,1,0:T(8,128)S(1)}, u32[]{:S(2)}, u32[]{:S(2)}) collective-permute-start(f32[11,16,256]{2,1,0:T(8,128)} %get-tuple-element.18), channel_id=1, source_target_pairs={{0,224},{32,64},{64,32},{96,128},{128,96},{160,192},{192,160},{224... | collective-permute-start | bytes 540680 | tf_op jit(solution)/shard_map/ppermute | solution.py:488
  18.7 2.9 %collective-permute-start.1 = (f32[11,16,256]{2,1,0:T(8,128)}, f32[11,16,256]{2,1,0:T(8,128)S(1)}, u32[]{:S(2)}, u32[]{:S(2)}) collective-permute-start(f32[11,16,256]{2,1,0:T(8,128)} %get-tuple-element.19), channel_id=1, source_target_pairs={{0,32},{32,0},{64,96},{96,64},{128,160},{160,128},{192,224},{224,1... | collective-permute-start | bytes 540680 | tf_op jit(solution)/shard_map/ppermute | solution.py:488
  21.6 2.8 %collective-permute-done.cross.refs_3_ = f32[11,16,256]{2,1,0:T(8,128)S(1)} collective-permute-done((f32[11,16,256]{2,1,0:T(8,128)}, f32[11,16,256]{2,1,0:T(8,128)S(1)}, u32[]{:S(2)}, u32[]{:S(2)}) %collective-permute-start) | collective-permute-done | bytes 180256 | tf_op jit(solution)/shard_map/ppermute | solution.py:488
  24.3 0.0 collective-permute-done.1.inner.refs_4_
  24.3 0.0 copy-done
  24.3 0.0 copy-done.1
  24.3 0.0 copy-done.2
  24.3 0.6 shard_map.42
  25.0 5.0 %collective-permute-start.2 = (f32[232,256]{1,0:T(8,128)S(1)}, f32[232,256]{1,0:T(8,128)S(1)}, u32[]{:S(2)}, u32[]{:S(2)}) collective-permute-start(f32[232,256]{1,0:T(8,128)S(1)} %get-tuple-element.20), channel_id=1, source_target_pairs={{0,31},{1,2},{2,1},{3,4},{4,3},{5,6},{6,5},{7,8},{8,7},{9,10},{10,... | collective-permute-start | bytes 712712 | tf_op jit(solution)/shard_map/ppermute | solution.py:490
  30.0 0.0 collective-permute-start.3
  30.0 4.3 %collective-permute-done.2.refs_5_ = f32[232,256]{1,0:T(8,128)S(1)} collective-permute-done((f32[232,256]{1,0:T(8,128)S(1)}, f32[232,256]{1,0:T(8,128)S(1)}, u32[]{:S(2)}, u32[]{:S(2)}) %collective-permute-start.2) | collective-permute-done | bytes 237600 | tf_op jit(solution)/shard_map/ppermute | solution.py:490
  34.3 1.0 %collective-permute-done.3.refs_6_ = f32[232,256]{1,0:T(8,128)S(1)} collective-permute-done((f32[232,256]{1,0:T(8,128)S(1)}, f32[232,256]{1,0:T(8,128)S(1)}, u32[]{:S(2)}, u32[]{:S(2)}) %collective-permute-start.3) | collective-permute-done | bytes 237600 | tf_op jit(solution)/shard_map/ppermute | solution.py:490
  35.2 2.7 %shard_map.43 = (f32[64,256]{1,0:T(8,128)S(1)}, f32[208,256]{1,0:T(8,128)S(1)}, f32[4,8,2,32,128]{4,3,2,1,0:T(8,128)S(1)}, f32[10,2,32,128]{3,2,1,0:T(8,128)S(1)...) custom-call(s32[2]{0:T(128)S(1)} %copy-done.2, f32[4,4,16,256]{3,2,1,0:T(8,128)S(1)} %copy-done, ...), custom_call_target="tpu_custom_call" | custom-call | tf_op jit(solution)/shard_map/pallas_call | solution.py:456
  37.9 6.0 %collective-permute-start.5 = (f32[208,256]{1,0:T(8,128)S(1)}, f32[208,256]{1,0:T(8,128)S(1)}, u32[]{:S(2)}, u32[]{:S(2)}) collective-permute-start(f32[208,256]{1,0:T(8,128)S(1)} %get-tuple-element.23), channel_id=1, source_target_pairs={{0,224},{32,64},{64,32},{96,128},{128,96},{160,192},{192,160},{224... | collective-permute-start | bytes 638984 | tf_op jit(solution)/shard_map/ppermute | solution.py:498
  43.9 4.3 %collective-permute-start.7 = (f32[64,256]{1,0:T(8,128)S(1)}, f32[64,256]{1,0:T(8,128)S(1)}, u32[]{:S(2)}, u32[]{:S(2)}) collective-permute-start(f32[64,256]{1,0:T(8,128)S(1)} %get-tuple-element.22.refs_1_), channel_id=1, source_target_pairs={{0,128},{32,160},{64,192},{96,224},{128,0},{160,32},{192,64},{224,... | collective-permute-start | bytes 196616 | tf_op jit(solution)/shard_map/ppermute | solution.py:499
  48.2 1.7 %collective-permute-start.6 = (f32[64,256]{1,0:T(8,128)S(1)}, f32[64,256]{1,0:T(8,128)S(1)}, u32[]{:S(2)}, u32[]{:S(2)}) collective-permute-start(f32[64,256]{1,0:T(8,128)S(1)} %get-tuple-element.22.refs_1_), channel_id=1, source_target_pairs={{0,64},{32,224},{64,128},{96,32},{128,192},{160,96},{192,0},{224,1... | collective-permute-start | bytes 196616 | tf_op jit(solution)/shard_map/ppermute | solution.py:500
  50.0 0.0 collective-permute-start.4
  50.0 0.0 collective-permute-done.5.refs_3_.refs_14_
  50.0 7.1 %collective-permute-done.7.refs_5_ = f32[64,256]{1,0:T(8,128)S(1)} collective-permute-done((f32[64,256]{1,0:T(8,128)S(1)}, f32[64,256]{1,0:T(8,128)S(1)}, u32[]{:S(2)}, u32[]{:S(2)}) %collective-permute-start.7) | collective-permute-done | bytes 65568 | tf_op jit(solution)/shard_map/ppermute | solution.py:499
  57.0 0.0 collective-permute-done.6.refs_4_
  57.1 0.5 collective-permute-start.8
  57.6 0.0 collective-permute-done.4.refs_2_.refs_13_
  57.6 1.1 %collective-permute-done.8.refs_6_ = f32[192,256]{1,0:T(8,128)S(1)} collective-permute-done((f32[192,256]{1,0:T(8,128)S(1)}, f32[192,256]{1,0:T(8,128)S(1)}, u32[]{:S(2)}, u32[]{:S(2)}) %collective-permute-start.8) | collective-permute-done | bytes 196640 | tf_op jit(solution)/shard_map/ppermute | solution.py:502
  58.7 1.6 %shard_map.44 = (f32[192,128]{1,0:T(8,128)S(1)}, f32[80,128]{1,0:T(8,128)S(1)}, f32[4,10,16,128]{3,2,1,0:T(8,128)S(1)}, f32[4,10,16,128]{3,2,1,0:T(8,128)S(1)}, ...) custom-call(s32[2]{0:T(128)S(1)} %copy-done.2, f32[64,256]{1,0:T(8,128)S(1)} %get-tuple-element.22.refs_1_, ...), custom_call_target="tpu_custom_call" | custom-call | tf_op jit(solution)/shard_map/pallas_call | solution.py:456
  60.2 3.0 %collective-permute-start.9 = (f32[192,128]{1,0:T(8,128)S(1)}, f32[192,128]{1,0:T(8,128)S(1)}, u32[]{:S(2)}, u32[]{:S(2)}) collective-permute-start(f32[192,128]{1,0:T(8,128)S(1)} %get-tuple-element.25), channel_id=1, source_target_pairs={{0,1},{1,2},{2,3},{3,4},{4,5},{5,6},{6,7},{7,8},{8,9},{9,10},{10,1... | collective-permute-start | bytes 294920 | tf_op jit(solution)/shard_map/ppermute | solution.py:514
  63.2 0.0 collective-permute-start.10
  63.2 4.6 %collective-permute-done.10.refs_3_ = f32[80,128]{1,0:T(8,128)S(1)} collective-permute-done((f32[80,128]{1,0:T(8,128)S(1)}, f32[80,128]{1,0:T(8,128)S(1)}, u32[]{:S(2)}, u32[]{:S(2)}) %collective-permute-start.10) | collective-permute-done | bytes 40992 | tf_op jit(solution)/shard_map/ppermute | solution.py:515
  67.8 0.0 collective-permute-done.9.refs_2_
  67.9 2.4 %collective-permute-start.11 = (f32[272,128]{1,0:T(8,128)S(1)}, f32[272,128]{1,0:T(8,128)S(1)}, u32[]{:S(2)}, u32[]{:S(2)}) collective-permute-start(f32[272,128]{1,0:T(8,128)S(1)} %pad_maximum_fusion.1), channel_id=1, source_target_pairs={{0,32},{32,0},{64,96},{96,64},{128,160},{160,128},{192,224},{224,1... | collective-permute-start | bytes 417800 | tf_op jit(solution)/shard_map/ppermute | solution.py:516
  70.2 1.0 %collective-permute-done.11.refs_4_ = f32[272,128]{1,0:T(8,128)S(1)} collective-permute-done((f32[272,128]{1,0:T(8,128)S(1)}, f32[272,128]{1,0:T(8,128)S(1)}, u32[]{:S(2)}, u32[]{:S(2)}) %collective-permute-start.11) | collective-permute-done | bytes 139296 | tf_op jit(solution)/shard_map/ppermute | solution.py:516
  71.2 5.4 %shard_map.45 = (f32[4,4,16,256]{3,2,1,0:T(8,128)}, f32[4,4,16,256]{3,2,1,0:T(8,128)}) custom-call(s32[2]{0:T(128)S(1)} %copy-done.2, f32[80,128]{1,0:T(8,128)S(1)} %get-tuple-element.24.refs_1_, f32[192,128]{1,0:T(8,128)S(1)} %collective-permute-done.9.refs_2_, f32[80,128]{1,0:T(8,128)S(1)} %collective-permute-done.10.refs_3_, ...), custom_call_target="tpu_custom_call" | custom-call | tf_op jit(solution)/shard_map/pallas_call | solution.py:456
  (3 shorter events, 0.0 us)
Async XLA Ops:
  0.6 23.7 %copy-start = (f32[4,4,16,256]{3,2,1,0:T(8,128)S(1)}, f32[4,4,16,256]{3,2,1,0:T(8,128)}, u32[]{:S(2)}) copy-start(f32[4,4,16,256]{3,2,1,0:T(8,128)} %refs_1_.1) | copy-start | bytes 786436
  1.3 23.0 %copy-start.1 = (f32[4,16,256]{2,1,0:T(8,128)S(1)}, f32[4,16,256]{2,1,0:T(8,128)}, u32[]{:S(2)}) copy-start(f32[4,16,256]{2,1,0:T(8,128)} %refs_2_.1) | copy-start | bytes 196612
  14.2 10.1 %copy-start.2 = (s32[2]{0:T(128)S(1)}, s32[2]{0:T(128)}, u32[]{:S(2)}) copy-start(s32[2]{0:T(128)} %pad_add_fusion.idx.refs_0_) | copy-start | bytes 28
  14.2 10.1 %collective-permute-start = (f32[11,16,256]{2,1,0:T(8,128)}, f32[11,16,256]{2,1,0:T(8,128)S(1)}, u32[]{:S(2)}, u32[]{:S(2)}) collective-permute-start(f32[11,16,256]{2,1,0:T(8,128)} %get-tuple-element.18), channel_id=1, source_target_pairs={{0,224},{32,64},{64,32},{96,128},{128,96},{160,192},{192,160},{224... | collective-permute-start | bytes 540680 | tf_op jit(solution)/shard_map/ppermute | solution.py:488
  18.7 5.6 %collective-permute-start.1 = (f32[11,16,256]{2,1,0:T(8,128)}, f32[11,16,256]{2,1,0:T(8,128)S(1)}, u32[]{:S(2)}, u32[]{:S(2)}) collective-permute-start(f32[11,16,256]{2,1,0:T(8,128)} %get-tuple-element.19), channel_id=1, source_target_pairs={{0,32},{32,0},{64,96},{96,64},{128,160},{160,128},{192,224},{224,1... | collective-permute-start | bytes 540680 | tf_op jit(solution)/shard_map/ppermute | solution.py:488
  25.0 9.3 %collective-permute-start.2 = (f32[232,256]{1,0:T(8,128)S(1)}, f32[232,256]{1,0:T(8,128)S(1)}, u32[]{:S(2)}, u32[]{:S(2)}) collective-permute-start(f32[232,256]{1,0:T(8,128)S(1)} %get-tuple-element.20), channel_id=1, source_target_pairs={{0,31},{1,2},{2,1},{3,4},{4,3},{5,6},{6,5},{7,8},{8,7},{9,10},{10,... | collective-permute-start | bytes 712712 | tf_op jit(solution)/shard_map/ppermute | solution.py:490
  30.0 5.3 %collective-permute-start.3 = (f32[232,256]{1,0:T(8,128)S(1)}, f32[232,256]{1,0:T(8,128)S(1)}, u32[]{:S(2)}, u32[]{:S(2)}) collective-permute-start(f32[232,256]{1,0:T(8,128)S(1)} %get-tuple-element.21), channel_id=1, source_target_pairs={{0,1},{1,0},{2,3},{3,2},{4,5},{5,4},{6,7},{7,6},{8,9},{9,8},{10,11... | collective-permute-start | bytes 712712 | tf_op jit(solution)/shard_map/ppermute | solution.py:490
  37.9 12.0 %collective-permute-start.5 = (f32[208,256]{1,0:T(8,128)S(1)}, f32[208,256]{1,0:T(8,128)S(1)}, u32[]{:S(2)}, u32[]{:S(2)}) collective-permute-start(f32[208,256]{1,0:T(8,128)S(1)} %get-tuple-element.23), channel_id=1, source_target_pairs={{0,224},{32,64},{64,32},{96,128},{128,96},{160,192},{192,160},{224... | collective-permute-start | bytes 638984 | tf_op jit(solution)/shard_map/ppermute | solution.py:498
  43.9 13.1 %collective-permute-start.7 = (f32[64,256]{1,0:T(8,128)S(1)}, f32[64,256]{1,0:T(8,128)S(1)}, u32[]{:S(2)}, u32[]{:S(2)}) collective-permute-start(f32[64,256]{1,0:T(8,128)S(1)} %get-tuple-element.22.refs_1_), channel_id=1, source_target_pairs={{0,128},{32,160},{64,192},{96,224},{128,0},{160,32},{192,64},{224,... | collective-permute-start | bytes 196616 | tf_op jit(solution)/shard_map/ppermute | solution.py:499
  48.2 8.8 %collective-permute-start.6 = (f32[64,256]{1,0:T(8,128)S(1)}, f32[64,256]{1,0:T(8,128)S(1)}, u32[]{:S(2)}, u32[]{:S(2)}) collective-permute-start(f32[64,256]{1,0:T(8,128)S(1)} %get-tuple-element.22.refs_1_), channel_id=1, source_target_pairs={{0,64},{32,224},{64,128},{96,32},{128,192},{160,96},{192,0},{224,1... | collective-permute-start | bytes 196616 | tf_op jit(solution)/shard_map/ppermute | solution.py:500
  50.0 7.6 %collective-permute-start.4 = (f32[208,256]{1,0:T(8,128)S(1)}, f32[208,256]{1,0:T(8,128)S(1)}, u32[]{:S(2)}, u32[]{:S(2)}) collective-permute-start(f32[208,256]{1,0:T(8,128)S(1)} %get-tuple-element.23), channel_id=1, source_target_pairs={{0,32},{32,0},{64,96},{96,64},{128,160},{160,128},{192,224},{224,1... | collective-permute-start | bytes 638984 | tf_op jit(solution)/shard_map/ppermute | solution.py:501
  57.1 1.6 %collective-permute-start.8 = (f32[192,256]{1,0:T(8,128)S(1)}, f32[192,256]{1,0:T(8,128)S(1)}, u32[]{:S(2)}, u32[]{:S(2)}) collective-permute-start(f32[192,256]{1,0:T(8,128)S(1)} %pad_maximum_fusion), channel_id=1, source_target_pairs={{0,32},{32,0},{64,96},{96,64},{128,160},{160,128},{192,224},{224,1... | collective-permute-start | bytes 589832 | tf_op jit(solution)/shard_map/ppermute | solution.py:502
  60.2 7.6 %collective-permute-start.9 = (f32[192,128]{1,0:T(8,128)S(1)}, f32[192,128]{1,0:T(8,128)S(1)}, u32[]{:S(2)}, u32[]{:S(2)}) collective-permute-start(f32[192,128]{1,0:T(8,128)S(1)} %get-tuple-element.25), channel_id=1, source_target_pairs={{0,1},{1,2},{2,3},{3,4},{4,5},{5,6},{6,7},{7,8},{8,9},{9,10},{10,1... | collective-permute-start | bytes 294920 | tf_op jit(solution)/shard_map/ppermute | solution.py:514
  63.2 4.7 %collective-permute-start.10 = (f32[80,128]{1,0:T(8,128)S(1)}, f32[80,128]{1,0:T(8,128)S(1)}, u32[]{:S(2)}, u32[]{:S(2)}) collective-permute-start(f32[80,128]{1,0:T(8,128)S(1)} %get-tuple-element.24.refs_1_), channel_id=1, source_target_pairs={{0,2},{1,3},{2,4},{3,5},{4,6},{5,7},{6,8},{7,9},{8,10},{9,11},{10,... | collective-permute-start | bytes 122888 | tf_op jit(solution)/shard_map/ppermute | solution.py:515
  67.9 3.4 %collective-permute-start.11 = (f32[272,128]{1,0:T(8,128)S(1)}, f32[272,128]{1,0:T(8,128)S(1)}, u32[]{:S(2)}, u32[]{:S(2)}) collective-permute-start(f32[272,128]{1,0:T(8,128)S(1)} %pad_maximum_fusion.1), channel_id=1, source_target_pairs={{0,32},{32,0},{64,96},{96,64},{128,160},{160,128},{192,224},{224,1... | collective-permute-start | bytes 417800 | tf_op jit(solution)/shard_map/ppermute | solution.py:516

commit v5 on v4

--- a/solution.py
+++ b/solution.py
@@ -481,9 +481,9 @@
         pack_first,
         out_shape=[jax.ShapeDtypeStruct((11, 16, 256), F32)] * 2,
         in_specs=[pl.BlockSpec(memory_space=pltpu.SMEM), pl.BlockSpec(memory_space=pl.ANY), pl.BlockSpec(memory_space=pl.ANY)],
-        out_specs=[pl.BlockSpec(memory_space=pl.ANY)] * 2,
+        out_specs=[pl.BlockSpec(memory_space=pltpu.VMEM)] * 2,
         scratch_shapes=[pltpu.SemaphoreType.DMA((2, 5))],
-        compiler_params=pltpu.CompilerParams(vmem_limit_bytes=56 * 1024 * 1024),
+        compiler_params=pltpu.CompilerParams(vmem_limit_bytes=int(53.5 * 1024 * 1024)),
     )(idx, forcing, viscosity)
     cross, inner = lax.ppermute(cross, "grp", beside), lax.ppermute(inner, "grp", swap)
     to_even, to_odd = call(pack_second, [(SECOND_ROWS, 256)] * 2, [], idx, forcing, viscosity, cross, inner)

time: 76.7 us -> 65.4 us (0.85)
  Pallas kernels: 23.2 us -> 11.8 us
  local copies, waits for them, and re-layouts: 0.02 us -> 0.85 us
    pallas_call x1, Pallas kernels: 12.9 us -> 1.52 us  [local(): pl.pallas_call(pack_first, out_shape=[jax.ShapeDtypeStruct((11, 16, 256),...]
    unnamed x6, local copies, waits for them, and re-layouts: 0.01 us -> 0.85 us
where the time goes in v5:
time: 65.4 us; the launch traced here: 65.3 us
  starting transfers between devices  30.2 us (46%)
  waiting for transfers between devices  21.6 us (33%)
  Pallas kernels  11.8 us (18%)
  local copies, waits for them, and re-layouts  0.85 us (1%)
  between operations  0.69 us (1%)
    pallas_call x4, Pallas kernels, call(): pl.pallas_call(kernel, out_shape=[jax.ShapeDtypeStruct(shape, F32) for sh...  10.3 us
    ppermute x1, waiting for transfers between devices, local(): c2 = lax.ppermute(mid, 'grp', far_chip)  7.07 us
    ppermute x1, starting transfers between devices, local(): xco = lax.ppermute(pay, 'grp', beside)  6.08 us
    ppermute x1, starting transfers between devices, local(): lax.ppermute(to_odd, 'dev', odd)  4.88 us
    ppermute x1, waiting for transfers between devices, local(): by2 = lax.ppermute(low, ('grp', 'dev'), along(2))  4.62 us
    ppermute x1, starting transfers between devices, local(): lax.ppermute(cross, 'grp', beside)  4.47 us
    ppermute x1, waiting for transfers between devices, local(): lax.ppermute(to_odd, 'dev', odd)  4.38 us
    ppermute x1, starting transfers between devices, local(): c2 = lax.ppermute(mid, 'grp', far_chip)  4.32 us
  transfers between devices with their start and end apart: 12, of which 7 were waited for; matrix products, arithmetic and copies ran while one was open for 0% of the time, Pallas kernels for 0%

profile of v5, /device:TPU:1, one launch (start us, length us, event | category | flops | bytes accessed | tf_op | source)
XLA Modules:
  0.0 65.3 jit_solution(6101760196090135548)
XLA Ops:
  0.6 0.0 copy-start
  0.6 0.1 pad_add_fusion.idx.refs_0_
  0.7 0.0 copy-start.1
  0.7 0.8 %copy-done.1 = f32[4,16,256]{2,1,0:T(8,128)S(1)} copy-done((f32[4,16,256]{2,1,0:T(8,128)S(1)}, f32[4,16,256]{2,1,0:T(8,128)}, u32[]{:S(2)}) %copy-start.1) | copy-done | bytes 65560
  1.6 1.5 %shard_map.41 = (f32[11,16,256]{2,1,0:T(8,128)S(1)}, f32[11,16,256]{2,1,0:T(8,128)S(1)}) custom-call(s32[2]{0:T(128)S(1)} %pad_add_fusion.idx.refs_0_, f32[4,4,16,256]{3,2,1,0:T(8,128)} %refs_1_.1, f32[4,16,256]{2,1,0:T(8,128)S(1)} %copy-done.1), custom_call_target="tpu_custom_call" | custom-call | tf_op jit(solution)/shard_map/pallas_call | solution.py:480
  3.1 4.5 %collective-permute-start = (f32[11,16,256]{2,1,0:T(8,128)S(1)}, f32[11,16,256]{2,1,0:T(8,128)S(1)}, u32[]{:S(2)}, u32[]{:S(2)}) collective-permute-start(f32[11,16,256]{2,1,0:T(8,128)S(1)} %get-tuple-element.18), channel_id=1, source_target_pairs={{0,224},{32,64},{64,32},{96,128},{128,96},{160,192},{192,160},{224... | collective-permute-start | bytes 540680 | tf_op jit(solution)/shard_map/ppermute | solution.py:488
  7.6 0.0 copy-start.2
  7.6 2.9 %collective-permute-start.1 = (f32[11,16,256]{2,1,0:T(8,128)S(1)}, f32[11,16,256]{2,1,0:T(8,128)S(1)}, u32[]{:S(2)}, u32[]{:S(2)}) collective-permute-start(f32[11,16,256]{2,1,0:T(8,128)S(1)} %get-tuple-element.19), channel_id=1, source_target_pairs={{0,32},{32,0},{64,96},{96,64},{128,160},{160,128},{192,224},{224,1... | collective-permute-start | bytes 540680 | tf_op jit(solution)/shard_map/ppermute | solution.py:488
  10.4 2.5 %collective-permute-done.cross.refs_3_ = f32[11,16,256]{2,1,0:T(8,128)S(1)} collective-permute-done((f32[11,16,256]{2,1,0:T(8,128)S(1)}, f32[11,16,256]{2,1,0:T(8,128)S(1)}, u32[]{:S(2)}, u32[]{:S(2)}) %collective-permute-start) | collective-permute-done | bytes 180256 | tf_op jit(solution)/shard_map/ppermute | solution.py:488
  13.0 0.0 collective-permute-done.1.inner.refs_4_
  13.0 0.0 copy-done
  13.0 0.6 shard_map.42
  13.6 4.9 %collective-permute-start.2 = (f32[232,256]{1,0:T(8,128)S(1)}, f32[232,256]{1,0:T(8,128)S(1)}, u32[]{:S(2)}, u32[]{:S(2)}) collective-permute-start(f32[232,256]{1,0:T(8,128)S(1)} %get-tuple-element.20), channel_id=1, source_target_pairs={{0,31},{1,2},{2,1},{3,4},{4,3},{5,6},{6,5},{7,8},{8,7},{9,10},{10,... | collective-permute-start | bytes 712712 | tf_op jit(solution)/shard_map/ppermute | solution.py:490
  18.5 0.0 collective-permute-start.3
  18.5 4.4 %collective-permute-done.2.refs_5_ = f32[232,256]{1,0:T(8,128)S(1)} collective-permute-done((f32[232,256]{1,0:T(8,128)S(1)}, f32[232,256]{1,0:T(8,128)S(1)}, u32[]{:S(2)}, u32[]{:S(2)}) %collective-permute-start.2) | collective-permute-done | bytes 237600 | tf_op jit(solution)/shard_map/ppermute | solution.py:490
  22.9 0.9 %collective-permute-done.3.refs_6_ = f32[232,256]{1,0:T(8,128)S(1)} collective-permute-done((f32[232,256]{1,0:T(8,128)S(1)}, f32[232,256]{1,0:T(8,128)S(1)}, u32[]{:S(2)}, u32[]{:S(2)}) %collective-permute-start.3) | collective-permute-done | bytes 237600 | tf_op jit(solution)/shard_map/ppermute | solution.py:490
  23.8 0.0 copy-done.2
  23.8 2.7 %shard_map.43 = (f32[64,256]{1,0:T(8,128)S(1)}, f32[208,256]{1,0:T(8,128)S(1)}, f32[4,8,2,32,128]{4,3,2,1,0:T(8,128)S(1)}, f32[10,2,32,128]{3,2,1,0:T(8,128)S(1)...) custom-call(s32[2]{0:T(128)S(1)} %pad_add_fusion.idx.refs_0_, f32[4,4,16,256]{3,2,1,0:T(8,128)S(1)} %copy-done, ...), custom_call_target="tpu_custom_call" | custom-call | tf_op jit(solution)/shard_map/pallas_call | solution.py:456
  26.5 6.1 %collective-permute-start.5 = (f32[208,256]{1,0:T(8,128)S(1)}, f32[208,256]{1,0:T(8,128)S(1)}, u32[]{:S(2)}, u32[]{:S(2)}) collective-permute-start(f32[208,256]{1,0:T(8,128)S(1)} %get-tuple-element.23), channel_id=1, source_target_pairs={{0,224},{32,64},{64,32},{96,128},{128,96},{160,192},{192,160},{224... | collective-permute-start | bytes 638984 | tf_op jit(solution)/shard_map/ppermute | solution.py:498
  32.5 4.3 %collective-permute-start.7 = (f32[64,256]{1,0:T(8,128)S(1)}, f32[64,256]{1,0:T(8,128)S(1)}, u32[]{:S(2)}, u32[]{:S(2)}) collective-permute-start(f32[64,256]{1,0:T(8,128)S(1)} %get-tuple-element.22.refs_1_), channel_id=1, source_target_pairs={{0,128},{32,160},{64,192},{96,224},{128,0},{160,32},{192,64},{224,... | collective-permute-start | bytes 196616 | tf_op jit(solution)/shard_map/ppermute | solution.py:499
  36.9 1.7 %collective-permute-start.6 = (f32[64,256]{1,0:T(8,128)S(1)}, f32[64,256]{1,0:T(8,128)S(1)}, u32[]{:S(2)}, u32[]{:S(2)}) collective-permute-start(f32[64,256]{1,0:T(8,128)S(1)} %get-tuple-element.22.refs_1_), channel_id=1, source_target_pairs={{0,64},{32,224},{64,128},{96,32},{128,192},{160,96},{192,0},{224,1... | collective-permute-start | bytes 196616 | tf_op jit(solution)/shard_map/ppermute | solution.py:500
  38.6 0.0 collective-permute-start.4
  38.6 0.0 collective-permute-done.5.refs_3_.refs_14_
  38.6 7.1 %collective-permute-done.7.refs_5_ = f32[64,256]{1,0:T(8,128)S(1)} collective-permute-done((f32[64,256]{1,0:T(8,128)S(1)}, f32[64,256]{1,0:T(8,128)S(1)}, u32[]{:S(2)}, u32[]{:S(2)}) %collective-permute-start.7) | collective-permute-done | bytes 65568 | tf_op jit(solution)/shard_map/ppermute | solution.py:499
  45.7 0.0 collective-permute-done.6.refs_4_
  45.7 0.5 collective-permute-start.8
  46.2 0.0 collective-permute-done.4.refs_2_.refs_13_
  46.2 1.1 %collective-permute-done.8.refs_6_ = f32[192,256]{1,0:T(8,128)S(1)} collective-permute-done((f32[192,256]{1,0:T(8,128)S(1)}, f32[192,256]{1,0:T(8,128)S(1)}, u32[]{:S(2)}, u32[]{:S(2)}) %collective-permute-start.8) | collective-permute-done | bytes 196640 | tf_op jit(solution)/shard_map/ppermute | solution.py:502
  47.3 1.6 %shard_map.44 = (f32[192,128]{1,0:T(8,128)S(1)}, f32[80,128]{1,0:T(8,128)S(1)}, f32[4,10,16,128]{3,2,1,0:T(8,128)S(1)}, f32[4,10,16,128]{3,2,1,0:T(8,128)S(1)}, ...) custom-call(s32[2]{0:T(128)S(1)} %pad_add_fusion.idx.refs_0_, f32[64,256]{1,0:T(8,128)S(1)} %get-tuple-element.22.refs_1_, ...), custom_call_target="tpu_custom_call" | custom-call | tf_op jit(solution)/shard_map/pallas_call | solution.py:456
  48.8 3.0 %collective-permute-start.9 = (f32[192,128]{1,0:T(8,128)S(1)}, f32[192,128]{1,0:T(8,128)S(1)}, u32[]{:S(2)}, u32[]{:S(2)}) collective-permute-start(f32[192,128]{1,0:T(8,128)S(1)} %get-tuple-element.25), channel_id=1, source_target_pairs={{0,1},{1,2},{2,3},{3,4},{4,5},{5,6},{6,7},{7,8},{8,9},{9,10},{10,1... | collective-permute-start | bytes 294920 | tf_op jit(solution)/shard_map/ppermute | solution.py:514
  51.8 0.0 collective-permute-start.10
  51.8 4.6 %collective-permute-done.10.refs_3_ = f32[80,128]{1,0:T(8,128)S(1)} collective-permute-done((f32[80,128]{1,0:T(8,128)S(1)}, f32[80,128]{1,0:T(8,128)S(1)}, u32[]{:S(2)}, u32[]{:S(2)}) %collective-permute-start.10) | collective-permute-done | bytes 40992 | tf_op jit(solution)/shard_map/ppermute | solution.py:515
  56.5 0.0 collective-permute-done.9.refs_2_
  56.5 2.4 %collective-permute-start.11 = (f32[272,128]{1,0:T(8,128)S(1)}, f32[272,128]{1,0:T(8,128)S(1)}, u32[]{:S(2)}, u32[]{:S(2)}) collective-permute-start(f32[272,128]{1,0:T(8,128)S(1)} %pad_maximum_fusion.1), channel_id=1, source_target_pairs={{0,32},{32,0},{64,96},{96,64},{128,160},{160,128},{192,224},{224,1... | collective-permute-start | bytes 417800 | tf_op jit(solution)/shard_map/ppermute | solution.py:516
  58.9 1.0 %collective-permute-done.11.refs_4_ = f32[272,128]{1,0:T(8,128)S(1)} collective-permute-done((f32[272,128]{1,0:T(8,128)S(1)}, f32[272,128]{1,0:T(8,128)S(1)}, u32[]{:S(2)}, u32[]{:S(2)}) %collective-permute-start.11) | collective-permute-done | bytes 139296 | tf_op jit(solution)/shard_map/ppermute | solution.py:516
  59.9 5.4 %shard_map.45 = (f32[4,4,16,256]{3,2,1,0:T(8,128)}, f32[4,4,16,256]{3,2,1,0:T(8,128)}) custom-call(s32[2]{0:T(128)S(1)} %pad_add_fusion.idx.refs_0_, f32[80,128]{1,0:T(8,128)S(1)} %get-tuple-element.24.refs_1_, f32[192,128]{1,0:T(8,128)S(1)} %collective-permute-done.9.refs_2_, f32[80,128]{1,0:T(8,128)S(1)} %collective-permute-done.10.refs_3_, ...), custom_call_target="tpu_custom_call" | custom-call | tf_op jit(solution)/shard_map/pallas_call | solution.py:456
  (3 shorter events, 0.0 us)
Async XLA Ops:
  0.6 12.3 %copy-start = (f32[4,4,16,256]{3,2,1,0:T(8,128)S(1)}, f32[4,4,16,256]{3,2,1,0:T(8,128)}, u32[]{:S(2)}) copy-start(f32[4,4,16,256]{3,2,1,0:T(8,128)} %refs_1_.1) | copy-start | bytes 786436
  0.7 0.8 %copy-start.1 = (f32[4,16,256]{2,1,0:T(8,128)S(1)}, f32[4,16,256]{2,1,0:T(8,128)}, u32[]{:S(2)}) copy-start(f32[4,16,256]{2,1,0:T(8,128)} %refs_2_.1) | copy-start | bytes 196612
  3.1 9.9 %collective-permute-start = (f32[11,16,256]{2,1,0:T(8,128)S(1)}, f32[11,16,256]{2,1,0:T(8,128)S(1)}, u32[]{:S(2)}, u32[]{:S(2)}) collective-permute-start(f32[11,16,256]{2,1,0:T(8,128)S(1)} %get-tuple-element.18), channel_id=1, source_target_pairs={{0,224},{32,64},{64,32},{96,128},{128,96},{160,192},{192,160},{224... | collective-permute-start | bytes 540680 | tf_op jit(solution)/shard_map/ppermute | solution.py:488
  7.6 16.2 %copy-start.2 = (f32[4,16,256]{2,1,0:T(8,128)S(1)}, f32[4,16,256]{2,1,0:T(8,128)}, u32[]{:S(2)}) copy-start(f32[4,16,256]{2,1,0:T(8,128)} %refs_2_.1) | copy-start | bytes 196612
  7.6 5.4 %collective-permute-start.1 = (f32[11,16,256]{2,1,0:T(8,128)S(1)}, f32[11,16,256]{2,1,0:T(8,128)S(1)}, u32[]{:S(2)}, u32[]{:S(2)}) collective-permute-start(f32[11,16,256]{2,1,0:T(8,128)S(1)} %get-tuple-element.19), channel_id=1, source_target_pairs={{0,32},{32,0},{64,96},{96,64},{128,160},{160,128},{192,224},{224,1... | collective-permute-start | bytes 540680 | tf_op jit(solution)/shard_map/ppermute | solution.py:488
  13.6 9.3 %collective-permute-start.2 = (f32[232,256]{1,0:T(8,128)S(1)}, f32[232,256]{1,0:T(8,128)S(1)}, u32[]{:S(2)}, u32[]{:S(2)}) collective-permute-start(f32[232,256]{1,0:T(8,128)S(1)} %get-tuple-element.20), channel_id=1, source_target_pairs={{0,31},{1,2},{2,1},{3,4},{4,3},{5,6},{6,5},{7,8},{8,7},{9,10},{10,... | collective-permute-start | bytes 712712 | tf_op jit(solution)/shard_map/ppermute | solution.py:490
  18.5 5.3 %collective-permute-start.3 = (f32[232,256]{1,0:T(8,128)S(1)}, f32[232,256]{1,0:T(8,128)S(1)}, u32[]{:S(2)}, u32[]{:S(2)}) collective-permute-start(f32[232,256]{1,0:T(8,128)S(1)} %get-tuple-element.21), channel_id=1, source_target_pairs={{0,1},{1,0},{2,3},{3,2},{4,5},{5,4},{6,7},{7,6},{8,9},{9,8},{10,11... | collective-permute-start | bytes 712712 | tf_op jit(solution)/shard_map/ppermute | solution.py:490
  26.5 12.1 %collective-permute-start.5 = (f32[208,256]{1,0:T(8,128)S(1)}, f32[208,256]{1,0:T(8,128)S(1)}, u32[]{:S(2)}, u32[]{:S(2)}) collective-permute-start(f32[208,256]{1,0:T(8,128)S(1)} %get-tuple-element.23), channel_id=1, source_target_pairs={{0,224},{32,64},{64,32},{96,128},{128,96},{160,192},{192,160},{224... | collective-permute-start | bytes 638984 | tf_op jit(solution)/shard_map/ppermute | solution.py:498
  32.5 13.1 %collective-permute-start.7 = (f32[64,256]{1,0:T(8,128)S(1)}, f32[64,256]{1,0:T(8,128)S(1)}, u32[]{:S(2)}, u32[]{:S(2)}) collective-permute-start(f32[64,256]{1,0:T(8,128)S(1)} %get-tuple-element.22.refs_1_), channel_id=1, source_target_pairs={{0,128},{32,160},{64,192},{96,224},{128,0},{160,32},{192,64},{224,... | collective-permute-start | bytes 196616 | tf_op jit(solution)/shard_map/ppermute | solution.py:499
  36.9 8.8 %collective-permute-start.6 = (f32[64,256]{1,0:T(8,128)S(1)}, f32[64,256]{1,0:T(8,128)S(1)}, u32[]{:S(2)}, u32[]{:S(2)}) collective-permute-start(f32[64,256]{1,0:T(8,128)S(1)} %get-tuple-element.22.refs_1_), channel_id=1, source_target_pairs={{0,64},{32,224},{64,128},{96,32},{128,192},{160,96},{192,0},{224,1... | collective-permute-start | bytes 196616 | tf_op jit(solution)/shard_map/ppermute | solution.py:500
  38.6 7.6 %collective-permute-start.4 = (f32[208,256]{1,0:T(8,128)S(1)}, f32[208,256]{1,0:T(8,128)S(1)}, u32[]{:S(2)}, u32[]{:S(2)}) collective-permute-start(f32[208,256]{1,0:T(8,128)S(1)} %get-tuple-element.23), channel_id=1, source_target_pairs={{0,32},{32,0},{64,96},{96,64},{128,160},{160,128},{192,224},{224,1... | collective-permute-start | bytes 638984 | tf_op jit(solution)/shard_map/ppermute | solution.py:501
  45.7 1.6 %collective-permute-start.8 = (f32[192,256]{1,0:T(8,128)S(1)}, f32[192,256]{1,0:T(8,128)S(1)}, u32[]{:S(2)}, u32[]{:S(2)}) collective-permute-start(f32[192,256]{1,0:T(8,128)S(1)} %pad_maximum_fusion), channel_id=1, source_target_pairs={{0,32},{32,0},{64,96},{96,64},{128,160},{160,128},{192,224},{224,1... | collective-permute-start | bytes 589832 | tf_op jit(solution)/shard_map/ppermute | solution.py:502
  48.8 7.6 %collective-permute-start.9 = (f32[192,128]{1,0:T(8,128)S(1)}, f32[192,128]{1,0:T(8,128)S(1)}, u32[]{:S(2)}, u32[]{:S(2)}) collective-permute-start(f32[192,128]{1,0:T(8,128)S(1)} %get-tuple-element.25), channel_id=1, source_target_pairs={{0,1},{1,2},{2,3},{3,4},{4,5},{5,6},{6,7},{7,8},{8,9},{9,10},{10,1... | collective-permute-start | bytes 294920 | tf_op jit(solution)/shard_map/ppermute | solution.py:514
  51.8 4.7 %collective-permute-start.10 = (f32[80,128]{1,0:T(8,128)S(1)}, f32[80,128]{1,0:T(8,128)S(1)}, u32[]{:S(2)}, u32[]{:S(2)}) collective-permute-start(f32[80,128]{1,0:T(8,128)S(1)} %get-tuple-element.24.refs_1_), channel_id=1, source_target_pairs={{0,2},{1,3},{2,4},{3,5},{4,6},{5,7},{6,8},{7,9},{8,10},{9,11},{10,... | collective-permute-start | bytes 122888 | tf_op jit(solution)/shard_map/ppermute | solution.py:515
  56.5 3.4 %collective-permute-start.11 = (f32[272,128]{1,0:T(8,128)S(1)}, f32[272,128]{1,0:T(8,128)S(1)}, u32[]{:S(2)}, u32[]{:S(2)}) collective-permute-start(f32[272,128]{1,0:T(8,128)S(1)} %pad_maximum_fusion.1), channel_id=1, source_target_pairs={{0,32},{32,0},{64,96},{96,64},{128,160},{160,128},{192,224},{224,1... | collective-permute-start | bytes 417800 | tf_op jit(solution)/shard_map/ppermute | solution.py:516

commit v6 on v5

--- a/solution.py
+++ b/solution.py
@@ -110,32 +110,35 @@
     return (at >= 0) & (at < count)
 
 
-def fold_matrix(fine, transpose=False):
-    shape = (fine // 2, fine) if transpose else (fine, fine // 2)
-    a = lax.broadcasted_iota(jnp.int32, shape, 1 if transpose else 0)
-    b = lax.broadcasted_iota(jnp.int32, shape, 0 if transpose else 1)
-    return jnp.where(a // 2 == b, 1.0, 0.0).astype(F32)
-
-
-def exact_dot(a, b):
-    return jnp.dot(a, b, precision=lax.Precision.HIGHEST, preferred_element_type=F32)
+def take(value, at, axis):
+    return jnp.take_along_axis(value, at, axis=axis)
+
+
+def fold(value):
+    a = lax.broadcasted_iota(jnp.int32, (256, 128), 0)
+    b = lax.broadcasted_iota(jnp.int32, (256, 128), 1)
+    pairs = jnp.where(a // 2 == b, 1.0, 0.0).astype(jnp.bfloat16)
+    total = None
+    for _ in range(3):
+        part = value.astype(jnp.bfloat16)
+        term = jnp.dot(part, pairs, preferred_element_type=F32)
+        total = term if total is None else total + term
+        value = value - part.astype(F32)
+    return total
+
+
+def spread(value):
+    lane = lax.broadcasted_iota(jnp.int32, (8, 128), 1)
+    row = lax.broadcasted_iota(jnp.int32, (8, 128), 0)
+    out = []
+    for n in range(2):
+        wide = take(value, lane // 2 + 64 * n, 1)
+        out.append(jnp.concatenate([take(wide, row // 2 + 4 * m, 0) for m in range(2)], 0))
+    return out
 
 
 def pick(condition, a, b):
     return jnp.where(condition, a, b)
-
-
-def pack_first(idx, f, e, cross_o, inner_o, sems):
-    core = idx[0] % 2
-    copies = []
-    for n, (out, side) in enumerate(((cross_o, core), (inner_o, 1 - core))):
-        for c in range(4):
-            copies.append(pltpu.make_async_copy(f.at[c, pl.ds(2 * side, 2)], out.at[pl.ds(2 * c, 2)], sems.at[n, c]))
-        copies.append(pltpu.make_async_copy(e.at[pl.ds(side, 3)], out.at[pl.ds(8, 3)], sems.at[n, 4]))
-    for copy in copies:
-        copy.start()
-    for copy in copies:
-        copy.wait()
 
 
 def halo_first(idx, cross, inner, n):
@@ -234,7 +237,7 @@
             pair[2 * c + m, 0:4, :] = jnp.zeros((4, 256), F32)
             pair[2 * c + m, 28:32, :] = jnp.zeros((4, 256), F32)
         pair[8 + m] = get(ew, (2 * m + 3,), 0, 32) + get(ew, (2 * m + 4,), 0, 32)
-    half[...] = exact_dot(pair[...].reshape(320, 256), fold_matrix(256)) * 0.125
+    half[...] = fold(pair[...].reshape(320, 256)) * 0.125
     coarse = half[pl.ds(0, 160, stride=2), :] + half[pl.ds(1, 160, stride=2), :]
     coarse = coarse.reshape(10, 16, 128)
     for m in range(2):
@@ -329,7 +332,7 @@
 
 
 def up_all(groups, devs, idx, low, by1, by2, swapped, y_i, b_i, e1, w1, x1, ew, wt, fw, own_edge, far_edge, sol_o, res_o,
-           e2, w2, b2, z0, z1, b1, ya, yb, rep, half, va, vb):
+           e2, w2, b2, z0, z1, b1, ya, yb, rep, va, vb):
     g, d = idx[0], idx[1]
     core = g % 2
     zero = jnp.zeros((32, 128), F32)
@@ -418,18 +421,18 @@
         for row in (0, 8):
             sweep_chunk(ya, yb, at, row, 1, 2.0, e1, at, w1, at, b1, at)
 
-    spread = fold_matrix(256, True)
-    wide = exact_dot(ya[:, 2:8].reshape(384, 128), spread)
-    for n in range(2):
-        for parity in range(2):
-            half[n, pl.ds(parity, 384, stride=2), :] = wide[:, 128 * n : 128 * n + 128]
     low_x, high_x = jnp.where(g > 0, 1.0, 0.0), jnp.where(g < groups - 1, 1.0, 0.0)
     for c in range(4):
-        for layer in range(1, 11):
-            for n in range(2):
-                at = (6 * c + layer // 2) * 32
-                rows = half[n, at : at + 32, :]
-                va[c, layer, n] = rows + x1[c, layer - 2, n] if 3 <= layer <= 8 else rows
+        for m in range(6):
+            for k in range(2):
+                both = spread(ya[c, 2 + m, 8 * k : 8 * k + 8, :])
+                rows = slice(16 * k, 16 * k + 16)
+                for layer in (2 * m, 2 * m + 1):
+                    for n in range(2):
+                        if 3 <= layer <= 8:
+                            va[c, layer, n, rows, :] = both[n] + x1[c, layer - 2, n, rows, :]
+                        elif 1 <= layer <= 10:
+                            va[c, layer, n, rows, :] = both[n]
         for j in range(2):
             at = 64 + 18 * (2 * c + j)
             own, far = own_edge[at : at + 18, :], far_edge[at : at + 18, :]
@@ -477,14 +480,11 @@
         to = [(g, (d - step if g % 2 else d + step) % devs) for g in range(groups) for d in range(devs)]
         return [(i, g * devs + d) for i, (g, d) in enumerate(to)]
 
-    cross, inner = pl.pallas_call(
-        pack_first,
-        out_shape=[jax.ShapeDtypeStruct((11, 16, 256), F32)] * 2,
-        in_specs=[pl.BlockSpec(memory_space=pltpu.SMEM), pl.BlockSpec(memory_space=pl.ANY), pl.BlockSpec(memory_space=pl.ANY)],
-        out_specs=[pl.BlockSpec(memory_space=pltpu.VMEM)] * 2,
-        scratch_shapes=[pltpu.SemaphoreType.DMA((2, 5))],
-        compiler_params=pltpu.CompilerParams(vmem_limit_bytes=int(53.5 * 1024 * 1024)),
-    )(idx, forcing, viscosity)
+    f_first, f_last, visc = lax.optimization_barrier((forcing[:, 0:2], forcing[:, 2:4], viscosity))
+    first = jnp.concatenate([f_first.reshape(8, 16, 256), visc[0:3]], axis=0)
+    last = jnp.concatenate([f_last.reshape(8, 16, 256), visc[1:4]], axis=0)
+    cross, inner = pick(idx[0] % 2 == 0, first, last), pick(idx[0] % 2 == 0, last, first)
+    cross, inner = lax.optimization_barrier((cross, inner))
     cross, inner = lax.ppermute(cross, "grp", beside), lax.ppermute(inner, "grp", swap)
     to_even, to_odd = call(pack_second, [(SECOND_ROWS, 256)] * 2, [], idx, forcing, viscosity, cross, inner)
     from_odd, from_even = lax.ppermute(to_odd, "dev", odd), lax.ppermute(to_even, "dev", even)
@@ -519,7 +519,7 @@
         lambda *refs: up_all(groups, devs, *refs),
         [(4, 4, 16, 256), (4, 4, 16, 256)],
         [(deep, 32, 128), (deep, 32, 128), (4, deep, 32, 128), (4, deep, 32, 128), (4, deep, 32, 128),
-         (4, 10, 16, 128), (4, 10, 16, 128), (4, 10, 16, 128), (4, 5, 16, 128), (2, 768, 128),
+         (4, 10, 16, 128), (4, 10, 16, 128), (4, 10, 16, 128), (4, 5, 16, 128),
          (4, 12, 2, 32, 128), (4, 12, 2, 32, 128)],
         idx, low, by1, by2, swapped, y_w, b_w, e_w, w_w, x1, ew, wt, fw, partner, xco,
     ))

time: 65.4 us -> 63.5 us (0.971)
  Pallas kernels: 11.8 us -> 9.75 us
    pallas_call x1 -> x0, Pallas kernels: 1.52 us -> none  [local(): pl.pallas_call(pack_first, out_shape=[jax.ShapeDtypeStruct((11, 16, 256),...]
    slice x0 -> x2, local copies, waits for them, and re-layouts: none -> 1.03 us  [the longest x1 1.03 us: local(): forcing[:, 2:4]]
    unnamed x6 -> x4, local copies, waits for them, and re-layouts: 0.85 us -> 0.01 us
where the time goes in v6:
time: 63.5 us; the launch traced here: 63.4 us
  starting transfers between devices  30.2 us (48%)
  waiting for transfers between devices  21.5 us (34%)
  Pallas kernels  9.75 us (15%)
  local copies, waits for them, and re-layouts  1.05 us (2%)
  between operations  0.73 us (1%)
    pallas_call x4, Pallas kernels, call(): pl.pallas_call(kernel, out_shape=[jax.ShapeDtypeStruct(shape, F32) for sh...  9.75 us
    ppermute x1, waiting for transfers between devices, local(): c2 = lax.ppermute(mid, 'grp', far_chip)  7.07 us
    ppermute x1, starting transfers between devices, local(): xco = lax.ppermute(pay, 'grp', beside)  6.08 us
    ppermute x1, starting transfers between devices, local(): lax.ppermute(to_odd, 'dev', odd)  4.88 us
    ppermute x1, waiting for transfers between devices, local(): by2 = lax.ppermute(low, ('grp', 'dev'), along(2))  4.61 us
    ppermute x1, starting transfers between devices, local(): lax.ppermute(cross, 'grp', beside)  4.47 us
    ppermute x1, waiting for transfers between devices, local(): lax.ppermute(to_odd, 'dev', odd)  4.38 us
    ppermute x1, starting transfers between devices, local(): c2 = lax.ppermute(mid, 'grp', far_chip)  4.32 us
  transfers between devices with their start and end apart: 12, of which 7 were waited for; matrix products, arithmetic and copies ran while one was open for 0% of the time, Pallas kernels for 0%

profile of v6, /device:TPU:1, one launch (start us, length us, event | category | flops | bytes accessed | tf_op | source)
XLA Modules:
  0.0 63.4 jit_solution(7658399972757416209)
XLA Ops:
  0.6 0.0 copy-start.1
  0.7 1.0 %fusion.2 = (f32[4,2,16,256]{3,2,1,0:T(8,128)S(1)}, f32[4,2,16,256]{3,2,1,0:T(8,128)S(1)}) fusion(f32[4,4,16,256]{3,2,1,0:T(8,128)} %refs_1_.1), kind=kLoop, calls=%fused_computation.7 | loop fusion | bytes 524288 | tf_op jit(solution)/shard_map/slice | solution.py:483
  1.7 0.0 copy-done.1
  1.7 0.0 copy-start
  1.8 4.5 %collective-permute-start = (f32[11,16,256]{2,1,0:T(8,128)S(1)}, f32[11,16,256]{2,1,0:T(8,128)S(1)}, u32[]{:S(2)}, u32[]{:S(2)}) collective-permute-start(f32[11,16,256]{2,1,0:T(8,128)S(1)} %get-tuple-element.24), channel_id=1, source_target_pairs={{0,224},{32,64},{64,32},{96,128},{128,96},{160,192},{192,160},{224... | collective-permute-start | bytes 540680 | tf_op jit(solution)/shard_map/ppermute | solution.py:488
  6.2 2.9 %collective-permute-start.1 = (f32[11,16,256]{2,1,0:T(8,128)S(1)}, f32[11,16,256]{2,1,0:T(8,128)S(1)}, u32[]{:S(2)}, u32[]{:S(2)}) collective-permute-start(f32[11,16,256]{2,1,0:T(8,128)S(1)} %get-tuple-element.25), channel_id=1, source_target_pairs={{0,32},{32,0},{64,96},{96,64},{128,160},{160,128},{192,224},{224,1... | collective-permute-start | bytes 540680 | tf_op jit(solution)/shard_map/ppermute | solution.py:488
  9.1 0.1 pad_add_fusion.idx.refs_0_
  9.2 2.5 %collective-permute-done.cross.refs_3_ = f32[11,16,256]{2,1,0:T(8,128)S(1)} collective-permute-done((f32[11,16,256]{2,1,0:T(8,128)S(1)}, f32[11,16,256]{2,1,0:T(8,128)S(1)}, u32[]{:S(2)}, u32[]{:S(2)}) %collective-permute-start) | collective-permute-done | bytes 180256 | tf_op jit(solution)/shard_map/ppermute | solution.py:488
  11.6 0.0 collective-permute-done.1.inner.refs_4_
  11.6 0.0 copy-done
  11.6 0.6 %shard_map.41 = (f32[232,256]{1,0:T(8,128)S(1)}, f32[232,256]{1,0:T(8,128)S(1)}) custom-call(s32[2]{0:T(128)S(1)} %pad_add_fusion.idx.refs_0_, f32[4,4,16,256]{3,2,1,0:T(8,128)S(1)} %copy-done, f32[4,16,256]{2,1,0:T(8,128)S(1)} %copy-done.1, f32[11,16,256]{2,1,0:T(8,128)S(1)} %collective-permute-done.cross.refs_3_, ...), custom_call_target="tpu_custom_call" | custom-call | tf_op jit(solution)/shard_map/pallas_call | solution.py:459
  12.3 4.9 %collective-permute-start.2 = (f32[232,256]{1,0:T(8,128)S(1)}, f32[232,256]{1,0:T(8,128)S(1)}, u32[]{:S(2)}, u32[]{:S(2)}) collective-permute-start(f32[232,256]{1,0:T(8,128)S(1)} %get-tuple-element.26), channel_id=1, source_target_pairs={{0,31},{1,2},{2,1},{3,4},{4,3},{5,6},{6,5},{7,8},{8,7},{9,10},{10,... | collective-permute-start | bytes 712712 | tf_op jit(solution)/shard_map/ppermute | solution.py:490
  17.2 0.0 collective-permute-start.3
  17.2 4.4 %collective-permute-done.2.refs_5_ = f32[232,256]{1,0:T(8,128)S(1)} collective-permute-done((f32[232,256]{1,0:T(8,128)S(1)}, f32[232,256]{1,0:T(8,128)S(1)}, u32[]{:S(2)}, u32[]{:S(2)}) %collective-permute-start.2) | collective-permute-done | bytes 237600 | tf_op jit(solution)/shard_map/ppermute | solution.py:490
  21.6 0.9 %collective-permute-done.3.refs_6_ = f32[232,256]{1,0:T(8,128)S(1)} collective-permute-done((f32[232,256]{1,0:T(8,128)S(1)}, f32[232,256]{1,0:T(8,128)S(1)}, u32[]{:S(2)}, u32[]{:S(2)}) %collective-permute-start.3) | collective-permute-done | bytes 237600 | tf_op jit(solution)/shard_map/ppermute | solution.py:490
  22.4 2.5 %shard_map.42 = (f32[64,256]{1,0:T(8,128)S(1)}, f32[208,256]{1,0:T(8,128)S(1)}, f32[4,8,2,32,128]{4,3,2,1,0:T(8,128)S(1)}, f32[10,2,32,128]{3,2,1,0:T(8,128)S(1)...) custom-call(s32[2]{0:T(128)S(1)} %pad_add_fusion.idx.refs_0_, f32[4,4,16,256]{3,2,1,0:T(8,128)S(1)} %copy-done, ...), custom_call_target="tpu_custom_call" | custom-call | tf_op jit(solution)/shard_map/pallas_call | solution.py:459
  24.9 6.1 %collective-permute-start.5 = (f32[208,256]{1,0:T(8,128)S(1)}, f32[208,256]{1,0:T(8,128)S(1)}, u32[]{:S(2)}, u32[]{:S(2)}) collective-permute-start(f32[208,256]{1,0:T(8,128)S(1)} %get-tuple-element.29), channel_id=1, source_target_pairs={{0,224},{32,64},{64,32},{96,128},{128,96},{160,192},{192,160},{224... | collective-permute-start | bytes 638984 | tf_op jit(solution)/shard_map/ppermute | solution.py:498
  31.0 4.3 %collective-permute-start.7 = (f32[64,256]{1,0:T(8,128)S(1)}, f32[64,256]{1,0:T(8,128)S(1)}, u32[]{:S(2)}, u32[]{:S(2)}) collective-permute-start(f32[64,256]{1,0:T(8,128)S(1)} %get-tuple-element.28.refs_1_), channel_id=1, source_target_pairs={{0,128},{32,160},{64,192},{96,224},{128,0},{160,32},{192,64},{224,... | collective-permute-start | bytes 196616 | tf_op jit(solution)/shard_map/ppermute | solution.py:499
  35.3 1.7 %collective-permute-start.6 = (f32[64,256]{1,0:T(8,128)S(1)}, f32[64,256]{1,0:T(8,128)S(1)}, u32[]{:S(2)}, u32[]{:S(2)}) collective-permute-start(f32[64,256]{1,0:T(8,128)S(1)} %get-tuple-element.28.refs_1_), channel_id=1, source_target_pairs={{0,64},{32,224},{64,128},{96,32},{128,192},{160,96},{192,0},{224,1... | collective-permute-start | bytes 196616 | tf_op jit(solution)/shard_map/ppermute | solution.py:500
  37.0 0.0 collective-permute-start.4
  37.0 0.0 collective-permute-done.5.refs_3_.refs_14_
  37.0 7.1 %collective-permute-done.7.refs_5_ = f32[64,256]{1,0:T(8,128)S(1)} collective-permute-done((f32[64,256]{1,0:T(8,128)S(1)}, f32[64,256]{1,0:T(8,128)S(1)}, u32[]{:S(2)}, u32[]{:S(2)}) %collective-permute-start.7) | collective-permute-done | bytes 65568 | tf_op jit(solution)/shard_map/ppermute | solution.py:499
  44.1 0.0 collective-permute-done.6.refs_4_
  44.1 0.5 collective-permute-start.8
  44.6 0.0 collective-permute-done.4.refs_2_.refs_13_
  44.6 1.1 %collective-permute-done.8.refs_6_ = f32[192,256]{1,0:T(8,128)S(1)} collective-permute-done((f32[192,256]{1,0:T(8,128)S(1)}, f32[192,256]{1,0:T(8,128)S(1)}, u32[]{:S(2)}, u32[]{:S(2)}) %collective-permute-start.8) | collective-permute-done | bytes 196640 | tf_op jit(solution)/shard_map/ppermute | solution.py:502
  45.7 1.6 %shard_map.43 = (f32[192,128]{1,0:T(8,128)S(1)}, f32[80,128]{1,0:T(8,128)S(1)}, f32[4,10,16,128]{3,2,1,0:T(8,128)S(1)}, f32[4,10,16,128]{3,2,1,0:T(8,128)S(1)}, ...) custom-call(s32[2]{0:T(128)S(1)} %pad_add_fusion.idx.refs_0_, f32[64,256]{1,0:T(8,128)S(1)} %get-tuple-element.28.refs_1_, ...), custom_call_target="tpu_custom_call" | custom-call | tf_op jit(solution)/shard_map/pallas_call | solution.py:459
  47.3 3.0 %collective-permute-start.9 = (f32[192,128]{1,0:T(8,128)S(1)}, f32[192,128]{1,0:T(8,128)S(1)}, u32[]{:S(2)}, u32[]{:S(2)}) collective-permute-start(f32[192,128]{1,0:T(8,128)S(1)} %get-tuple-element.31), channel_id=1, source_target_pairs={{0,1},{1,2},{2,3},{3,4},{4,5},{5,6},{6,7},{7,8},{8,9},{9,10},{10,1... | collective-permute-start | bytes 294920 | tf_op jit(solution)/shard_map/ppermute | solution.py:514
  50.2 0.0 collective-permute-start.10
  50.3 4.6 %collective-permute-done.10.refs_3_ = f32[80,128]{1,0:T(8,128)S(1)} collective-permute-done((f32[80,128]{1,0:T(8,128)S(1)}, f32[80,128]{1,0:T(8,128)S(1)}, u32[]{:S(2)}, u32[]{:S(2)}) %collective-permute-start.10) | collective-permute-done | bytes 40992 | tf_op jit(solution)/shard_map/ppermute | solution.py:515
  54.9 0.0 collective-permute-done.9.refs_2_
  54.9 2.4 %collective-permute-start.11 = (f32[272,128]{1,0:T(8,128)S(1)}, f32[272,128]{1,0:T(8,128)S(1)}, u32[]{:S(2)}, u32[]{:S(2)}) collective-permute-start(f32[272,128]{1,0:T(8,128)S(1)} %pad_maximum_fusion.3), channel_id=1, source_target_pairs={{0,32},{32,0},{64,96},{96,64},{128,160},{160,128},{192,224},{224,1... | collective-permute-start | bytes 417800 | tf_op jit(solution)/shard_map/ppermute | solution.py:516
  57.3 1.0 %collective-permute-done.11.refs_4_ = f32[272,128]{1,0:T(8,128)S(1)} collective-permute-done((f32[272,128]{1,0:T(8,128)S(1)}, f32[272,128]{1,0:T(8,128)S(1)}, u32[]{:S(2)}, u32[]{:S(2)}) %collective-permute-start.11) | collective-permute-done | bytes 139296 | tf_op jit(solution)/shard_map/ppermute | solution.py:516
  58.3 5.1 %shard_map.44 = (f32[4,4,16,256]{3,2,1,0:T(8,128)}, f32[4,4,16,256]{3,2,1,0:T(8,128)}) custom-call(s32[2]{0:T(128)S(1)} %pad_add_fusion.idx.refs_0_, f32[80,128]{1,0:T(8,128)S(1)} %get-tuple-element.30.refs_1_, f32[192,128]{1,0:T(8,128)S(1)} %collective-permute-done.9.refs_2_, f32[80,128]{1,0:T(8,128)S(1)} %collective-permute-done.10.refs_3_, ...), custom_call_target="tpu_custom_call" | custom-call | tf_op jit(solution)/shard_map/pallas_call | solution.py:459
  (5 shorter events, 0.1 us)
Async XLA Ops:
  0.6 1.0 %copy-start.1 = (f32[4,16,256]{2,1,0:T(8,128)S(1)}, f32[4,16,256]{2,1,0:T(8,128)}, u32[]{:S(2)}) copy-start(f32[4,16,256]{2,1,0:T(8,128)} %refs_2_.1) | copy-start | bytes 196612
  1.7 9.9 %copy-start = (f32[4,4,16,256]{3,2,1,0:T(8,128)S(1)}, f32[4,4,16,256]{3,2,1,0:T(8,128)}, u32[]{:S(2)}) copy-start(f32[4,4,16,256]{3,2,1,0:T(8,128)} %refs_1_.1) | copy-start | bytes 786436
  1.8 9.9 %collective-permute-start = (f32[11,16,256]{2,1,0:T(8,128)S(1)}, f32[11,16,256]{2,1,0:T(8,128)S(1)}, u32[]{:S(2)}, u32[]{:S(2)}) collective-permute-start(f32[11,16,256]{2,1,0:T(8,128)S(1)} %get-tuple-element.24), channel_id=1, source_target_pairs={{0,224},{32,64},{64,32},{96,128},{128,96},{160,192},{192,160},{224... | collective-permute-start | bytes 540680 | tf_op jit(solution)/shard_map/ppermute | solution.py:488
  6.2 5.4 %collective-permute-start.1 = (f32[11,16,256]{2,1,0:T(8,128)S(1)}, f32[11,16,256]{2,1,0:T(8,128)S(1)}, u32[]{:S(2)}, u32[]{:S(2)}) collective-permute-start(f32[11,16,256]{2,1,0:T(8,128)S(1)} %get-tuple-element.25), channel_id=1, source_target_pairs={{0,32},{32,0},{64,96},{96,64},{128,160},{160,128},{192,224},{224,1... | collective-permute-start | bytes 540680 | tf_op jit(solution)/shard_map/ppermute | solution.py:488
  12.3 9.3 %collective-permute-start.2 = (f32[232,256]{1,0:T(8,128)S(1)}, f32[232,256]{1,0:T(8,128)S(1)}, u32[]{:S(2)}, u32[]{:S(2)}) collective-permute-start(f32[232,256]{1,0:T(8,128)S(1)} %get-tuple-element.26), channel_id=1, source_target_pairs={{0,31},{1,2},{2,1},{3,4},{4,3},{5,6},{6,5},{7,8},{8,7},{9,10},{10,... | collective-permute-start | bytes 712712 | tf_op jit(solution)/shard_map/ppermute | solution.py:490
  17.2 5.3 %collective-permute-start.3 = (f32[232,256]{1,0:T(8,128)S(1)}, f32[232,256]{1,0:T(8,128)S(1)}, u32[]{:S(2)}, u32[]{:S(2)}) collective-permute-start(f32[232,256]{1,0:T(8,128)S(1)} %get-tuple-element.27), channel_id=1, source_target_pairs={{0,1},{1,0},{2,3},{3,2},{4,5},{5,4},{6,7},{7,6},{8,9},{9,8},{10,11... | collective-permute-start | bytes 712712 | tf_op jit(solution)/shard_map/ppermute | solution.py:490
  24.9 12.1 %collective-permute-start.5 = (f32[208,256]{1,0:T(8,128)S(1)}, f32[208,256]{1,0:T(8,128)S(1)}, u32[]{:S(2)}, u32[]{:S(2)}) collective-permute-start(f32[208,256]{1,0:T(8,128)S(1)} %get-tuple-element.29), channel_id=1, source_target_pairs={{0,224},{32,64},{64,32},{96,128},{128,96},{160,192},{192,160},{224... | collective-permute-start | bytes 638984 | tf_op jit(solution)/shard_map/ppermute | solution.py:498
  31.0 13.1 %collective-permute-start.7 = (f32[64,256]{1,0:T(8,128)S(1)}, f32[64,256]{1,0:T(8,128)S(1)}, u32[]{:S(2)}, u32[]{:S(2)}) collective-permute-start(f32[64,256]{1,0:T(8,128)S(1)} %get-tuple-element.28.refs_1_), channel_id=1, source_target_pairs={{0,128},{32,160},{64,192},{96,224},{128,0},{160,32},{192,64},{224,... | collective-permute-start | bytes 196616 | tf_op jit(solution)/shard_map/ppermute | solution.py:499
  35.3 8.8 %collective-permute-start.6 = (f32[64,256]{1,0:T(8,128)S(1)}, f32[64,256]{1,0:T(8,128)S(1)}, u32[]{:S(2)}, u32[]{:S(2)}) collective-permute-start(f32[64,256]{1,0:T(8,128)S(1)} %get-tuple-element.28.refs_1_), channel_id=1, source_target_pairs={{0,64},{32,224},{64,128},{96,32},{128,192},{160,96},{192,0},{224,1... | collective-permute-start | bytes 196616 | tf_op jit(solution)/shard_map/ppermute | solution.py:500
  37.0 7.6 %collective-permute-start.4 = (f32[208,256]{1,0:T(8,128)S(1)}, f32[208,256]{1,0:T(8,128)S(1)}, u32[]{:S(2)}, u32[]{:S(2)}) collective-permute-start(f32[208,256]{1,0:T(8,128)S(1)} %get-tuple-element.29), channel_id=1, source_target_pairs={{0,32},{32,0},{64,96},{96,64},{128,160},{160,128},{192,224},{224,1... | collective-permute-start | bytes 638984 | tf_op jit(solution)/shard_map/ppermute | solution.py:501
  44.1 1.6 %collective-permute-start.8 = (f32[192,256]{1,0:T(8,128)S(1)}, f32[192,256]{1,0:T(8,128)S(1)}, u32[]{:S(2)}, u32[]{:S(2)}) collective-permute-start(f32[192,256]{1,0:T(8,128)S(1)} %pad_maximum_fusion), channel_id=1, source_target_pairs={{0,32},{32,0},{64,96},{96,64},{128,160},{160,128},{192,224},{224,1... | collective-permute-start | bytes 589832 | tf_op jit(solution)/shard_map/ppermute | solution.py:502
  47.3 7.6 %collective-permute-start.9 = (f32[192,128]{1,0:T(8,128)S(1)}, f32[192,128]{1,0:T(8,128)S(1)}, u32[]{:S(2)}, u32[]{:S(2)}) collective-permute-start(f32[192,128]{1,0:T(8,128)S(1)} %get-tuple-element.31), channel_id=1, source_target_pairs={{0,1},{1,2},{2,3},{3,4},{4,5},{5,6},{6,7},{7,8},{8,9},{9,10},{10,1... | collective-permute-start | bytes 294920 | tf_op jit(solution)/shard_map/ppermute | solution.py:514
  50.2 4.7 %collective-permute-start.10 = (f32[80,128]{1,0:T(8,128)S(1)}, f32[80,128]{1,0:T(8,128)S(1)}, u32[]{:S(2)}, u32[]{:S(2)}) collective-permute-start(f32[80,128]{1,0:T(8,128)S(1)} %get-tuple-element.30.refs_1_), channel_id=1, source_target_pairs={{0,2},{1,3},{2,4},{3,5},{4,6},{5,7},{6,8},{7,9},{8,10},{9,11},{10,... | collective-permute-start | bytes 122888 | tf_op jit(solution)/shard_map/ppermute | solution.py:515
  54.9 3.4 %collective-permute-start.11 = (f32[272,128]{1,0:T(8,128)S(1)}, f32[272,128]{1,0:T(8,128)S(1)}, u32[]{:S(2)}, u32[]{:S(2)}) collective-permute-start(f32[272,128]{1,0:T(8,128)S(1)} %pad_maximum_fusion.3), channel_id=1, source_target_pairs={{0,32},{32,0},{64,96},{96,64},{128,160},{160,128},{192,224},{224,1... | collective-permute-start | bytes 417800 | tf_op jit(solution)/shard_map/ppermute | solution.py:516

commit v7 on v6

--- a/solution.py
+++ b/solution.py
@@ -73,16 +73,20 @@
     return here, flux, grad, div
 
 
+def times(spacing, value):
+    return value if spacing == 1.0 else spacing * value
+
+
 def sweep_chunk(out, field, layer, row, step, spacing, visc, visc_layer, weight, weight_layer, source, source_layer):
     e_here, sums, _ = sums_of(visc, visc_layer, row, step)
     here, flux, grad, div = stencil(field, layer, row, step, sums)
     w = get(weight, (weight_layer,), row)
     for c in range(3):
         b = get(source, (c, source_layer), row)
-        value = (1.0 - OMEGA) * here[c] + w * (b + (0.5 / (spacing * spacing)) * flux[c] - (0.5 / spacing) * grad[c])
+        value = (1.0 - OMEGA) * here[c] + w * (b + flux[c] - times(spacing, grad[c]))
         put(out, (c, layer), row, value)
     b = get(source, (3, source_layer), row)
-    put(out, (3, layer), row, here[3] + (BETA * e_here) * (b - (0.5 / spacing) * div))
+    put(out, (3, layer), row, here[3] + (BETA * 0.5 / (spacing * spacing) * e_here) * (b - times(spacing, div)))
 
 
 def residual_chunk(field, layer, row, step, spacing, visc, visc_layer, source, source_layer):
@@ -91,17 +95,17 @@
     out = []
     for c in range(3):
         b = get(source, (c, source_layer), row)
-        out.append(b - ((0.5 / (spacing * spacing)) * (total * here[c] - flux[c]) + (0.5 / spacing) * grad[c]))
-    out.append(get(source, (3, source_layer), row) - (0.5 / spacing) * div)
+        out.append(b - (total * here[c] - flux[c] + times(spacing, grad[c])))
+    out.append(get(source, (3, source_layer), row) - times(spacing, div))
     return out
 
 
 def start_chunk(out, layer, row, step, spacing, visc, visc_layer, weight, weight_layer, source, source_layer, inside):
     e_here, _, total = sums_of(visc, visc_layer, row, step)
-    w = jnp.where(inside, (2.0 * OMEGA * spacing * spacing) / total, 0.0)
+    w = jnp.where(inside, OMEGA / total, 0.0)
     put(weight, (weight_layer,), row, w)
     for c in range(4):
-        scale = w if c < 3 else BETA * e_here
+        scale = w if c < 3 else BETA * 0.5 / (spacing * spacing) * e_here
         put(out, (c, layer), row, scale * get(source, (c, source_layer), row))
 
 
@@ -216,16 +220,16 @@
             at = F_AT[layer] + F_ROWS[layer] * c
             before, after = halo_second(slice(at, at + F_ROWS[layer]))
             zero = jnp.zeros((8 - F_ROWS[layer], 256), F32)
-            put(fw, (c, layer), 0, jnp.concatenate([zero, before], 0))
-            put(fw, (c, layer), 8, own)
-            put(fw, (c, layer), 24, jnp.concatenate([after, zero], 0))
+            put(fw, (c, layer), 0, jnp.concatenate([zero, 2.0 * before], 0))
+            put(fw, (c, layer), 8, 2.0 * own)
+            put(fw, (c, layer), 24, jnp.concatenate([2.0 * after, zero], 0))
     for layer in range(8):
         layer_in = (4 * g - 2 + layer >= 0) & (4 * g - 2 + layer < 4 * groups)
-        for row in (0, 8, 16, 24):
+        for row in (0, 8, 16, 24) if 0 < layer < 7 else (4, 12, 20):
             inside = rows_inside(row, 16 * d - 8, 16 * devs, 256) & layer_in
             start_chunk(x0, layer, row, 1, 1.0, ew, layer + 1, wt, layer, fw, layer, inside)
     for layer in range(1, 7):
-        for row in (0, 8, 16, 24):
+        for row in (0, 8, 16, 24) if 1 < layer < 6 else (4, 12, 20):
             sweep_chunk(x1, x0, layer, row, 1, 1.0, ew, layer + 1, wt, layer, fw, layer)
     for m in range(2):
         for row in (4, 12, 20):
@@ -237,14 +241,14 @@
             pair[2 * c + m, 0:4, :] = jnp.zeros((4, 256), F32)
             pair[2 * c + m, 28:32, :] = jnp.zeros((4, 256), F32)
         pair[8 + m] = get(ew, (2 * m + 3,), 0, 32) + get(ew, (2 * m + 4,), 0, 32)
-    half[...] = fold(pair[...].reshape(320, 256)) * 0.125
+    half[...] = fold(pair[...].reshape(320, 256))
     coarse = half[pl.ds(0, 160, stride=2), :] + half[pl.ds(1, 160, stride=2), :]
     coarse = coarse.reshape(10, 16, 128)
     for m in range(2):
         lanes = slice(128 * m, 128 * m + 128)
         for c in range(4):
-            mid_o[12 * c : 12 * c + 12, lanes] = pay_o[12 * c : 12 * c + 12, lanes] = coarse[2 * c + m, 2:14, :]
-        mid_o[48:64, lanes] = pay_o[48:64, lanes] = coarse[8 + m]
+            mid_o[12 * c : 12 * c + 12, lanes] = pay_o[12 * c : 12 * c + 12, lanes] = coarse[2 * c + m, 2:14, :] * 0.5
+        mid_o[48:64, lanes] = pay_o[48:64, lanes] = coarse[8 + m] * 0.125
     for c in range(4):
         for j in range(2):
             at = 64 + 18 * (2 * c + j)
@@ -307,7 +311,7 @@
         for c in range(5):
             rows = pair[m, c, pl.ds(0, 4, stride=2), :] + pair[m, c, pl.ds(1, 4, stride=2), :]
             mate = jnp.where(lane % 2 == 0, pltpu.roll(rows, 127, 1), pltpu.roll(rows, 1, 1))
-            low[c, m, 0:4, :] = (rows + mate) * 0.125
+            low[c, m, 0:4, :] = (rows + mate) * (0.5 if c < 4 else 0.125)
     for c in range(5):
         for q in range(groups // 2):
             packed = jnp.where(lane % 2 == 0, low[c, 2 * q, 0:4, :], low[c, 2 * q + 1, 0:4, :])
@@ -382,9 +386,9 @@
             inside = rows_inside(row, 4 * d - 10, 4 * devs, 128)
             start_chunk(z0, i, row, 2, 4.0, e2, i, w2, i, b2, i, inside)
     here, other = z0, z1
-    for _ in range(COARSE - 1):
+    for k in range(COARSE - 1):
         for i in range(2, groups + 2):
-            for row in (4, 12):
+            for row in (4, 12) if k < COARSE - 2 else (8,):
                 sweep_chunk(other, here, i, row, 2, 4.0, e2, i, w2, i, b2, i)
         here, other = other, here
     z = here
@@ -415,10 +419,10 @@
         for j in range(10):
             ya[c, j] = ya[c, j] + rep[c, j // 2]
     for at in range(1, 9):
-        for row in (0, 8):
+        for row in (0, 8) if 1 < at < 8 else (4,):
             sweep_chunk(yb, ya, at, row, 1, 2.0, e1, at, w1, at, b1, at)
     for at in range(2, 8):
-        for row in (0, 8):
+        for row in (0, 8) if 2 < at < 7 else (4,):
             sweep_chunk(ya, yb, at, row, 1, 2.0, e1, at, w1, at, b1, at)
 
     low_x, high_x = jnp.where(g > 0, 1.0, 0.0), jnp.where(g < groups - 1, 1.0, 0.0)
@@ -441,17 +445,17 @@
             put(va, (c, 1 + j), 7, get(va, (c, 1 + j), 7, 18) + before)
             put(va, (c, 9 + j), 7, get(va, (c, 9 + j), 7, 18) + after)
     for at in range(2, 10):
-        for row in (4, 12, 20):
+        for row in (4, 12, 20) if 2 < at < 9 else (8, 16):
             sweep_chunk(vb, va, at, row, 1, 1.0, ew, at - 1, wt, at - 2, fw, at - 2)
     for at in range(3, 9):
-        for row in (4, 12, 20):
+        for row in (4, 12, 20) if 3 < at < 8 else (8, 16):
             sweep_chunk(va, vb, at, row, 1, 1.0, ew, at - 1, wt, at - 2, fw, at - 2)
     for i in range(4):
         for row in (8, 16):
             out = residual_chunk(va, i + 4, row, 1, 1.0, ew, i + 3, fw, i + 2)
             for c in range(4):
                 sol_o[c, i, row - 8 : row, :] = get(va, (c, i + 4), row)
-                res_o[c, i, row - 8 : row, :] = out[c]
+                res_o[c, i, row - 8 : row, :] = 0.5 * out[c]
 
 
 def call(kernel, outs, scratch, *args):

time: 63.5 us -> 62.8 us (0.989)
  Pallas kernels: 9.75 us -> 9.08 us
    pallas_call x4, Pallas kernels: 9.75 us -> 9.08 us  [call(): pl.pallas_call(kernel, out_shape=[jax.ShapeDtypeStruct(shape, F32) for sh...]
where the time goes in v7:
time: 62.8 us; the launch traced here: 62.7 us
  starting transfers between devices  30.2 us (48%)
  waiting for transfers between devices  21.5 us (34%)
  Pallas kernels  9.08 us (14%)
  local copies, waits for them, and re-layouts  1.05 us (2%)
  between operations  0.73 us (1%)
    pallas_call x4, Pallas kernels, call(): pl.pallas_call(kernel, out_shape=[jax.ShapeDtypeStruct(shape, F32) for sh...  9.08 us
    ppermute x1, waiting for transfers between devices, local(): c2 = lax.ppermute(mid, 'grp', far_chip)  7.07 us
    ppermute x1, starting transfers between devices, local(): xco = lax.ppermute(pay, 'grp', beside)  6.08 us
    ppermute x1, starting transfers between devices, local(): lax.ppermute(to_odd, 'dev', odd)  4.88 us
    ppermute x1, waiting for transfers between devices, local(): by2 = lax.ppermute(low, ('grp', 'dev'), along(2))  4.61 us
    ppermute x1, starting transfers between devices, local(): lax.ppermute(cross, 'grp', beside)  4.47 us
    ppermute x1, waiting for transfers between devices, local(): lax.ppermute(to_odd, 'dev', odd)  4.38 us
    ppermute x1, starting transfers between devices, local(): c2 = lax.ppermute(mid, 'grp', far_chip)  4.32 us
  transfers between devices with their start and end apart: 12, of which 7 were waited for; matrix products, arithmetic and copies ran while one was open for 0% of the time, Pallas kernels for 0%

profile of v7, /device:TPU:1, one launch (start us, length us, event | category | flops | bytes accessed | tf_op | source)
XLA Modules:
  0.0 62.7 jit_solution(5031258271801182696)
XLA Ops:
  0.6 0.0 copy-start.1
  0.7 1.0 %fusion.2 = (f32[4,2,16,256]{3,2,1,0:T(8,128)S(1)}, f32[4,2,16,256]{3,2,1,0:T(8,128)S(1)}) fusion(f32[4,4,16,256]{3,2,1,0:T(8,128)} %refs_1_.1), kind=kLoop, calls=%fused_computation.7 | loop fusion | bytes 524288 | tf_op jit(solution)/shard_map/slice | solution.py:487
  1.7 0.0 copy-done.1
  1.7 0.0 copy-start
  1.8 4.5 %collective-permute-start = (f32[11,16,256]{2,1,0:T(8,128)S(1)}, f32[11,16,256]{2,1,0:T(8,128)S(1)}, u32[]{:S(2)}, u32[]{:S(2)}) collective-permute-start(f32[11,16,256]{2,1,0:T(8,128)S(1)} %get-tuple-element.24), channel_id=1, source_target_pairs={{0,224},{32,64},{64,32},{96,128},{128,96},{160,192},{192,160},{224... | collective-permute-start | bytes 540680 | tf_op jit(solution)/shard_map/ppermute | solution.py:492
  6.2 2.9 %collective-permute-start.1 = (f32[11,16,256]{2,1,0:T(8,128)S(1)}, f32[11,16,256]{2,1,0:T(8,128)S(1)}, u32[]{:S(2)}, u32[]{:S(2)}) collective-permute-start(f32[11,16,256]{2,1,0:T(8,128)S(1)} %get-tuple-element.25), channel_id=1, source_target_pairs={{0,32},{32,0},{64,96},{96,64},{128,160},{160,128},{192,224},{224,1... | collective-permute-start | bytes 540680 | tf_op jit(solution)/shard_map/ppermute | solution.py:492
  9.1 0.1 pad_add_fusion.idx.refs_0_
  9.2 2.5 %collective-permute-done.cross.refs_3_ = f32[11,16,256]{2,1,0:T(8,128)S(1)} collective-permute-done((f32[11,16,256]{2,1,0:T(8,128)S(1)}, f32[11,16,256]{2,1,0:T(8,128)S(1)}, u32[]{:S(2)}, u32[]{:S(2)}) %collective-permute-start) | collective-permute-done | bytes 180256 | tf_op jit(solution)/shard_map/ppermute | solution.py:492
  11.6 0.0 collective-permute-done.1.inner.refs_4_
  11.6 0.0 copy-done
  11.6 0.6 %shard_map.41 = (f32[232,256]{1,0:T(8,128)S(1)}, f32[232,256]{1,0:T(8,128)S(1)}) custom-call(s32[2]{0:T(128)S(1)} %pad_add_fusion.idx.refs_0_, f32[4,4,16,256]{3,2,1,0:T(8,128)S(1)} %copy-done, f32[4,16,256]{2,1,0:T(8,128)S(1)} %copy-done.1, f32[11,16,256]{2,1,0:T(8,128)S(1)} %collective-permute-done.cross.refs_3_, ...), custom_call_target="tpu_custom_call" | custom-call | tf_op jit(solution)/shard_map/pallas_call | solution.py:463
  12.3 4.9 %collective-permute-start.2 = (f32[232,256]{1,0:T(8,128)S(1)}, f32[232,256]{1,0:T(8,128)S(1)}, u32[]{:S(2)}, u32[]{:S(2)}) collective-permute-start(f32[232,256]{1,0:T(8,128)S(1)} %get-tuple-element.26), channel_id=1, source_target_pairs={{0,31},{1,2},{2,1},{3,4},{4,3},{5,6},{6,5},{7,8},{8,7},{9,10},{10,... | collective-permute-start | bytes 712712 | tf_op jit(solution)/shard_map/ppermute | solution.py:494
  17.2 0.0 collective-permute-start.3
  17.2 4.4 %collective-permute-done.2.refs_5_ = f32[232,256]{1,0:T(8,128)S(1)} collective-permute-done((f32[232,256]{1,0:T(8,128)S(1)}, f32[232,256]{1,0:T(8,128)S(1)}, u32[]{:S(2)}, u32[]{:S(2)}) %collective-permute-start.2) | collective-permute-done | bytes 237600 | tf_op jit(solution)/shard_map/ppermute | solution.py:494
  21.6 0.9 %collective-permute-done.3.refs_6_ = f32[232,256]{1,0:T(8,128)S(1)} collective-permute-done((f32[232,256]{1,0:T(8,128)S(1)}, f32[232,256]{1,0:T(8,128)S(1)}, u32[]{:S(2)}, u32[]{:S(2)}) %collective-permute-start.3) | collective-permute-done | bytes 237600 | tf_op jit(solution)/shard_map/ppermute | solution.py:494
  22.4 2.4 %shard_map.42 = (f32[64,256]{1,0:T(8,128)S(1)}, f32[208,256]{1,0:T(8,128)S(1)}, f32[4,8,2,32,128]{4,3,2,1,0:T(8,128)S(1)}, f32[10,2,32,128]{3,2,1,0:T(8,128)S(1)...) custom-call(s32[2]{0:T(128)S(1)} %pad_add_fusion.idx.refs_0_, f32[4,4,16,256]{3,2,1,0:T(8,128)S(1)} %copy-done, ...), custom_call_target="tpu_custom_call" | custom-call | tf_op jit(solution)/shard_map/pallas_call | solution.py:463
  24.8 6.1 %collective-permute-start.5 = (f32[208,256]{1,0:T(8,128)S(1)}, f32[208,256]{1,0:T(8,128)S(1)}, u32[]{:S(2)}, u32[]{:S(2)}) collective-permute-start(f32[208,256]{1,0:T(8,128)S(1)} %get-tuple-element.29), channel_id=1, source_target_pairs={{0,224},{32,64},{64,32},{96,128},{128,96},{160,192},{192,160},{224... | collective-permute-start | bytes 638984 | tf_op jit(solution)/shard_map/ppermute | solution.py:502
  30.9 4.3 %collective-permute-start.7 = (f32[64,256]{1,0:T(8,128)S(1)}, f32[64,256]{1,0:T(8,128)S(1)}, u32[]{:S(2)}, u32[]{:S(2)}) collective-permute-start(f32[64,256]{1,0:T(8,128)S(1)} %get-tuple-element.28.refs_1_), channel_id=1, source_target_pairs={{0,128},{32,160},{64,192},{96,224},{128,0},{160,32},{192,64},{224,... | collective-permute-start | bytes 196616 | tf_op jit(solution)/shard_map/ppermute | solution.py:503
  35.2 1.7 %collective-permute-start.6 = (f32[64,256]{1,0:T(8,128)S(1)}, f32[64,256]{1,0:T(8,128)S(1)}, u32[]{:S(2)}, u32[]{:S(2)}) collective-permute-start(f32[64,256]{1,0:T(8,128)S(1)} %get-tuple-element.28.refs_1_), channel_id=1, source_target_pairs={{0,64},{32,224},{64,128},{96,32},{128,192},{160,96},{192,0},{224,1... | collective-permute-start | bytes 196616 | tf_op jit(solution)/shard_map/ppermute | solution.py:504
  37.0 0.0 collective-permute-start.4
  37.0 0.0 collective-permute-done.5.refs_3_.refs_14_
  37.0 7.1 %collective-permute-done.7.refs_5_ = f32[64,256]{1,0:T(8,128)S(1)} collective-permute-done((f32[64,256]{1,0:T(8,128)S(1)}, f32[64,256]{1,0:T(8,128)S(1)}, u32[]{:S(2)}, u32[]{:S(2)}) %collective-permute-start.7) | collective-permute-done | bytes 65568 | tf_op jit(solution)/shard_map/ppermute | solution.py:503
  44.1 0.0 collective-permute-done.6.refs_4_
  44.1 0.5 collective-permute-start.8
  44.6 0.0 collective-permute-done.4.refs_2_.refs_13_
  44.6 1.1 %collective-permute-done.8.refs_6_ = f32[192,256]{1,0:T(8,128)S(1)} collective-permute-done((f32[192,256]{1,0:T(8,128)S(1)}, f32[192,256]{1,0:T(8,128)S(1)}, u32[]{:S(2)}, u32[]{:S(2)}) %collective-permute-start.8) | collective-permute-done | bytes 196640 | tf_op jit(solution)/shard_map/ppermute | solution.py:506
  45.7 1.5 %shard_map.43 = (f32[192,128]{1,0:T(8,128)S(1)}, f32[80,128]{1,0:T(8,128)S(1)}, f32[4,10,16,128]{3,2,1,0:T(8,128)S(1)}, f32[4,10,16,128]{3,2,1,0:T(8,128)S(1)}, ...) custom-call(s32[2]{0:T(128)S(1)} %pad_add_fusion.idx.refs_0_, f32[64,256]{1,0:T(8,128)S(1)} %get-tuple-element.28.refs_1_, ...), custom_call_target="tpu_custom_call" | custom-call | tf_op jit(solution)/shard_map/pallas_call | solution.py:463
  47.2 3.0 %collective-permute-start.9 = (f32[192,128]{1,0:T(8,128)S(1)}, f32[192,128]{1,0:T(8,128)S(1)}, u32[]{:S(2)}, u32[]{:S(2)}) collective-permute-start(f32[192,128]{1,0:T(8,128)S(1)} %get-tuple-element.31), channel_id=1, source_target_pairs={{0,1},{1,2},{2,3},{3,4},{4,5},{5,6},{6,7},{7,8},{8,9},{9,10},{10,1... | collective-permute-start | bytes 294920 | tf_op jit(solution)/shard_map/ppermute | solution.py:518
  50.2 0.0 collective-permute-start.10
  50.2 4.6 %collective-permute-done.10.refs_3_ = f32[80,128]{1,0:T(8,128)S(1)} collective-permute-done((f32[80,128]{1,0:T(8,128)S(1)}, f32[80,128]{1,0:T(8,128)S(1)}, u32[]{:S(2)}, u32[]{:S(2)}) %collective-permute-start.10) | collective-permute-done | bytes 40992 | tf_op jit(solution)/shard_map/ppermute | solution.py:519
  54.8 0.0 collective-permute-done.9.refs_2_
  54.8 2.4 %collective-permute-start.11 = (f32[272,128]{1,0:T(8,128)S(1)}, f32[272,128]{1,0:T(8,128)S(1)}, u32[]{:S(2)}, u32[]{:S(2)}) collective-permute-start(f32[272,128]{1,0:T(8,128)S(1)} %pad_maximum_fusion.3), channel_id=1, source_target_pairs={{0,32},{32,0},{64,96},{96,64},{128,160},{160,128},{192,224},{224,1... | collective-permute-start | bytes 417800 | tf_op jit(solution)/shard_map/ppermute | solution.py:520
  57.2 1.0 %collective-permute-done.11.refs_4_ = f32[272,128]{1,0:T(8,128)S(1)} collective-permute-done((f32[272,128]{1,0:T(8,128)S(1)}, f32[272,128]{1,0:T(8,128)S(1)}, u32[]{:S(2)}, u32[]{:S(2)}) %collective-permute-start.11) | collective-permute-done | bytes 139296 | tf_op jit(solution)/shard_map/ppermute | solution.py:520
  58.2 4.5 %shard_map.44 = (f32[4,4,16,256]{3,2,1,0:T(8,128)}, f32[4,4,16,256]{3,2,1,0:T(8,128)}) custom-call(s32[2]{0:T(128)S(1)} %pad_add_fusion.idx.refs_0_, f32[80,128]{1,0:T(8,128)S(1)} %get-tuple-element.30.refs_1_, f32[192,128]{1,0:T(8,128)S(1)} %collective-permute-done.9.refs_2_, f32[80,128]{1,0:T(8,128)S(1)} %collective-permute-done.10.refs_3_, ...), custom_call_target="tpu_custom_call" | custom-call | tf_op jit(solution)/shard_map/pallas_call | solution.py:463
  (5 shorter events, 0.1 us)
Async XLA Ops:
  0.6 1.0 %copy-start.1 = (f32[4,16,256]{2,1,0:T(8,128)S(1)}, f32[4,16,256]{2,1,0:T(8,128)}, u32[]{:S(2)}) copy-start(f32[4,16,256]{2,1,0:T(8,128)} %refs_2_.1) | copy-start | bytes 196612
  1.7 9.9 %copy-start = (f32[4,4,16,256]{3,2,1,0:T(8,128)S(1)}, f32[4,4,16,256]{3,2,1,0:T(8,128)}, u32[]{:S(2)}) copy-start(f32[4,4,16,256]{3,2,1,0:T(8,128)} %refs_1_.1) | copy-start | bytes 786436
  1.8 9.9 %collective-permute-start = (f32[11,16,256]{2,1,0:T(8,128)S(1)}, f32[11,16,256]{2,1,0:T(8,128)S(1)}, u32[]{:S(2)}, u32[]{:S(2)}) collective-permute-start(f32[11,16,256]{2,1,0:T(8,128)S(1)} %get-tuple-element.24), channel_id=1, source_target_pairs={{0,224},{32,64},{64,32},{96,128},{128,96},{160,192},{192,160},{224... | collective-permute-start | bytes 540680 | tf_op jit(solution)/shard_map/ppermute | solution.py:492
  6.2 5.4 %collective-permute-start.1 = (f32[11,16,256]{2,1,0:T(8,128)S(1)}, f32[11,16,256]{2,1,0:T(8,128)S(1)}, u32[]{:S(2)}, u32[]{:S(2)}) collective-permute-start(f32[11,16,256]{2,1,0:T(8,128)S(1)} %get-tuple-element.25), channel_id=1, source_target_pairs={{0,32},{32,0},{64,96},{96,64},{128,160},{160,128},{192,224},{224,1... | collective-permute-start | bytes 540680 | tf_op jit(solution)/shard_map/ppermute | solution.py:492
  12.3 9.3 %collective-permute-start.2 = (f32[232,256]{1,0:T(8,128)S(1)}, f32[232,256]{1,0:T(8,128)S(1)}, u32[]{:S(2)}, u32[]{:S(2)}) collective-permute-start(f32[232,256]{1,0:T(8,128)S(1)} %get-tuple-element.26), channel_id=1, source_target_pairs={{0,31},{1,2},{2,1},{3,4},{4,3},{5,6},{6,5},{7,8},{8,7},{9,10},{10,... | collective-permute-start | bytes 712712 | tf_op jit(solution)/shard_map/ppermute | solution.py:494
  17.2 5.3 %collective-permute-start.3 = (f32[232,256]{1,0:T(8,128)S(1)}, f32[232,256]{1,0:T(8,128)S(1)}, u32[]{:S(2)}, u32[]{:S(2)}) collective-permute-start(f32[232,256]{1,0:T(8,128)S(1)} %get-tuple-element.27), channel_id=1, source_target_pairs={{0,1},{1,0},{2,3},{3,2},{4,5},{5,4},{6,7},{7,6},{8,9},{9,8},{10,11... | collective-permute-start | bytes 712712 | tf_op jit(solution)/shard_map/ppermute | solution.py:494
  24.8 12.1 %collective-permute-start.5 = (f32[208,256]{1,0:T(8,128)S(1)}, f32[208,256]{1,0:T(8,128)S(1)}, u32[]{:S(2)}, u32[]{:S(2)}) collective-permute-start(f32[208,256]{1,0:T(8,128)S(1)} %get-tuple-element.29), channel_id=1, source_target_pairs={{0,224},{32,64},{64,32},{96,128},{128,96},{160,192},{192,160},{224... | collective-permute-start | bytes 638984 | tf_op jit(solution)/shard_map/ppermute | solution.py:502
  30.9 13.1 %collective-permute-start.7 = (f32[64,256]{1,0:T(8,128)S(1)}, f32[64,256]{1,0:T(8,128)S(1)}, u32[]{:S(2)}, u32[]{:S(2)}) collective-permute-start(f32[64,256]{1,0:T(8,128)S(1)} %get-tuple-element.28.refs_1_), channel_id=1, source_target_pairs={{0,128},{32,160},{64,192},{96,224},{128,0},{160,32},{192,64},{224,... | collective-permute-start | bytes 196616 | tf_op jit(solution)/shard_map/ppermute | solution.py:503
  35.2 8.8 %collective-permute-start.6 = (f32[64,256]{1,0:T(8,128)S(1)}, f32[64,256]{1,0:T(8,128)S(1)}, u32[]{:S(2)}, u32[]{:S(2)}) collective-permute-start(f32[64,256]{1,0:T(8,128)S(1)} %get-tuple-element.28.refs_1_), channel_id=1, source_target_pairs={{0,64},{32,224},{64,128},{96,32},{128,192},{160,96},{192,0},{224,1... | collective-permute-start | bytes 196616 | tf_op jit(solution)/shard_map/ppermute | solution.py:504
  37.0 7.6 %collective-permute-start.4 = (f32[208,256]{1,0:T(8,128)S(1)}, f32[208,256]{1,0:T(8,128)S(1)}, u32[]{:S(2)}, u32[]{:S(2)}) collective-permute-start(f32[208,256]{1,0:T(8,128)S(1)} %get-tuple-element.29), channel_id=1, source_target_pairs={{0,32},{32,0},{64,96},{96,64},{128,160},{160,128},{192,224},{224,1... | collective-permute-start | bytes 638984 | tf_op jit(solution)/shard_map/ppermute | solution.py:505
  44.1 1.6 %collective-permute-start.8 = (f32[192,256]{1,0:T(8,128)S(1)}, f32[192,256]{1,0:T(8,128)S(1)}, u32[]{:S(2)}, u32[]{:S(2)}) collective-permute-start(f32[192,256]{1,0:T(8,128)S(1)} %pad_maximum_fusion), channel_id=1, source_target_pairs={{0,32},{32,0},{64,96},{96,64},{128,160},{160,128},{192,224},{224,1... | collective-permute-start | bytes 589832 | tf_op jit(solution)/shard_map/ppermute | solution.py:506
  47.2 7.6 %collective-permute-start.9 = (f32[192,128]{1,0:T(8,128)S(1)}, f32[192,128]{1,0:T(8,128)S(1)}, u32[]{:S(2)}, u32[]{:S(2)}) collective-permute-start(f32[192,128]{1,0:T(8,128)S(1)} %get-tuple-element.31), channel_id=1, source_target_pairs={{0,1},{1,2},{2,3},{3,4},{4,5},{5,6},{6,7},{7,8},{8,9},{9,10},{10,1... | collective-permute-start | bytes 294920 | tf_op jit(solution)/shard_map/ppermute | solution.py:518
  50.2 4.7 %collective-permute-start.10 = (f32[80,128]{1,0:T(8,128)S(1)}, f32[80,128]{1,0:T(8,128)S(1)}, u32[]{:S(2)}, u32[]{:S(2)}) collective-permute-start(f32[80,128]{1,0:T(8,128)S(1)} %get-tuple-element.30.refs_1_), channel_id=1, source_target_pairs={{0,2},{1,3},{2,4},{3,5},{4,6},{5,7},{6,8},{7,9},{8,10},{9,11},{10,... | collective-permute-start | bytes 122888 | tf_op jit(solution)/shard_map/ppermute | solution.py:519
  54.8 3.4 %collective-permute-start.11 = (f32[272,128]{1,0:T(8,128)S(1)}, f32[272,128]{1,0:T(8,128)S(1)}, u32[]{:S(2)}, u32[]{:S(2)}) collective-permute-start(f32[272,128]{1,0:T(8,128)S(1)} %pad_maximum_fusion.3), channel_id=1, source_target_pairs={{0,32},{32,0},{64,96},{96,64},{128,160},{160,128},{192,224},{224,1... | collective-permute-start | bytes 417800 | tf_op jit(solution)/shard_map/ppermute | solution.py:520

commit v8 on v7

--- a/solution.py
+++ b/solution.py
@@ -478,18 +478,23 @@
     next_chip = [(i, (i - 2) % groups if i % 2 else (i + 2) % groups) for i in range(groups)]
     far_chip = [(i, (i + 4) % groups) for i in range(groups)]
     even = [(i, i ^ 1) for i in range(devs)]
-    odd = [(i, (i + 1) % devs if i % 2 else (i - 1) % devs) for i in range(devs)]
+    odd = [(i, min(max(i + 1 if i % 2 else i - 1, 0), devs - 1)) for i in range(devs)]
+    beside_inside = [(i, min(max(i + 1 if i % 2 else i - 1, 0), groups - 1)) for i in range(groups)]
 
     def along(step):
-        to = [(g, (d - step if g % 2 else d + step) % devs) for g in range(groups) for d in range(devs)]
-        return [(i, g * devs + d) for i, (g, d) in enumerate(to)]
+        pairs = []
+        for g in range(groups):
+            for d in range(devs):
+                to = d - step if g % 2 else d + step
+                pairs.append((g * devs + d, g * devs + to if 0 <= to < devs else (g ^ 1) * devs + d))
+        return pairs
 
     f_first, f_last, visc = lax.optimization_barrier((forcing[:, 0:2], forcing[:, 2:4], viscosity))
     first = jnp.concatenate([f_first.reshape(8, 16, 256), visc[0:3]], axis=0)
     last = jnp.concatenate([f_last.reshape(8, 16, 256), visc[1:4]], axis=0)
     cross, inner = pick(idx[0] % 2 == 0, first, last), pick(idx[0] % 2 == 0, last, first)
     cross, inner = lax.optimization_barrier((cross, inner))
-    cross, inner = lax.ppermute(cross, "grp", beside), lax.ppermute(inner, "grp", swap)
+    cross, inner = lax.ppermute(cross, "grp", beside_inside), lax.ppermute(inner, "grp", swap)
     to_even, to_odd = call(pack_second, [(SECOND_ROWS, 256)] * 2, [], idx, forcing, viscosity, cross, inner)
     from_odd, from_even = lax.ppermute(to_odd, "dev", odd), lax.ppermute(to_even, "dev", even)
     mid, pay, x1, ew, wt, fw = call(

time: 62.8 us -> 61.4 us (0.978)
  the two profiles are of different devices: /device:TPU:1 before, /device:TPU:25 now
where the time goes in v8:
time: 61.4 us; the launch traced here: 61.2 us
  starting transfers between devices  31.7 us (52%)
  waiting for transfers between devices  18.6 us (30%)
  Pallas kernels  9.08 us (15%)
  local copies, waits for them, and re-layouts  1.05 us (2%)
  between operations  0.76 us (1%)
    pallas_call x4, Pallas kernels, call(): pl.pallas_call(kernel, out_shape=[jax.ShapeDtypeStruct(shape, F32) for sh...  9.08 us
    ppermute x1, starting transfers between devices, local(): lax.ppermute(cross, 'grp', beside_inside)  5.59 us
    ppermute x1, starting transfers between devices, local(): xco = lax.ppermute(pay, 'grp', beside)  5.34 us
    ppermute x1, waiting for transfers between devices, local(): lax.ppermute(to_odd, 'dev', odd)  5.03 us
    ppermute x1, waiting for transfers between devices, local(): lax.ppermute(cross, 'grp', beside_inside)  4.91 us
    ppermute x1, starting transfers between devices, local(): lax.ppermute(to_odd, 'dev', odd)  4.72 us
    ppermute x1, starting transfers between devices, local(): cpm = lax.ppermute(mid, 'grp', next_chip)  3.82 us
    ppermute x1, starting transfers between devices, local(): swapped = lax.ppermute(jnp.concatenate([by1, by2], axis=0), 'grp', swap)  3.03 us
  transfers between devices with their start and end apart: 12, of which 9 were waited for; matrix products, arithmetic and copies ran while one was open for 0% of the time, Pallas kernels for 0%

profile of v8, /device:TPU:25, one launch (start us, length us, event | category | flops | bytes accessed | tf_op | source)
XLA Modules:
  0.0 61.2 jit_solution(4788877470332711831)
XLA Ops:
  0.6 0.0 copy-start.1
  0.7 1.0 %fusion.2 = (f32[4,2,16,256]{3,2,1,0:T(8,128)S(1)}, f32[4,2,16,256]{3,2,1,0:T(8,128)S(1)}) fusion(f32[4,4,16,256]{3,2,1,0:T(8,128)} %refs_1_.1), kind=kLoop, calls=%fused_computation.7 | loop fusion | bytes 524288 | tf_op jit(solution)/shard_map/slice | solution.py:492
  1.7 0.0 copy-done.1
  1.7 0.0 copy-start
  1.8 5.6 %collective-permute-start = (f32[11,16,256]{2,1,0:T(8,128)S(1)}, f32[11,16,256]{2,1,0:T(8,128)S(1)}, u32[]{:S(2)}, u32[]{:S(2)}) collective-permute-start(f32[11,16,256]{2,1,0:T(8,128)S(1)} %get-tuple-element.24), channel_id=1, source_target_pairs={{0,0},{32,64},{64,32},{96,128},{128,96},{160,192},{192,160},{224,2... | collective-permute-start | bytes 540680 | tf_op jit(solution)/shard_map/ppermute | solution.py:497
  7.4 0.1 collective-permute-start.1
  7.5 0.1 pad_add_fusion.idx.refs_0_
  7.5 4.9 %collective-permute-done.cross.refs_3_ = f32[11,16,256]{2,1,0:T(8,128)S(1)} collective-permute-done((f32[11,16,256]{2,1,0:T(8,128)S(1)}, f32[11,16,256]{2,1,0:T(8,128)S(1)}, u32[]{:S(2)}, u32[]{:S(2)}) %collective-permute-start) | collective-permute-done | bytes 180256 | tf_op jit(solution)/shard_map/ppermute | solution.py:497
  12.5 0.0 collective-permute-done.1.inner.refs_4_
  12.5 0.0 copy-done
  12.5 0.6 %shard_map.41 = (f32[232,256]{1,0:T(8,128)S(1)}, f32[232,256]{1,0:T(8,128)S(1)}) custom-call(s32[2]{0:T(128)S(1)} %pad_add_fusion.idx.refs_0_, f32[4,4,16,256]{3,2,1,0:T(8,128)S(1)} %copy-done, f32[4,16,256]{2,1,0:T(8,128)S(1)} %copy-done.1, f32[11,16,256]{2,1,0:T(8,128)S(1)} %collective-permute-done.cross.refs_3_, ...), custom_call_target="tpu_custom_call" | custom-call | tf_op jit(solution)/shard_map/pallas_call | solution.py:463
  13.1 4.7 %collective-permute-start.2 = (f32[232,256]{1,0:T(8,128)S(1)}, f32[232,256]{1,0:T(8,128)S(1)}, u32[]{:S(2)}, u32[]{:S(2)}) collective-permute-start(f32[232,256]{1,0:T(8,128)S(1)} %get-tuple-element.26), channel_id=1, source_target_pairs={{0,0},{1,2},{2,1},{3,4},{4,3},{5,6},{6,5},{7,8},{8,7},{9,10},{10,9... | collective-permute-start | bytes 712712 | tf_op jit(solution)/shard_map/ppermute | solution.py:499
  17.8 0.1 collective-permute-start.3
  17.9 5.0 %collective-permute-done.2.refs_5_ = f32[232,256]{1,0:T(8,128)S(1)} collective-permute-done((f32[232,256]{1,0:T(8,128)S(1)}, f32[232,256]{1,0:T(8,128)S(1)}, u32[]{:S(2)}, u32[]{:S(2)}) %collective-permute-start.2) | collective-permute-done | bytes 237600 | tf_op jit(solution)/shard_map/ppermute | solution.py:499
  23.0 0.9 %collective-permute-done.3.refs_6_ = f32[232,256]{1,0:T(8,128)S(1)} collective-permute-done((f32[232,256]{1,0:T(8,128)S(1)}, f32[232,256]{1,0:T(8,128)S(1)}, u32[]{:S(2)}, u32[]{:S(2)}) %collective-permute-start.3) | collective-permute-done | bytes 237600 | tf_op jit(solution)/shard_map/ppermute | solution.py:499
  23.9 2.4 %shard_map.42 = (f32[64,256]{1,0:T(8,128)S(1)}, f32[208,256]{1,0:T(8,128)S(1)}, f32[4,8,2,32,128]{4,3,2,1,0:T(8,128)S(1)}, f32[10,2,32,128]{3,2,1,0:T(8,128)S(1)...) custom-call(s32[2]{0:T(128)S(1)} %pad_add_fusion.idx.refs_0_, f32[4,4,16,256]{3,2,1,0:T(8,128)S(1)} %copy-done, ...), custom_call_target="tpu_custom_call" | custom-call | tf_op jit(solution)/shard_map/pallas_call | solution.py:463
  26.3 5.3 %collective-permute-start.5 = (f32[208,256]{1,0:T(8,128)S(1)}, f32[208,256]{1,0:T(8,128)S(1)}, u32[]{:S(2)}, u32[]{:S(2)}) collective-permute-start(f32[208,256]{1,0:T(8,128)S(1)} %get-tuple-element.29), channel_id=1, source_target_pairs={{0,224},{32,64},{64,32},{96,128},{128,96},{160,192},{192,160},{224... | collective-permute-start | bytes 638984 | tf_op jit(solution)/shard_map/ppermute | solution.py:507
  31.7 3.0 %collective-permute-start.7 = (f32[64,256]{1,0:T(8,128)S(1)}, f32[64,256]{1,0:T(8,128)S(1)}, u32[]{:S(2)}, u32[]{:S(2)}) collective-permute-start(f32[64,256]{1,0:T(8,128)S(1)} %get-tuple-element.28.refs_1_), channel_id=1, source_target_pairs={{0,128},{32,160},{64,192},{96,224},{128,0},{160,32},{192,64},{224,... | collective-permute-start | bytes 196616 | tf_op jit(solution)/shard_map/ppermute | solution.py:508
  34.6 3.8 %collective-permute-start.6 = (f32[64,256]{1,0:T(8,128)S(1)}, f32[64,256]{1,0:T(8,128)S(1)}, u32[]{:S(2)}, u32[]{:S(2)}) collective-permute-start(f32[64,256]{1,0:T(8,128)S(1)} %get-tuple-element.28.refs_1_), channel_id=1, source_target_pairs={{0,64},{32,224},{64,128},{96,32},{128,192},{160,96},{192,0},{224,1... | collective-permute-start | bytes 196616 | tf_op jit(solution)/shard_map/ppermute | solution.py:509
  38.5 0.0 collective-permute-start.4
  38.5 2.5 %collective-permute-done.5.refs_3_.refs_14_ = f32[208,256]{1,0:T(8,128)S(1)} collective-permute-done((f32[208,256]{1,0:T(8,128)S(1)}, f32[208,256]{1,0:T(8,128)S(1)}, u32[]{:S(2)}, u32[]{:S(2)}) %collective-permute-start.5) | collective-permute-done | bytes 213024 | tf_op jit(solution)/shard_map/ppermute | solution.py:507
  41.0 0.1 collective-permute-done.7.refs_5_
  41.1 0.2 collective-permute-done.6.refs_4_
  41.3 2.8 %collective-permute-start.8 = (f32[192,256]{1,0:T(8,128)S(1)}, f32[192,256]{1,0:T(8,128)S(1)}, u32[]{:S(2)}, u32[]{:S(2)}) collective-permute-start(f32[192,256]{1,0:T(8,128)S(1)} %pad_maximum_fusion), channel_id=1, source_target_pairs={{0,32},{32,0},{64,96},{96,64},{128,160},{160,128},{192,224},{224,1... | collective-permute-start | bytes 589832 | tf_op jit(solution)/shard_map/ppermute | solution.py:511
  44.1 0.0 collective-permute-done.4.refs_2_.refs_13_
  44.1 1.1 %collective-permute-done.8.refs_6_ = f32[192,256]{1,0:T(8,128)S(1)} collective-permute-done((f32[192,256]{1,0:T(8,128)S(1)}, f32[192,256]{1,0:T(8,128)S(1)}, u32[]{:S(2)}, u32[]{:S(2)}) %collective-permute-start.8) | collective-permute-done | bytes 196640 | tf_op jit(solution)/shard_map/ppermute | solution.py:511
  45.2 1.5 %shard_map.43 = (f32[192,128]{1,0:T(8,128)S(1)}, f32[80,128]{1,0:T(8,128)S(1)}, f32[4,10,16,128]{3,2,1,0:T(8,128)S(1)}, f32[4,10,16,128]{3,2,1,0:T(8,128)S(1)}, ...) custom-call(s32[2]{0:T(128)S(1)} %pad_add_fusion.idx.refs_0_, f32[64,256]{1,0:T(8,128)S(1)} %get-tuple-element.28.refs_1_, ...), custom_call_target="tpu_custom_call" | custom-call | tf_op jit(solution)/shard_map/pallas_call | solution.py:463
  46.7 1.6 %collective-permute-start.9 = (f32[192,128]{1,0:T(8,128)S(1)}, f32[192,128]{1,0:T(8,128)S(1)}, u32[]{:S(2)}, u32[]{:S(2)}) collective-permute-start(f32[192,128]{1,0:T(8,128)S(1)} %get-tuple-element.31), channel_id=1, source_target_pairs={{0,1},{1,2},{2,3},{3,4},{4,5},{5,6},{6,7},{7,8},{8,9},{9,10},{10,1... | collective-permute-start | bytes 294920 | tf_op jit(solution)/shard_map/ppermute | solution.py:523
  48.4 1.6 %collective-permute-start.10 = (f32[80,128]{1,0:T(8,128)S(1)}, f32[80,128]{1,0:T(8,128)S(1)}, u32[]{:S(2)}, u32[]{:S(2)}) collective-permute-start(f32[80,128]{1,0:T(8,128)S(1)} %get-tuple-element.30.refs_1_), channel_id=1, source_target_pairs={{0,2},{1,3},{2,4},{3,5},{4,6},{5,7},{6,8},{7,9},{8,10},{9,11},{10,... | collective-permute-start | bytes 122888 | tf_op jit(solution)/shard_map/ppermute | solution.py:524
  49.9 2.8 %collective-permute-done.10.refs_3_ = f32[80,128]{1,0:T(8,128)S(1)} collective-permute-done((f32[80,128]{1,0:T(8,128)S(1)}, f32[80,128]{1,0:T(8,128)S(1)}, u32[]{:S(2)}, u32[]{:S(2)}) %collective-permute-start.10) | collective-permute-done | bytes 40992 | tf_op jit(solution)/shard_map/ppermute | solution.py:524
  52.7 0.0 collective-permute-done.9.refs_2_
  52.7 3.0 %collective-permute-start.11 = (f32[272,128]{1,0:T(8,128)S(1)}, f32[272,128]{1,0:T(8,128)S(1)}, u32[]{:S(2)}, u32[]{:S(2)}) collective-permute-start(f32[272,128]{1,0:T(8,128)S(1)} %pad_maximum_fusion.3), channel_id=1, source_target_pairs={{0,32},{32,0},{64,96},{96,64},{128,160},{160,128},{192,224},{224,1... | collective-permute-start | bytes 417800 | tf_op jit(solution)/shard_map/ppermute | solution.py:525
  55.8 1.0 %collective-permute-done.11.refs_4_ = f32[272,128]{1,0:T(8,128)S(1)} collective-permute-done((f32[272,128]{1,0:T(8,128)S(1)}, f32[272,128]{1,0:T(8,128)S(1)}, u32[]{:S(2)}, u32[]{:S(2)}) %collective-permute-start.11) | collective-permute-done | bytes 139296 | tf_op jit(solution)/shard_map/ppermute | solution.py:525
  56.8 4.5 %shard_map.44 = (f32[4,4,16,256]{3,2,1,0:T(8,128)}, f32[4,4,16,256]{3,2,1,0:T(8,128)}) custom-call(s32[2]{0:T(128)S(1)} %pad_add_fusion.idx.refs_0_, f32[80,128]{1,0:T(8,128)S(1)} %get-tuple-element.30.refs_1_, f32[192,128]{1,0:T(8,128)S(1)} %collective-permute-done.9.refs_2_, f32[80,128]{1,0:T(8,128)S(1)} %collective-permute-done.10.refs_3_, ...), custom_call_target="tpu_custom_call" | custom-call | tf_op jit(solution)/shard_map/pallas_call | solution.py:463
  (5 shorter events, 0.1 us)
Async XLA Ops:
  0.6 1.0 %copy-start.1 = (f32[4,16,256]{2,1,0:T(8,128)S(1)}, f32[4,16,256]{2,1,0:T(8,128)}, u32[]{:S(2)}) copy-start(f32[4,16,256]{2,1,0:T(8,128)} %refs_2_.1) | copy-start | bytes 196612
  1.7 10.7 %copy-start = (f32[4,4,16,256]{3,2,1,0:T(8,128)S(1)}, f32[4,4,16,256]{3,2,1,0:T(8,128)}, u32[]{:S(2)}) copy-start(f32[4,4,16,256]{3,2,1,0:T(8,128)} %refs_1_.1) | copy-start | bytes 786436
  1.8 10.7 %collective-permute-start = (f32[11,16,256]{2,1,0:T(8,128)S(1)}, f32[11,16,256]{2,1,0:T(8,128)S(1)}, u32[]{:S(2)}, u32[]{:S(2)}) collective-permute-start(f32[11,16,256]{2,1,0:T(8,128)S(1)} %get-tuple-element.24), channel_id=1, source_target_pairs={{0,0},{32,64},{64,32},{96,128},{128,96},{160,192},{192,160},{224,2... | collective-permute-start | bytes 540680 | tf_op jit(solution)/shard_map/ppermute | solution.py:497
  7.4 5.1 %collective-permute-start.1 = (f32[11,16,256]{2,1,0:T(8,128)S(1)}, f32[11,16,256]{2,1,0:T(8,128)S(1)}, u32[]{:S(2)}, u32[]{:S(2)}) collective-permute-start(f32[11,16,256]{2,1,0:T(8,128)S(1)} %get-tuple-element.25), channel_id=1, source_target_pairs={{0,32},{32,0},{64,96},{96,64},{128,160},{160,128},{192,224},{224,1... | collective-permute-start | bytes 540680 | tf_op jit(solution)/shard_map/ppermute | solution.py:497
  13.1 9.9 %collective-permute-start.2 = (f32[232,256]{1,0:T(8,128)S(1)}, f32[232,256]{1,0:T(8,128)S(1)}, u32[]{:S(2)}, u32[]{:S(2)}) collective-permute-start(f32[232,256]{1,0:T(8,128)S(1)} %get-tuple-element.26), channel_id=1, source_target_pairs={{0,0},{1,2},{2,1},{3,4},{4,3},{5,6},{6,5},{7,8},{8,7},{9,10},{10,9... | collective-permute-start | bytes 712712 | tf_op jit(solution)/shard_map/ppermute | solution.py:499
  17.8 6.1 %collective-permute-start.3 = (f32[232,256]{1,0:T(8,128)S(1)}, f32[232,256]{1,0:T(8,128)S(1)}, u32[]{:S(2)}, u32[]{:S(2)}) collective-permute-start(f32[232,256]{1,0:T(8,128)S(1)} %get-tuple-element.27), channel_id=1, source_target_pairs={{0,1},{1,0},{2,3},{3,2},{4,5},{5,4},{6,7},{7,6},{8,9},{9,8},{10,11... | collective-permute-start | bytes 712712 | tf_op jit(solution)/shard_map/ppermute | solution.py:499
  26.3 14.6 %collective-permute-start.5 = (f32[208,256]{1,0:T(8,128)S(1)}, f32[208,256]{1,0:T(8,128)S(1)}, u32[]{:S(2)}, u32[]{:S(2)}) collective-permute-start(f32[208,256]{1,0:T(8,128)S(1)} %get-tuple-element.29), channel_id=1, source_target_pairs={{0,224},{32,64},{64,32},{96,128},{128,96},{160,192},{192,160},{224... | collective-permute-start | bytes 638984 | tf_op jit(solution)/shard_map/ppermute | solution.py:507
  31.7 9.4 %collective-permute-start.7 = (f32[64,256]{1,0:T(8,128)S(1)}, f32[64,256]{1,0:T(8,128)S(1)}, u32[]{:S(2)}, u32[]{:S(2)}) collective-permute-start(f32[64,256]{1,0:T(8,128)S(1)} %get-tuple-element.28.refs_1_), channel_id=1, source_target_pairs={{0,128},{32,160},{64,192},{96,224},{128,0},{160,32},{192,64},{224,... | collective-permute-start | bytes 196616 | tf_op jit(solution)/shard_map/ppermute | solution.py:508
  34.6 6.6 %collective-permute-start.6 = (f32[64,256]{1,0:T(8,128)S(1)}, f32[64,256]{1,0:T(8,128)S(1)}, u32[]{:S(2)}, u32[]{:S(2)}) collective-permute-start(f32[64,256]{1,0:T(8,128)S(1)} %get-tuple-element.28.refs_1_), channel_id=1, source_target_pairs={{0,64},{32,224},{64,128},{96,32},{128,192},{160,96},{192,0},{224,1... | collective-permute-start | bytes 196616 | tf_op jit(solution)/shard_map/ppermute | solution.py:509
  38.5 5.6 %collective-permute-start.4 = (f32[208,256]{1,0:T(8,128)S(1)}, f32[208,256]{1,0:T(8,128)S(1)}, u32[]{:S(2)}, u32[]{:S(2)}) collective-permute-start(f32[208,256]{1,0:T(8,128)S(1)} %get-tuple-element.29), channel_id=1, source_target_pairs={{0,32},{32,0},{64,96},{96,64},{128,160},{160,128},{192,224},{224,1... | collective-permute-start | bytes 638984 | tf_op jit(solution)/shard_map/ppermute | solution.py:510
  41.3 3.9 %collective-permute-start.8 = (f32[192,256]{1,0:T(8,128)S(1)}, f32[192,256]{1,0:T(8,128)S(1)}, u32[]{:S(2)}, u32[]{:S(2)}) collective-permute-start(f32[192,256]{1,0:T(8,128)S(1)} %pad_maximum_fusion), channel_id=1, source_target_pairs={{0,32},{32,0},{64,96},{96,64},{128,160},{160,128},{192,224},{224,1... | collective-permute-start | bytes 589832 | tf_op jit(solution)/shard_map/ppermute | solution.py:511
  46.7 6.0 %collective-permute-start.9 = (f32[192,128]{1,0:T(8,128)S(1)}, f32[192,128]{1,0:T(8,128)S(1)}, u32[]{:S(2)}, u32[]{:S(2)}) collective-permute-start(f32[192,128]{1,0:T(8,128)S(1)} %get-tuple-element.31), channel_id=1, source_target_pairs={{0,1},{1,2},{2,3},{3,4},{4,5},{5,6},{6,7},{7,8},{8,9},{9,10},{10,1... | collective-permute-start | bytes 294920 | tf_op jit(solution)/shard_map/ppermute | solution.py:523
  48.4 4.4 %collective-permute-start.10 = (f32[80,128]{1,0:T(8,128)S(1)}, f32[80,128]{1,0:T(8,128)S(1)}, u32[]{:S(2)}, u32[]{:S(2)}) collective-permute-start(f32[80,128]{1,0:T(8,128)S(1)} %get-tuple-element.30.refs_1_), channel_id=1, source_target_pairs={{0,2},{1,3},{2,4},{3,5},{4,6},{5,7},{6,8},{7,9},{8,10},{9,11},{10,... | collective-permute-start | bytes 122888 | tf_op jit(solution)/shard_map/ppermute | solution.py:524
  52.7 4.0 %collective-permute-start.11 = (f32[272,128]{1,0:T(8,128)S(1)}, f32[272,128]{1,0:T(8,128)S(1)}, u32[]{:S(2)}, u32[]{:S(2)}) collective-permute-start(f32[272,128]{1,0:T(8,128)S(1)} %pad_maximum_fusion.3), channel_id=1, source_target_pairs={{0,32},{32,0},{64,96},{96,64},{128,160},{160,128},{192,224},{224,1... | collective-permute-start | bytes 417800 | tf_op jit(solution)/shard_map/ppermute | solution.py:525

commit v9 on v7

--- a/solution.py
+++ b/solution.py
@@ -478,20 +478,29 @@
     next_chip = [(i, (i - 2) % groups if i % 2 else (i + 2) % groups) for i in range(groups)]
     far_chip = [(i, (i + 4) % groups) for i in range(groups)]
     even = [(i, i ^ 1) for i in range(devs)]
-    odd = [(i, (i + 1) % devs if i % 2 else (i - 1) % devs) for i in range(devs)]
+
+    def pairs_of(to):
+        every = [(g, d) for g in range(groups) for d in range(devs)]
+        return [(g * devs + d, to(g, d)[0] * devs + to(g, d)[1]) for g, d in every]
+
+    cross_pairs = pairs_of(lambda g, d: (beside[g][1], d) if 0 < g < groups - 1 else (g, d ^ 1))
+    odd_pairs = pairs_of(lambda g, d: (g, d + 1 if d % 2 else d - 1) if 0 < d < devs - 1 else (g ^ 1, d))
 
     def along(step):
-        to = [(g, (d - step if g % 2 else d + step) % devs) for g in range(groups) for d in range(devs)]
-        return [(i, g * devs + d) for i, (g, d) in enumerate(to)]
+        def to(g, d):
+            there = d - step if g % 2 else d + step
+            return (g, there) if 0 <= there < devs else (g ^ 1, d)
+
+        return pairs_of(to)
 
     f_first, f_last, visc = lax.optimization_barrier((forcing[:, 0:2], forcing[:, 2:4], viscosity))
     first = jnp.concatenate([f_first.reshape(8, 16, 256), visc[0:3]], axis=0)
     last = jnp.concatenate([f_last.reshape(8, 16, 256), visc[1:4]], axis=0)
     cross, inner = pick(idx[0] % 2 == 0, first, last), pick(idx[0] % 2 == 0, last, first)
     cross, inner = lax.optimization_barrier((cross, inner))
-    cross, inner = lax.ppermute(cross, "grp", beside), lax.ppermute(inner, "grp", swap)
+    cross, inner = lax.ppermute(cross, ("grp", "dev"), cross_pairs), lax.ppermute(inner, "grp", swap)
     to_even, to_odd = call(pack_second, [(SECOND_ROWS, 256)] * 2, [], idx, forcing, viscosity, cross, inner)
-    from_odd, from_even = lax.ppermute(to_odd, "dev", odd), lax.ppermute(to_even, "dev", even)
+    from_odd, from_even = lax.ppermute(to_odd, ("grp", "dev"), odd_pairs), lax.ppermute(to_even, "dev", even)
     mid, pay, x1, ew, wt, fw = call(
         lambda *refs: fine_down(groups, devs, *refs),
         [(64, 256), (208, 256), (4, 8, 2, 32, 128), (10, 2, 32, 128), (8, 2, 32, 128), (4, 8, 2, 32, 128)],

time: 62.8 us -> 57.5 us (0.916)
  the two profiles are of different devices: /device:TPU:1 before, /device:TPU:9 now
where the time goes in v9:
time: 57.5 us; the launch traced here: 57.4 us
  starting transfers between devices  24 us (42%)
  waiting for transfers between devices  22.4 us (39%)
  Pallas kernels  9.08 us (16%)
  local copies, waits for them, and re-layouts  1.05 us (2%)
  between operations  0.73 us (1%)
    pallas_call x4, Pallas kernels, call(): pl.pallas_call(kernel, out_shape=[jax.ShapeDtypeStruct(shape, F32) for sh...  9.08 us
    ppermute x1, waiting for transfers between devices, local(): lax.ppermute(to_odd, ('grp', 'dev'), odd_pairs)  5.95 us
    ppermute x1, waiting for transfers between devices, local(): by2 = lax.ppermute(low, ('grp', 'dev'), along(2))  5.33 us
    ppermute x1, waiting for transfers between devices, local(): lax.ppermute(cross, ('grp', 'dev'), cross_pairs)  5.03 us
    ppermute x1, starting transfers between devices, local(): xco = lax.ppermute(pay, 'grp', beside)  4.38 us
    ppermute x1, starting transfers between devices, local(): cpm = lax.ppermute(mid, 'grp', next_chip)  4.04 us
    ppermute x1, starting transfers between devices, local(): lax.ppermute(cross, ('grp', 'dev'), cross_pairs)  3.64 us
    ppermute x1, starting transfers between devices, local(): c2 = lax.ppermute(mid, 'grp', far_chip)  3.15 us
  transfers between devices with their start and end apart: 12, of which 8 were waited for; matrix products, arithmetic and copies ran while one was open for 0% of the time, Pallas kernels for 0%

profile of v9, /device:TPU:9, one launch (start us, length us, event | category | flops | bytes accessed | tf_op | source)
XLA Modules:
  0.0 57.4 jit_solution(12934040538970149920)
XLA Ops:
  0.6 0.0 copy-start.1
  0.7 1.0 %fusion.2 = (f32[4,2,16,256]{3,2,1,0:T(8,128)S(1)}, f32[4,2,16,256]{3,2,1,0:T(8,128)S(1)}) fusion(f32[4,4,16,256]{3,2,1,0:T(8,128)} %refs_1_.1), kind=kLoop, calls=%fused_computation.7 | loop fusion | bytes 524288 | tf_op jit(solution)/shard_map/slice | solution.py:496
  1.7 0.0 copy-done.1
  1.7 0.0 copy-start
  1.8 3.6 %collective-permute-start = (f32[11,16,256]{2,1,0:T(8,128)S(1)}, f32[11,16,256]{2,1,0:T(8,128)S(1)}, u32[]{:S(2)}, u32[]{:S(2)}) collective-permute-start(f32[11,16,256]{2,1,0:T(8,128)S(1)} %get-tuple-element.24), channel_id=1, source_target_pairs={{0,1},{1,0},{2,3},{3,2},{4,5},{5,4},{6,7},{7,6},{8,9},{9,8},{10,11... | collective-permute-start | bytes 540680 | tf_op jit(solution)/shard_map/ppermute | solution.py:501
  5.4 0.0 collective-permute-start.1
  5.4 0.1 pad_add_fusion.idx.refs_0_
  5.5 5.0 %collective-permute-done.cross.refs_3_ = f32[11,16,256]{2,1,0:T(8,128)S(1)} collective-permute-done((f32[11,16,256]{2,1,0:T(8,128)S(1)}, f32[11,16,256]{2,1,0:T(8,128)S(1)}, u32[]{:S(2)}, u32[]{:S(2)}) %collective-permute-start) | collective-permute-done | bytes 180256 | tf_op jit(solution)/shard_map/ppermute | solution.py:501
  10.5 0.0 collective-permute-done.1.inner.refs_4_
  10.5 0.0 copy-done
  10.5 0.6 %shard_map.41 = (f32[232,256]{1,0:T(8,128)S(1)}, f32[232,256]{1,0:T(8,128)S(1)}) custom-call(s32[2]{0:T(128)S(1)} %pad_add_fusion.idx.refs_0_, f32[4,4,16,256]{3,2,1,0:T(8,128)S(1)} %copy-done, f32[4,16,256]{2,1,0:T(8,128)S(1)} %copy-done.1, f32[11,16,256]{2,1,0:T(8,128)S(1)} %collective-permute-done.cross.refs_3_, ...), custom_call_target="tpu_custom_call" | custom-call | tf_op jit(solution)/shard_map/pallas_call | solution.py:463
  11.2 2.6 %collective-permute-start.2 = (f32[232,256]{1,0:T(8,128)S(1)}, f32[232,256]{1,0:T(8,128)S(1)}, u32[]{:S(2)}, u32[]{:S(2)}) collective-permute-start(f32[232,256]{1,0:T(8,128)S(1)} %get-tuple-element.26), channel_id=1, source_target_pairs={{0,32},{1,2},{2,1},{3,4},{4,3},{5,6},{6,5},{7,8},{8,7},{9,10},{10,... | collective-permute-start | bytes 712712 | tf_op jit(solution)/shard_map/ppermute | solution.py:503
  13.8 0.0 collective-permute-start.3
  13.8 6.0 %collective-permute-done.2.refs_5_ = f32[232,256]{1,0:T(8,128)S(1)} collective-permute-done((f32[232,256]{1,0:T(8,128)S(1)}, f32[232,256]{1,0:T(8,128)S(1)}, u32[]{:S(2)}, u32[]{:S(2)}) %collective-permute-start.2) | collective-permute-done | bytes 237600 | tf_op jit(solution)/shard_map/ppermute | solution.py:503
  19.7 1.0 %collective-permute-done.3.refs_6_ = f32[232,256]{1,0:T(8,128)S(1)} collective-permute-done((f32[232,256]{1,0:T(8,128)S(1)}, f32[232,256]{1,0:T(8,128)S(1)}, u32[]{:S(2)}, u32[]{:S(2)}) %collective-permute-start.3) | collective-permute-done | bytes 237600 | tf_op jit(solution)/shard_map/ppermute | solution.py:503
  20.7 2.4 %shard_map.42 = (f32[64,256]{1,0:T(8,128)S(1)}, f32[208,256]{1,0:T(8,128)S(1)}, f32[4,8,2,32,128]{4,3,2,1,0:T(8,128)S(1)}, f32[10,2,32,128]{3,2,1,0:T(8,128)S(1)...) custom-call(s32[2]{0:T(128)S(1)} %pad_add_fusion.idx.refs_0_, f32[4,4,16,256]{3,2,1,0:T(8,128)S(1)} %copy-done, ...), custom_call_target="tpu_custom_call" | custom-call | tf_op jit(solution)/shard_map/pallas_call | solution.py:463
  23.1 4.4 %collective-permute-start.5 = (f32[208,256]{1,0:T(8,128)S(1)}, f32[208,256]{1,0:T(8,128)S(1)}, u32[]{:S(2)}, u32[]{:S(2)}) collective-permute-start(f32[208,256]{1,0:T(8,128)S(1)} %get-tuple-element.29), channel_id=1, source_target_pairs={{0,224},{32,64},{64,32},{96,128},{128,96},{160,192},{192,160},{224... | collective-permute-start | bytes 638984 | tf_op jit(solution)/shard_map/ppermute | solution.py:511
  27.5 3.2 %collective-permute-start.7 = (f32[64,256]{1,0:T(8,128)S(1)}, f32[64,256]{1,0:T(8,128)S(1)}, u32[]{:S(2)}, u32[]{:S(2)}) collective-permute-start(f32[64,256]{1,0:T(8,128)S(1)} %get-tuple-element.28.refs_1_), channel_id=1, source_target_pairs={{0,128},{32,160},{64,192},{96,224},{128,0},{160,32},{192,64},{224,... | collective-permute-start | bytes 196616 | tf_op jit(solution)/shard_map/ppermute | solution.py:512
  30.7 4.0 %collective-permute-start.6 = (f32[64,256]{1,0:T(8,128)S(1)}, f32[64,256]{1,0:T(8,128)S(1)}, u32[]{:S(2)}, u32[]{:S(2)}) collective-permute-start(f32[64,256]{1,0:T(8,128)S(1)} %get-tuple-element.28.refs_1_), channel_id=1, source_target_pairs={{0,64},{32,224},{64,128},{96,32},{128,192},{160,96},{192,0},{224,1... | collective-permute-start | bytes 196616 | tf_op jit(solution)/shard_map/ppermute | solution.py:513
  34.7 0.0 collective-permute-start.4
  34.7 0.0 collective-permute-done.5.refs_3_.refs_14_
  34.7 2.4 %collective-permute-done.7.refs_5_ = f32[64,256]{1,0:T(8,128)S(1)} collective-permute-done((f32[64,256]{1,0:T(8,128)S(1)}, f32[64,256]{1,0:T(8,128)S(1)}, u32[]{:S(2)}, u32[]{:S(2)}) %collective-permute-start.7) | collective-permute-done | bytes 65568 | tf_op jit(solution)/shard_map/ppermute | solution.py:512
  37.1 0.4 collective-permute-done.6.refs_4_
  37.5 2.7 %collective-permute-start.8 = (f32[192,256]{1,0:T(8,128)S(1)}, f32[192,256]{1,0:T(8,128)S(1)}, u32[]{:S(2)}, u32[]{:S(2)}) collective-permute-start(f32[192,256]{1,0:T(8,128)S(1)} %pad_maximum_fusion), channel_id=1, source_target_pairs={{0,32},{32,0},{64,96},{96,64},{128,160},{160,128},{192,224},{224,1... | collective-permute-start | bytes 589832 | tf_op jit(solution)/shard_map/ppermute | solution.py:515
  40.3 0.0 collective-permute-done.4.refs_2_.refs_13_
  40.3 1.1 %collective-permute-done.8.refs_6_ = f32[192,256]{1,0:T(8,128)S(1)} collective-permute-done((f32[192,256]{1,0:T(8,128)S(1)}, f32[192,256]{1,0:T(8,128)S(1)}, u32[]{:S(2)}, u32[]{:S(2)}) %collective-permute-start.8) | collective-permute-done | bytes 196640 | tf_op jit(solution)/shard_map/ppermute | solution.py:515
  41.4 1.5 %shard_map.43 = (f32[192,128]{1,0:T(8,128)S(1)}, f32[80,128]{1,0:T(8,128)S(1)}, f32[4,10,16,128]{3,2,1,0:T(8,128)S(1)}, f32[4,10,16,128]{3,2,1,0:T(8,128)S(1)}, ...) custom-call(s32[2]{0:T(128)S(1)} %pad_add_fusion.idx.refs_0_, f32[64,256]{1,0:T(8,128)S(1)} %get-tuple-element.28.refs_1_, ...), custom_call_target="tpu_custom_call" | custom-call | tf_op jit(solution)/shard_map/pallas_call | solution.py:463
  42.9 3.0 %collective-permute-start.9 = (f32[192,128]{1,0:T(8,128)S(1)}, f32[192,128]{1,0:T(8,128)S(1)}, u32[]{:S(2)}, u32[]{:S(2)}) collective-permute-start(f32[192,128]{1,0:T(8,128)S(1)} %get-tuple-element.31), channel_id=1, source_target_pairs={{0,1},{1,2},{2,3},{3,4},{4,5},{5,6},{6,7},{7,8},{8,9},{9,10},{10,1... | collective-permute-start | bytes 294920 | tf_op jit(solution)/shard_map/ppermute | solution.py:527
  45.9 0.0 collective-permute-start.10
  45.9 5.3 %collective-permute-done.10.refs_3_ = f32[80,128]{1,0:T(8,128)S(1)} collective-permute-done((f32[80,128]{1,0:T(8,128)S(1)}, f32[80,128]{1,0:T(8,128)S(1)}, u32[]{:S(2)}, u32[]{:S(2)}) %collective-permute-start.10) | collective-permute-done | bytes 40992 | tf_op jit(solution)/shard_map/ppermute | solution.py:528
  51.3 0.0 collective-permute-done.9.refs_2_
  51.3 0.4 collective-permute-start.11
  51.7 1.2 %collective-permute-done.11.refs_4_ = f32[272,128]{1,0:T(8,128)S(1)} collective-permute-done((f32[272,128]{1,0:T(8,128)S(1)}, f32[272,128]{1,0:T(8,128)S(1)}, u32[]{:S(2)}, u32[]{:S(2)}) %collective-permute-start.11) | collective-permute-done | bytes 139296 | tf_op jit(solution)/shard_map/ppermute | solution.py:529
  52.9 4.5 %shard_map.44 = (f32[4,4,16,256]{3,2,1,0:T(8,128)}, f32[4,4,16,256]{3,2,1,0:T(8,128)}) custom-call(s32[2]{0:T(128)S(1)} %pad_add_fusion.idx.refs_0_, f32[80,128]{1,0:T(8,128)S(1)} %get-tuple-element.30.refs_1_, f32[192,128]{1,0:T(8,128)S(1)} %collective-permute-done.9.refs_2_, f32[80,128]{1,0:T(8,128)S(1)} %collective-permute-done.10.refs_3_, ...), custom_call_target="tpu_custom_call" | custom-call | tf_op jit(solution)/shard_map/pallas_call | solution.py:463
  (5 shorter events, 0.1 us)
Async XLA Ops:
  0.6 1.0 %copy-start.1 = (f32[4,16,256]{2,1,0:T(8,128)S(1)}, f32[4,16,256]{2,1,0:T(8,128)}, u32[]{:S(2)}) copy-start(f32[4,16,256]{2,1,0:T(8,128)} %refs_2_.1) | copy-start | bytes 196612
  1.7 8.8 %copy-start = (f32[4,4,16,256]{3,2,1,0:T(8,128)S(1)}, f32[4,4,16,256]{3,2,1,0:T(8,128)}, u32[]{:S(2)}) copy-start(f32[4,4,16,256]{3,2,1,0:T(8,128)} %refs_1_.1) | copy-start | bytes 786436
  1.8 8.7 %collective-permute-start = (f32[11,16,256]{2,1,0:T(8,128)S(1)}, f32[11,16,256]{2,1,0:T(8,128)S(1)}, u32[]{:S(2)}, u32[]{:S(2)}) collective-permute-start(f32[11,16,256]{2,1,0:T(8,128)S(1)} %get-tuple-element.24), channel_id=1, source_target_pairs={{0,1},{1,0},{2,3},{3,2},{4,5},{5,4},{6,7},{7,6},{8,9},{9,8},{10,11... | collective-permute-start | bytes 540680 | tf_op jit(solution)/shard_map/ppermute | solution.py:501
  5.4 5.1 %collective-permute-start.1 = (f32[11,16,256]{2,1,0:T(8,128)S(1)}, f32[11,16,256]{2,1,0:T(8,128)S(1)}, u32[]{:S(2)}, u32[]{:S(2)}) collective-permute-start(f32[11,16,256]{2,1,0:T(8,128)S(1)} %get-tuple-element.25), channel_id=1, source_target_pairs={{0,32},{32,0},{64,96},{96,64},{128,160},{160,128},{192,224},{224,1... | collective-permute-start | bytes 540680 | tf_op jit(solution)/shard_map/ppermute | solution.py:501
  11.2 8.6 %collective-permute-start.2 = (f32[232,256]{1,0:T(8,128)S(1)}, f32[232,256]{1,0:T(8,128)S(1)}, u32[]{:S(2)}, u32[]{:S(2)}) collective-permute-start(f32[232,256]{1,0:T(8,128)S(1)} %get-tuple-element.26), channel_id=1, source_target_pairs={{0,32},{1,2},{2,1},{3,4},{4,3},{5,6},{6,5},{7,8},{8,7},{9,10},{10,... | collective-permute-start | bytes 712712 | tf_op jit(solution)/shard_map/ppermute | solution.py:503
  13.8 6.9 %collective-permute-start.3 = (f32[232,256]{1,0:T(8,128)S(1)}, f32[232,256]{1,0:T(8,128)S(1)}, u32[]{:S(2)}, u32[]{:S(2)}) collective-permute-start(f32[232,256]{1,0:T(8,128)S(1)} %get-tuple-element.27), channel_id=1, source_target_pairs={{0,1},{1,0},{2,3},{3,2},{4,5},{5,4},{6,7},{7,6},{8,9},{9,8},{10,11... | collective-permute-start | bytes 712712 | tf_op jit(solution)/shard_map/ppermute | solution.py:503
  23.1 11.6 %collective-permute-start.5 = (f32[208,256]{1,0:T(8,128)S(1)}, f32[208,256]{1,0:T(8,128)S(1)}, u32[]{:S(2)}, u32[]{:S(2)}) collective-permute-start(f32[208,256]{1,0:T(8,128)S(1)} %get-tuple-element.29), channel_id=1, source_target_pairs={{0,224},{32,64},{64,32},{96,128},{128,96},{160,192},{192,160},{224... | collective-permute-start | bytes 638984 | tf_op jit(solution)/shard_map/ppermute | solution.py:511
  27.5 9.6 %collective-permute-start.7 = (f32[64,256]{1,0:T(8,128)S(1)}, f32[64,256]{1,0:T(8,128)S(1)}, u32[]{:S(2)}, u32[]{:S(2)}) collective-permute-start(f32[64,256]{1,0:T(8,128)S(1)} %get-tuple-element.28.refs_1_), channel_id=1, source_target_pairs={{0,128},{32,160},{64,192},{96,224},{128,0},{160,32},{192,64},{224,... | collective-permute-start | bytes 196616 | tf_op jit(solution)/shard_map/ppermute | solution.py:512
  30.7 6.9 %collective-permute-start.6 = (f32[64,256]{1,0:T(8,128)S(1)}, f32[64,256]{1,0:T(8,128)S(1)}, u32[]{:S(2)}, u32[]{:S(2)}) collective-permute-start(f32[64,256]{1,0:T(8,128)S(1)} %get-tuple-element.28.refs_1_), channel_id=1, source_target_pairs={{0,64},{32,224},{64,128},{96,32},{128,192},{160,96},{192,0},{224,1... | collective-permute-start | bytes 196616 | tf_op jit(solution)/shard_map/ppermute | solution.py:513
  34.7 5.6 %collective-permute-start.4 = (f32[208,256]{1,0:T(8,128)S(1)}, f32[208,256]{1,0:T(8,128)S(1)}, u32[]{:S(2)}, u32[]{:S(2)}) collective-permute-start(f32[208,256]{1,0:T(8,128)S(1)} %get-tuple-element.29), channel_id=1, source_target_pairs={{0,32},{32,0},{64,96},{96,64},{128,160},{160,128},{192,224},{224,1... | collective-permute-start | bytes 638984 | tf_op jit(solution)/shard_map/ppermute | solution.py:514
  37.5 3.8 %collective-permute-start.8 = (f32[192,256]{1,0:T(8,128)S(1)}, f32[192,256]{1,0:T(8,128)S(1)}, u32[]{:S(2)}, u32[]{:S(2)}) collective-permute-start(f32[192,256]{1,0:T(8,128)S(1)} %pad_maximum_fusion), channel_id=1, source_target_pairs={{0,32},{32,0},{64,96},{96,64},{128,160},{160,128},{192,224},{224,1... | collective-permute-start | bytes 589832 | tf_op jit(solution)/shard_map/ppermute | solution.py:515
  42.9 8.4 %collective-permute-start.9 = (f32[192,128]{1,0:T(8,128)S(1)}, f32[192,128]{1,0:T(8,128)S(1)}, u32[]{:S(2)}, u32[]{:S(2)}) collective-permute-start(f32[192,128]{1,0:T(8,128)S(1)} %get-tuple-element.31), channel_id=1, source_target_pairs={{0,1},{1,2},{2,3},{3,4},{4,5},{5,6},{6,7},{7,8},{8,9},{9,10},{10,1... | collective-permute-start | bytes 294920 | tf_op jit(solution)/shard_map/ppermute | solution.py:527
  45.9 5.3 %collective-permute-start.10 = (f32[80,128]{1,0:T(8,128)S(1)}, f32[80,128]{1,0:T(8,128)S(1)}, u32[]{:S(2)}, u32[]{:S(2)}) collective-permute-start(f32[80,128]{1,0:T(8,128)S(1)} %get-tuple-element.30.refs_1_), channel_id=1, source_target_pairs={{0,2},{1,3},{2,4},{3,5},{4,6},{5,7},{6,8},{7,9},{8,10},{9,11},{10,... | collective-permute-start | bytes 122888 | tf_op jit(solution)/shard_map/ppermute | solution.py:528
  51.3 1.6 %collective-permute-start.11 = (f32[272,128]{1,0:T(8,128)S(1)}, f32[272,128]{1,0:T(8,128)S(1)}, u32[]{:S(2)}, u32[]{:S(2)}) collective-permute-start(f32[272,128]{1,0:T(8,128)S(1)} %pad_maximum_fusion.3), channel_id=1, source_target_pairs={{0,32},{32,0},{64,96},{96,64},{128,160},{160,128},{192,224},{224,1... | collective-permute-start | bytes 417800 | tf_op jit(solution)/shard_map/ppermute | solution.py:529

commit v10 on v9

--- a/solution.py
+++ b/solution.py
@@ -159,7 +159,7 @@
 
 
 def pack_second(idx, f, e, cross, inner, even_o, odd_o):
-    even = idx[1] % 2 == 0
+    even = (idx[0] + idx[1]) % 2 == 0
 
     def write(at, rows, value):
         size = value.shape[0]
@@ -190,7 +190,7 @@
     g, d = idx[0], idx[1]
     low_x, high_x = jnp.where(g > 0, 1.0, 0.0), jnp.where(g < groups - 1, 1.0, 0.0)
     low_y, high_y = jnp.where(d > 0, 1.0, 0.0), jnp.where(d < devs - 1, 1.0, 0.0)
-    even_dev = d % 2 == 0
+    even_dev = (g + d) % 2 == 0
 
     def halo_second(at):
         a, b = odd[at, :], even[at, :]
@@ -477,14 +477,16 @@
     beside = [(i, (i + 1) % groups if i % 2 else (i - 1) % groups) for i in range(groups)]
     next_chip = [(i, (i - 2) % groups if i % 2 else (i + 2) % groups) for i in range(groups)]
     far_chip = [(i, (i + 4) % groups) for i in range(groups)]
-    even = [(i, i ^ 1) for i in range(devs)]
 
     def pairs_of(to):
         every = [(g, d) for g in range(groups) for d in range(devs)]
         return [(g * devs + d, to(g, d)[0] * devs + to(g, d)[1]) for g, d in every]
 
     cross_pairs = pairs_of(lambda g, d: (beside[g][1], d) if 0 < g < groups - 1 else (g, d ^ 1))
-    odd_pairs = pairs_of(lambda g, d: (g, d + 1 if d % 2 else d - 1) if 0 < d < devs - 1 else (g ^ 1, d))
+
+    def second(first_core):
+        odd = lambda g, d: (g, d + 1 if d % 2 else d - 1) if 0 < d < devs - 1 else (g ^ 2, d)
+        return pairs_of(lambda g, d: odd(g, d) if g % 2 == first_core else (g, d ^ 1))
 
     def along(step):
         def to(g, d):
@@ -500,7 +502,7 @@
     cross, inner = lax.optimization_barrier((cross, inner))
     cross, inner = lax.ppermute(cross, ("grp", "dev"), cross_pairs), lax.ppermute(inner, "grp", swap)
     to_even, to_odd = call(pack_second, [(SECOND_ROWS, 256)] * 2, [], idx, forcing, viscosity, cross, inner)
-    from_odd, from_even = lax.ppermute(to_odd, ("grp", "dev"), odd_pairs), lax.ppermute(to_even, "dev", even)
+    from_odd, from_even = lax.ppermute(to_odd, ("grp", "dev"), second(0)), lax.ppermute(to_even, ("grp", "dev"), second(1))
     mid, pay, x1, ew, wt, fw = call(
         lambda *refs: fine_down(groups, devs, *refs),
         [(64, 256), (208, 256), (4, 8, 2, 32, 128), (10, 2, 32, 128), (8, 2, 32, 128), (4, 8, 2, 32, 128)],

time: 57.5 us -> 61.2 us (1.064)
  the two profiles are of different devices: /device:TPU:9 before, /device:TPU:31 now
where the time goes in v10:
time: 61.2 us; the launch traced here: 61.1 us
  starting transfers between devices  25.1 us (41%)
  waiting for transfers between devices  25 us (41%)
  Pallas kernels  9.08 us (15%)
  local copies, waits for them, and re-layouts  1.05 us (2%)
  between operations  0.75 us (1%)
    pallas_call x4, Pallas kernels, call(): pl.pallas_call(kernel, out_shape=[jax.ShapeDtypeStruct(shape, F32) for sh...  9.08 us
    ppermute x1, starting transfers between devices, local(): xco = lax.ppermute(pay, 'grp', beside)  7.5 us
    ppermute x1, waiting for transfers between devices, local(): by2 = lax.ppermute(low, ('grp', 'dev'), along(2))  6.31 us
    ppermute x1, waiting for transfers between devices, local(): lax.ppermute(to_odd, ('grp', 'dev'), second(0))  5.82 us
    ppermute x1, waiting for transfers between devices, local(): lax.ppermute(cross, ('grp', 'dev'), cross_pairs)  5.03 us
    ppermute x1, starting transfers between devices, local(): swapped = lax.ppermute(jnp.concatenate([by1, by2], axis=0), 'grp', swap)  3.85 us
    ppermute x1, waiting for transfers between devices, local(): c2 = lax.ppermute(mid, 'grp', far_chip)  3.83 us
    ppermute x1, starting transfers between devices, local(): cpm = lax.ppermute(mid, 'grp', next_chip)  3.69 us
  transfers between devices with their start and end apart: 12, of which 8 were waited for; matrix products, arithmetic and copies ran while one was open for 0% of the time, Pallas kernels for 0%

profile of v10, /device:TPU:31, one launch (start us, length us, event | category | flops | bytes accessed | tf_op | source)
XLA Modules:
  0.0 61.1 jit_solution(17568774491452694958)
XLA Ops:
  0.6 0.0 copy-start.1
  0.7 1.0 %fusion.2 = (f32[4,2,16,256]{3,2,1,0:T(8,128)S(1)}, f32[4,2,16,256]{3,2,1,0:T(8,128)S(1)}) fusion(f32[4,4,16,256]{3,2,1,0:T(8,128)} %refs_1_.1), kind=kLoop, calls=%fused_computation.7 | loop fusion | bytes 524288 | tf_op jit(solution)/shard_map/slice | solution.py:498
  1.7 0.0 copy-done.1
  1.7 0.0 copy-start
  1.8 3.6 %collective-permute-start = (f32[11,16,256]{2,1,0:T(8,128)S(1)}, f32[11,16,256]{2,1,0:T(8,128)S(1)}, u32[]{:S(2)}, u32[]{:S(2)}) collective-permute-start(f32[11,16,256]{2,1,0:T(8,128)S(1)} %get-tuple-element.24), channel_id=1, source_target_pairs={{0,1},{1,0},{2,3},{3,2},{4,5},{5,4},{6,7},{7,6},{8,9},{9,8},{10,11... | collective-permute-start | bytes 540680 | tf_op jit(solution)/shard_map/ppermute | solution.py:503
  5.4 0.0 collective-permute-start.1
  5.4 0.1 pad_add_fusion.idx.refs_0_
  5.5 5.0 %collective-permute-done.cross.refs_3_ = f32[11,16,256]{2,1,0:T(8,128)S(1)} collective-permute-done((f32[11,16,256]{2,1,0:T(8,128)S(1)}, f32[11,16,256]{2,1,0:T(8,128)S(1)}, u32[]{:S(2)}, u32[]{:S(2)}) %collective-permute-start) | collective-permute-done | bytes 180256 | tf_op jit(solution)/shard_map/ppermute | solution.py:503
  10.5 0.0 collective-permute-done.1.inner.refs_4_
  10.5 0.0 copy-done
  10.5 0.6 %shard_map.41 = (f32[232,256]{1,0:T(8,128)S(1)}, f32[232,256]{1,0:T(8,128)S(1)}) custom-call(s32[2]{0:T(128)S(1)} %pad_add_fusion.idx.refs_0_, f32[4,4,16,256]{3,2,1,0:T(8,128)S(1)} %copy-done, f32[4,16,256]{2,1,0:T(8,128)S(1)} %copy-done.1, f32[11,16,256]{2,1,0:T(8,128)S(1)} %collective-permute-done.cross.refs_3_, ...), custom_call_target="tpu_custom_call" | custom-call | tf_op jit(solution)/shard_map/pallas_call | solution.py:463
  11.2 0.6 %collective-permute-start.2 = (f32[232,256]{1,0:T(8,128)S(1)}, f32[232,256]{1,0:T(8,128)S(1)}, u32[]{:S(2)}, u32[]{:S(2)}) collective-permute-start(f32[232,256]{1,0:T(8,128)S(1)} %get-tuple-element.26), channel_id=1, source_target_pairs={{0,64},{1,2},{2,1},{3,4},{4,3},{5,6},{6,5},{7,8},{8,7},{9,10},{10,... | collective-permute-start | bytes 712712 | tf_op jit(solution)/shard_map/ppermute | solution.py:505
  11.8 1.0 %collective-permute-start.3 = (f32[232,256]{1,0:T(8,128)S(1)}, f32[232,256]{1,0:T(8,128)S(1)}, u32[]{:S(2)}, u32[]{:S(2)}) collective-permute-start(f32[232,256]{1,0:T(8,128)S(1)} %get-tuple-element.27), channel_id=1, source_target_pairs={{0,1},{1,0},{2,3},{3,2},{4,5},{5,4},{6,7},{7,6},{8,9},{9,8},{10,11... | collective-permute-start | bytes 712712 | tf_op jit(solution)/shard_map/ppermute | solution.py:505
  12.8 5.8 %collective-permute-done.2.refs_5_ = f32[232,256]{1,0:T(8,128)S(1)} collective-permute-done((f32[232,256]{1,0:T(8,128)S(1)}, f32[232,256]{1,0:T(8,128)S(1)}, u32[]{:S(2)}, u32[]{:S(2)}) %collective-permute-start.2) | collective-permute-done | bytes 237600 | tf_op jit(solution)/shard_map/ppermute | solution.py:505
  18.6 0.2 collective-permute-done.3.refs_6_
  18.9 2.4 %shard_map.42 = (f32[64,256]{1,0:T(8,128)S(1)}, f32[208,256]{1,0:T(8,128)S(1)}, f32[4,8,2,32,128]{4,3,2,1,0:T(8,128)S(1)}, f32[10,2,32,128]{3,2,1,0:T(8,128)S(1)...) custom-call(s32[2]{0:T(128)S(1)} %pad_add_fusion.idx.refs_0_, f32[4,4,16,256]{3,2,1,0:T(8,128)S(1)} %copy-done, ...), custom_call_target="tpu_custom_call" | custom-call | tf_op jit(solution)/shard_map/pallas_call | solution.py:463
  21.3 7.5 %collective-permute-start.5 = (f32[208,256]{1,0:T(8,128)S(1)}, f32[208,256]{1,0:T(8,128)S(1)}, u32[]{:S(2)}, u32[]{:S(2)}) collective-permute-start(f32[208,256]{1,0:T(8,128)S(1)} %get-tuple-element.29), channel_id=1, source_target_pairs={{0,224},{32,64},{64,32},{96,128},{128,96},{160,192},{192,160},{224... | collective-permute-start | bytes 638984 | tf_op jit(solution)/shard_map/ppermute | solution.py:513
  28.8 1.9 %collective-permute-start.7 = (f32[64,256]{1,0:T(8,128)S(1)}, f32[64,256]{1,0:T(8,128)S(1)}, u32[]{:S(2)}, u32[]{:S(2)}) collective-permute-start(f32[64,256]{1,0:T(8,128)S(1)} %get-tuple-element.28.refs_1_), channel_id=1, source_target_pairs={{0,128},{32,160},{64,192},{96,224},{128,0},{160,32},{192,64},{224,... | collective-permute-start | bytes 196616 | tf_op jit(solution)/shard_map/ppermute | solution.py:514
  30.7 3.7 %collective-permute-start.6 = (f32[64,256]{1,0:T(8,128)S(1)}, f32[64,256]{1,0:T(8,128)S(1)}, u32[]{:S(2)}, u32[]{:S(2)}) collective-permute-start(f32[64,256]{1,0:T(8,128)S(1)} %get-tuple-element.28.refs_1_), channel_id=1, source_target_pairs={{0,64},{32,224},{64,128},{96,32},{128,192},{160,96},{192,0},{224,1... | collective-permute-start | bytes 196616 | tf_op jit(solution)/shard_map/ppermute | solution.py:515
  34.4 0.0 collective-permute-start.4
  34.4 1.4 %collective-permute-done.5.refs_3_.refs_14_ = f32[208,256]{1,0:T(8,128)S(1)} collective-permute-done((f32[208,256]{1,0:T(8,128)S(1)}, f32[208,256]{1,0:T(8,128)S(1)}, u32[]{:S(2)}, u32[]{:S(2)}) %collective-permute-start.5) | collective-permute-done | bytes 213024 | tf_op jit(solution)/shard_map/ppermute | solution.py:513
  35.7 3.8 %collective-permute-done.7.refs_5_ = f32[64,256]{1,0:T(8,128)S(1)} collective-permute-done((f32[64,256]{1,0:T(8,128)S(1)}, f32[64,256]{1,0:T(8,128)S(1)}, u32[]{:S(2)}, u32[]{:S(2)}) %collective-permute-start.7) | collective-permute-done | bytes 65568 | tf_op jit(solution)/shard_map/ppermute | solution.py:514
  39.6 0.0 collective-permute-done.6.refs_4_
  39.6 0.1 collective-permute-start.8
  39.7 0.0 collective-permute-done.4.refs_2_.refs_13_
  39.7 1.4 %collective-permute-done.8.refs_6_ = f32[192,256]{1,0:T(8,128)S(1)} collective-permute-done((f32[192,256]{1,0:T(8,128)S(1)}, f32[192,256]{1,0:T(8,128)S(1)}, u32[]{:S(2)}, u32[]{:S(2)}) %collective-permute-start.8) | collective-permute-done | bytes 196640 | tf_op jit(solution)/shard_map/ppermute | solution.py:517
  41.1 1.5 %shard_map.43 = (f32[192,128]{1,0:T(8,128)S(1)}, f32[80,128]{1,0:T(8,128)S(1)}, f32[4,10,16,128]{3,2,1,0:T(8,128)S(1)}, f32[4,10,16,128]{3,2,1,0:T(8,128)S(1)}, ...) custom-call(s32[2]{0:T(128)S(1)} %pad_add_fusion.idx.refs_0_, f32[64,256]{1,0:T(8,128)S(1)} %get-tuple-element.28.refs_1_, ...), custom_call_target="tpu_custom_call" | custom-call | tf_op jit(solution)/shard_map/pallas_call | solution.py:463
  42.7 0.1 collective-permute-start.9
  42.8 2.7 %collective-permute-start.10 = (f32[80,128]{1,0:T(8,128)S(1)}, f32[80,128]{1,0:T(8,128)S(1)}, u32[]{:S(2)}, u32[]{:S(2)}) collective-permute-start(f32[80,128]{1,0:T(8,128)S(1)} %get-tuple-element.30.refs_1_), channel_id=1, source_target_pairs={{0,2},{1,3},{2,4},{3,5},{4,6},{5,7},{6,8},{7,9},{8,10},{9,11},{10,... | collective-permute-start | bytes 122888 | tf_op jit(solution)/shard_map/ppermute | solution.py:530
  45.4 6.3 %collective-permute-done.10.refs_3_ = f32[80,128]{1,0:T(8,128)S(1)} collective-permute-done((f32[80,128]{1,0:T(8,128)S(1)}, f32[80,128]{1,0:T(8,128)S(1)}, u32[]{:S(2)}, u32[]{:S(2)}) %collective-permute-start.10) | collective-permute-done | bytes 40992 | tf_op jit(solution)/shard_map/ppermute | solution.py:530
  51.7 0.0 collective-permute-done.9.refs_2_
  51.8 3.9 %collective-permute-start.11 = (f32[272,128]{1,0:T(8,128)S(1)}, f32[272,128]{1,0:T(8,128)S(1)}, u32[]{:S(2)}, u32[]{:S(2)}) collective-permute-start(f32[272,128]{1,0:T(8,128)S(1)} %pad_maximum_fusion.3), channel_id=1, source_target_pairs={{0,32},{32,0},{64,96},{96,64},{128,160},{160,128},{192,224},{224,1... | collective-permute-start | bytes 417800 | tf_op jit(solution)/shard_map/ppermute | solution.py:531
  55.6 1.0 %collective-permute-done.11.refs_4_ = f32[272,128]{1,0:T(8,128)S(1)} collective-permute-done((f32[272,128]{1,0:T(8,128)S(1)}, f32[272,128]{1,0:T(8,128)S(1)}, u32[]{:S(2)}, u32[]{:S(2)}) %collective-permute-start.11) | collective-permute-done | bytes 139296 | tf_op jit(solution)/shard_map/ppermute | solution.py:531
  56.6 4.5 %shard_map.44 = (f32[4,4,16,256]{3,2,1,0:T(8,128)}, f32[4,4,16,256]{3,2,1,0:T(8,128)}) custom-call(s32[2]{0:T(128)S(1)} %pad_add_fusion.idx.refs_0_, f32[80,128]{1,0:T(8,128)S(1)} %get-tuple-element.30.refs_1_, f32[192,128]{1,0:T(8,128)S(1)} %collective-permute-done.9.refs_2_, f32[80,128]{1,0:T(8,128)S(1)} %collective-permute-done.10.refs_3_, ...), custom_call_target="tpu_custom_call" | custom-call | tf_op jit(solution)/shard_map/pallas_call | solution.py:463
  (5 shorter events, 0.1 us)
Async XLA Ops:
  0.6 1.0 %copy-start.1 = (f32[4,16,256]{2,1,0:T(8,128)S(1)}, f32[4,16,256]{2,1,0:T(8,128)}, u32[]{:S(2)}) copy-start(f32[4,16,256]{2,1,0:T(8,128)} %refs_2_.1) | copy-start | bytes 196612
  1.7 8.8 %copy-start = (f32[4,4,16,256]{3,2,1,0:T(8,128)S(1)}, f32[4,4,16,256]{3,2,1,0:T(8,128)}, u32[]{:S(2)}) copy-start(f32[4,4,16,256]{3,2,1,0:T(8,128)} %refs_1_.1) | copy-start | bytes 786436
  1.8 8.7 %collective-permute-start = (f32[11,16,256]{2,1,0:T(8,128)S(1)}, f32[11,16,256]{2,1,0:T(8,128)S(1)}, u32[]{:S(2)}, u32[]{:S(2)}) collective-permute-start(f32[11,16,256]{2,1,0:T(8,128)S(1)} %get-tuple-element.24), channel_id=1, source_target_pairs={{0,1},{1,0},{2,3},{3,2},{4,5},{5,4},{6,7},{7,6},{8,9},{9,8},{10,11... | collective-permute-start | bytes 540680 | tf_op jit(solution)/shard_map/ppermute | solution.py:503
  5.4 5.1 %collective-permute-start.1 = (f32[11,16,256]{2,1,0:T(8,128)S(1)}, f32[11,16,256]{2,1,0:T(8,128)S(1)}, u32[]{:S(2)}, u32[]{:S(2)}) collective-permute-start(f32[11,16,256]{2,1,0:T(8,128)S(1)} %get-tuple-element.25), channel_id=1, source_target_pairs={{0,32},{32,0},{64,96},{96,64},{128,160},{160,128},{192,224},{224,1... | collective-permute-start | bytes 540680 | tf_op jit(solution)/shard_map/ppermute | solution.py:503
  11.2 7.5 %collective-permute-start.2 = (f32[232,256]{1,0:T(8,128)S(1)}, f32[232,256]{1,0:T(8,128)S(1)}, u32[]{:S(2)}, u32[]{:S(2)}) collective-permute-start(f32[232,256]{1,0:T(8,128)S(1)} %get-tuple-element.26), channel_id=1, source_target_pairs={{0,64},{1,2},{2,1},{3,4},{4,3},{5,6},{6,5},{7,8},{8,7},{9,10},{10,... | collective-permute-start | bytes 712712 | tf_op jit(solution)/shard_map/ppermute | solution.py:505
  11.8 7.1 %collective-permute-start.3 = (f32[232,256]{1,0:T(8,128)S(1)}, f32[232,256]{1,0:T(8,128)S(1)}, u32[]{:S(2)}, u32[]{:S(2)}) collective-permute-start(f32[232,256]{1,0:T(8,128)S(1)} %get-tuple-element.27), channel_id=1, source_target_pairs={{0,1},{1,0},{2,3},{3,2},{4,5},{5,4},{6,7},{7,6},{8,9},{9,8},{10,11... | collective-permute-start | bytes 712712 | tf_op jit(solution)/shard_map/ppermute | solution.py:505
  21.3 14.4 %collective-permute-start.5 = (f32[208,256]{1,0:T(8,128)S(1)}, f32[208,256]{1,0:T(8,128)S(1)}, u32[]{:S(2)}, u32[]{:S(2)}) collective-permute-start(f32[208,256]{1,0:T(8,128)S(1)} %get-tuple-element.29), channel_id=1, source_target_pairs={{0,224},{32,64},{64,32},{96,128},{128,96},{160,192},{192,160},{224... | collective-permute-start | bytes 638984 | tf_op jit(solution)/shard_map/ppermute | solution.py:513
  28.8 10.8 %collective-permute-start.7 = (f32[64,256]{1,0:T(8,128)S(1)}, f32[64,256]{1,0:T(8,128)S(1)}, u32[]{:S(2)}, u32[]{:S(2)}) collective-permute-start(f32[64,256]{1,0:T(8,128)S(1)} %get-tuple-element.28.refs_1_), channel_id=1, source_target_pairs={{0,128},{32,160},{64,192},{96,224},{128,0},{160,32},{192,64},{224,... | collective-permute-start | bytes 196616 | tf_op jit(solution)/shard_map/ppermute | solution.py:514
  30.7 8.9 %collective-permute-start.6 = (f32[64,256]{1,0:T(8,128)S(1)}, f32[64,256]{1,0:T(8,128)S(1)}, u32[]{:S(2)}, u32[]{:S(2)}) collective-permute-start(f32[64,256]{1,0:T(8,128)S(1)} %get-tuple-element.28.refs_1_), channel_id=1, source_target_pairs={{0,64},{32,224},{64,128},{96,32},{128,192},{160,96},{192,0},{224,1... | collective-permute-start | bytes 196616 | tf_op jit(solution)/shard_map/ppermute | solution.py:515
  34.4 5.3 %collective-permute-start.4 = (f32[208,256]{1,0:T(8,128)S(1)}, f32[208,256]{1,0:T(8,128)S(1)}, u32[]{:S(2)}, u32[]{:S(2)}) collective-permute-start(f32[208,256]{1,0:T(8,128)S(1)} %get-tuple-element.29), channel_id=1, source_target_pairs={{0,32},{32,0},{64,96},{96,64},{128,160},{160,128},{192,224},{224,1... | collective-permute-start | bytes 638984 | tf_op jit(solution)/shard_map/ppermute | solution.py:516
  39.6 1.5 %collective-permute-start.8 = (f32[192,256]{1,0:T(8,128)S(1)}, f32[192,256]{1,0:T(8,128)S(1)}, u32[]{:S(2)}, u32[]{:S(2)}) collective-permute-start(f32[192,256]{1,0:T(8,128)S(1)} %pad_maximum_fusion), channel_id=1, source_target_pairs={{0,32},{32,0},{64,96},{96,64},{128,160},{160,128},{192,224},{224,1... | collective-permute-start | bytes 589832 | tf_op jit(solution)/shard_map/ppermute | solution.py:517
  42.7 9.1 %collective-permute-start.9 = (f32[192,128]{1,0:T(8,128)S(1)}, f32[192,128]{1,0:T(8,128)S(1)}, u32[]{:S(2)}, u32[]{:S(2)}) collective-permute-start(f32[192,128]{1,0:T(8,128)S(1)} %get-tuple-element.31), channel_id=1, source_target_pairs={{0,1},{1,2},{2,3},{3,4},{4,5},{5,6},{6,7},{7,8},{8,9},{9,10},{10,1... | collective-permute-start | bytes 294920 | tf_op jit(solution)/shard_map/ppermute | solution.py:529
  42.8 9.0 %collective-permute-start.10 = (f32[80,128]{1,0:T(8,128)S(1)}, f32[80,128]{1,0:T(8,128)S(1)}, u32[]{:S(2)}, u32[]{:S(2)}) collective-permute-start(f32[80,128]{1,0:T(8,128)S(1)} %get-tuple-element.30.refs_1_), channel_id=1, source_target_pairs={{0,2},{1,3},{2,4},{3,5},{4,6},{5,7},{6,8},{7,9},{8,10},{9,11},{10,... | collective-permute-start | bytes 122888 | tf_op jit(solution)/shard_map/ppermute | solution.py:530
  51.8 4.9 %collective-permute-start.11 = (f32[272,128]{1,0:T(8,128)S(1)}, f32[272,128]{1,0:T(8,128)S(1)}, u32[]{:S(2)}, u32[]{:S(2)}) collective-permute-start(f32[272,128]{1,0:T(8,128)S(1)} %pad_maximum_fusion.3), channel_id=1, source_target_pairs={{0,32},{32,0},{64,96},{96,64},{128,160},{160,128},{192,224},{224,1... | collective-permute-start | bytes 417800 | tf_op jit(solution)/shard_map/ppermute | solution.py:531

commit v11 on v9

--- a/solution.py
+++ b/solution.py
@@ -255,7 +255,7 @@
             pay_o[at : at + 18, :] = get(x1, (c, 3 + j), 7, 18)
 
 
-def mid_down(groups, devs, idx, own, partner, xco, cpm, c2, s3, next_o, low_o, y_o, b_o, e_o, w_o, bw, ew, wt, y0, y1, pair, low):
+def mid_down(groups, devs, idx, own, partner, xco, cpm, c2, s1, s3, next_o, low_o, y_o, b_o, e_o, w_o, bw, ew, wt, y0, y1, pair, low):
     g, d = idx[0], idx[1]
     chips = groups // 2
     chip, core = g // 2, g % 2
@@ -289,10 +289,10 @@
     place(partner, 0, chip, other)
     place(xco, 0, beside, other)
     place(cpm, 0, beside, core)
-    place(s3, 0, across, core)
-    place(s3, 64, across, other)
+    place(s1, 0, across, core)
+    place(s3, 0, across, other)
     place(c2, 0, far, core)
-    place(s3, 128, far, other)
+    place(s3, 64, far, other)
     for i in range(4, layers + 4):
         for row in (0, 8):
             inside = rows_inside(row, 8 * d - 4, 8 * devs, 128)
@@ -512,7 +512,8 @@
     c2 = lax.ppermute(mid, "grp", far_chip)
     cpm = lax.ppermute(mid, "grp", next_chip)
     partner = lax.ppermute(pay, "grp", swap)
-    s3 = lax.ppermute(jnp.concatenate([xco[:64], cpm, c2], axis=0), "grp", swap)
+    s1 = lax.ppermute(xco[:64], "grp", swap)
+    s3 = lax.ppermute(jnp.concatenate([cpm, c2], axis=0), "grp", swap)
 
     layers = 2 * groups + 8
     tall = 20 * (groups // 2)
@@ -521,7 +522,7 @@
         [(tall + 112, 128), (tall, 128), (4, 10, 16, 128), (4, 10, 16, 128), (10, 16, 128), (10, 16, 128)],
         [(4, layers, 16, 128), (layers, 16, 128), (layers, 16, 128), (4, layers, 16, 128), (4, layers, 16, 128),
          (groups, 5, 8, 128), (5, groups, 8, 128)],
-        idx, mid, partner, xco, cpm, c2, s3,
+        idx, mid, partner, xco, cpm, c2, s1, s3,
     )
 
     by1 = lax.ppermute(to_next, ("grp", "dev"), along(1))

time: 57.5 us -> 58.1 us (1.010)
  the two profiles are of different devices: /device:TPU:9 before, /device:TPU:49 now
where the time goes in v11:
time: 58.1 us; the launch traced here: 58 us
  starting transfers between devices  28.9 us (50%)
  waiting for transfers between devices  18.1 us (31%)
  Pallas kernels  9.08 us (16%)
  local copies, waits for them, and re-layouts  1.05 us (2%)
  between operations  0.73 us (1%)
    pallas_call x4, Pallas kernels, call(): pl.pallas_call(kernel, out_shape=[jax.ShapeDtypeStruct(shape, F32) for sh...  9.08 us
    ppermute x1, starting transfers between devices, local(): s3 = lax.ppermute(jnp.concatenate([cpm, c2], axis=0), 'grp', swap)  7.98 us
    ppermute x1, starting transfers between devices, local(): c2 = lax.ppermute(mid, 'grp', far_chip)  6.22 us
    ppermute x1, waiting for transfers between devices, local(): lax.ppermute(to_odd, ('grp', 'dev'), odd_pairs)  5.55 us
    ppermute x1, waiting for transfers between devices, local(): by2 = lax.ppermute(low, ('grp', 'dev'), along(2))  4.79 us
    ppermute x1, waiting for transfers between devices, local(): lax.ppermute(cross, ('grp', 'dev'), cross_pairs)  3.84 us
    ppermute x1, starting transfers between devices, local(): lax.ppermute(cross, ('grp', 'dev'), cross_pairs)  3.64 us
    ppermute x1, starting transfers between devices, local(): lax.ppermute(to_odd, ('grp', 'dev'), odd_pairs)  3.3 us
  transfers between devices with their start and end apart: 13, of which 7 were waited for; matrix products, arithmetic and copies ran while one was open for 0% of the time, Pallas kernels for 0%

profile of v11, /device:TPU:49, one launch (start us, length us, event | category | flops | bytes accessed | tf_op | source)
XLA Modules:
  0.0 58.0 jit_solution(10672563582360503166)
XLA Ops:
  0.6 0.0 copy-start.1
  0.7 1.0 %fusion.2 = (f32[4,2,16,256]{3,2,1,0:T(8,128)S(1)}, f32[4,2,16,256]{3,2,1,0:T(8,128)S(1)}) fusion(f32[4,4,16,256]{3,2,1,0:T(8,128)} %refs_1_.1), kind=kLoop, calls=%fused_computation.7 | loop fusion | bytes 524288 | tf_op jit(solution)/shard_map/slice | solution.py:496
  1.7 0.0 copy-done.1
  1.7 0.0 copy-start
  1.8 3.6 %collective-permute-start = (f32[11,16,256]{2,1,0:T(8,128)S(1)}, f32[11,16,256]{2,1,0:T(8,128)S(1)}, u32[]{:S(2)}, u32[]{:S(2)}) collective-permute-start(f32[11,16,256]{2,1,0:T(8,128)S(1)} %get-tuple-element.24), channel_id=1, source_target_pairs={{0,1},{1,0},{2,3},{3,2},{4,5},{5,4},{6,7},{7,6},{8,9},{9,8},{10,11... | collective-permute-start | bytes 540680 | tf_op jit(solution)/shard_map/ppermute | solution.py:501
  5.4 0.0 collective-permute-start.1
  5.4 0.1 pad_add_fusion.idx.refs_0_
  5.5 3.8 %collective-permute-done.cross.refs_3_ = f32[11,16,256]{2,1,0:T(8,128)S(1)} collective-permute-done((f32[11,16,256]{2,1,0:T(8,128)S(1)}, f32[11,16,256]{2,1,0:T(8,128)S(1)}, u32[]{:S(2)}, u32[]{:S(2)}) %collective-permute-start) | collective-permute-done | bytes 180256 | tf_op jit(solution)/shard_map/ppermute | solution.py:501
  9.3 0.0 collective-permute-done.1.inner.refs_4_
  9.3 0.0 copy-done
  9.3 0.6 %shard_map.41 = (f32[232,256]{1,0:T(8,128)S(1)}, f32[232,256]{1,0:T(8,128)S(1)}) custom-call(s32[2]{0:T(128)S(1)} %pad_add_fusion.idx.refs_0_, f32[4,4,16,256]{3,2,1,0:T(8,128)S(1)} %copy-done, f32[4,16,256]{2,1,0:T(8,128)S(1)} %copy-done.1, f32[11,16,256]{2,1,0:T(8,128)S(1)} %collective-permute-done.cross.refs_3_, ...), custom_call_target="tpu_custom_call" | custom-call | tf_op jit(solution)/shard_map/pallas_call | solution.py:463
  10.0 3.3 %collective-permute-start.2 = (f32[232,256]{1,0:T(8,128)S(1)}, f32[232,256]{1,0:T(8,128)S(1)}, u32[]{:S(2)}, u32[]{:S(2)}) collective-permute-start(f32[232,256]{1,0:T(8,128)S(1)} %get-tuple-element.26), channel_id=1, source_target_pairs={{0,32},{1,2},{2,1},{3,4},{4,3},{5,6},{6,5},{7,8},{8,7},{9,10},{10,... | collective-permute-start | bytes 712712 | tf_op jit(solution)/shard_map/ppermute | solution.py:503
  13.3 0.0 collective-permute-start.3
  13.3 5.6 %collective-permute-done.2.refs_5_ = f32[232,256]{1,0:T(8,128)S(1)} collective-permute-done((f32[232,256]{1,0:T(8,128)S(1)}, f32[232,256]{1,0:T(8,128)S(1)}, u32[]{:S(2)}, u32[]{:S(2)}) %collective-permute-start.2) | collective-permute-done | bytes 237600 | tf_op jit(solution)/shard_map/ppermute | solution.py:503
  18.8 0.2 collective-permute-done.3.refs_6_
  19.0 2.4 %shard_map.42 = (f32[64,256]{1,0:T(8,128)S(1)}, f32[208,256]{1,0:T(8,128)S(1)}, f32[4,8,2,32,128]{4,3,2,1,0:T(8,128)S(1)}, f32[10,2,32,128]{3,2,1,0:T(8,128)S(1)...) custom-call(s32[2]{0:T(128)S(1)} %pad_add_fusion.idx.refs_0_, f32[4,4,16,256]{3,2,1,0:T(8,128)S(1)} %copy-done, ...), custom_call_target="tpu_custom_call" | custom-call | tf_op jit(solution)/shard_map/pallas_call | solution.py:463
  21.4 6.2 %collective-permute-start.7 = (f32[64,256]{1,0:T(8,128)S(1)}, f32[64,256]{1,0:T(8,128)S(1)}, u32[]{:S(2)}, u32[]{:S(2)}) collective-permute-start(f32[64,256]{1,0:T(8,128)S(1)} %get-tuple-element.28.refs_1_), channel_id=1, source_target_pairs={{0,128},{32,160},{64,192},{96,224},{128,0},{160,32},{192,64},{224,... | collective-permute-start | bytes 196616 | tf_op jit(solution)/shard_map/ppermute | solution.py:512
  27.7 1.8 %collective-permute-start.6 = (f32[64,256]{1,0:T(8,128)S(1)}, f32[64,256]{1,0:T(8,128)S(1)}, u32[]{:S(2)}, u32[]{:S(2)}) collective-permute-start(f32[64,256]{1,0:T(8,128)S(1)} %get-tuple-element.28.refs_1_), channel_id=1, source_target_pairs={{0,64},{32,224},{64,128},{96,32},{128,192},{160,96},{192,0},{224,1... | collective-permute-start | bytes 196616 | tf_op jit(solution)/shard_map/ppermute | solution.py:513
  29.4 1.4 %collective-permute-start.5 = (f32[208,256]{1,0:T(8,128)S(1)}, f32[208,256]{1,0:T(8,128)S(1)}, u32[]{:S(2)}, u32[]{:S(2)}) collective-permute-start(f32[208,256]{1,0:T(8,128)S(1)} %get-tuple-element.29), channel_id=1, source_target_pairs={{0,224},{32,64},{64,32},{96,128},{128,96},{160,192},{192,160},{224... | collective-permute-start | bytes 638984 | tf_op jit(solution)/shard_map/ppermute | solution.py:511
  30.8 0.0 collective-permute-start.4
  30.8 0.0 collective-permute-done.7.refs_5_
  30.8 1.8 %collective-permute-done.6.refs_4_ = f32[64,256]{1,0:T(8,128)S(1)} collective-permute-done((f32[64,256]{1,0:T(8,128)S(1)}, f32[64,256]{1,0:T(8,128)S(1)}, u32[]{:S(2)}, u32[]{:S(2)}) %collective-permute-start.6) | collective-permute-done | bytes 65568 | tf_op jit(solution)/shard_map/ppermute | solution.py:513
  32.6 8.0 %collective-permute-start.9 = (f32[128,256]{1,0:T(8,128)S(1)}, f32[128,256]{1,0:T(8,128)S(1)}, u32[]{:S(2)}, u32[]{:S(2)}) collective-permute-start(f32[128,256]{1,0:T(8,128)S(1)} %pad_maximum_fusion.3), channel_id=1, source_target_pairs={{0,32},{32,0},{64,96},{96,64},{128,160},{160,128},{192,224},{224,1... | collective-permute-start | bytes 393224 | tf_op jit(solution)/shard_map/ppermute | solution.py:516
  40.6 0.0 collective-permute-done.5.refs_3_.refs_14_
  40.6 1.1 %collective-permute-start.8 = (f32[64,256]{1,0:T(8,128)S(1)}, f32[64,256]{1,0:T(8,128)S(1)}, u32[]{:S(2)}, u32[]{:S(2)}) collective-permute-start(f32[64,256]{1,0:T(8,128)S(1)} %slice.20), channel_id=1, source_target_pairs={{0,32},{32,0},{64,96},{96,64},{128,160},{160,128},{192,224},{224,1... | collective-permute-start | bytes 196616 | tf_op jit(solution)/shard_map/ppermute | solution.py:515
  41.7 0.0 collective-permute-done.9.refs_7_
  41.7 0.0 collective-permute-done.4.refs_2_.refs_13_
  41.7 0.9 %collective-permute-done.8.refs_6_ = f32[64,256]{1,0:T(8,128)S(1)} collective-permute-done((f32[64,256]{1,0:T(8,128)S(1)}, f32[64,256]{1,0:T(8,128)S(1)}, u32[]{:S(2)}, u32[]{:S(2)}) %collective-permute-start.8) | collective-permute-done | bytes 65568 | tf_op jit(solution)/shard_map/ppermute | solution.py:515
  42.6 1.5 %shard_map.43 = (f32[192,128]{1,0:T(8,128)S(1)}, f32[80,128]{1,0:T(8,128)S(1)}, f32[4,10,16,128]{3,2,1,0:T(8,128)S(1)}, f32[4,10,16,128]{3,2,1,0:T(8,128)S(1)}, ...) custom-call(s32[2]{0:T(128)S(1)} %pad_add_fusion.idx.refs_0_, f32[64,256]{1,0:T(8,128)S(1)} %get-tuple-element.28.refs_1_, ...), custom_call_target="tpu_custom_call" | custom-call | tf_op jit(solution)/shard_map/pallas_call | solution.py:463
  44.2 1.6 %collective-permute-start.10 = (f32[192,128]{1,0:T(8,128)S(1)}, f32[192,128]{1,0:T(8,128)S(1)}, u32[]{:S(2)}, u32[]{:S(2)}) collective-permute-start(f32[192,128]{1,0:T(8,128)S(1)} %get-tuple-element.31), channel_id=1, source_target_pairs={{0,1},{1,2},{2,3},{3,4},{4,5},{5,6},{6,7},{7,8},{8,9},{9,10},{10,1... | collective-permute-start | bytes 294920 | tf_op jit(solution)/shard_map/ppermute | solution.py:528
  45.7 0.0 collective-permute-start.11
  45.7 4.8 %collective-permute-done.11.refs_3_ = f32[80,128]{1,0:T(8,128)S(1)} collective-permute-done((f32[80,128]{1,0:T(8,128)S(1)}, f32[80,128]{1,0:T(8,128)S(1)}, u32[]{:S(2)}, u32[]{:S(2)}) %collective-permute-start.11) | collective-permute-done | bytes 40992 | tf_op jit(solution)/shard_map/ppermute | solution.py:529
  50.5 0.0 collective-permute-done.10.refs_2_
  50.5 2.0 %collective-permute-start.12 = (f32[272,128]{1,0:T(8,128)S(1)}, f32[272,128]{1,0:T(8,128)S(1)}, u32[]{:S(2)}, u32[]{:S(2)}) collective-permute-start(f32[272,128]{1,0:T(8,128)S(1)} %pad_maximum_fusion.2), channel_id=1, source_target_pairs={{0,32},{32,0},{64,96},{96,64},{128,160},{160,128},{192,224},{224,1... | collective-permute-start | bytes 417800 | tf_op jit(solution)/shard_map/ppermute | solution.py:530
  52.5 1.0 %collective-permute-done.12.refs_4_ = f32[272,128]{1,0:T(8,128)S(1)} collective-permute-done((f32[272,128]{1,0:T(8,128)S(1)}, f32[272,128]{1,0:T(8,128)S(1)}, u32[]{:S(2)}, u32[]{:S(2)}) %collective-permute-start.12) | collective-permute-done | bytes 139296 | tf_op jit(solution)/shard_map/ppermute | solution.py:530
  53.5 4.5 %shard_map.44 = (f32[4,4,16,256]{3,2,1,0:T(8,128)}, f32[4,4,16,256]{3,2,1,0:T(8,128)}) custom-call(s32[2]{0:T(128)S(1)} %pad_add_fusion.idx.refs_0_, f32[80,128]{1,0:T(8,128)S(1)} %get-tuple-element.30.refs_1_, f32[192,128]{1,0:T(8,128)S(1)} %collective-permute-done.10.refs_2_, f32[80,128]{1,0:T(8,128)S(1)} %collective-permute-done.11.refs_3_, ...), custom_call_target="tpu_custom_call" | custom-call | tf_op jit(solution)/shard_map/pallas_call | solution.py:463
  (5 shorter events, 0.1 us)
Async XLA Ops:
  0.6 1.0 %copy-start.1 = (f32[4,16,256]{2,1,0:T(8,128)S(1)}, f32[4,16,256]{2,1,0:T(8,128)}, u32[]{:S(2)}) copy-start(f32[4,16,256]{2,1,0:T(8,128)} %refs_2_.1) | copy-start | bytes 196612
  1.7 7.6 %copy-start = (f32[4,4,16,256]{3,2,1,0:T(8,128)S(1)}, f32[4,4,16,256]{3,2,1,0:T(8,128)}, u32[]{:S(2)}) copy-start(f32[4,4,16,256]{3,2,1,0:T(8,128)} %refs_1_.1) | copy-start | bytes 786436
  1.8 7.6 %collective-permute-start = (f32[11,16,256]{2,1,0:T(8,128)S(1)}, f32[11,16,256]{2,1,0:T(8,128)S(1)}, u32[]{:S(2)}, u32[]{:S(2)}) collective-permute-start(f32[11,16,256]{2,1,0:T(8,128)S(1)} %get-tuple-element.24), channel_id=1, source_target_pairs={{0,1},{1,0},{2,3},{3,2},{4,5},{5,4},{6,7},{7,6},{8,9},{9,8},{10,11... | collective-permute-start | bytes 540680 | tf_op jit(solution)/shard_map/ppermute | solution.py:501
  5.4 3.9 %collective-permute-start.1 = (f32[11,16,256]{2,1,0:T(8,128)S(1)}, f32[11,16,256]{2,1,0:T(8,128)S(1)}, u32[]{:S(2)}, u32[]{:S(2)}) collective-permute-start(f32[11,16,256]{2,1,0:T(8,128)S(1)} %get-tuple-element.25), channel_id=1, source_target_pairs={{0,32},{32,0},{64,96},{96,64},{128,160},{160,128},{192,224},{224,1... | collective-permute-start | bytes 540680 | tf_op jit(solution)/shard_map/ppermute | solution.py:501
  10.0 8.9 %collective-permute-start.2 = (f32[232,256]{1,0:T(8,128)S(1)}, f32[232,256]{1,0:T(8,128)S(1)}, u32[]{:S(2)}, u32[]{:S(2)}) collective-permute-start(f32[232,256]{1,0:T(8,128)S(1)} %get-tuple-element.26), channel_id=1, source_target_pairs={{0,32},{1,2},{2,1},{3,4},{4,3},{5,6},{6,5},{7,8},{8,7},{9,10},{10,... | collective-permute-start | bytes 712712 | tf_op jit(solution)/shard_map/ppermute | solution.py:503
  13.3 5.8 %collective-permute-start.3 = (f32[232,256]{1,0:T(8,128)S(1)}, f32[232,256]{1,0:T(8,128)S(1)}, u32[]{:S(2)}, u32[]{:S(2)}) collective-permute-start(f32[232,256]{1,0:T(8,128)S(1)} %get-tuple-element.27), channel_id=1, source_target_pairs={{0,1},{1,0},{2,3},{3,2},{4,5},{5,4},{6,7},{7,6},{8,9},{9,8},{10,11... | collective-permute-start | bytes 712712 | tf_op jit(solution)/shard_map/ppermute | solution.py:503
  21.4 9.4 %collective-permute-start.7 = (f32[64,256]{1,0:T(8,128)S(1)}, f32[64,256]{1,0:T(8,128)S(1)}, u32[]{:S(2)}, u32[]{:S(2)}) collective-permute-start(f32[64,256]{1,0:T(8,128)S(1)} %get-tuple-element.28.refs_1_), channel_id=1, source_target_pairs={{0,128},{32,160},{64,192},{96,224},{128,0},{160,32},{192,64},{224,... | collective-permute-start | bytes 196616 | tf_op jit(solution)/shard_map/ppermute | solution.py:512
  27.7 5.0 %collective-permute-start.6 = (f32[64,256]{1,0:T(8,128)S(1)}, f32[64,256]{1,0:T(8,128)S(1)}, u32[]{:S(2)}, u32[]{:S(2)}) collective-permute-start(f32[64,256]{1,0:T(8,128)S(1)} %get-tuple-element.28.refs_1_), channel_id=1, source_target_pairs={{0,64},{32,224},{64,128},{96,32},{128,192},{160,96},{192,0},{224,1... | collective-permute-start | bytes 196616 | tf_op jit(solution)/shard_map/ppermute | solution.py:513
  29.4 11.2 %collective-permute-start.5 = (f32[208,256]{1,0:T(8,128)S(1)}, f32[208,256]{1,0:T(8,128)S(1)}, u32[]{:S(2)}, u32[]{:S(2)}) collective-permute-start(f32[208,256]{1,0:T(8,128)S(1)} %get-tuple-element.29), channel_id=1, source_target_pairs={{0,224},{32,64},{64,32},{96,128},{128,96},{160,192},{192,160},{224... | collective-permute-start | bytes 638984 | tf_op jit(solution)/shard_map/ppermute | solution.py:511
  30.8 10.9 %collective-permute-start.4 = (f32[208,256]{1,0:T(8,128)S(1)}, f32[208,256]{1,0:T(8,128)S(1)}, u32[]{:S(2)}, u32[]{:S(2)}) collective-permute-start(f32[208,256]{1,0:T(8,128)S(1)} %get-tuple-element.29), channel_id=1, source_target_pairs={{0,32},{32,0},{64,96},{96,64},{128,160},{160,128},{192,224},{224,1... | collective-permute-start | bytes 638984 | tf_op jit(solution)/shard_map/ppermute | solution.py:514
  32.6 9.1 %collective-permute-start.9 = (f32[128,256]{1,0:T(8,128)S(1)}, f32[128,256]{1,0:T(8,128)S(1)}, u32[]{:S(2)}, u32[]{:S(2)}) collective-permute-start(f32[128,256]{1,0:T(8,128)S(1)} %pad_maximum_fusion.3), channel_id=1, source_target_pairs={{0,32},{32,0},{64,96},{96,64},{128,160},{160,128},{192,224},{224,1... | collective-permute-start | bytes 393224 | tf_op jit(solution)/shard_map/ppermute | solution.py:516
  40.6 2.0 %collective-permute-start.8 = (f32[64,256]{1,0:T(8,128)S(1)}, f32[64,256]{1,0:T(8,128)S(1)}, u32[]{:S(2)}, u32[]{:S(2)}) collective-permute-start(f32[64,256]{1,0:T(8,128)S(1)} %slice.20), channel_id=1, source_target_pairs={{0,32},{32,0},{64,96},{96,64},{128,160},{160,128},{192,224},{224,1... | collective-permute-start | bytes 196616 | tf_op jit(solution)/shard_map/ppermute | solution.py:515
  44.2 6.4 %collective-permute-start.10 = (f32[192,128]{1,0:T(8,128)S(1)}, f32[192,128]{1,0:T(8,128)S(1)}, u32[]{:S(2)}, u32[]{:S(2)}) collective-permute-start(f32[192,128]{1,0:T(8,128)S(1)} %get-tuple-element.31), channel_id=1, source_target_pairs={{0,1},{1,2},{2,3},{3,4},{4,5},{5,6},{6,7},{7,8},{8,9},{9,10},{10,1... | collective-permute-start | bytes 294920 | tf_op jit(solution)/shard_map/ppermute | solution.py:528
  45.7 4.8 %collective-permute-start.11 = (f32[80,128]{1,0:T(8,128)S(1)}, f32[80,128]{1,0:T(8,128)S(1)}, u32[]{:S(2)}, u32[]{:S(2)}) collective-permute-start(f32[80,128]{1,0:T(8,128)S(1)} %get-tuple-element.30.refs_1_), channel_id=1, source_target_pairs={{0,2},{1,3},{2,4},{3,5},{4,6},{5,7},{6,8},{7,9},{8,10},{9,11},{10,... | collective-permute-start | bytes 122888 | tf_op jit(solution)/shard_map/ppermute | solution.py:529
  50.5 2.9 %collective-permute-start.12 = (f32[272,128]{1,0:T(8,128)S(1)}, f32[272,128]{1,0:T(8,128)S(1)}, u32[]{:S(2)}, u32[]{:S(2)}) collective-permute-start(f32[272,128]{1,0:T(8,128)S(1)} %pad_maximum_fusion.2), channel_id=1, source_target_pairs={{0,32},{32,0},{64,96},{96,64},{128,160},{160,128},{192,224},{224,1... | collective-permute-start | bytes 417800 | tf_op jit(solution)/shard_map/ppermute | solution.py:530
